TPU v7x, 32 devices: a whole 2x2x4 slice. The times are simulated.
32 devices in a mesh: leaf: 4 (over z), ctx: 8 (over y, x, core).
Axes of the slice: x: 2, y: 2, z: 4, core: 2. Of those that a mesh axis runs over, the one named last changes fastest.
Arguments:
- queries: bfloat16 [4096, 8192], P(('leaf', 'ctx')), may hold values from -38 to 38, as said below
- seg_keys: bfloat16 [4096, 1024], P(('leaf', 'ctx')), may hold values from -6 to 6
- seg_values: bfloat16 [4096, 1024], P(('leaf', 'ctx')), may hold values from -6 to 6
- root_keys: bfloat16 [1024, 1024], P('ctx'), may hold values from -6 to 6, as said below
- root_values: bfloat16 [1024, 1024], P('ctx'), may hold values from -6 to 6
- expansion: int32 [2, 4], replicated, may hold values from 0 to 3, as said below
- root_offsets: int32 [4], replicated, may hold values from 256 to 1024
Outputs:
- attended: bfloat16 [4096, 8192], P(('leaf', 'ctx'))
Inputs may be any that keep to these rules, and one draw needn't show every extreme that they name: queries of order one, with some rows much larger. `root_keys`: keys of order one. `expansion`: group 4 - 1 is the root: it has depth 0 and is its own parent; every other group's parent has depth one less than its own.
All inputs are finite; a program needn't handle non-finite values.
Results may differ from a plain program's by a relative error of at most 0.0065.
Values may be sent and summed in bfloat16 or wider, within the bound.
No kernel may reach another device: no remote copies, remote signals or barrier semaphores. Data moves between devices by JAX's collectives and lax.ppermute only.
A program may use at most 128 MiB of HBM per device.

v0:
```python
import math

import jax
import jax.numpy as jnp
from jax import lax
from jax.sharding import PartitionSpec as P

HQ = 64
KVH = 8
HD = 128


def on_device(queries, seg_keys, seg_values, root_keys, root_values, expansion, root_offsets):
    q_rows = queries.shape[0]
    group_width = HQ // KVH
    score_scale = 1.0 / math.sqrt(HD)
    group_idx = lax.axis_index("leaf")
    part_pos = lax.axis_index("ctx")
    parent = expansion[0, group_idx]
    tree_depth = expansion[1, group_idx]
    visible = root_offsets[group_idx]
    query_pos = part_pos * q_rows + jnp.arange(q_rows, dtype=jnp.int32)
    query_heads = queries.reshape(q_rows, KVH, group_width, HD).transpose(1, 2, 0, 3)

    def attend(state_now, key_rows, value_rows, allowed):
        run_max, run_sum, run_acc = state_now
        count_keys = key_rows.shape[0]
        key_grid = key_rows.reshape(count_keys, KVH, HD)
        value_grid = value_rows.reshape(count_keys, KVH, HD)

        def head_step(unused, item):
            head_index, head_query, old_max, old_sum, old_acc = item
            head_keys = lax.dynamic_index_in_dim(key_grid, head_index, 1, keepdims=False)
            head_values = lax.dynamic_index_in_dim(value_grid, head_index, 1, keepdims=False)
            scores = (
                jnp.einsum("gqd,kd->gqk", head_query, head_keys, preferred_element_type=jnp.float32)
                * score_scale
            )
            scores = jnp.where(allowed[None], scores, -1e30)
            new_max = jnp.maximum(old_max, jnp.max(scores, axis=-1))
            shrink = jnp.exp(old_max - new_max)
            weights = jnp.where(allowed[None], jnp.exp(scores - new_max[..., None]), 0.0)
            new_sum = old_sum * shrink + jnp.sum(weights, axis=-1)
            new_acc = old_acc * shrink[..., None] + jnp.einsum(
                "gqk,kd->gqd",
                weights.astype(jnp.bfloat16),
                head_values,
                preferred_element_type=jnp.float32,
            )
            return (unused, (new_max, new_sum, new_acc))

        head_ids = jnp.arange(KVH, dtype=jnp.int32)
        unused, updated = lax.scan(head_step, 0, (head_ids, query_heads, run_max, run_sum, run_acc))
        return updated

    every_key, every_value = (
        lax.all_gather(seg_keys, "leaf", axis=0, tiled=True),
        lax.all_gather(seg_values, "leaf", axis=0, tiled=True),
    )
    parent_keys = lax.dynamic_slice_in_dim(every_key, parent * q_rows, q_rows, 0)
    parent_values = lax.dynamic_slice_in_dim(every_value, parent * q_rows, q_rows, 0)
    initial = (
        jnp.full((KVH, group_width, q_rows), -1e30, jnp.float32),
        jnp.zeros((KVH, group_width, q_rows), jnp.float32),
        jnp.zeros((KVH, group_width, q_rows, HD), jnp.float32),
    )
    key_rows = lax.all_gather(root_keys, "ctx", axis=0, tiled=True)
    value_rows = lax.all_gather(root_values, "ctx", axis=0, tiled=True)
    count_keys = key_rows.shape[0]
    key_pos = jnp.arange(count_keys, dtype=jnp.int32)
    allowed = jnp.broadcast_to((key_pos < visible)[None, :], (q_rows, count_keys))
    state_now = attend(initial, key_rows, value_rows, allowed)
    key_rows = lax.all_gather(seg_keys, "ctx", axis=0, tiled=True)
    value_rows = lax.all_gather(seg_values, "ctx", axis=0, tiled=True)
    count_keys = key_rows.shape[0]
    key_pos = jnp.arange(count_keys, dtype=jnp.int32)
    allowed = key_pos[None, :] <= query_pos[:, None]
    state_now = attend(state_now, key_rows, value_rows, allowed)
    key_rows = lax.all_gather(parent_keys, "ctx", axis=0, tiled=True)
    value_rows = lax.all_gather(parent_values, "ctx", axis=0, tiled=True)
    count_keys = key_rows.shape[0]
    allowed = jnp.broadcast_to(tree_depth > 0, (q_rows, count_keys))
    state_now = attend(state_now, key_rows, value_rows, allowed)
    run_max, run_sum, run_acc = state_now
    blended = run_acc / run_sum[..., None]
    return blended.transpose(2, 0, 1, 3).reshape(q_rows, HQ * HD).astype(jnp.bfloat16)


def solution(mesh):
    return jax.shard_map(
        on_device,
        mesh=mesh,
        in_specs=(
            P(("leaf", "ctx"), None),
            P(("leaf", "ctx"), None),
            P(("leaf", "ctx"), None),
            P("ctx", None),
            P("ctx", None),
            P(),
            P(),
        ),
        out_specs=P(("leaf", "ctx"), None),
        check_vma=False,
    )
```

profile of v0, /device:TPU:0, one launch (start us, length us, event | category | flops | bytes accessed | tf_op | source)
XLA Modules:
  0.0 358.8 jit_solution(7768883979528182031)
XLA Ops:
  17.4 24.5 %all-gather.21.cloned.1.call-done = bf16[512,1024]{0,1:T(8,128)(2,1)} async-done(((bf16[128,1024]{0,1:T(8,128)(2,1)}), bf16[512,1024]{0,1:T(8,128)(2,1)}) %all-gather.21.cloned.1.call-update) | async-done | bytes 1048592 | tf_op jit(solution)/shard_map/all_gather | solution.py:58
  46.6 3.1 copy.12
  50.9 21.1 %all-gather.17.cloned.1.call-done = bf16[512,1024]{0,1:T(8,128)(2,1)} async-done(((bf16[128,1024]{0,1:T(8,128)(2,1)}), bf16[512,1024]{0,1:T(8,128)(2,1)}) %all-gather.17.cloned.1.call-update) | async-done | bytes 1048592 | tf_op jit(solution)/shard_map/all_gather | solution.py:57
  73.6 26.7 %all-gather.9.cloned.1.call-done = bf16[1024,1024]{0,1:T(8,128)(2,1)} async-done(((bf16[128,1024]{0,1:T(8,128)(2,1)}), bf16[1024,1024]{0,1:T(8,128)(2,1)}) %all-gather.9.cloned.1.call-update) | async-done | bytes 2097168 | tf_op jit(solution)/shard_map/all_gather | solution.py:67
  100.4 30.0 %all-gather.11.cloned.1.call-done = bf16[1024,1024]{0,1:T(8,128)(2,1)} async-done(((bf16[128,1024]{0,1:T(8,128)(2,1)}), bf16[1024,1024]{0,1:T(8,128)(2,1)}) %all-gather.11.cloned.1.call-update) | async-done | bytes 2097168 | tf_op jit(solution)/shard_map/all_gather | solution.py:68
  132.8 66.7 %while.43 = (s32[]{:T(128)}, f32[8,8,128]{2,1,0:T(8,128)S(1)}, f32[8,8,128]{2,1,0:T(8,128)S(1)}, f32[8,8,128,128]{3,2,1,0:T(8,128)}, bf16[8,8,128,128]{3,2,1,0:T...) while((s32[]{:T(128)}, f32[8,8,128]{2,1,0:T(8,128)S(1)}, ...), condition=%wide.region_3.4_spmd.clone, body=%wide.region_0.3_spmd.clone.sunk | while | flops 550638592 | bytes 13947055 | solution.py:53
  145.4 2.8 fusion.124
  153.7 2.8 fusion.124
  162.1 2.9 fusion.124
  170.5 2.8 fusion.124
  178.8 2.8 fusion.124
  187.1 2.8 fusion.124
  202.1 71.5 %while.44 = (s32[]{:T(128)}, f32[8,8,128]{2,1,0:T(8,128)S(1)}, f32[8,8,128]{2,1,0:T(8,128)S(1)}, f32[8,8,128,128]{3,2,1,0:T(8,128)}, f32[8,8,128]{2,1,0:T(8,128)...) while((s32[]{:T(128)}, f32[8,8,128]{2,1,0:T(8,128)S(1)}, ...), condition=%wide.region_7.8_spmd.clone, body=%wide.region_4.7_spmd.clone.sunk | while | flops 550899712 | bytes 15005387 | solution.py:53
  206.4 3.3 fusion.131
  215.3 3.3 fusion.131
  224.3 3.3 fusion.131
  233.2 3.3 fusion.131
  242.2 3.3 fusion.131
  251.1 3.3 fusion.131
  260.0 3.3 fusion.131
  269.0 3.3 fusion.131
  276.2 68.2 %while.45 = (s32[]{:T(128)}, f32[8,8,128]{2,1,0:T(8,128)S(1)}, f32[8,8,128,128]{3,2,1,0:T(8,128)}, f32[8,8,128]{2,1,0:T(8,128)S(1)}, f32[8,8,128]{2,1,0:T(8,128)...) while((s32[]{:T(128)}, f32[8,8,128]{2,1,0:T(8,128)S(1)}, ...), condition=%wide.region_11.12_spmd.clone, body=%wide.region_8.11_spmd.clone.sunk | while | flops 550768640 | bytes 14477508 | solution.py:53
  280.4 3.0 fusion.138
  289.0 3.0 fusion.138
  297.5 3.0 fusion.138
  306.0 3.0 fusion.138
  314.6 3.0 fusion.138
  323.1 3.0 fusion.138
  331.6 3.0 fusion.138
  340.2 3.0 fusion.138
  344.4 3.0 fusion.98
  348.8 3.1 copy.34
  (177 shorter events, 120.2 us)
Async XLA Ops:
  6.5 37.1 %copy-start.1 = (s32[4]{0:T(128)S(1)}, s32[4]{0:T(128)}, u32[]{:S(2)}) copy-start(s32[4]{0:T(128)} %param.19) | copy-start | bytes 52
  6.5 37.6 %copy-start = (bf16[128,8192]{1,0:T(8,128)(2,1)S(1)}, bf16[128,8192]{1,0:T(8,128)(2,1)}, u32[]{:S(2)}) copy-start(bf16[128,8192]{1,0:T(8,128)(2,1)} %param.13) | copy-start | bytes 6291460
  6.5 35.3 %all-gather.21.cloned.1.call-start = ((), (), s32[]{:S(2)}) async-start(), calls=%async_computation.6 | async-start | bytes 1310720 | tf_op jit(solution)/shard_map/all_gather | solution.py:58
  8.5 63.4 %all-gather.17.cloned.1.call-start = ((), (), s32[]{:S(2)}) async-start(), calls=%async_computation.4 | async-start | bytes 1310720 | tf_op jit(solution)/shard_map/all_gather | solution.py:57
  10.4 90.0 %all-gather.9.cloned.1.call-start = ((), (), s32[]{:S(2)}) async-start(), calls=%async_computation | async-start | bytes 2359296 | tf_op jit(solution)/shard_map/all_gather | solution.py:67
  12.2 118.1 %all-gather.11.cloned.1.call-start = ((), (), s32[]{:S(2)}) async-start(), calls=%async_computation.1 | async-start | bytes 2359296 | tf_op jit(solution)/shard_map/all_gather | solution.py:68
  14.1 185.5 %all-gather.13.cloned.1.call-start = ((), (), s32[]{:S(2)}) async-start(), calls=%async_computation.2 | async-start | bytes 2359296 | tf_op jit(solution)/shard_map/all_gather | solution.py:73
  14.7 184.9 %all-gather.15.cloned.1.call-start = ((), (), s32[]{:S(2)}) async-start(), calls=%async_computation.3 | async-start | bytes 2359296 | tf_op jit(solution)/shard_map/all_gather | solution.py:74
  15.3 258.4 %all-gather.23.cloned.1.call-start = ((), (), s32[]{:S(2)}) async-start(), calls=%async_computation.7 | async-start | bytes 2359296 | tf_op jit(solution)/shard_map/all_gather | solution.py:80
  43.5 230.1 %all-gather.19.cloned.1.call-start = ((), (), s32[]{:S(2)}) async-start(), calls=%async_computation.5 | async-start | bytes 2359296 | tf_op jit(solution)/shard_map/all_gather | solution.py:79
Sparse Core Ops, SparseCore 0:
  8.9 32.8 all-gather.20
  43.4 28.4 all-gather.16
  73.8 26.4 all-gather.8
  102.1 28.1 all-gather.10
  132.1 28.1 all-gather.12
  162.0 28.1 all-gather.14
  192.1 28.1 all-gather.22
  222.2 28.2 all-gather.18
where the time goes:
time: 361 us; the launch traced here: 359 us
  matrix products  116 us (32%)
  waiting for transfers between devices  103 us (29%)
  loops' own time  44.9 us (12%)
  local copies, waits for them, and re-layouts  44.3 us (12%)
  other arithmetic  35.1 us (10%)
  between operations  14.9 us (4%)
    dot_general x24, matrix products, head_step(): jnp.einsum('gqk,kd->gqd', weights.astype(jnp.bfloat16), head_values, pref...  72.9 us
    another operation x3, loops' own time, attend(): lax.scan(head_step, 0, (head_ids, query_heads, run_max, run_sum, run_acc))  44.9 us
    dot_general x24, matrix products, head_step(): jnp.einsum('gqd,kd->gqk', head_query, head_keys, preferred_element_type=j...  42.9 us
    all_gather x1, waiting for transfers between devices, on_device(): value_rows = lax.all_gather(root_values, 'ctx', axis=0, tiled=True)  30 us
    reduce_sum x24, other arithmetic, head_step(): new_sum = old_sum * shrink + jnp.sum(weights, axis=-1)  29.7 us
    all_gather x1, waiting for transfers between devices, on_device(): key_rows = lax.all_gather(root_keys, 'ctx', axis=0, tiled=True)  26.7 us
    all_gather x1, waiting for transfers between devices, on_device(): lax.all_gather(seg_values, 'leaf', axis=0, tiled=True)  24.5 us
    all_gather x1, waiting for transfers between devices, on_device(): lax.all_gather(seg_keys, 'leaf', axis=0, tiled=True)  21.1 us
  transfers between devices with their start and end apart: 8, of which 4 were waited for; matrix products, arithmetic and copies ran while one was open for 36% of the time, Pallas kernels for 0%

commit v1 on v0

v1 whole, which is shorter than its diff:
```python
import functools
import math

import jax
import jax.numpy as jnp
from jax import lax
from jax.experimental import pallas as pl
from jax.experimental.pallas import tpu as pltpu
from jax.sharding import PartitionSpec as P

HQ = 64
KVH = 8
HD = 128
GW = HQ // KVH
HALF_KV = KVH // 2
NEG = -1e30
Q_SCALE = math.log2(math.e) / math.sqrt(HD)
ROW_BLOCK = 512


def attend_kernel(ny, rows, groups, first, last, *refs):
    refs = list(refs)
    exp_ref, off_ref, q0_ref, q1_ref = refs[:4]
    refs = refs[4:]
    key_refs, value_refs = [], []
    for parts in groups:
        key_refs.append([refs.pop(0) for _ in parts])
        value_refs.append([refs.pop(0) for _ in parts])
    if not first:
        acc_in, ml_in = refs.pop(0), refs.pop(0)
    if last:
        outs = [refs.pop(0), refs.pop(0)]
    else:
        acc_out, ml_out = refs.pop(0), refs.pop(0)
    qs, accs, ms = refs
    stacked = GW * rows

    group = lax.axis_index("leaf")
    spot = lax.axis_index("ctx")
    core, chip = lax.rem(spot, 2), spot // 2
    chip_x, chip_y = lax.rem(chip, 2), chip // 2
    visible = off_ref[group]
    depth = exp_ref[1, group]

    def block_start(dx, dy, flip):
        x = lax.rem(chip_x + dx, 2)
        y = lax.rem(chip_y - dy + ny, ny)
        k = lax.rem(core + flip, 2)
        return ((y * 2 + x) * 2 + k) * rows

    for s, q_ref in enumerate((q0_ref, q1_ref)):
        for g in range(GW):
            q = q_ref[:, g * HD : (g + 1) * HD].astype(jnp.float32) * Q_SCALE
            high = q.astype(jnp.bfloat16)
            low = (q - high.astype(jnp.float32)).astype(jnp.bfloat16)
            qs[s, g * rows : (g + 1) * rows, :HD] = high
            qs[s, g * rows : (g + 1) * rows, HD:] = low
    if first:
        accs[...] = jnp.zeros_like(accs)
        ms[...] = jnp.full_like(ms, NEG)
    else:
        for s in range(2):
            accs[s, :, :HD] = acc_in[0, s]
            ml = ml_in[0, s]
            accs[s, :, HD:] = jnp.broadcast_to(ml[:, HD - 1 :], ml.shape)
            ms[s] = jnp.broadcast_to(ml[:, :1], ml.shape)

    for parts, k_refs, v_refs in zip(groups, key_refs, value_refs):
        blocks = [block for part in parts for block in part]
        width = len(blocks) * rows
        for s in range(2):
            first_row = block_start(0, 0, s)
            limits = []
            full, some = jnp.bool_(True), jnp.bool_(False)
            for kind, dx, dy, flip in blocks:
                if kind == "root":
                    limit = visible - block_start(dx, dy, flip)
                    some_here = limit > 0
                elif kind == "own":
                    limit = first_row - block_start(dx, dy, flip) + 1
                    some_here = limit + rows - 1 > 0
                else:
                    limit = jnp.where(depth > 0, rows, 0)
                    some_here = limit > 0
                limits.append(limit)
                full = full & (limit >= rows)
                some = some | some_here

            def step(masked):
                keys = jnp.concatenate([ref[...] for ref in k_refs], axis=0)
                keys = jnp.concatenate([keys, keys], axis=1)
                values = jnp.concatenate([ref[...] for ref in v_refs], axis=0)
                values = jnp.concatenate([values, jnp.ones_like(values)], axis=1)
                for base in range(0, stacked, ROW_BLOCK):
                    size = min(ROW_BLOCK, stacked)
                    here = slice(base, base + size)
                    scores = lax.dot_general(
                        qs[s, here, :], keys, (((1,), (1,)), ((), ())), preferred_element_type=jnp.float32
                    )
                    if masked:
                        column = lax.broadcasted_iota(jnp.int32, (rows, rows), 1)
                        line = lax.broadcasted_iota(jnp.int32, (rows, rows), 0)
                        allowed = []
                        for (kind, *_), limit in zip(blocks, limits):
                            ahead = column - line if kind == "own" else column
                            allowed.append(jnp.where(ahead < limit, 0.0, NEG))
                        bias = jnp.concatenate(allowed, axis=1)
                        scores = scores + jnp.concatenate([bias] * (size // rows), axis=0)
                    old = ms[s, here, :]
                    new = jnp.maximum(old, jnp.max(scores, axis=1, keepdims=True))
                    weights = jnp.exp2(scores - jnp.concatenate([new] * (width // HD), axis=1))
                    update = jnp.dot(weights.astype(jnp.bfloat16), values, preferred_element_type=jnp.float32)
                    shrink = jnp.exp2(old - new)
                    accs[s, here, :] = accs[s, here, :] * jnp.concatenate([shrink, shrink], axis=1) + update
                    ms[s, here, :] = new

            @pl.when(full)
            def _():
                step(False)

            @pl.when(jnp.logical_not(full) & some)
            def _():
                step(True)

    for s in range(2):
        if last:
            done = (accs[s, :, :HD] / accs[s, :, HD:]).astype(jnp.bfloat16)
            for g in range(GW):
                outs[s][:, g * HD : (g + 1) * HD] = done[g * rows : (g + 1) * rows]
        else:
            acc_out[0, s] = accs[s, :, :HD]
            lane = lax.broadcasted_iota(jnp.int32, (stacked, HD), 1)
            ml_out[0, s] = jnp.where(lane < HD // 2, ms[s], accs[s, :, HD:])


def attend(ny, q_pair, tables, groups, state, last):
    rows = q_pair[0].shape[0]
    stacked = GW * rows
    first = state is None
    smem = pl.BlockSpec(memory_space=pltpu.SMEM)
    q_spec = pl.BlockSpec((rows, GW * HD), lambda h: (0, h))
    state_spec = pl.BlockSpec((1, 2, stacked, HD), lambda h: (h, 0, 0, 0))
    operands = [*tables, *q_pair]
    specs = [smem, smem, q_spec, q_spec]
    total = 0
    for parts in groups:
        for shift in (0, HALF_KV):
            for array, _ in parts:
                operands.append(array)
                specs.append(pl.BlockSpec((array.shape[0], HD), functools.partial(lambda s, h: (0, s + h), shift)))
        total += sum(array.shape[0] for array, _ in parts)
    if not first:
        operands += list(state)
        specs += [state_spec, state_spec]
    if last:
        out_shape = [jax.ShapeDtypeStruct((rows, HALF_KV * GW * HD), jnp.bfloat16)] * 2
        out_specs = [q_spec, q_spec]
    else:
        out_shape = [jax.ShapeDtypeStruct((HALF_KV, 2, stacked, HD), jnp.float32)] * 2
        out_specs = [state_spec, state_spec]
    scores = HALF_KV * 2 * stacked * total
    return pl.pallas_call(
        functools.partial(
            attend_kernel, ny, rows, tuple(tuple(b for _, b in parts) for parts in groups), first, last
        ),
        grid=(HALF_KV,),
        in_specs=specs,
        out_specs=out_specs,
        out_shape=out_shape,
        scratch_shapes=[
            pltpu.VMEM((2, stacked, 2 * HD), jnp.bfloat16),
            pltpu.VMEM((2, stacked, 2 * HD), jnp.float32),
            pltpu.VMEM((2, stacked, HD), jnp.float32),
        ],
        compiler_params=pltpu.CompilerParams(vmem_limit_bytes=48 * 2**20),
        cost_estimate=pl.CostEstimate(flops=8 * scores * HD, bytes_accessed=20 * 2**20, transcendentals=scores),
    )(*operands)


def on_device(queries, seg_keys, seg_values, root_keys, root_values, expansion, root_offsets):
    leaves, spots = lax.axis_size("leaf"), lax.axis_size("ctx")
    ny = spots // 4
    rows = queries.shape[0]
    group = lax.axis_index("leaf")
    core = lax.rem(lax.axis_index("ctx"), 2)

    def halves(array):
        half = array.shape[1] // 2
        return (
            lax.dynamic_slice_in_dim(array, core * half, half, 1),
            lax.dynamic_slice_in_dim(array, (1 - core) * half, half, 1),
        )

    def index(x, y, k):
        return ((y % ny) * 2 + x % 2) * 2 + k % 2

    places = [(x, y, k) for y in range(ny) for x in range(2) for k in range(2)]

    def to_core(array):
        return lax.ppermute(array, "ctx", [(index(x, y, k), index(x, y, k + 1)) for x, y, k in places])

    def to_x(array):
        return lax.ppermute(array, "ctx", [(index(x, y, k), index(x + 1, y, k)) for x, y, k in places])

    def to_y(array, step):
        return lax.ppermute(array, "ctx", [(index(x, y, k), index(x, y + step, k)) for x, y, k in places])

    def packed(keys, values):
        (key_mine, key_other), (value_mine, value_other) = halves(keys), halves(values)
        return jnp.concatenate([key_mine, value_mine], axis=1), jnp.concatenate([key_other, value_other], axis=1)

    own_mine, own_other = packed(seg_keys, seg_values)
    root_mine, root_other = packed(root_keys, root_values)
    got = to_core(jnp.concatenate([own_other, root_other], axis=0))
    q_mine, q_other = halves(queries)
    q_pair = (q_mine, to_core(q_other))
    tables = (expansion, root_offsets)
    local = jnp.concatenate([own_mine, root_mine, got], axis=0)
    segment = jnp.concatenate([own_mine, got[:rows]], axis=0)

    def blocks(dx, dy, flips=(0, 1), kinds=("own", "root")):
        return tuple((kind, dx, dy, flip) for flip in flips for kind in kinds)

    parent = expansion[0, group]
    parent_rows = segment
    up, down = segment, segment
    for step in range(1, leaves):
        down = lax.ppermute(down, "leaf", [(i, i - 1) for i in range(1, leaves - step + 1)])
        parent_rows = jnp.where(parent == group + step, down, parent_rows)
        if step < leaves - 1:
            up = lax.ppermute(up, "leaf", [(i, i + 1) for i in range(step - 1, leaves - 2)])
            parent_rows = jnp.where(parent == group - step, up, parent_rows)

    state = attend(ny, q_pair, tables, [[(local, blocks(0, 0))]], None, False)
    from_x = to_x(local)
    from_y = [to_y(local, step) for step in range(1, ny)]
    near = [[(from_x, blocks(1, 0))]] + [[(a, blocks(0, i + 1))] for i, a in enumerate(from_y)]
    state = attend(ny, q_pair, tables, near, state, False)
    far = []
    for step in range(1, ny):
        top = to_y(from_x[: 2 * rows], step)
        low = to_x(from_y[step - 1][2 * rows :])
        far.append([(top, blocks(1, step, (0,))), (low, blocks(1, step, (1,)))])
    kin = (("kin", 0, 0, 0),)
    far.append([(parent_rows, kin * 2)])
    state = attend(ny, q_pair, tables, far, state, False)
    kin_x = to_x(parent_rows)
    kin_y = [to_y(parent_rows, step) for step in range(1, ny)]
    groups = [[(kin_x, kin * 2), (kin_y[0], kin * 2)]] + [[(a, kin * 2)] for a in kin_y[1:]]
    for step in range(1, ny):
        top = to_y(kin_x[:rows], step)
        low = to_x(kin_y[step - 1][rows:])
        groups.append([(top, kin), (low, kin)])
    out_mine, out_other = attend(ny, q_pair, tables, groups, state, True)
    out_got = to_core(out_other)
    return jnp.where(
        core == 0,
        jnp.concatenate([out_mine, out_got], axis=1),
        jnp.concatenate([out_got, out_mine], axis=1),
    )


def solution(mesh):
    return jax.shard_map(
        on_device,
        mesh=mesh,
        in_specs=(
            P(("leaf", "ctx"), None),
            P(("leaf", "ctx"), None),
            P(("leaf", "ctx"), None),
            P("ctx", None),
            P("ctx", None),
            P(),
            P(),
        ),
        out_specs=P(("leaf", "ctx"), None),
        check_vma=False,
    )
```

time: 361 us -> 140 us (0.39)
  the two profiles are of different devices: /device:TPU:0 before, /device:TPU:13 now
where the time goes in v1:
time: 140 us
  Pallas kernels  71.8 us (51%)
  starting transfers between devices  34 us (24%)
  waiting for transfers between devices  18.7 us (13%)
  local copies, waits for them, and re-layouts  7.65 us (5%)
  other arithmetic  4.47 us (3%)
  between operations  3.32 us (2%)
    pallas_call x4, Pallas kernels, attend(): pl.pallas_call(functools.partial(attend_kernel, ny, rows, tuple((tuple((b...  71.8 us
    ppermute x4, starting transfers between devices, to_x(): lax.ppermute(array, 'ctx', [(index(x, y, k), index(x + 1, y, k)) for x, y...  12.2 us
    ppermute x3, waiting for transfers between devices, on_device(): lax.ppermute(down, 'leaf', [(i, i - 1) for i in range(1, leaves - step +...  12.2 us
    ppermute x2, starting transfers between devices, on_device(): lax.ppermute(up, 'leaf', [(i, i + 1) for i in range(step - 1, leaves - 2)])  7.21 us
    ppermute x3, starting transfers between devices, on_device(): lax.ppermute(down, 'leaf', [(i, i - 1) for i in range(1, leaves - step +...  7.11 us
    ppermute x3, starting transfers between devices, to_core(): lax.ppermute(array, 'ctx', [(index(x, y, k), index(x, y, k + 1)) for x, y...  5.09 us
    ppermute x3, waiting for transfers between devices, to_core(): lax.ppermute(array, 'ctx', [(index(x, y, k), index(x, y, k + 1)) for x, y...  4.04 us
    dynamic_slice x2, local copies, waits for them, and re-layouts, halves(): lax.dynamic_slice_in_dim(array, core * half, half, 1)  3.13 us
  transfers between devices with their start and end apart: 16, of which 6 were waited for; matrix products, arithmetic and copies ran while one was open for 3% of the time, Pallas kernels for 35%

profile of v1, /device:TPU:13, one launch (start us, length us, event | category | flops | bytes accessed | tf_op | source)
XLA Modules:
  0.0 140.0 jit_solution(15113669687187543413)
XLA Ops:
  0.0 1.8 %constant_dynamic-slice_fusion = (bf16[128,512]{1,0:T(8,128)(2,1)}, bf16[128,512]{1,0:T(8,128)(2,1)S(1)}, bf16[128,512]{1,0:T(8,128)(2,1)S(1)}, bf16[128,512]{1,0:T(8,128)(2,1)}) fusion(bf16[128,1024]{1,0:T(8,128)(2,1)} %param.11, s32[]{:T(128)S(6)} %select_n.66, s32[]{:T(128)S(6)} %select_n.67, bf16[128,1024]{1,0:T(8,128)(2,1)} %param.10), kind=kLoop, calls=%fused_computation.5 | loop fusion | bytes 1048584 | tf_op jit(solution)/shard_map/dynamic_slice | solution.py:190
  1.8 1.3 constant_dynamic-slice_fusion.6
  3.1 0.9 maximum_maximum_fusion
  4.0 0.7 collective-permute-start.1
  4.7 1.7 %collective-permute-done.1 = bf16[256,1024]{1,0:T(8,128)(2,1)S(1)} collective-permute-done((bf16[256,1024]{1,0:T(8,128)(2,1)}, bf16[256,1024]{1,0:T(8,128)(2,1)S(1)}, u32[]{:S(2)}, u32[]{:S(2)}) %collective-permute-start.1) | collective-permute-done | bytes 524320 | tf_op jit(solution)/shard_map/ppermute | solution.py:200
  6.5 0.7 copy-done.6
  7.2 2.2 %collective-permute-start.2 = (bf16[256,1024]{1,0:T(8,128)(2,1)S(1)}, bf16[256,1024]{1,0:T(8,128)(2,1)S(1)}, u32[]{:S(2)}, u32[]{:S(2)}) collective-permute-start(bf16[256,1024]{1,0:T(8,128)(2,1)S(1)} %pad_maximum_fusion.1), channel_id=1, source_target_pairs={{8,0},{16,8},{24,16},{9,1},{17,9},{25,17},{10,2},{18,10},{26,18},{... | collective-permute-start | bytes 1572872 | tf_op jit(solution)/shard_map/ppermute | solution.py:228
  9.5 1.2 constant_dynamic-slice_fusion.9
  10.6 0.7 collective-permute-start
  11.4 1.3 collective-permute-start.11
  12.9 3.2 %collective-permute-start.5 = (bf16[256,1024]{1,0:T(8,128)(2,1)S(1)}, bf16[256,1024]{1,0:T(8,128)(2,1)}, u32[]{:S(2)}, u32[]{:S(2)}) collective-permute-start(bf16[256,1024]{1,0:T(8,128)(2,1)S(1)} %pad_maximum_fusion.1), channel_id=1, source_target_pairs={{0,8},{8,16},{1,9},{9,17},{2,10},{10,18},{3,11},{11,19},{4,12},{12... | collective-permute-start | bytes 1572872 | tf_op jit(solution)/shard_map/ppermute | solution.py:231
  16.1 6.4 %collective-permute-done.2 = bf16[256,1024]{1,0:T(8,128)(2,1)S(1)} collective-permute-done((bf16[256,1024]{1,0:T(8,128)(2,1)S(1)}, bf16[256,1024]{1,0:T(8,128)(2,1)S(1)}, u32[]{:S(2)}, u32[]{:S(2)}) %collective-permute-start.2) | collective-permute-done | bytes 524320 | tf_op jit(solution)/shard_map/ppermute | solution.py:228
  22.5 0.8 copy-done.8
  23.3 2.1 %collective-permute-start.3 = (bf16[256,1024]{1,0:T(8,128)(2,1)S(1)}, bf16[256,1024]{1,0:T(8,128)(2,1)}, u32[]{:S(2)}, u32[]{:S(2)}) collective-permute-start(bf16[256,1024]{1,0:T(8,128)(2,1)S(1)} %collective-permute-done.2), channel_id=1, source_target_pairs={{8,0},{16,8},{9,1},{17,9},{10,2},{18,10},{11,3},{19,11},{12,4},{20... | collective-permute-start | bytes 1572872 | tf_op jit(solution)/shard_map/ppermute | solution.py:228
  25.4 2.4 %collective-permute-done.5 = bf16[256,1024]{1,0:T(8,128)(2,1)} collective-permute-done((bf16[256,1024]{1,0:T(8,128)(2,1)S(1)}, bf16[256,1024]{1,0:T(8,128)(2,1)}, u32[]{:S(2)}, u32[]{:S(2)}) %collective-permute-start.5) | collective-permute-done | bytes 524320 | tf_op jit(solution)/shard_map/ppermute | solution.py:231
  27.8 4.0 %collective-permute-start.6 = (bf16[256,1024]{1,0:T(8,128)(2,1)}, bf16[256,1024]{1,0:T(8,128)(2,1)}, u32[]{:S(2)}, u32[]{:S(2)}) collective-permute-start(bf16[256,1024]{1,0:T(8,128)(2,1)} %collective-permute-done.5), channel_id=1, source_target_pairs={{8,16},{9,17},{10,18},{11,19},{12,20},{13,21},{14,22},{15,23}} | collective-permute-start | bytes 1572872 | tf_op jit(solution)/shard_map/ppermute | solution.py:231
  31.8 5.8 %collective-permute-done.3 = bf16[256,1024]{1,0:T(8,128)(2,1)} collective-permute-done((bf16[256,1024]{1,0:T(8,128)(2,1)S(1)}, bf16[256,1024]{1,0:T(8,128)(2,1)}, u32[]{:S(2)}, u32[]{:S(2)}) %collective-permute-start.3) | collective-permute-done | bytes 524320 | tf_op jit(solution)/shard_map/ppermute | solution.py:228
  37.6 2.8 %collective-permute-start.4 = (bf16[256,1024]{1,0:T(8,128)(2,1)}, bf16[256,1024]{1,0:T(8,128)(2,1)}, u32[]{:S(2)}, u32[]{:S(2)}) collective-permute-start(bf16[256,1024]{1,0:T(8,128)(2,1)} %collective-permute-done.3), channel_id=1, source_target_pairs={{8,0},{9,1},{10,2},{11,3},{12,4},{13,5},{14,6},{15,7}} | collective-permute-start | bytes 1572872 | tf_op jit(solution)/shard_map/ppermute | solution.py:228
  40.5 0.6 constant_dynamic-slice_fusion.8
  44.2 9.7 %shard_map.73 = (f32[4,2,1024,128]{3,2,1,0:T(8,128)}, f32[4,2,1024,128]{3,2,1,0:T(8,128)}) custom-call(s32[2,4]{1,0:T(2,128)S(1)} %copy-done, s32[4]{0:T(128)S(1)} %copy-done.1, bf16[128,4096]{1,0:T(8,128)(2,1)S(1)} %get-tuple-element.22.refs_2_, bf16[128,4096]{1,0:T(8,128)(2,1)} %collective-permute-done.refs_3_, ...), custom_call_target="tpu_custom_call" | custom-call | flops 4294967296 | bytes 20971520 | tf_op jit(solution)/shard_map/pallas_call | solution.py:162
  53.9 0.8 collective-permute-start.12
  54.8 1.1 slice.24
  55.8 0.8 collective-permute-start.14
  56.6 1.7 %select_select_fusion.refs_8_.refs_9_ = bf16[256,1024]{1,0:T(8,128)(2,1)S(1)} fusion(bf16[256,1024]{1,0:T(8,128)(2,1)} %collective-permute-done.4, bf16[256,1024]{1,0:T(8,128)(2,1)} %collective-permute-done.6, bf16[256,1024]{1,0:T(8,128)(2,1)} %collective-permute-done.3, bf16[256,1024]{1,0:T(8,128)(2,1)} %collective-permute-done.5, ...), kind=kLoop, calls=%fused_computation.4 | loop fusion | flops 2883584 | bytes 3670021 | tf_op jit(solution)/shard_map/jit(_where)/select_n | solution.py:229
  58.3 1.3 collective-permute-start.8
  59.9 16.4 %shard_map.74 = (f32[4,2,1024,128]{3,2,1,0:T(8,128)}, f32[4,2,1024,128]{3,2,1,0:T(8,128)}) custom-call(s32[2,4]{1,0:T(2,128)S(1)} %copy-done, s32[4]{0:T(128)S(1)} %copy-done.1, bf16[128,4096]{1,0:T(8,128)(2,1)S(1)} %get-tuple-element.22.refs_2_, bf16[128,4096]{1,0:T(8,128)(2,1)} %collective-permute-done.refs_3_, ...), custom_call_target="tpu_custom_call" | custom-call | flops 8589934592 | bytes 20971520 | tf_op jit(solution)/shard_map/pallas_call | solution.py:162
  76.4 9.9 %collective-permute-start.10 = (bf16[128,1024]{1,0:T(8,128)(2,1)S(1)}, bf16[128,1024]{1,0:T(8,128)(2,1)S(1)}, u32[]{:S(2)}, u32[]{:S(2)}) collective-permute-start(bf16[128,1024]{1,0:T(8,128)(2,1)S(1)} %slice.22), channel_id=1, source_target_pairs={{0,2},{1,3},{2,0},{3,1},{4,6},{5,7},{6,4},{7,5},{8,10},{9,11},{10,... | collective-permute-start | bytes 786440 | tf_op jit(solution)/shard_map/ppermute | solution.py:203
  86.4 23.5 %shard_map.75 = (f32[4,2,1024,128]{3,2,1,0:T(8,128)}, f32[4,2,1024,128]{3,2,1,0:T(8,128)}) custom-call(s32[2,4]{1,0:T(2,128)S(1)} %copy-done, s32[4]{0:T(128)S(1)} %copy-done.1, bf16[128,4096]{1,0:T(8,128)(2,1)S(1)} %get-tuple-element.22.refs_2_, bf16[128,4096]{1,0:T(8,128)(2,1)} %collective-permute-done.refs_3_, ...), custom_call_target="tpu_custom_call" | custom-call | flops 6442450944 | bytes 20971520 | tf_op jit(solution)/shard_map/pallas_call | solution.py:162
  109.9 22.3 %shard_map.76 = (bf16[128,4096]{1,0:T(8,128)(2,1)S(1)}, bf16[128,4096]{1,0:T(8,128)(2,1)S(1)}) custom-call(s32[2,4]{1,0:T(2,128)S(1)} %copy-done, s32[4]{0:T(128)S(1)} %copy-done.1, bf16[128,4096]{1,0:T(8,128)(2,1)S(1)} %get-tuple-element.22.refs_2_, bf16[128,4096]{1,0:T(8,128)(2,1)} %collective-permute-done.refs_3_, ...), custom_call_target="tpu_custom_call" | custom-call | flops 6442450944 | bytes 20971520 | tf_op jit(solution)/shard_map/pallas_call | solution.py:162
  132.2 3.8 %collective-permute-start.15 = (bf16[128,4096]{1,0:T(8,128)(2,1)S(1)}, bf16[128,4096]{1,0:T(8,128)(2,1)S(1)}, u32[]{:S(2)}, u32[]{:S(2)}) collective-permute-start(bf16[128,4096]{1,0:T(8,128)(2,1)S(1)} %get-tuple-element.20), channel_id=1, source_target_pairs={{0,1},{1,0},{2,3},{3,2},{4,5},{5,4},{6,7},{7,6},{8,9},{9,8},{10,11... | collective-permute-start | bytes 3145736 | tf_op jit(solution)/shard_map/ppermute | solution.py:200
  135.9 2.3 %collective-permute-done.15 = bf16[128,4096]{1,0:T(8,128)(2,1)S(1)} collective-permute-done((bf16[128,4096]{1,0:T(8,128)(2,1)S(1)}, bf16[128,4096]{1,0:T(8,128)(2,1)S(1)}, u32[]{:S(2)}, u32[]{:S(2)}) %collective-permute-start.15) | collective-permute-done | bytes 1048608 | tf_op jit(solution)/shard_map/ppermute | solution.py:200
  138.2 1.8 %maximum_select_fusion = bf16[128,8192]{1,0:T(8,128)(2,1)} fusion(bf16[128,4096]{1,0:T(8,128)(2,1)S(1)} %collective-permute-done.15, bf16[128,4096]{1,0:T(8,128)(2,1)S(1)} %get-tuple-element.19, pred[]{:T(512)S(6)} %eq.18), kind=kLoop, calls=%fused_computation | loop fusion | flops 9437184 | bytes 4194305 | tf_op jit(solution)/shard_map/jit(_where)/select_n | solution.py:256
  (42 shorter events, 0.9 us)
Async XLA Ops:
  1.8 7.6 %copy-start.2 = (bf16[128,8192]{1,0:T(8,128)(2,1)S(1)}, bf16[128,8192]{1,0:T(8,128)(2,1)}, u32[]{:S(2)}) copy-start(bf16[128,8192]{1,0:T(8,128)(2,1)} %param.7) | copy-start | bytes 6291460
  3.1 3.4 %copy-start.3 = (bf16[128,512]{1,0:T(8,128)(2,1)}, bf16[128,512]{1,0:T(8,128)(2,1)S(1)}, u32[]{:S(2)}) copy-start(bf16[128,512]{1,0:T(8,128)(2,1)S(1)} %get-tuple-element.34) | copy-start | bytes 393220
  4.0 2.4 %collective-permute-start.1 = (bf16[256,1024]{1,0:T(8,128)(2,1)}, bf16[256,1024]{1,0:T(8,128)(2,1)S(1)}, u32[]{:S(2)}, u32[]{:S(2)}) collective-permute-start(bf16[256,1024]{1,0:T(8,128)(2,1)} %maximum_maximum_fusion), channel_id=1, source_target_pairs={{0,1},{1,0},{2,3},{3,2},{4,5},{5,4},{6,7},{7,6},{8,9},{9,8},{10,11... | collective-permute-start | bytes 1572872 | tf_op jit(solution)/shard_map/ppermute | solution.py:200
  6.4 0.8 copy-start.6
  7.2 4.1 %copy-start.10 = (bf16[128,512]{1,0:T(8,128)(2,1)S(1)}, bf16[128,512]{1,0:T(8,128)(2,1)}, u32[]{:S(2)}) copy-start(bf16[128,512]{1,0:T(8,128)(2,1)} %get-tuple-element.25) | copy-start | bytes 393220
  7.2 4.1 %copy-start.11 = (bf16[128,512]{1,0:T(8,128)(2,1)S(1)}, bf16[128,512]{1,0:T(8,128)(2,1)}, u32[]{:S(2)}) copy-start(bf16[128,512]{1,0:T(8,128)(2,1)} %get-tuple-element.32) | copy-start | bytes 393220
  7.2 15.3 %collective-permute-start.2 = (bf16[256,1024]{1,0:T(8,128)(2,1)S(1)}, bf16[256,1024]{1,0:T(8,128)(2,1)S(1)}, u32[]{:S(2)}, u32[]{:S(2)}) collective-permute-start(bf16[256,1024]{1,0:T(8,128)(2,1)S(1)} %pad_maximum_fusion.1), channel_id=1, source_target_pairs={{8,0},{16,8},{24,16},{9,1},{17,9},{25,17},{10,2},{18,10},{26,18},{... | collective-permute-start | bytes 1572872 | tf_op jit(solution)/shard_map/ppermute | solution.py:228
  9.5 1.8 %copy-start.4 = (bf16[128,512]{1,0:T(8,128)(2,1)S(1)}, bf16[128,512]{1,0:T(8,128)(2,1)}, u32[]{:S(2)}) copy-start(bf16[128,512]{1,0:T(8,128)(2,1)} %copy-done.3) | copy-start | bytes 393220
  9.5 1.8 %copy-start.7 = (bf16[256,1024]{1,0:T(8,128)(2,1)S(1)}, bf16[256,1024]{1,0:T(8,128)(2,1)}, u32[]{:S(2)}) copy-start(bf16[256,1024]{1,0:T(8,128)(2,1)} %copy-done.6) | copy-start | bytes 1572868
  10.6 29.8 %copy-start = (s32[2,4]{1,0:T(2,128)S(1)}, s32[2,4]{1,0:T(2,128)}, u32[]{:S(2)}) copy-start(s32[2,4]{1,0:T(2,128)} %refs_0_.7) | copy-start | bytes 100
  10.6 33.6 %copy-start.1 = (s32[4]{0:T(128)S(1)}, s32[4]{0:T(128)}, u32[]{:S(2)}) copy-start(s32[4]{0:T(128)} %refs_1_.7) | copy-start | bytes 52
  10.6 33.6 %collective-permute-start = (bf16[128,4096]{1,0:T(8,128)(2,1)}, bf16[128,4096]{1,0:T(8,128)(2,1)}, u32[]{:S(2)}, u32[]{:S(2)}) collective-permute-start(bf16[128,4096]{1,0:T(8,128)(2,1)} %get-tuple-element.21), channel_id=1, source_target_pairs={{0,1},{1,0},{2,3},{3,2},{4,5},{5,4},{6,7},{7,6},{8,9},{9,8},{10,11... | collective-permute-start | bytes 3145736 | tf_op jit(solution)/shard_map/ppermute | solution.py:200
  11.4 42.5 %collective-permute-start.11 = (bf16[512,1024]{1,0:T(8,128)(2,1)S(1)}, bf16[512,1024]{1,0:T(8,128)(2,1)S(1)}, u32[]{:S(2)}, u32[]{:S(2)}) collective-permute-start(bf16[512,1024]{1,0:T(8,128)(2,1)S(1)} %pad_maximum_fusion.refs_4_.refs_5_), channel_id=1, source_target_pairs={{0,2},{1,3},{2,0},{3,1},{4,6},{5,7},{6,4},{7,5},{8,10},{9,11},{10,... | collective-permute-start | bytes 3145736 | tf_op jit(solution)/shard_map/ppermute | solution.py:203
  12.7 42.1 %collective-permute-start.13 = (bf16[512,1024]{1,0:T(8,128)(2,1)S(1)}, bf16[512,1024]{1,0:T(8,128)(2,1)}, u32[]{:S(2)}, u32[]{:S(2)}) collective-permute-start(bf16[512,1024]{1,0:T(8,128)(2,1)S(1)} %pad_maximum_fusion.refs_4_.refs_5_), channel_id=1, source_target_pairs={{0,4},{1,5},{2,6},{3,7},{4,0},{5,1},{6,2},{7,3},{8,12},{9,13},{10,... | collective-permute-start | bytes 3145736 | tf_op jit(solution)/shard_map/ppermute | solution.py:206
  12.9 14.9 %collective-permute-start.5 = (bf16[256,1024]{1,0:T(8,128)(2,1)S(1)}, bf16[256,1024]{1,0:T(8,128)(2,1)}, u32[]{:S(2)}, u32[]{:S(2)}) collective-permute-start(bf16[256,1024]{1,0:T(8,128)(2,1)S(1)} %pad_maximum_fusion.1), channel_id=1, source_target_pairs={{0,8},{8,16},{1,9},{9,17},{2,10},{10,18},{3,11},{11,19},{4,12},{12... | collective-permute-start | bytes 1572872 | tf_op jit(solution)/shard_map/ppermute | solution.py:231
  22.5 0.8 copy-start.8
  23.3 14.3 %collective-permute-start.3 = (bf16[256,1024]{1,0:T(8,128)(2,1)S(1)}, bf16[256,1024]{1,0:T(8,128)(2,1)}, u32[]{:S(2)}, u32[]{:S(2)}) collective-permute-start(bf16[256,1024]{1,0:T(8,128)(2,1)S(1)} %collective-permute-done.2), channel_id=1, source_target_pairs={{8,0},{16,8},{9,1},{17,9},{10,2},{18,10},{11,3},{19,11},{12,4},{20... | collective-permute-start | bytes 1572872 | tf_op jit(solution)/shard_map/ppermute | solution.py:228
  27.8 28.8 %collective-permute-start.6 = (bf16[256,1024]{1,0:T(8,128)(2,1)}, bf16[256,1024]{1,0:T(8,128)(2,1)}, u32[]{:S(2)}, u32[]{:S(2)}) collective-permute-start(bf16[256,1024]{1,0:T(8,128)(2,1)} %collective-permute-done.5), channel_id=1, source_target_pairs={{8,16},{9,17},{10,18},{11,19},{12,20},{13,21},{14,22},{15,23}} | collective-permute-start | bytes 1572872 | tf_op jit(solution)/shard_map/ppermute | solution.py:231
  37.6 19.0 %collective-permute-start.4 = (bf16[256,1024]{1,0:T(8,128)(2,1)}, bf16[256,1024]{1,0:T(8,128)(2,1)}, u32[]{:S(2)}, u32[]{:S(2)}) collective-permute-start(bf16[256,1024]{1,0:T(8,128)(2,1)} %collective-permute-done.3), channel_id=1, source_target_pairs={{8,0},{9,1},{10,2},{11,3},{12,4},{13,5},{14,6},{15,7}} | collective-permute-start | bytes 1572872 | tf_op jit(solution)/shard_map/ppermute | solution.py:228
  53.9 2.7 %copy-start.5 = (bf16[128,512]{1,0:T(8,128)(2,1)S(1)}, bf16[128,512]{1,0:T(8,128)(2,1)}, u32[]{:S(2)}) copy-start(bf16[128,512]{1,0:T(8,128)(2,1)} %copy-done.3) | copy-start | bytes 393220
  53.9 2.7 %copy-start.9 = (bf16[256,1024]{1,0:T(8,128)(2,1)S(1)}, bf16[256,1024]{1,0:T(8,128)(2,1)}, u32[]{:S(2)}) copy-start(bf16[256,1024]{1,0:T(8,128)(2,1)} %copy-done.8) | copy-start | bytes 1572868
  53.9 32.5 %collective-permute-start.12 = (bf16[256,1024]{1,0:T(8,128)(2,1)S(1)}, bf16[256,1024]{1,0:T(8,128)(2,1)S(1)}, u32[]{:S(2)}, u32[]{:S(2)}) collective-permute-start(bf16[256,1024]{1,0:T(8,128)(2,1)S(1)} %slice.23), channel_id=1, source_target_pairs={{0,4},{1,5},{2,6},{3,7},{4,0},{5,1},{6,2},{7,3},{8,12},{9,13},{10,... | collective-permute-start | bytes 1572872 | tf_op jit(solution)/shard_map/ppermute | solution.py:206
  55.8 30.6 %collective-permute-start.14 = (bf16[256,1024]{1,0:T(8,128)(2,1)S(1)}, bf16[256,1024]{1,0:T(8,128)(2,1)S(1)}, u32[]{:S(2)}, u32[]{:S(2)}) collective-permute-start(bf16[256,1024]{1,0:T(8,128)(2,1)S(1)} %slice.24), channel_id=1, source_target_pairs={{0,2},{1,3},{2,0},{3,1},{4,6},{5,7},{6,4},{7,5},{8,10},{9,11},{10,... | collective-permute-start | bytes 1572872 | tf_op jit(solution)/shard_map/ppermute | solution.py:203
  58.3 18.1 %collective-permute-start.8 = (bf16[256,1024]{1,0:T(8,128)(2,1)S(1)}, bf16[256,1024]{1,0:T(8,128)(2,1)S(1)}, u32[]{:S(2)}, u32[]{:S(2)}) collective-permute-start(bf16[256,1024]{1,0:T(8,128)(2,1)S(1)} %select_select_fusion.refs_8_.refs_9_), channel_id=1, source_target_pairs={{0,4},{1,5},{2,6},{3,7},{4,0},{5,1},{6,2},{7,3},{8,12},{9,13},{10,... | collective-permute-start | bytes 1572872 | tf_op jit(solution)/shard_map/ppermute | solution.py:206
  59.6 26.7 %collective-permute-start.7 = (bf16[256,1024]{1,0:T(8,128)(2,1)S(1)}, bf16[256,1024]{1,0:T(8,128)(2,1)S(1)}, u32[]{:S(2)}, u32[]{:S(2)}) collective-permute-start(bf16[256,1024]{1,0:T(8,128)(2,1)S(1)} %select_select_fusion.refs_8_.refs_9_), channel_id=1, source_target_pairs={{0,2},{1,3},{2,0},{3,1},{4,6},{5,7},{6,4},{7,5},{8,10},{9,11},{10,... | collective-permute-start | bytes 1572872 | tf_op jit(solution)/shard_map/ppermute | solution.py:203
  76.4 33.5 %collective-permute-start.10 = (bf16[128,1024]{1,0:T(8,128)(2,1)S(1)}, bf16[128,1024]{1,0:T(8,128)(2,1)S(1)}, u32[]{:S(2)}, u32[]{:S(2)}) collective-permute-start(bf16[128,1024]{1,0:T(8,128)(2,1)S(1)} %slice.22), channel_id=1, source_target_pairs={{0,2},{1,3},{2,0},{3,1},{4,6},{5,7},{6,4},{7,5},{8,10},{9,11},{10,... | collective-permute-start | bytes 786440 | tf_op jit(solution)/shard_map/ppermute | solution.py:203
  86.3 23.6 %collective-permute-start.9 = (bf16[128,1024]{1,0:T(8,128)(2,1)S(1)}, bf16[128,1024]{1,0:T(8,128)(2,1)S(1)}, u32[]{:S(2)}, u32[]{:S(2)}) collective-permute-start(bf16[128,1024]{1,0:T(8,128)(2,1)S(1)} %slice.21), channel_id=1, source_target_pairs={{0,4},{1,5},{2,6},{3,7},{4,0},{5,1},{6,2},{7,3},{8,12},{9,13},{10,... | collective-permute-start | bytes 786440 | tf_op jit(solution)/shard_map/ppermute | solution.py:206
  132.2 6.0 %collective-permute-start.15 = (bf16[128,4096]{1,0:T(8,128)(2,1)S(1)}, bf16[128,4096]{1,0:T(8,128)(2,1)S(1)}, u32[]{:S(2)}, u32[]{:S(2)}) collective-permute-start(bf16[128,4096]{1,0:T(8,128)(2,1)S(1)} %get-tuple-element.20), channel_id=1, source_target_pairs={{0,1},{1,0},{2,3},{3,2},{4,5},{5,4},{6,7},{7,6},{8,9},{9,8},{10,11... | collective-permute-start | bytes 3145736 | tf_op jit(solution)/shard_map/ppermute | solution.py:200

commit v2 on v1

v2 whole, which is shorter than its diff:
```python
import functools
import math

import jax
import jax.numpy as jnp
from jax import lax
from jax.experimental import pallas as pl
from jax.experimental.pallas import tpu as pltpu
from jax.sharding import PartitionSpec as P

HQ = 64
KVH = 8
HD = 128
GW = HQ // KVH
HALF_KV = KVH // 2
NEG = -1e30
Q_SCALE = math.log2(math.e) / math.sqrt(HD)
ROW_BLOCK = 256


def attend_kernel(ny, rows, arrays, groups, first, last, *refs):
    refs = list(refs)
    take = lambda count: [refs.pop(0) for _ in range(count)]
    exp_ref, off_ref = take(2)
    q_refs = take(2 if first else 1)
    key_refs = take(arrays)
    value_refs = take(arrays)
    if not first:
        acc_in, ml_in = take(2)
    if first:
        (q_out,) = take(1)
        qs = q_out
    else:
        qs = q_refs[0]
    if last:
        outs = take(2)
    else:
        acc_out, ml_out = take(2)
    accs, ms = refs
    stacked = GW * rows

    group = lax.axis_index("leaf")
    spot = lax.axis_index("ctx")
    core, chip = lax.rem(spot, 2), spot // 2
    chip_x, chip_y = lax.rem(chip, 2), chip // 2
    visible = off_ref[group]
    depth = exp_ref[1, group]

    def block_start(dx, dy, flip):
        x = lax.rem(chip_x + dx, 2)
        y = lax.rem(chip_y - dy + ny, ny)
        k = lax.rem(core + flip, 2)
        return ((y * 2 + x) * 2 + k) * rows

    if first:
        for s, q_ref in enumerate(q_refs):
            for g in range(GW):
                q = q_ref[:, g * HD : (g + 1) * HD].astype(jnp.float32) * Q_SCALE
                high = q.astype(jnp.bfloat16)
                low = (q - high.astype(jnp.float32)).astype(jnp.bfloat16)
                q_out[0, s, g * rows : (g + 1) * rows, :HD] = high
                q_out[0, s, g * rows : (g + 1) * rows, HD:] = low
    else:
        for s in range(2):
            accs[s, :, :HD] = acc_in[0, s]
            ml = ml_in[0, s]
            accs[s, :, HD:] = jnp.broadcast_to(ml[:, HD - 1 :], ml.shape)
            ms[s] = jnp.broadcast_to(ml[:, :1], ml.shape)

    def step(members, limits, masked, fresh):
        width = len(members) * rows
        cut = lambda refs: [refs[a][b * rows : (b + 1) * rows, :] for a, b, _ in members]
        keys = jnp.concatenate(cut(key_refs), axis=0)
        keys = jnp.concatenate([keys, keys], axis=1)
        values = jnp.concatenate(cut(value_refs), axis=0)
        values = jnp.concatenate([values, jnp.ones_like(values)], axis=1)
        size = min(ROW_BLOCK, stacked)
        todo = [(s, slice(base, base + size)) for s in range(2) for base in range(0, stacked, size)]

        def score(s, here):
            return lax.dot_general(
                qs[0, s, here, :], keys, (((1,), (1,)), ((), ())), preferred_element_type=jnp.float32
            )

        def bias_of(s):
            column = lax.broadcasted_iota(jnp.int32, (rows, rows), 1)
            line = lax.broadcasted_iota(jnp.int32, (rows, rows), 0)
            allowed = []
            for (_, _, block), limit in zip(members, limits[s]):
                ahead = column - line if block[0] == "own" else column
                allowed.append(jnp.where(ahead < limit, 0.0, NEG))
            return jnp.concatenate(allowed, axis=1)

        following = score(*todo[0])
        for at, (s, here) in enumerate(todo):
            scores = following
            if at + 1 < len(todo):
                following = score(*todo[at + 1])
            if masked:
                bias = bias_of(s)
                scores = scores + jnp.concatenate([bias] * (size // rows), axis=0)
            new = jnp.max(scores, axis=1, keepdims=True)
            if fresh:
                new = jnp.broadcast_to(new, (size, HD))
            else:
                old = ms[s, here, :]
                new = jnp.maximum(old, new)
            weights = jnp.exp2(scores - jnp.concatenate([new] * (width // HD), axis=1))
            update = jnp.dot(weights.astype(jnp.bfloat16), values, preferred_element_type=jnp.float32)
            if fresh:
                accs[s, here, :] = update
            else:
                shrink = jnp.exp2(old - new)
                accs[s, here, :] = accs[s, here, :] * jnp.concatenate([shrink, shrink], axis=1) + update
            ms[s, here, :] = new

    for number, members in enumerate(groups):
        limits = []
        full, some = jnp.bool_(True), jnp.bool_(False)
        for s in range(2):
            first_row = block_start(0, 0, s)
            limits.append([])
            for _, _, (kind, dx, dy, flip) in members:
                if kind == "root":
                    limit = visible - block_start(dx, dy, flip)
                    some_here = limit > 0
                elif kind == "own":
                    limit = first_row - block_start(dx, dy, flip) + 1
                    some_here = limit + rows - 1 > 0
                else:
                    limit = jnp.where(depth > 0, rows, 0)
                    some_here = limit > 0
                limits[s].append(limit)
                full = full & (limit >= rows)
                some = some | some_here
        kinds = {block[0] for _, _, block in members}
        if first and number == 0:
            step(members, limits, True, True)
            continue
        pl.when(full)(functools.partial(step, members, limits, False, False))
        if kinds != {"kin"}:
            pl.when(jnp.logical_not(full) & some)(functools.partial(step, members, limits, True, False))

    for s in range(2):
        if last:
            done = (accs[s, :, :HD] / accs[s, :, HD:]).astype(jnp.bfloat16)
            for g in range(GW):
                outs[s][:, g * HD : (g + 1) * HD] = done[g * rows : (g + 1) * rows]
        else:
            acc_out[0, s] = accs[s, :, :HD]
            lane = lax.broadcasted_iota(jnp.int32, (stacked, HD), 1)
            ml_out[0, s] = jnp.where(lane < HD // 2, ms[s], accs[s, :, HD:])


def attend(ny, rows, tables, queries, arrays, groups, state, last):
    stacked = GW * rows
    first = state is None
    smem = pl.BlockSpec(memory_space=pltpu.SMEM)
    row_spec = pl.BlockSpec((rows, GW * HD), lambda h: (0, h))
    q_spec = pl.BlockSpec((1, 2, stacked, 2 * HD), lambda h: (h, 0, 0, 0))
    state_spec = pl.BlockSpec((1, 2, stacked, HD), lambda h: (h, 0, 0, 0))
    operands = [*tables, *queries]
    specs = [smem, smem] + ([row_spec, row_spec] if first else [q_spec])
    for shift in (0, HALF_KV):
        for array in arrays:
            operands.append(array)
            specs.append(pl.BlockSpec((array.shape[0], HD), functools.partial(lambda s, h: (0, s + h), shift)))
    out_shape, out_specs = [], []
    if first:
        out_shape.append(jax.ShapeDtypeStruct((HALF_KV, 2, stacked, 2 * HD), jnp.bfloat16))
        out_specs.append(q_spec)
    else:
        operands += list(state)
        specs += [state_spec, state_spec]
    if last:
        out_shape += [jax.ShapeDtypeStruct((rows, HALF_KV * GW * HD), jnp.bfloat16)] * 2
        out_specs += [row_spec, row_spec]
    else:
        out_shape += [jax.ShapeDtypeStruct((HALF_KV, 2, stacked, HD), jnp.float32)] * 2
        out_specs += [state_spec, state_spec]
    scores = HALF_KV * 2 * stacked * rows * sum(len(members) for members in groups)
    return pl.pallas_call(
        functools.partial(attend_kernel, ny, rows, len(arrays), groups, first, last),
        grid=(HALF_KV,),
        in_specs=specs,
        out_specs=out_specs,
        out_shape=out_shape,
        scratch_shapes=[
            pltpu.VMEM((2, stacked, 2 * HD), jnp.float32),
            pltpu.VMEM((2, stacked, HD), jnp.float32),
        ],
        compiler_params=pltpu.CompilerParams(vmem_limit_bytes=40 * 2**20),
        cost_estimate=pl.CostEstimate(flops=8 * scores * HD, bytes_accessed=20 * 2**20, transcendentals=scores),
    )(*operands)


def on_device(queries, seg_keys, seg_values, root_keys, root_values, expansion, root_offsets):
    leaves, spots = lax.axis_size("leaf"), lax.axis_size("ctx")
    ny = spots // 4
    rows = queries.shape[0]
    group = lax.axis_index("leaf")
    core = lax.rem(lax.axis_index("ctx"), 2)

    def halves(array):
        half = array.shape[1] // 2
        return (
            lax.dynamic_slice_in_dim(array, core * half, half, 1),
            lax.dynamic_slice_in_dim(array, (1 - core) * half, half, 1),
        )

    def index(x, y, k):
        return ((y % ny) * 2 + x % 2) * 2 + k % 2

    places = [(x, y, k) for y in range(ny) for x in range(2) for k in range(2)]

    def to_core(array):
        return lax.ppermute(array, "ctx", [(index(x, y, k), index(x, y, k + 1)) for x, y, k in places])

    def to_x(array):
        return lax.ppermute(array, "ctx", [(index(x, y, k), index(x + 1, y, k)) for x, y, k in places])

    def to_y(array, step):
        return lax.ppermute(array, "ctx", [(index(x, y, k), index(x, y + step, k)) for x, y, k in places])

    def packed(keys, values):
        (key_mine, key_other), (value_mine, value_other) = halves(keys), halves(values)
        return jnp.concatenate([key_mine, value_mine], axis=1), jnp.concatenate([key_other, value_other], axis=1)

    own_mine, own_other = packed(seg_keys, seg_values)
    root_mine, root_other = packed(root_keys, root_values)
    got = to_core(jnp.concatenate([own_other, root_other], axis=0))
    q_mine, q_other = halves(queries)
    q_pair = (q_mine, to_core(q_other))
    tables = (expansion, root_offsets)
    local = jnp.concatenate([own_mine, root_mine, got], axis=0)
    segment = jnp.concatenate([own_mine, got[:rows]], axis=0)

    kinds = ("own", "root")

    def members(array, dx, dy, flips=(0, 1), wanted=kinds):
        return tuple(
            (array, f * 2 + kinds.index(kind), (kind, dx, dy, flip))
            for f, flip in enumerate(flips)
            for kind in wanted
        )

    def kin(*counts):
        return tuple((array, b, ("kin", 0, 0, 0)) for array, count in counts for b in range(count))

    run = functools.partial(attend, ny, rows, tables)
    steps = range(1, ny)

    parent = expansion[0, group]
    choices = []

    def hop(step, down, up):
        down = lax.ppermute(down, "leaf", [(i, i - 1) for i in range(1, leaves - step + 1)])
        choices.append((group + step, down))
        if step < leaves - 1:
            up = lax.ppermute(up, "leaf", [(i, i + 1) for i in range(step - 1, leaves - 2)])
            choices.append((group - step, up))
        return down, up

    down, up = hop(1, segment, segment)
    from_x = to_x(local)
    from_y = [to_y(local, step) for step in steps]
    q_ready, *state = run(q_pair, [local], (members(0, 0, 0),), None, False)
    if leaves > 2:
        down, up, state = lax.optimization_barrier((down, up, state))
        down, up = hop(2, down, up)

    tops = [to_y(from_x[: 2 * rows], step) for step in steps]
    lows = [to_x(array[2 * rows :]) for array in from_y]
    near = [members(0, 1, 0, wanted=(kind,)) + members(1, 0, 1, wanted=(kind,)) for kind in kinds]
    near += [members(step, 0, step) for step in steps if step > 1]
    state = run([q_ready], [from_x, *from_y], tuple(near), state, False)
    for step in range(3, leaves):
        down, up, state = lax.optimization_barrier((down, up, state))
        down, up = hop(step, down, up)
    far, arrays = [], []
    for step, top, low in zip(steps, tops, lows):
        far.append(
            members(len(arrays), 1, step, (0,)) + members(len(arrays) + 1, 1, step, (1,))
        )
        arrays += [top, low]
    state = run([q_ready], arrays, tuple(far), state, False)

    owners, helds = zip(*choices)
    helds, state = lax.optimization_barrier((helds, state))
    parent_rows = segment
    for owner, held in zip(owners, helds):
        parent_rows = jnp.where(parent == owner, held, parent_rows)
    kin_x = to_x(parent_rows)
    kin_y = [to_y(parent_rows, step) for step in steps]
    tops = [to_y(kin_x[:rows], step) for step in steps]
    lows = [to_x(array[rows:]) for array in kin_y]
    arrays = [parent_rows, kin_x, *kin_y, *tops, *lows]
    last_groups = [kin((0, 2), (1, 2), (2, 2), (1 + ny, 1), (2 * ny, 1))]
    for step in steps:
        if step > 1:
            last_groups.append(kin((1 + step, 2), (ny + step, 1), (2 * ny - 1 + step, 1)))
    out_mine, out_other = run([q_ready], arrays, tuple(last_groups), state, True)
    out_got = to_core(out_other)
    return jnp.where(
        core == 0,
        jnp.concatenate([out_mine, out_got], axis=1),
        jnp.concatenate([out_got, out_mine], axis=1),
    )


def solution(mesh):
    return jax.shard_map(
        on_device,
        mesh=mesh,
        in_specs=(
            P(("leaf", "ctx"), None),
            P(("leaf", "ctx"), None),
            P(("leaf", "ctx"), None),
            P("ctx", None),
            P("ctx", None),
            P(),
            P(),
        ),
        out_specs=P(("leaf", "ctx"), None),
        check_vma=False,
    )
```

time: 140 us -> 124 us (0.89)
  the two profiles are of different devices: /device:TPU:13 before, /device:TPU:0 now
where the time goes in v2:
time: 124 us
  Pallas kernels  43.2 us (35%)
  starting transfers between devices  32.4 us (26%)
  waiting for transfers between devices  23 us (19%)
  local copies, waits for them, and re-layouts  17.8 us (14%)
  other arithmetic  4.44 us (4%)
  between operations  3.35 us (3%)
    pallas_call x4, Pallas kernels, attend(): pl.pallas_call(functools.partial(attend_kernel, ny, rows, len(arrays), gr...  43.2 us
    ppermute x4, starting transfers between devices, to_x(): lax.ppermute(array, 'ctx', [(index(x, y, k), index(x + 1, y, k)) for x, y...  16.5 us
    unnamed x22, local copies, waits for them, and re-layouts  12.9 us
    ppermute x4, waiting for transfers between devices, to_x(): lax.ppermute(array, 'ctx', [(index(x, y, k), index(x + 1, y, k)) for x, y...  12.3 us
    ppermute x4, waiting for transfers between devices, to_y(): lax.ppermute(array, 'ctx', [(index(x, y, k), index(x, y + step, k)) for x...  6.57 us
    ppermute x4, starting transfers between devices, to_y(): lax.ppermute(array, 'ctx', [(index(x, y, k), index(x, y + step, k)) for x...  5.91 us
    ppermute x2, starting transfers between devices, hop(): lax.ppermute(up, 'leaf', [(i, i + 1) for i in range(step - 1, leaves - 2)])  5.27 us
    ppermute x3, waiting for transfers between devices, to_core(): lax.ppermute(array, 'ctx', [(index(x, y, k), index(x, y, k + 1)) for x, y...  4.1 us
  transfers between devices with their start and end apart: 16, of which 7 were waited for; matrix products, arithmetic and copies ran while one was open for 2% of the time, Pallas kernels for 22%

profile of v2, /device:TPU:0, one launch (start us, length us, event | category | flops | bytes accessed | tf_op | source)
XLA Modules:
  0.0 124.1 jit_solution(67387353812407519)
XLA Ops:
  0.0 1.3 %constant_dynamic-slice_fusion.7 = (bf16[128,512]{1,0:T(8,128)(2,1)S(1)}, bf16[128,512]{1,0:T(8,128)(2,1)S(1)}, bf16[128,512]{1,0:T(8,128)(2,1)S(1)}, bf16[128,512]{1,0:T(8,128)(2,1)S(1)}) fusion(bf16[128,1024]{1,0:T(8,128)(2,1)} %param.9, s32[]{:T(128)S(6)} %select_n.64, s32[]{:T(128)S(6)} %select_n.65, bf16[128,1024]{1,0:T(8,128)(2,1)} %param.8), kind=kLoop, calls=%fused_computation.12 | loop fusion | bytes 1048584 | tf_op jit(solution)/shard_map/dynamic_slice | solution.py:207
  1.3 1.1 constant_dynamic-slice_fusion.5
  2.4 0.9 maximum_maximum_fusion
  4.0 1.5 %collective-permute-done.1 = bf16[256,1024]{1,0:T(8,128)(2,1)S(1)} collective-permute-done((bf16[256,1024]{1,0:T(8,128)(2,1)}, bf16[256,1024]{1,0:T(8,128)(2,1)S(1)}, u32[]{:S(2)}, u32[]{:S(2)}) %collective-permute-start.1) | collective-permute-done | bytes 524320 | tf_op jit(solution)/shard_map/ppermute | solution.py:217
  5.6 3.0 %collective-permute-start.7 = (bf16[512,1024]{1,0:T(8,128)(2,1)S(1)}, bf16[512,1024]{1,0:T(8,128)(2,1)S(1)}, u32[]{:S(2)}, u32[]{:S(2)}) collective-permute-start(bf16[512,1024]{1,0:T(8,128)(2,1)S(1)} %pad_maximum_fusion.refs_4_.refs_5_), channel_id=1, source_target_pairs={{0,4},{1,5},{2,6},{3,7},{4,0},{5,1},{6,2},{7,3},{8,12},{9,13},{10,... | collective-permute-start | bytes 3145736 | tf_op jit(solution)/shard_map/ppermute | solution.py:223
  8.5 1.5 %collective-permute-start.6 = (bf16[512,1024]{1,0:T(8,128)(2,1)S(1)}, bf16[512,1024]{1,0:T(8,128)(2,1)S(1)}, u32[]{:S(2)}, u32[]{:S(2)}) collective-permute-start(bf16[512,1024]{1,0:T(8,128)(2,1)S(1)} %pad_maximum_fusion.refs_4_.refs_5_), channel_id=1, source_target_pairs={{0,2},{1,3},{2,0},{3,1},{4,6},{5,7},{6,4},{7,5},{8,10},{9,11},{10,... | collective-permute-start | bytes 3145736 | tf_op jit(solution)/shard_map/ppermute | solution.py:220
  10.1 1.3 %collective-permute-start.2 = (bf16[256,1024]{1,0:T(8,128)(2,1)S(1)}, bf16[256,1024]{1,0:T(8,128)(2,1)S(1)}, u32[]{:S(2)}, u32[]{:S(2)}) collective-permute-start(bf16[256,1024]{1,0:T(8,128)(2,1)S(1)} %pad_maximum_fusion.1), channel_id=1, source_target_pairs={{8,0},{16,8},{24,16},{9,1},{17,9},{25,17},{10,2},{18,10},{26,18},{... | collective-permute-start | bytes 1572872 | tf_op jit(solution)/shard_map/ppermute | solution.py:257
  11.4 4.6 %collective-permute-start.3 = (bf16[256,1024]{1,0:T(8,128)(2,1)S(1)}, bf16[256,1024]{1,0:T(8,128)(2,1)S(1)}, u32[]{:S(2)}, u32[]{:S(2)}) collective-permute-start(bf16[256,1024]{1,0:T(8,128)(2,1)S(1)} %pad_maximum_fusion.1), channel_id=1, source_target_pairs={{0,8},{8,16},{1,9},{9,17},{2,10},{10,18},{3,11},{11,19},{4,12},{12... | collective-permute-start | bytes 1572872 | tf_op jit(solution)/shard_map/ppermute | solution.py:260
  16.0 9.0 %shard_map.73 = (bf16[4,2,1024,256]{3,2,1,0:T(8,128)(2,1)S(1)}, f32[4,2,1024,128]{3,2,1,0:T(8,128)S(1)}, f32[4,2,1024,128]{3,2,1,0:T(8,128)}) custom-call(s32[2,4]{1,0:T(2,128)S(1)} %copy-done, s32[4]{0:T(128)S(1)} %copy-done.1, bf16[128,4096]{1,0:T(8,128)(2,1)S(1)} %get-tuple-element.52.refs_2_, bf16[128,4096]{1,0:T(8,128)(2,1)S(1)} %collective-permute-done.refs_3_, ...), custom_call_target="tpu_custom_call" | custom-call | flops 4294967296 | bytes 20971520 | tf_op jit(solution)/shard_map/pallas_call | solution.py:182
  25.0 2.0 %copy-done.2 = bf16[4,2,1024,256]{3,2,1,0:T(8,128)(2,1)} copy-done((bf16[4,2,1024,256]{3,2,1,0:T(8,128)(2,1)}, bf16[4,2,1024,256]{3,2,1,0:T(8,128)(2,1)S(1)}, u32[]{:S(2)}) %copy-start.2) | copy-done | bytes 4194328
  27.0 2.0 %copy-done.7 = f32[4,2,1024,128]{3,2,1,0:T(8,128)} copy-done((f32[4,2,1024,128]{3,2,1,0:T(8,128)}, f32[4,2,1024,128]{3,2,1,0:T(8,128)S(1)}, u32[]{:S(2)}) %copy-start.7) | copy-done | bytes 4194328
  29.0 1.3 %collective-permute-start.4 = (bf16[256,1024]{1,0:T(8,128)(2,1)S(1)}, bf16[256,1024]{1,0:T(8,128)(2,1)S(1)}, u32[]{:S(2)}, u32[]{:S(2)}) collective-permute-start(bf16[256,1024]{1,0:T(8,128)(2,1)S(1)} %collective-permute-done.2), channel_id=1, source_target_pairs={{8,0},{16,8},{9,1},{17,9},{10,2},{18,10},{11,3},{19,11},{12,4},{20... | collective-permute-start | bytes 1572872 | tf_op jit(solution)/shard_map/ppermute | solution.py:257
  31.0 1.0 collective-permute-done.7.refs_4_.refs_6_
  32.0 0.8 slice.22
  32.8 1.7 %collective-permute-start.10 = (bf16[256,1024]{1,0:T(8,128)(2,1)}, bf16[256,1024]{1,0:T(8,128)(2,1)S(1)}, u32[]{:S(2)}, u32[]{:S(2)}) collective-permute-start(bf16[256,1024]{1,0:T(8,128)(2,1)} %slice.22), channel_id=1, source_target_pairs={{0,2},{1,3},{2,0},{3,1},{4,6},{5,7},{6,4},{7,5},{8,10},{9,11},{10,... | collective-permute-start | bytes 1572872 | tf_op jit(solution)/shard_map/ppermute | solution.py:220
  35.4 1.5 %collective-permute-start.9 = (bf16[256,1024]{1,0:T(8,128)(2,1)}, bf16[256,1024]{1,0:T(8,128)(2,1)S(1)}, u32[]{:S(2)}, u32[]{:S(2)}) collective-permute-start(bf16[256,1024]{1,0:T(8,128)(2,1)} %slice.21), channel_id=1, source_target_pairs={{0,4},{1,5},{2,6},{3,7},{4,0},{5,1},{6,2},{7,3},{8,12},{9,13},{10,... | collective-permute-start | bytes 1572872 | tf_op jit(solution)/shard_map/ppermute | solution.py:223
  36.9 12.3 %shard_map.74 = (f32[4,2,1024,128]{3,2,1,0:T(8,128)S(1)}, f32[4,2,1024,128]{3,2,1,0:T(8,128)S(1)}) custom-call(s32[2,4]{1,0:T(2,128)S(1)} %copy-done, s32[4]{0:T(128)S(1)} %copy-done.1, bf16[4,2,1024,256]{3,2,1,0:T(8,128)(2,1)} %copy-done.2, bf16[512,1024]{1,0:T(8,128)(2,1)S(1)} %collective-permute-done.6.refs_3_.refs_5_, ...), custom_call_target="tpu_custom_call" | custom-call | flops 8589934592 | bytes 20971520 | tf_op jit(solution)/shard_map/pallas_call | solution.py:182
  49.1 2.0 %copy-done.4 = f32[4,2,1024,128]{3,2,1,0:T(8,128)} copy-done((f32[4,2,1024,128]{3,2,1,0:T(8,128)}, f32[4,2,1024,128]{3,2,1,0:T(8,128)S(1)}, u32[]{:S(2)}) %copy-start.4) | copy-done | bytes 4194328
  51.2 2.0 %copy-done.5 = f32[4,2,1024,128]{3,2,1,0:T(8,128)} copy-done((f32[4,2,1024,128]{3,2,1,0:T(8,128)}, f32[4,2,1024,128]{3,2,1,0:T(8,128)S(1)}, u32[]{:S(2)}) %copy-start.5) | copy-done | bytes 4194328
  54.0 1.5 %collective-permute-start.8 = (bf16[256,1024]{1,0:T(8,128)(2,1)S(1)}, bf16[256,1024]{1,0:T(8,128)(2,1)}, u32[]{:S(2)}, u32[]{:S(2)}) collective-permute-start(bf16[256,1024]{1,0:T(8,128)(2,1)S(1)} %collective-permute-done.4), channel_id=1, source_target_pairs={{8,0},{9,1},{10,2},{11,3},{12,4},{13,5},{14,6},{15,7}} | collective-permute-start | bytes 1572872 | tf_op jit(solution)/shard_map/ppermute | solution.py:257
  59.2 2.2 %copy-done.3 = bf16[4,2,1024,256]{3,2,1,0:T(8,128)(2,1)S(1)} copy-done((bf16[4,2,1024,256]{3,2,1,0:T(8,128)(2,1)S(1)}, bf16[4,2,1024,256]{3,2,1,0:T(8,128)(2,1)}, u32[]{:S(2)}) %copy-start.3) | copy-done | bytes 4194328
  61.4 6.0 %shard_map.75 = (f32[4,2,1024,128]{3,2,1,0:T(8,128)S(1)}, f32[4,2,1024,128]{3,2,1,0:T(8,128)S(1)}) custom-call(s32[2,4]{1,0:T(2,128)S(1)} %copy-done, s32[4]{0:T(128)S(1)} %copy-done.1, bf16[4,2,1024,256]{3,2,1,0:T(8,128)(2,1)S(1)} %copy-done.3, bf16[256,1024]{1,0:T(8,128)(2,1)S(1)} %collective-permute-done.9.refs_3_.refs_5_, ...), custom_call_target="tpu_custom_call" | custom-call | flops 4294967296 | bytes 20971520 | tf_op jit(solution)/shard_map/pallas_call | solution.py:182
  67.4 1.9 %copy-done.6 = f32[4,2,1024,128]{3,2,1,0:T(8,128)} copy-done((f32[4,2,1024,128]{3,2,1,0:T(8,128)}, f32[4,2,1024,128]{3,2,1,0:T(8,128)S(1)}, u32[]{:S(2)}) %copy-start.6) | copy-done | bytes 4194328
  69.4 1.6 %select_select_fusion.refs_3_.refs_8_ = bf16[256,1024]{1,0:T(8,128)(2,1)S(1)} fusion(bf16[256,1024]{1,0:T(8,128)(2,1)} %collective-permute-done.8, bf16[256,1024]{1,0:T(8,128)(2,1)S(1)} %copy-done.10, bf16[256,1024]{1,0:T(8,128)(2,1)S(1)} %collective-permute-done.4, bf16[256,1024]{1,0:T(8,128)(2,1)S(1)} %collective-permute-done.3, ...), kind=kLoop, calls=%fused_computation.4 | loop fusion | flops 2883584 | bytes 3670021 | tf_op jit(solution)/shard_map/jit(_where)/select_n | solution.py:292
  71.0 13.3 %collective-permute-start.11 = (bf16[256,1024]{1,0:T(8,128)(2,1)S(1)}, bf16[256,1024]{1,0:T(8,128)(2,1)S(1)}, u32[]{:S(2)}, u32[]{:S(2)}) collective-permute-start(bf16[256,1024]{1,0:T(8,128)(2,1)S(1)} %select_select_fusion.refs_3_.refs_8_), channel_id=1, source_target_pairs={{0,2},{1,3},{2,0},{3,1},{4,6},{5,7},{6,4},{7,5},{8,10},{9,11},{10,... | collective-permute-start | bytes 1572872 | tf_op jit(solution)/shard_map/ppermute | solution.py:220
  84.3 10.8 %collective-permute-done.11.refs_4_.refs_9_ = bf16[256,1024]{1,0:T(8,128)(2,1)S(1)} collective-permute-done((bf16[256,1024]{1,0:T(8,128)(2,1)S(1)}, bf16[256,1024]{1,0:T(8,128)(2,1)S(1)}, u32[]{:S(2)}, u32[]{:S(2)}) %collective-permute-start.11) | collective-permute-done | bytes 524320 | tf_op jit(solution)/shard_map/ppermute | solution.py:220
  95.1 1.4 %collective-permute-start.13 = (bf16[128,1024]{1,0:T(8,128)(2,1)S(1)}, bf16[128,1024]{1,0:T(8,128)(2,1)S(1)}, u32[]{:S(2)}, u32[]{:S(2)}) collective-permute-start(bf16[128,1024]{1,0:T(8,128)(2,1)S(1)} %slice.23), channel_id=1, source_target_pairs={{0,4},{1,5},{2,6},{3,7},{4,0},{5,1},{6,2},{7,3},{8,12},{9,13},{10,... | collective-permute-start | bytes 786440 | tf_op jit(solution)/shard_map/ppermute | solution.py:223
  97.3 4.9 %collective-permute-done.13.refs_6_.refs_11_ = bf16[128,1024]{1,0:T(8,128)(2,1)S(1)} collective-permute-done((bf16[128,1024]{1,0:T(8,128)(2,1)S(1)}, bf16[128,1024]{1,0:T(8,128)(2,1)S(1)}, u32[]{:S(2)}, u32[]{:S(2)}) %collective-permute-start.13) | collective-permute-done | bytes 262176 | tf_op jit(solution)/shard_map/ppermute | solution.py:223
  102.2 1.4 %collective-permute-done.14.refs_7_.refs_12_ = bf16[128,1024]{1,0:T(8,128)(2,1)S(1)} collective-permute-done((bf16[128,1024]{1,0:T(8,128)(2,1)S(1)}, bf16[128,1024]{1,0:T(8,128)(2,1)S(1)}, u32[]{:S(2)}, u32[]{:S(2)}) %collective-permute-start.14) | collective-permute-done | bytes 262176 | tf_op jit(solution)/shard_map/ppermute | solution.py:220
  103.6 15.9 %shard_map.76 = (bf16[128,4096]{1,0:T(8,128)(2,1)S(1)}, bf16[128,4096]{1,0:T(8,128)(2,1)S(1)}) custom-call(s32[2,4]{1,0:T(2,128)S(1)} %copy-done, s32[4]{0:T(128)S(1)} %copy-done.1, bf16[4,2,1024,256]{3,2,1,0:T(8,128)(2,1)S(1)} %copy-done.3, bf16[256,1024]{1,0:T(8,128)(2,1)S(1)} %select_select_fusion.refs_3_.refs_8_, ...), custom_call_target="tpu_custom_call" | custom-call | flops 8589934592 | bytes 20971520 | tf_op jit(solution)/shard_map/pallas_call | solution.py:182
  119.7 2.6 %collective-permute-done.15 = bf16[128,4096]{1,0:T(8,128)(2,1)S(1)} collective-permute-done((bf16[128,4096]{1,0:T(8,128)(2,1)S(1)}, bf16[128,4096]{1,0:T(8,128)(2,1)S(1)}, u32[]{:S(2)}, u32[]{:S(2)}) %collective-permute-start.15) | collective-permute-done | bytes 1048608 | tf_op jit(solution)/shard_map/ppermute | solution.py:217
  122.3 1.8 %maximum_select_fusion = bf16[128,8192]{1,0:T(8,128)(2,1)} fusion(bf16[128,4096]{1,0:T(8,128)(2,1)S(1)} %collective-permute-done.15, bf16[128,4096]{1,0:T(8,128)(2,1)S(1)} %get-tuple-element.49, pred[]{:T(512)S(6)} %eq.18), kind=kLoop, calls=%fused_computation | loop fusion | flops 9437184 | bytes 4194305 | tf_op jit(solution)/shard_map/jit(_where)/select_n | solution.py:304
  (40 shorter events, 4.6 us)
Async XLA Ops:
  0.0 3.7 %copy-start.8 = (bf16[128,8192]{1,0:T(8,128)(2,1)S(1)}, bf16[128,8192]{1,0:T(8,128)(2,1)}, u32[]{:S(2)}) copy-start(bf16[128,8192]{1,0:T(8,128)(2,1)} %param.7) | copy-start | bytes 6291460
  3.3 2.2 %collective-permute-start.1 = (bf16[256,1024]{1,0:T(8,128)(2,1)}, bf16[256,1024]{1,0:T(8,128)(2,1)S(1)}, u32[]{:S(2)}, u32[]{:S(2)}) collective-permute-start(bf16[256,1024]{1,0:T(8,128)(2,1)} %maximum_maximum_fusion), channel_id=1, source_target_pairs={{0,1},{1,0},{2,3},{3,2},{4,5},{5,4},{6,7},{7,6},{8,9},{9,8},{10,11... | collective-permute-start | bytes 1572872 | tf_op jit(solution)/shard_map/ppermute | solution.py:217
  3.9 12.1 %copy-start = (s32[2,4]{1,0:T(2,128)S(1)}, s32[2,4]{1,0:T(2,128)}, u32[]{:S(2)}) copy-start(s32[2,4]{1,0:T(2,128)} %refs_0_.7) | copy-start | bytes 100
  3.9 12.1 %copy-start.1 = (s32[4]{0:T(128)S(1)}, s32[4]{0:T(128)}, u32[]{:S(2)}) copy-start(s32[4]{0:T(128)} %refs_1_.7) | copy-start | bytes 52
  3.9 12.1 %collective-permute-start = (bf16[128,4096]{1,0:T(8,128)(2,1)S(1)}, bf16[128,4096]{1,0:T(8,128)(2,1)S(1)}, u32[]{:S(2)}, u32[]{:S(2)}) collective-permute-start(bf16[128,4096]{1,0:T(8,128)(2,1)S(1)} %get-tuple-element.51), channel_id=1, source_target_pairs={{0,1},{1,0},{2,3},{3,2},{4,5},{5,4},{6,7},{7,6},{8,9},{9,8},{10,11... | collective-permute-start | bytes 3145736 | tf_op jit(solution)/shard_map/ppermute | solution.py:217
  5.6 26.4 %collective-permute-start.7 = (bf16[512,1024]{1,0:T(8,128)(2,1)S(1)}, bf16[512,1024]{1,0:T(8,128)(2,1)S(1)}, u32[]{:S(2)}, u32[]{:S(2)}) collective-permute-start(bf16[512,1024]{1,0:T(8,128)(2,1)S(1)} %pad_maximum_fusion.refs_4_.refs_5_), channel_id=1, source_target_pairs={{0,4},{1,5},{2,6},{3,7},{4,0},{5,1},{6,2},{7,3},{8,12},{9,13},{10,... | collective-permute-start | bytes 3145736 | tf_op jit(solution)/shard_map/ppermute | solution.py:223
  8.5 26.0 %collective-permute-start.6 = (bf16[512,1024]{1,0:T(8,128)(2,1)S(1)}, bf16[512,1024]{1,0:T(8,128)(2,1)S(1)}, u32[]{:S(2)}, u32[]{:S(2)}) collective-permute-start(bf16[512,1024]{1,0:T(8,128)(2,1)S(1)} %pad_maximum_fusion.refs_4_.refs_5_), channel_id=1, source_target_pairs={{0,2},{1,3},{2,0},{3,1},{4,6},{5,7},{6,4},{7,5},{8,10},{9,11},{10,... | collective-permute-start | bytes 3145736 | tf_op jit(solution)/shard_map/ppermute | solution.py:220
  10.1 18.9 %collective-permute-start.2 = (bf16[256,1024]{1,0:T(8,128)(2,1)S(1)}, bf16[256,1024]{1,0:T(8,128)(2,1)S(1)}, u32[]{:S(2)}, u32[]{:S(2)}) collective-permute-start(bf16[256,1024]{1,0:T(8,128)(2,1)S(1)} %pad_maximum_fusion.1), channel_id=1, source_target_pairs={{8,0},{16,8},{24,16},{9,1},{17,9},{25,17},{10,2},{18,10},{26,18},{... | collective-permute-start | bytes 1572872 | tf_op jit(solution)/shard_map/ppermute | solution.py:257
  11.4 17.6 %collective-permute-start.3 = (bf16[256,1024]{1,0:T(8,128)(2,1)S(1)}, bf16[256,1024]{1,0:T(8,128)(2,1)S(1)}, u32[]{:S(2)}, u32[]{:S(2)}) collective-permute-start(bf16[256,1024]{1,0:T(8,128)(2,1)S(1)} %pad_maximum_fusion.1), channel_id=1, source_target_pairs={{0,8},{8,16},{1,9},{9,17},{2,10},{10,18},{3,11},{11,19},{4,12},{12... | collective-permute-start | bytes 1572872 | tf_op jit(solution)/shard_map/ppermute | solution.py:260
  25.0 2.0 %copy-start.2 = (bf16[4,2,1024,256]{3,2,1,0:T(8,128)(2,1)}, bf16[4,2,1024,256]{3,2,1,0:T(8,128)(2,1)S(1)}, u32[]{:S(2)}) copy-start(bf16[4,2,1024,256]{3,2,1,0:T(8,128)(2,1)S(1)} %get-tuple-element.28.refs_2_) | copy-start | bytes 12582916
  27.0 2.0 %copy-start.7 = (f32[4,2,1024,128]{3,2,1,0:T(8,128)}, f32[4,2,1024,128]{3,2,1,0:T(8,128)S(1)}, u32[]{:S(2)}) copy-start(f32[4,2,1024,128]{3,2,1,0:T(8,128)S(1)} %get-tuple-element.33.refs_7_) | copy-start | bytes 12582916
  29.0 24.2 %collective-permute-start.4 = (bf16[256,1024]{1,0:T(8,128)(2,1)S(1)}, bf16[256,1024]{1,0:T(8,128)(2,1)S(1)}, u32[]{:S(2)}, u32[]{:S(2)}) collective-permute-start(bf16[256,1024]{1,0:T(8,128)(2,1)S(1)} %collective-permute-done.2), channel_id=1, source_target_pairs={{8,0},{16,8},{9,1},{17,9},{10,2},{18,10},{11,3},{19,11},{12,4},{20... | collective-permute-start | bytes 1572872 | tf_op jit(solution)/shard_map/ppermute | solution.py:257
  30.3 22.9 %collective-permute-start.5 = (bf16[256,1024]{1,0:T(8,128)(2,1)S(1)}, bf16[256,1024]{1,0:T(8,128)(2,1)S(1)}, u32[]{:S(2)}, u32[]{:S(2)}) collective-permute-start(bf16[256,1024]{1,0:T(8,128)(2,1)S(1)} %collective-permute-done.3), channel_id=1, source_target_pairs={{8,16},{9,17},{10,18},{11,19},{12,20},{13,21},{14,22},{15,23}} | collective-permute-start | bytes 1572872 | tf_op jit(solution)/shard_map/ppermute | solution.py:260
  32.8 26.3 %collective-permute-start.10 = (bf16[256,1024]{1,0:T(8,128)(2,1)}, bf16[256,1024]{1,0:T(8,128)(2,1)S(1)}, u32[]{:S(2)}, u32[]{:S(2)}) collective-permute-start(bf16[256,1024]{1,0:T(8,128)(2,1)} %slice.22), channel_id=1, source_target_pairs={{0,2},{1,3},{2,0},{3,1},{4,6},{5,7},{6,4},{7,5},{8,10},{9,11},{10,... | collective-permute-start | bytes 1572872 | tf_op jit(solution)/shard_map/ppermute | solution.py:220
  35.4 23.8 %collective-permute-start.9 = (bf16[256,1024]{1,0:T(8,128)(2,1)}, bf16[256,1024]{1,0:T(8,128)(2,1)S(1)}, u32[]{:S(2)}, u32[]{:S(2)}) collective-permute-start(bf16[256,1024]{1,0:T(8,128)(2,1)} %slice.21), channel_id=1, source_target_pairs={{0,4},{1,5},{2,6},{3,7},{4,0},{5,1},{6,2},{7,3},{8,12},{9,13},{10,... | collective-permute-start | bytes 1572872 | tf_op jit(solution)/shard_map/ppermute | solution.py:223
  49.1 2.0 %copy-start.4 = (f32[4,2,1024,128]{3,2,1,0:T(8,128)}, f32[4,2,1024,128]{3,2,1,0:T(8,128)S(1)}, u32[]{:S(2)}) copy-start(f32[4,2,1024,128]{3,2,1,0:T(8,128)S(1)} %get-tuple-element.38.refs_7_) | copy-start | bytes 12582916
  51.2 2.0 %copy-start.5 = (f32[4,2,1024,128]{3,2,1,0:T(8,128)}, f32[4,2,1024,128]{3,2,1,0:T(8,128)S(1)}, u32[]{:S(2)}) copy-start(f32[4,2,1024,128]{3,2,1,0:T(8,128)S(1)} %get-tuple-element.39.refs_8_) | copy-start | bytes 12582916
  53.2 0.8 copy-start.9
  54.0 15.4 %collective-permute-start.8 = (bf16[256,1024]{1,0:T(8,128)(2,1)S(1)}, bf16[256,1024]{1,0:T(8,128)(2,1)}, u32[]{:S(2)}, u32[]{:S(2)}) collective-permute-start(bf16[256,1024]{1,0:T(8,128)(2,1)S(1)} %collective-permute-done.4), channel_id=1, source_target_pairs={{8,0},{9,1},{10,2},{11,3},{12,4},{13,5},{14,6},{15,7}} | collective-permute-start | bytes 1572872 | tf_op jit(solution)/shard_map/ppermute | solution.py:257
  59.2 2.2 %copy-start.3 = (bf16[4,2,1024,256]{3,2,1,0:T(8,128)(2,1)S(1)}, bf16[4,2,1024,256]{3,2,1,0:T(8,128)(2,1)}, u32[]{:S(2)}) copy-start(bf16[4,2,1024,256]{3,2,1,0:T(8,128)(2,1)} %copy-done.2) | copy-start | bytes 12582916
  61.4 8.0 %copy-start.10 = (bf16[256,1024]{1,0:T(8,128)(2,1)S(1)}, bf16[256,1024]{1,0:T(8,128)(2,1)}, u32[]{:S(2)}) copy-start(bf16[256,1024]{1,0:T(8,128)(2,1)} %copy-done.9) | copy-start | bytes 1572868
  67.4 2.0 %copy-start.6 = (f32[4,2,1024,128]{3,2,1,0:T(8,128)}, f32[4,2,1024,128]{3,2,1,0:T(8,128)S(1)}, u32[]{:S(2)}) copy-start(f32[4,2,1024,128]{3,2,1,0:T(8,128)S(1)} %get-tuple-element.48.refs_14_) | copy-start | bytes 12582916
  71.0 24.1 %collective-permute-start.11 = (bf16[256,1024]{1,0:T(8,128)(2,1)S(1)}, bf16[256,1024]{1,0:T(8,128)(2,1)S(1)}, u32[]{:S(2)}, u32[]{:S(2)}) collective-permute-start(bf16[256,1024]{1,0:T(8,128)(2,1)S(1)} %select_select_fusion.refs_3_.refs_8_), channel_id=1, source_target_pairs={{0,2},{1,3},{2,0},{3,1},{4,6},{5,7},{6,4},{7,5},{8,10},{9,11},{10,... | collective-permute-start | bytes 1572872 | tf_op jit(solution)/shard_map/ppermute | solution.py:220
  84.3 12.9 %collective-permute-start.12 = (bf16[256,1024]{1,0:T(8,128)(2,1)S(1)}, bf16[256,1024]{1,0:T(8,128)(2,1)S(1)}, u32[]{:S(2)}, u32[]{:S(2)}) collective-permute-start(bf16[256,1024]{1,0:T(8,128)(2,1)S(1)} %select_select_fusion.refs_3_.refs_8_), channel_id=1, source_target_pairs={{0,4},{1,5},{2,6},{3,7},{4,0},{5,1},{6,2},{7,3},{8,12},{9,13},{10,... | collective-permute-start | bytes 1572872 | tf_op jit(solution)/shard_map/ppermute | solution.py:223
  95.1 7.1 %collective-permute-start.13 = (bf16[128,1024]{1,0:T(8,128)(2,1)S(1)}, bf16[128,1024]{1,0:T(8,128)(2,1)S(1)}, u32[]{:S(2)}, u32[]{:S(2)}) collective-permute-start(bf16[128,1024]{1,0:T(8,128)(2,1)S(1)} %slice.23), channel_id=1, source_target_pairs={{0,4},{1,5},{2,6},{3,7},{4,0},{5,1},{6,2},{7,3},{8,12},{9,13},{10,... | collective-permute-start | bytes 786440 | tf_op jit(solution)/shard_map/ppermute | solution.py:223
  97.2 6.4 %collective-permute-start.14 = (bf16[128,1024]{1,0:T(8,128)(2,1)S(1)}, bf16[128,1024]{1,0:T(8,128)(2,1)S(1)}, u32[]{:S(2)}, u32[]{:S(2)}) collective-permute-start(bf16[128,1024]{1,0:T(8,128)(2,1)S(1)} %slice.24), channel_id=1, source_target_pairs={{0,2},{1,3},{2,0},{3,1},{4,6},{5,7},{6,4},{7,5},{8,10},{9,11},{10,... | collective-permute-start | bytes 786440 | tf_op jit(solution)/shard_map/ppermute | solution.py:220
  119.6 2.7 %collective-permute-start.15 = (bf16[128,4096]{1,0:T(8,128)(2,1)S(1)}, bf16[128,4096]{1,0:T(8,128)(2,1)S(1)}, u32[]{:S(2)}, u32[]{:S(2)}) collective-permute-start(bf16[128,4096]{1,0:T(8,128)(2,1)S(1)} %get-tuple-element.50), channel_id=1, source_target_pairs={{0,1},{1,0},{2,3},{3,2},{4,5},{5,4},{6,7},{7,6},{8,9},{9,8},{10,11... | collective-permute-start | bytes 3145736 | tf_op jit(solution)/shard_map/ppermute | solution.py:217

commit v3 on v2

--- a/solution.py
+++ b/solution.py
@@ -22,21 +22,17 @@
     refs = list(refs)
     take = lambda count: [refs.pop(0) for _ in range(count)]
     exp_ref, off_ref = take(2)
-    q_refs = take(2 if first else 1)
+    raw = take(2) if first else None
     key_refs = take(arrays)
     value_refs = take(arrays)
+    head = pl.program_id(0)
     if not first:
-        acc_in, ml_in = take(2)
-    if first:
-        (q_out,) = take(1)
-        qs = q_out
-    else:
-        qs = q_refs[0]
+        take(4)
     if last:
         outs = take(2)
     else:
-        acc_out, ml_out = take(2)
-    accs, ms = refs
+        take(1)[0][...] = jnp.zeros((8, HD), jnp.float32)
+    qs, accs, ms = take(3)
     stacked = GW * rows
 
     group = lax.axis_index("leaf")
@@ -53,19 +49,13 @@
         return ((y * 2 + x) * 2 + k) * rows
 
     if first:
-        for s, q_ref in enumerate(q_refs):
+        for s, q_ref in enumerate(raw):
             for g in range(GW):
                 q = q_ref[:, g * HD : (g + 1) * HD].astype(jnp.float32) * Q_SCALE
                 high = q.astype(jnp.bfloat16)
                 low = (q - high.astype(jnp.float32)).astype(jnp.bfloat16)
-                q_out[0, s, g * rows : (g + 1) * rows, :HD] = high
-                q_out[0, s, g * rows : (g + 1) * rows, HD:] = low
-    else:
-        for s in range(2):
-            accs[s, :, :HD] = acc_in[0, s]
-            ml = ml_in[0, s]
-            accs[s, :, HD:] = jnp.broadcast_to(ml[:, HD - 1 :], ml.shape)
-            ms[s] = jnp.broadcast_to(ml[:, :1], ml.shape)
+                qs[head, s, g * rows : (g + 1) * rows, :HD] = high
+                qs[head, s, g * rows : (g + 1) * rows, HD:] = low
 
     def step(members, limits, masked, fresh):
         width = len(members) * rows
@@ -79,7 +69,7 @@
 
         def score(s, here):
             return lax.dot_general(
-                qs[0, s, here, :], keys, (((1,), (1,)), ((), ())), preferred_element_type=jnp.float32
+                qs[head, s, here, :], keys, (((1,), (1,)), ((), ())), preferred_element_type=jnp.float32
             )
 
         def bias_of(s):
@@ -103,16 +93,16 @@
             if fresh:
                 new = jnp.broadcast_to(new, (size, HD))
             else:
-                old = ms[s, here, :]
+                old = ms[head, s, here, :]
                 new = jnp.maximum(old, new)
             weights = jnp.exp2(scores - jnp.concatenate([new] * (width // HD), axis=1))
             update = jnp.dot(weights.astype(jnp.bfloat16), values, preferred_element_type=jnp.float32)
             if fresh:
-                accs[s, here, :] = update
+                accs[head, s, here, :] = update
             else:
                 shrink = jnp.exp2(old - new)
-                accs[s, here, :] = accs[s, here, :] * jnp.concatenate([shrink, shrink], axis=1) + update
-            ms[s, here, :] = new
+                accs[head, s, here, :] = accs[head, s, here, :] * jnp.concatenate([shrink, shrink], axis=1) + update
+            ms[head, s, here, :] = new
 
     for number, members in enumerate(groups):
         limits = []
@@ -141,57 +131,63 @@
         if kinds != {"kin"}:
             pl.when(jnp.logical_not(full) & some)(functools.partial(step, members, limits, True, False))
 
-    for s in range(2):
-        if last:
-            done = (accs[s, :, :HD] / accs[s, :, HD:]).astype(jnp.bfloat16)
+    if last:
+        for s in range(2):
             for g in range(GW):
-                outs[s][:, g * HD : (g + 1) * HD] = done[g * rows : (g + 1) * rows]
-        else:
-            acc_out[0, s] = accs[s, :, :HD]
-            lane = lax.broadcasted_iota(jnp.int32, (stacked, HD), 1)
-            ml_out[0, s] = jnp.where(lane < HD // 2, ms[s], accs[s, :, HD:])
-
-
-def attend(ny, rows, tables, queries, arrays, groups, state, last):
+                here = slice(g * rows, (g + 1) * rows)
+                done = accs[head, s, here, :HD] / accs[head, s, here, HD:]
+                outs[s][:, g * HD : (g + 1) * HD] = done.astype(jnp.bfloat16)
+
+
+def attend(ny, rows, tables, arrays, groups, queries, state, last):
     stacked = GW * rows
     first = state is None
     smem = pl.BlockSpec(memory_space=pltpu.SMEM)
+    held = pl.BlockSpec(memory_space=pltpu.VMEM)
     row_spec = pl.BlockSpec((rows, GW * HD), lambda h: (0, h))
-    q_spec = pl.BlockSpec((1, 2, stacked, 2 * HD), lambda h: (h, 0, 0, 0))
-    state_spec = pl.BlockSpec((1, 2, stacked, HD), lambda h: (h, 0, 0, 0))
-    operands = [*tables, *queries]
-    specs = [smem, smem] + ([row_spec, row_spec] if first else [q_spec])
+    kept = [
+        ((HALF_KV, 2, stacked, 2 * HD), jnp.bfloat16),
+        ((HALF_KV, 2, stacked, 2 * HD), jnp.float32),
+        ((HALF_KV, 2, stacked, HD), jnp.float32),
+    ]
+    operands = [*tables]
+    specs = [smem, smem]
+    if first:
+        operands += queries
+        specs += [row_spec, row_spec]
     for shift in (0, HALF_KV):
         for array in arrays:
             operands.append(array)
             specs.append(pl.BlockSpec((array.shape[0], HD), functools.partial(lambda s, h: (0, s + h), shift)))
-    out_shape, out_specs = [], []
-    if first:
-        out_shape.append(jax.ShapeDtypeStruct((HALF_KV, 2, stacked, 2 * HD), jnp.bfloat16))
-        out_specs.append(q_spec)
+    aliases = {}
+    if last:
+        out_shape = [jax.ShapeDtypeStruct((rows, HALF_KV * GW * HD), jnp.bfloat16)] * 2
+        out_specs = [row_spec, row_spec]
     else:
-        operands += list(state)
-        specs += [state_spec, state_spec]
-    if last:
-        out_shape += [jax.ShapeDtypeStruct((rows, HALF_KV * GW * HD), jnp.bfloat16)] * 2
-        out_specs += [row_spec, row_spec]
-    else:
-        out_shape += [jax.ShapeDtypeStruct((HALF_KV, 2, stacked, HD), jnp.float32)] * 2
-        out_specs += [state_spec, state_spec]
+        out_shape = [jax.ShapeDtypeStruct((8, HD), jnp.float32)]
+        out_specs = [pl.BlockSpec((8, HD), lambda h: (0, 0))]
+    if not first:
+        mark, *state = state
+        operands.append(mark)
+        specs.append(pl.BlockSpec(memory_space=pl.ANY))
+        for i, array in enumerate(state):
+            aliases[len(operands)] = len(out_shape) + i
+            operands.append(pltpu.with_memory_space_constraint(array, pltpu.VMEM))
+            specs.append(held)
+    out_shape += [pltpu.VMEM(shape, dtype) for shape, dtype in kept]
+    out_specs += [held] * 3
     scores = HALF_KV * 2 * stacked * rows * sum(len(members) for members in groups)
-    return pl.pallas_call(
+    out = pl.pallas_call(
         functools.partial(attend_kernel, ny, rows, len(arrays), groups, first, last),
         grid=(HALF_KV,),
         in_specs=specs,
         out_specs=out_specs,
         out_shape=out_shape,
-        scratch_shapes=[
-            pltpu.VMEM((2, stacked, 2 * HD), jnp.float32),
-            pltpu.VMEM((2, stacked, HD), jnp.float32),
-        ],
-        compiler_params=pltpu.CompilerParams(vmem_limit_bytes=40 * 2**20),
-        cost_estimate=pl.CostEstimate(flops=8 * scores * HD, bytes_accessed=20 * 2**20, transcendentals=scores),
+        input_output_aliases=aliases,
+        compiler_params=pltpu.CompilerParams(vmem_limit_bytes=24 * 2**20),
+        cost_estimate=pl.CostEstimate(flops=8 * scores * HD, bytes_accessed=4 * 2**20, transcendentals=scores),
     )(*operands)
+    return out[:2] if last else list(out)
 
 
 def on_device(queries, seg_keys, seg_values, root_keys, root_values, expansion, root_offsets):
@@ -250,56 +246,33 @@
     run = functools.partial(attend, ny, rows, tables)
     steps = range(1, ny)
 
-    parent = expansion[0, group]
-    choices = []
-
-    def hop(step, down, up):
-        down = lax.ppermute(down, "leaf", [(i, i - 1) for i in range(1, leaves - step + 1)])
-        choices.append((group + step, down))
-        if step < leaves - 1:
-            up = lax.ppermute(up, "leaf", [(i, i + 1) for i in range(step - 1, leaves - 2)])
-            choices.append((group - step, up))
-        return down, up
-
-    down, up = hop(1, segment, segment)
+    every = lax.all_gather(segment, "leaf", axis=0, tiled=True)
     from_x = to_x(local)
     from_y = [to_y(local, step) for step in steps]
-    q_ready, *state = run(q_pair, [local], (members(0, 0, 0),), None, False)
-    if leaves > 2:
-        down, up, state = lax.optimization_barrier((down, up, state))
-        down, up = hop(2, down, up)
-
+    state = run([local], (members(0, 0, 0),), q_pair, None, False)
+    from_x, from_y, state[0] = lax.optimization_barrier((from_x, from_y, state[0]))
     tops = [to_y(from_x[: 2 * rows], step) for step in steps]
     lows = [to_x(array[2 * rows :]) for array in from_y]
     near = [members(0, 1, 0, wanted=(kind,)) + members(1, 0, 1, wanted=(kind,)) for kind in kinds]
     near += [members(step, 0, step) for step in steps if step > 1]
-    state = run([q_ready], [from_x, *from_y], tuple(near), state, False)
-    for step in range(3, leaves):
-        down, up, state = lax.optimization_barrier((down, up, state))
-        down, up = hop(step, down, up)
+    state = run([from_x, *from_y], tuple(near), None, state, False)
+
+    every, state[0] = lax.optimization_barrier((every, state[0]))
+    parent_rows = lax.dynamic_slice_in_dim(every, expansion[0, group] * 2 * rows, 2 * rows, 0)
+    parent_rows, state[0] = lax.optimization_barrier((parent_rows, state[0]))
+    kin_x = to_x(parent_rows)
+    kin_y = [to_y(parent_rows, step) for step in steps]
     far, arrays = [], []
     for step, top, low in zip(steps, tops, lows):
-        far.append(
-            members(len(arrays), 1, step, (0,)) + members(len(arrays) + 1, 1, step, (1,))
-        )
+        far.append(members(len(arrays), 1, step, (0,)) + members(len(arrays) + 1, 1, step, (1,)))
         arrays += [top, low]
-    state = run([q_ready], arrays, tuple(far), state, False)
-
-    owners, helds = zip(*choices)
-    helds, state = lax.optimization_barrier((helds, state))
-    parent_rows = segment
-    for owner, held in zip(owners, helds):
-        parent_rows = jnp.where(parent == owner, held, parent_rows)
-    kin_x = to_x(parent_rows)
-    kin_y = [to_y(parent_rows, step) for step in steps]
+    state = run(arrays, tuple(far), None, state, False)
     tops = [to_y(kin_x[:rows], step) for step in steps]
     lows = [to_x(array[rows:]) for array in kin_y]
-    arrays = [parent_rows, kin_x, *kin_y, *tops, *lows]
-    last_groups = [kin((0, 2), (1, 2), (2, 2), (1 + ny, 1), (2 * ny, 1))]
-    for step in steps:
-        if step > 1:
-            last_groups.append(kin((1 + step, 2), (ny + step, 1), (2 * ny - 1 + step, 1)))
-    out_mine, out_other = run([q_ready], arrays, tuple(last_groups), state, True)
+    groups = [kin((0, 2), (1, 2), (2, 2))] + [kin((1 + step, 2)) for step in steps if step > 1]
+    state = run([parent_rows, kin_x, *kin_y], tuple(groups), None, state, False)
+    groups = tuple(kin((step - 1, 1), (ny + step - 2, 1)) for step in steps)
+    out_mine, out_other = run([*tops, *lows], groups, None, state, True)
     out_got = to_core(out_other)
     return jnp.where(
         core == 0,

time: 124 us -> 118 us (0.952)
  between operations: 3.35 us -> 15.3 us
  Pallas kernels: 43.2 us -> 32.9 us
  starting transfers between devices: 32.4 us -> 23.1 us
  local copies, waits for them, and re-layouts: 17.8 us -> 23 us
  waiting for transfers between devices: 23 us -> 19.5 us
    pallas_call x4 -> x5, Pallas kernels: 43.2 us -> 32.9 us  [attend(): pl.pallas_call(functools.partial(attend_kernel, ny, rows, len(arrays), gr...]
    ppermute x5 -> x0, starting transfers between devices: 9.31 us -> none  [the longest x2 5.27 us: hop(): lax.ppermute(up, 'leaf', [(i, i + 1) for i in range(step - 1, leaves - 2)])]
    ppermute x4, waiting for transfers between devices: 6.57 us -> 1.57 us  [to_y(): lax.ppermute(array, 'ctx', [(index(x, y, k), index(x, y + step, k)) for x...]
    ppermute x4, starting transfers between devices: 16.5 us -> 11.8 us  [to_x(): lax.ppermute(array, 'ctx', [(index(x, y, k), index(x + 1, y, k)) for x, y...]
    ppermute x4, starting transfers between devices: 5.91 us -> 10.4 us  [to_y(): lax.ppermute(array, 'ctx', [(index(x, y, k), index(x, y + step, k)) for x...]
    unnamed x22 -> x24, local copies, waits for them, and re-layouts: 12.9 us -> 15.8 us
    select_n x1 -> x0, other arithmetic: 1.65 us -> none  [on_device(): parent_rows = jnp.where(parent == owner, held, parent_rows)]
    ppermute x4, waiting for transfers between devices: 12.3 us -> 13.7 us  [to_x(): lax.ppermute(array, 'ctx', [(index(x, y, k), index(x + 1, y, k)) for x, y...]
  transfers between devices with their start and end apart: 16 -> 12, of which waited for: 7 -> 5; matrix products, arithmetic and copies ran while one was open for 2% -> 4% of each run, Pallas kernels for 22% -> 23%
where the time goes in v3:
time: 118 us; the launch traced here: 117 us
  Pallas kernels  32.9 us (28%)
  starting transfers between devices  23.1 us (20%)
  local copies, waits for them, and re-layouts  23 us (19%)
  waiting for transfers between devices  19.5 us (17%)
  between operations  15.3 us (13%)
  other arithmetic  3.38 us (3%)
    pallas_call x5, Pallas kernels, attend(): pl.pallas_call(functools.partial(attend_kernel, ny, rows, len(arrays), gr...  32.9 us
    unnamed x24, local copies, waits for them, and re-layouts  15.8 us
    ppermute x4, waiting for transfers between devices, to_x(): lax.ppermute(array, 'ctx', [(index(x, y, k), index(x + 1, y, k)) for x, y...  13.7 us
    ppermute x4, starting transfers between devices, to_x(): lax.ppermute(array, 'ctx', [(index(x, y, k), index(x + 1, y, k)) for x, y...  11.8 us
    ppermute x4, starting transfers between devices, to_y(): lax.ppermute(array, 'ctx', [(index(x, y, k), index(x, y + step, k)) for x...  10.4 us
    ppermute x3, waiting for transfers between devices, to_core(): lax.ppermute(array, 'ctx', [(index(x, y, k), index(x, y, k + 1)) for x, y...  4.18 us
    dynamic_slice x2, local copies, waits for them, and re-layouts, halves(): lax.dynamic_slice_in_dim(array, core * half, half, 1)  3.08 us
  transfers between devices with their start and end apart: 12, of which 5 were waited for; matrix products, arithmetic and copies ran while one was open for 4% of the time, Pallas kernels for 23%

profile of v3, /device:TPU:0, one launch (start us, length us, event | category | flops | bytes accessed | tf_op | source)
XLA Modules:
  0.0 117.2 jit_solution(13824232284545605873)
XLA Ops:
  6.5 1.3 %constant_dynamic-slice_fusion.10 = (bf16[128,512]{1,0:T(8,128)(2,1)S(1)}, bf16[128,512]{1,0:T(8,128)(2,1)S(1)}, bf16[128,512]{1,0:T(8,128)(2,1)S(1)}, bf16[128,512]{1,0:T(8,128)(2,1)S(1)}) fusion(bf16[128,1024]{1,0:T(8,128)(2,1)} %param.9, s32[]{:T(128)S(6)} %select_n.33, s32[]{:T(128)S(6)} %select_n.34, bf16[128,1024]{1,0:T(8,128)(2,1)} %param.8), kind=kLoop, calls=%fused_computation.14 | loop fusion | bytes 1048584 | tf_op jit(solution)/shard_map/dynamic_slice | solution.py:203
  7.8 1.8 %constant_dynamic-slice_fusion.4 = (bf16[128,512]{1,0:T(8,128)(2,1)S(1)}, bf16[128,512]{1,0:T(8,128)(2,1)S(1)}, bf16[128,512]{1,0:T(8,128)(2,1)S(1)}, bf16[128,512]{1,0:T(8,128)(2,1)}) fusion(bf16[128,1024]{1,0:T(8,128)(2,1)} %param.11, s32[]{:T(128)S(6)} %select_n.33, s32[]{:T(128)S(6)} %select_n.34, bf16[128,1024]{1,0:T(8,128)(2,1)} %param.10), kind=kLoop, calls=%fused_computation.8 | loop fusion | bytes 1048584 | tf_op jit(solution)/shard_map/dynamic_slice | solution.py:203
  9.7 0.5 collective-permute-start
  10.2 1.5 %collective-permute-done = bf16[256,1024]{1,0:T(8,128)(2,1)S(1)} collective-permute-done((bf16[256,1024]{1,0:T(8,128)(2,1)S(1)}, bf16[256,1024]{1,0:T(8,128)(2,1)S(1)}, u32[]{:S(2)}, u32[]{:S(2)}) %collective-permute-start) | collective-permute-done | bytes 524320 | tf_op jit(solution)/shard_map/ppermute | solution.py:213
  11.8 0.8 copy-done.9
  12.6 0.9 pad_maximum_fusion.1
  13.5 1.1 constant_dynamic-slice_fusion.2
  15.1 2.7 %collective-permute-start.1 = (bf16[512,1024]{1,0:T(8,128)(2,1)S(1)}, bf16[512,1024]{1,0:T(8,128)(2,1)S(1)}, u32[]{:S(2)}, u32[]{:S(2)}) collective-permute-start(bf16[512,1024]{1,0:T(8,128)(2,1)S(1)} %pad_maximum_fusion.refs_4_.refs_5_), channel_id=1, source_target_pairs={{0,2},{1,3},{2,0},{3,1},{4,6},{5,7},{6,4},{7,5},{8,10},{9,11},{10,... | collective-permute-start | bytes 3145736 | tf_op jit(solution)/shard_map/ppermute | solution.py:216
  17.8 1.5 %collective-permute-start.2 = (bf16[512,1024]{1,0:T(8,128)(2,1)S(1)}, bf16[512,1024]{1,0:T(8,128)(2,1)}, u32[]{:S(2)}, u32[]{:S(2)}) collective-permute-start(bf16[512,1024]{1,0:T(8,128)(2,1)S(1)} %pad_maximum_fusion.refs_4_.refs_5_), channel_id=1, source_target_pairs={{0,4},{1,5},{2,6},{3,7},{4,0},{5,1},{6,2},{7,3},{8,12},{9,13},{10,... | collective-permute-start | bytes 3145736 | tf_op jit(solution)/shard_map/ppermute | solution.py:219
  19.4 0.6 fusion
  21.6 7.7 %shard_map.73 = (f32[8,128]{1,0:T(8,128)S(1)}, bf16[4,2,1024,256]{3,2,1,0:T(8,128)(2,1)S(1)}, f32[4,2,1024,256]{3,2,1,0:T(8,128)S(1)}, f32[4,2,1024,128]{3,2,1,0:T(8,128)S(1)}) custom-call(s32[2,4]{1,0:T(2,128)S(1)} %copy-done.6, s32[4]{0:T(128)S(1)} %copy-done.7, bf16[128,4096]{1,0:T(8,128)(2,1)S(1)} %get-tuple-element.56.refs_2_, ...), custom_call_target="tpu_custom_call" | custom-call | flops 4294967296 | bytes 4194304 | tf_op jit(solution)/shard_map/pallas_call | solution.py:180
  29.4 12.1 %collective-permute-done.1.refs_2_.refs_4_ = bf16[512,1024]{1,0:T(8,128)(2,1)S(1)} collective-permute-done((bf16[512,1024]{1,0:T(8,128)(2,1)S(1)}, bf16[512,1024]{1,0:T(8,128)(2,1)S(1)}, u32[]{:S(2)}, u32[]{:S(2)}) %collective-permute-start.1) | collective-permute-done | bytes 1048608 | tf_op jit(solution)/shard_map/ppermute | solution.py:216
  41.5 1.6 %collective-permute-done.2.refs_3_.refs_5_ = bf16[512,1024]{1,0:T(8,128)(2,1)} collective-permute-done((bf16[512,1024]{1,0:T(8,128)(2,1)S(1)}, bf16[512,1024]{1,0:T(8,128)(2,1)}, u32[]{:S(2)}, u32[]{:S(2)}) %collective-permute-start.2) | collective-permute-done | bytes 1048608 | tf_op jit(solution)/shard_map/ppermute | solution.py:219
  43.1 1.6 %collective-permute-start.8 = (bf16[256,1024]{1,0:T(8,128)(2,1)S(1)}, bf16[256,1024]{1,0:T(8,128)(2,1)S(1)}, u32[]{:S(2)}, u32[]{:S(2)}) collective-permute-start(bf16[256,1024]{1,0:T(8,128)(2,1)S(1)} %slice.18), channel_id=1, source_target_pairs={{0,4},{1,5},{2,6},{3,7},{4,0},{5,1},{6,2},{7,3},{8,12},{9,13},{10,... | collective-permute-start | bytes 1572872 | tf_op jit(solution)/shard_map/ppermute | solution.py:219
  44.7 1.9 %slice.19 = bf16[256,1024]{1,0:T(8,128)(2,1)} slice(bf16[512,1024]{1,0:T(8,128)(2,1)} %collective-permute-done.2.refs_3_.refs_5_), slice={[256:512], [0:1024]} | slice | bytes 1048576 | tf_op jit(solution)/shard_map/slice | solution.py:255
  46.6 0.5 collective-permute-start.9
  47.1 8.4 %shard_map.74 = (f32[8,128]{1,0:T(8,128)S(1)}, bf16[4,2,1024,256]{3,2,1,0:T(8,128)(2,1)S(1)}, f32[4,2,1024,256]{3,2,1,0:T(8,128)S(1)}, f32[4,2,1024,128]{3,2,1,0:T(8,128)S(1)}) custom-call(s32[2,4]{1,0:T(2,128)S(1)} %copy-done.6, s32[4]{0:T(128)S(1)} %copy-done.7, ...), custom_call_target="tpu_custom_call", output_to_operand_aliasing={{1}: (7, {}), {2}: (8, {}), {3}: (9, {})} | custom-call | flops 8589934592 | bytes 4194304 | tf_op jit(solution)/shard_map/pallas_call | solution.py:180
  55.5 3.3 %copy-done = f32[4,2,1024,256]{3,2,1,0:T(8,128)} copy-done((f32[4,2,1024,256]{3,2,1,0:T(8,128)}, f32[4,2,1024,256]{3,2,1,0:T(8,128)S(1)}, u32[]{:S(2)}) %copy-start) | copy-done | bytes 8388632
  58.8 2.0 %copy-done.2 = bf16[4,2,1024,256]{3,2,1,0:T(8,128)(2,1)} copy-done((bf16[4,2,1024,256]{3,2,1,0:T(8,128)(2,1)}, bf16[4,2,1024,256]{3,2,1,0:T(8,128)(2,1)S(1)}, u32[]{:S(2)}) %copy-start.2) | copy-done | bytes 4194328
  60.8 1.9 %copy-done.4 = f32[4,2,1024,128]{3,2,1,0:T(8,128)} copy-done((f32[4,2,1024,128]{3,2,1,0:T(8,128)}, f32[4,2,1024,128]{3,2,1,0:T(8,128)S(1)}, u32[]{:S(2)}) %copy-start.4) | copy-done | bytes 4194328
  62.7 1.1 constant_dynamic-slice_fusion.refs_2_.refs_5_
  63.8 8.4 %collective-permute-start.4 = (bf16[256,1024]{1,0:T(8,128)(2,1)S(1)}, bf16[256,1024]{1,0:T(8,128)(2,1)S(1)}, u32[]{:S(2)}, u32[]{:S(2)}) collective-permute-start(bf16[256,1024]{1,0:T(8,128)(2,1)S(1)} %constant_dynamic-slice_fusion.refs_2_.refs_5_), channel_id=1, source_target_pairs={{0,2},{1,3},{2,0},{3,1},{4,6},{5,7},{6,4},{7,5},{8,10},{9,11},{10,... | collective-permute-start | bytes 1572872 | tf_op jit(solution)/shard_map/ppermute | solution.py:216
  72.3 3.4 %copy-done.1 = f32[4,2,1024,256]{3,2,1,0:T(8,128)S(1)} copy-done((f32[4,2,1024,256]{3,2,1,0:T(8,128)S(1)}, f32[4,2,1024,256]{3,2,1,0:T(8,128)}, u32[]{:S(2)}) %copy-start.1) | copy-done | bytes 8388632
  75.7 2.2 %copy-done.3 = bf16[4,2,1024,256]{3,2,1,0:T(8,128)(2,1)S(1)} copy-done((bf16[4,2,1024,256]{3,2,1,0:T(8,128)(2,1)S(1)}, bf16[4,2,1024,256]{3,2,1,0:T(8,128)(2,1)}, u32[]{:S(2)}) %copy-start.3) | copy-done | bytes 4194328
  77.9 2.2 %copy-done.5 = f32[4,2,1024,128]{3,2,1,0:T(8,128)S(1)} copy-done((f32[4,2,1024,128]{3,2,1,0:T(8,128)S(1)}, f32[4,2,1024,128]{3,2,1,0:T(8,128)}, u32[]{:S(2)}) %copy-start.5) | copy-done | bytes 4194328
  80.1 1.4 %shard_map.75 = (f32[8,128]{1,0:T(8,128)S(1)}, bf16[4,2,1024,256]{3,2,1,0:T(8,128)(2,1)S(1)}, f32[4,2,1024,256]{3,2,1,0:T(8,128)S(1)}, f32[4,2,1024,128]{3,2,1,0:T(8,128)S(1)}) custom-call(s32[2,4]{1,0:T(2,128)S(1)} %copy-done.6, s32[4]{0:T(128)S(1)} %copy-done.7, ...), custom_call_target="tpu_custom_call", output_to_operand_aliasing={{1}: (7, {}), {2}: (8, {}), {3}: (9, {})} | custom-call | flops 4294967296 | bytes 4194304 | tf_op jit(solution)/shard_map/pallas_call | solution.py:180
  81.4 1.6 %collective-permute-done.4.refs_3_.refs_6_ = bf16[256,1024]{1,0:T(8,128)(2,1)S(1)} collective-permute-done((bf16[256,1024]{1,0:T(8,128)(2,1)S(1)}, bf16[256,1024]{1,0:T(8,128)(2,1)S(1)}, u32[]{:S(2)}, u32[]{:S(2)}) %collective-permute-start.4) | collective-permute-done | bytes 524320 | tf_op jit(solution)/shard_map/ppermute | solution.py:216
  83.0 7.2 %collective-permute-start.5 = (bf16[128,1024]{1,0:T(8,128)(2,1)S(1)}, bf16[128,1024]{1,0:T(8,128)(2,1)S(1)}, u32[]{:S(2)}, u32[]{:S(2)}) collective-permute-start(bf16[128,1024]{1,0:T(8,128)(2,1)S(1)} %slice.21), channel_id=1, source_target_pairs={{0,4},{1,5},{2,6},{3,7},{4,0},{5,1},{6,2},{7,3},{8,12},{9,13},{10,... | collective-permute-start | bytes 786440 | tf_op jit(solution)/shard_map/ppermute | solution.py:219
  90.3 9.9 %shard_map.76 = (f32[8,128]{1,0:T(8,128)S(1)}, bf16[4,2,1024,256]{3,2,1,0:T(8,128)(2,1)S(1)}, f32[4,2,1024,256]{3,2,1,0:T(8,128)S(1)}, f32[4,2,1024,128]{3,2,1,0:T(8,128)S(1)}) custom-call(s32[2,4]{1,0:T(2,128)S(1)} %copy-done.6, s32[4]{0:T(128)S(1)} %copy-done.7, ...), custom_call_target="tpu_custom_call", output_to_operand_aliasing={{1}: (9, {}), {2}: (10, {}), {3}: (11, {})} | custom-call | flops 6442450944 | bytes 4194304 | tf_op jit(solution)/shard_map/pallas_call | solution.py:180
  100.3 5.6 %shard_map.77 = (bf16[128,4096]{1,0:T(8,128)(2,1)S(1)}, bf16[128,4096]{1,0:T(8,128)(2,1)S(1)}, bf16[4,2,1024,256]{3,2,1,0:T(8,128)(2,1)S(1)}, f32[4,2,1024,256]{3,2,1,0:T(8,128)S(1)}, f32[4,2,1024,128]{3,2,1,0:T(8,128)S(1)}) custom-call(s32[2,4]{1,0:T(2,128)S(1)} %copy-done.6, ...), custom_call_target="tpu_custom_call", output_to_operand_aliasing={{2}: (7, {}), {3}: (8, {}), {4}: (9, {})} | custom-call | flops 2147483648 | bytes 4194304 | tf_op jit(solution)/shard_map/pallas_call | solution.py:180
  105.9 2.6 %collective-permute-done.10 = bf16[128,4096]{1,0:T(8,128)(2,1)S(1)} collective-permute-done((bf16[128,4096]{1,0:T(8,128)(2,1)S(1)}, bf16[128,4096]{1,0:T(8,128)(2,1)S(1)}, u32[]{:S(2)}, u32[]{:S(2)}) %collective-permute-start.10) | collective-permute-done | bytes 1048608 | tf_op jit(solution)/shard_map/ppermute | solution.py:213
  108.6 1.8 %maximum_select_fusion = bf16[128,8192]{1,0:T(8,128)(2,1)} fusion(bf16[128,4096]{1,0:T(8,128)(2,1)S(1)} %collective-permute-done.10, bf16[128,4096]{1,0:T(8,128)(2,1)S(1)} %get-tuple-element.53, pred[]{:T(512)S(6)} %eq.3), kind=kLoop, calls=%fused_computation | loop fusion | flops 9437184 | bytes 4194305 | tf_op jit(solution)/shard_map/jit(_where)/select_n | solution.py:277
  (36 shorter events, 0.9 us)
Async XLA Ops:
  6.5 6.9 %copy-start.8 = (bf16[128,8192]{1,0:T(8,128)(2,1)S(1)}, bf16[128,8192]{1,0:T(8,128)(2,1)}, u32[]{:S(2)}) copy-start(bf16[128,8192]{1,0:T(8,128)(2,1)} %param.7) | copy-start | bytes 6291460
  6.5 56.2 %all-gather.2.cloned.1.call-start = ((), (), s32[]{:S(2)}) async-start(), calls=%async_computation | async-start | bytes 2621440 | tf_op jit(solution)/shard_map/all_gather | solution.py:249
  9.7 9.7 %copy-start.6 = (s32[2,4]{1,0:T(2,128)S(1)}, s32[2,4]{1,0:T(2,128)}, u32[]{:S(2)}) copy-start(s32[2,4]{1,0:T(2,128)} %refs_0_.9) | copy-start | bytes 100
  9.7 11.9 %copy-start.7 = (s32[4]{0:T(128)S(1)}, s32[4]{0:T(128)}, u32[]{:S(2)}) copy-start(s32[4]{0:T(128)} %refs_1_.9) | copy-start | bytes 52
  9.7 2.1 %collective-permute-start = (bf16[256,1024]{1,0:T(8,128)(2,1)S(1)}, bf16[256,1024]{1,0:T(8,128)(2,1)S(1)}, u32[]{:S(2)}, u32[]{:S(2)}) collective-permute-start(bf16[256,1024]{1,0:T(8,128)(2,1)S(1)} %maximum_maximum_fusion), channel_id=1, source_target_pairs={{0,1},{1,0},{2,3},{3,2},{4,5},{5,4},{6,7},{7,6},{8,9},{9,8},{10,11... | collective-permute-start | bytes 1572872 | tf_op jit(solution)/shard_map/ppermute | solution.py:213
  11.8 0.8 copy-start.9
  13.5 1.5 %copy-start.10 = (bf16[256,1024]{1,0:T(8,128)(2,1)S(1)}, bf16[256,1024]{1,0:T(8,128)(2,1)}, u32[]{:S(2)}) copy-start(bf16[256,1024]{1,0:T(8,128)(2,1)} %copy-done.9) | copy-start | bytes 1572868
  13.5 1.5 %copy-start.11 = (bf16[128,512]{1,0:T(8,128)(2,1)S(1)}, bf16[128,512]{1,0:T(8,128)(2,1)}, u32[]{:S(2)}) copy-start(bf16[128,512]{1,0:T(8,128)(2,1)} %get-tuple-element.66) | copy-start | bytes 393220
  14.7 7.0 %collective-permute-start.3 = (bf16[128,4096]{1,0:T(8,128)(2,1)}, bf16[128,4096]{1,0:T(8,128)(2,1)}, u32[]{:S(2)}, u32[]{:S(2)}) collective-permute-start(bf16[128,4096]{1,0:T(8,128)(2,1)} %get-tuple-element.55), channel_id=1, source_target_pairs={{0,1},{1,0},{2,3},{3,2},{4,5},{5,4},{6,7},{7,6},{8,9},{9,8},{10,11... | collective-permute-start | bytes 3145736 | tf_op jit(solution)/shard_map/ppermute | solution.py:213
  15.1 26.4 %collective-permute-start.1 = (bf16[512,1024]{1,0:T(8,128)(2,1)S(1)}, bf16[512,1024]{1,0:T(8,128)(2,1)S(1)}, u32[]{:S(2)}, u32[]{:S(2)}) collective-permute-start(bf16[512,1024]{1,0:T(8,128)(2,1)S(1)} %pad_maximum_fusion.refs_4_.refs_5_), channel_id=1, source_target_pairs={{0,2},{1,3},{2,0},{3,1},{4,6},{5,7},{6,4},{7,5},{8,10},{9,11},{10,... | collective-permute-start | bytes 3145736 | tf_op jit(solution)/shard_map/ppermute | solution.py:216
  17.8 25.2 %collective-permute-start.2 = (bf16[512,1024]{1,0:T(8,128)(2,1)S(1)}, bf16[512,1024]{1,0:T(8,128)(2,1)}, u32[]{:S(2)}, u32[]{:S(2)}) collective-permute-start(bf16[512,1024]{1,0:T(8,128)(2,1)S(1)} %pad_maximum_fusion.refs_4_.refs_5_), channel_id=1, source_target_pairs={{0,4},{1,5},{2,6},{3,7},{4,0},{5,1},{6,2},{7,3},{8,12},{9,13},{10,... | collective-permute-start | bytes 3145736 | tf_op jit(solution)/shard_map/ppermute | solution.py:219
  43.1 29.2 %collective-permute-start.8 = (bf16[256,1024]{1,0:T(8,128)(2,1)S(1)}, bf16[256,1024]{1,0:T(8,128)(2,1)S(1)}, u32[]{:S(2)}, u32[]{:S(2)}) collective-permute-start(bf16[256,1024]{1,0:T(8,128)(2,1)S(1)} %slice.18), channel_id=1, source_target_pairs={{0,4},{1,5},{2,6},{3,7},{4,0},{5,1},{6,2},{7,3},{8,12},{9,13},{10,... | collective-permute-start | bytes 1572872 | tf_op jit(solution)/shard_map/ppermute | solution.py:219
  46.6 25.7 %collective-permute-start.9 = (bf16[256,1024]{1,0:T(8,128)(2,1)}, bf16[256,1024]{1,0:T(8,128)(2,1)S(1)}, u32[]{:S(2)}, u32[]{:S(2)}) collective-permute-start(bf16[256,1024]{1,0:T(8,128)(2,1)} %slice.19), channel_id=1, source_target_pairs={{0,2},{1,3},{2,0},{3,1},{4,6},{5,7},{6,4},{7,5},{8,10},{9,11},{10,... | collective-permute-start | bytes 1572872 | tf_op jit(solution)/shard_map/ppermute | solution.py:216
  55.5 3.3 %copy-start = (f32[4,2,1024,256]{3,2,1,0:T(8,128)}, f32[4,2,1024,256]{3,2,1,0:T(8,128)S(1)}, u32[]{:S(2)}) copy-start(f32[4,2,1024,256]{3,2,1,0:T(8,128)S(1)} %get-tuple-element.43.refs_8_) | copy-start | bytes 25165828
  58.8 2.0 %copy-start.2 = (bf16[4,2,1024,256]{3,2,1,0:T(8,128)(2,1)}, bf16[4,2,1024,256]{3,2,1,0:T(8,128)(2,1)S(1)}, u32[]{:S(2)}) copy-start(bf16[4,2,1024,256]{3,2,1,0:T(8,128)(2,1)S(1)} %get-tuple-element.42.refs_7_) | copy-start | bytes 12582916
  60.8 1.9 %copy-start.4 = (f32[4,2,1024,128]{3,2,1,0:T(8,128)}, f32[4,2,1024,128]{3,2,1,0:T(8,128)S(1)}, u32[]{:S(2)}) copy-start(f32[4,2,1024,128]{3,2,1,0:T(8,128)S(1)} %get-tuple-element.44.refs_9_) | copy-start | bytes 12582916
  63.8 19.2 %collective-permute-start.4 = (bf16[256,1024]{1,0:T(8,128)(2,1)S(1)}, bf16[256,1024]{1,0:T(8,128)(2,1)S(1)}, u32[]{:S(2)}, u32[]{:S(2)}) collective-permute-start(bf16[256,1024]{1,0:T(8,128)(2,1)S(1)} %constant_dynamic-slice_fusion.refs_2_.refs_5_), channel_id=1, source_target_pairs={{0,2},{1,3},{2,0},{3,1},{4,6},{5,7},{6,4},{7,5},{8,10},{9,11},{10,... | collective-permute-start | bytes 1572872 | tf_op jit(solution)/shard_map/ppermute | solution.py:216
  72.2 18.0 %collective-permute-start.6 = (bf16[256,1024]{1,0:T(8,128)(2,1)S(1)}, bf16[256,1024]{1,0:T(8,128)(2,1)S(1)}, u32[]{:S(2)}, u32[]{:S(2)}) collective-permute-start(bf16[256,1024]{1,0:T(8,128)(2,1)S(1)} %constant_dynamic-slice_fusion.refs_2_.refs_5_), channel_id=1, source_target_pairs={{0,4},{1,5},{2,6},{3,7},{4,0},{5,1},{6,2},{7,3},{8,12},{9,13},{10,... | collective-permute-start | bytes 1572872 | tf_op jit(solution)/shard_map/ppermute | solution.py:219
  72.3 3.4 %copy-start.1 = (f32[4,2,1024,256]{3,2,1,0:T(8,128)S(1)}, f32[4,2,1024,256]{3,2,1,0:T(8,128)}, u32[]{:S(2)}) copy-start(f32[4,2,1024,256]{3,2,1,0:T(8,128)} %copy-done) | copy-start | bytes 25165828
  75.7 2.2 %copy-start.3 = (bf16[4,2,1024,256]{3,2,1,0:T(8,128)(2,1)S(1)}, bf16[4,2,1024,256]{3,2,1,0:T(8,128)(2,1)}, u32[]{:S(2)}) copy-start(bf16[4,2,1024,256]{3,2,1,0:T(8,128)(2,1)} %copy-done.2) | copy-start | bytes 12582916
  77.9 2.2 %copy-start.5 = (f32[4,2,1024,128]{3,2,1,0:T(8,128)S(1)}, f32[4,2,1024,128]{3,2,1,0:T(8,128)}, u32[]{:S(2)}) copy-start(f32[4,2,1024,128]{3,2,1,0:T(8,128)} %copy-done.4) | copy-start | bytes 12582916
  83.0 17.2 %collective-permute-start.5 = (bf16[128,1024]{1,0:T(8,128)(2,1)S(1)}, bf16[128,1024]{1,0:T(8,128)(2,1)S(1)}, u32[]{:S(2)}, u32[]{:S(2)}) collective-permute-start(bf16[128,1024]{1,0:T(8,128)(2,1)S(1)} %slice.21), channel_id=1, source_target_pairs={{0,4},{1,5},{2,6},{3,7},{4,0},{5,1},{6,2},{7,3},{8,12},{9,13},{10,... | collective-permute-start | bytes 786440 | tf_op jit(solution)/shard_map/ppermute | solution.py:219
  90.3 10.0 %collective-permute-start.7 = (bf16[128,1024]{1,0:T(8,128)(2,1)S(1)}, bf16[128,1024]{1,0:T(8,128)(2,1)S(1)}, u32[]{:S(2)}, u32[]{:S(2)}) collective-permute-start(bf16[128,1024]{1,0:T(8,128)(2,1)S(1)} %slice.22), channel_id=1, source_target_pairs={{0,2},{1,3},{2,0},{3,1},{4,6},{5,7},{6,4},{7,5},{8,10},{9,11},{10,... | collective-permute-start | bytes 786440 | tf_op jit(solution)/shard_map/ppermute | solution.py:216
  105.8 2.7 %collective-permute-start.10 = (bf16[128,4096]{1,0:T(8,128)(2,1)S(1)}, bf16[128,4096]{1,0:T(8,128)(2,1)S(1)}, u32[]{:S(2)}, u32[]{:S(2)}) collective-permute-start(bf16[128,4096]{1,0:T(8,128)(2,1)S(1)} %get-tuple-element.54), channel_id=1, source_target_pairs={{0,1},{1,0},{2,3},{3,2},{4,5},{5,4},{6,7},{7,6},{8,9},{9,8},{10,11... | collective-permute-start | bytes 3145736 | tf_op jit(solution)/shard_map/ppermute | solution.py:213
Sparse Core Ops, SparseCore 0:
  13.6 48.5 all-gather.1

commit v4 on v3

--- a/solution.py
+++ b/solution.py
@@ -15,7 +15,7 @@
 HALF_KV = KVH // 2
 NEG = -1e30
 Q_SCALE = math.log2(math.e) / math.sqrt(HD)
-ROW_BLOCK = 256
+ROW_BLOCK = 512
 
 
 def attend_kernel(ny, rows, arrays, groups, first, last, *refs):
@@ -227,52 +227,77 @@
     got = to_core(jnp.concatenate([own_other, root_other], axis=0))
     q_mine, q_other = halves(queries)
     q_pair = (q_mine, to_core(q_other))
-    tables = (expansion, root_offsets)
-    local = jnp.concatenate([own_mine, root_mine, got], axis=0)
-    segment = jnp.concatenate([own_mine, got[:rows]], axis=0)
-
-    kinds = ("own", "root")
-
-    def members(array, dx, dy, flips=(0, 1), wanted=kinds):
-        return tuple(
-            (array, f * 2 + kinds.index(kind), (kind, dx, dy, flip))
-            for f, flip in enumerate(flips)
-            for kind in wanted
+    own = jnp.concatenate([own_mine, got[:rows]], axis=0)
+    root = jnp.concatenate([root_mine, got[rows:]], axis=0)
+    run = functools.partial(attend, ny, rows, (expansion, root_offsets))
+    steps = range(1, ny)
+
+    def members(array, kind, dx=0, dy=0, flips=(0, 1), first=0):
+        return tuple((array, first + i, (kind, dx, dy, flip)) for i, flip in enumerate(flips))
+
+    def after(state, *values):
+        *values, state[0] = lax.optimization_barrier((*values, state[0]))
+        return values
+
+    choices = []
+
+    def hop(step, down, up):
+        down = lax.ppermute(down, "leaf", [(i, i - 1) for i in range(1, leaves - step + 1)])
+        choices.append((group + step, down))
+        if step < leaves - 1:
+            up = lax.ppermute(up, "leaf", [(i, i + 1) for i in range(step - 1, leaves - 2)])
+            choices.append((group - step, up))
+        return down, up
+
+    down, up = hop(1, own, own)
+    own_x, own_y = to_x(own), [to_y(own, step) for step in steps]
+    root_x, root_y = to_x(root), [to_y(root, step) for step in steps]
+    state = run([own, root], (members(0, "own") + members(1, "root"),), q_pair, None, False)
+
+    if leaves > 2:
+        down, up = hop(2, *after(state, down, up))
+
+    def near(kind, arrays):
+        groups = [members(0, kind, 1) + members(1, kind, 0, 1)]
+        groups += [members(step, kind, 0, step) for step in steps if step > 1]
+        return run(arrays, tuple(groups), None, state, False)
+
+    state = near("own", [own_x, *own_y])
+    for step in range(3, leaves):
+        down, up = hop(step, *after(state, down, up))
+    own_x, root_x, *pairs = after(state, own_x, root_x, *own_y, *root_y)
+    own_y, root_y = pairs[: ny - 1], pairs[ny - 1 :]
+    tops = [to_y(jnp.concatenate([own_x[:rows], root_x[:rows]], axis=0), step) for step in steps]
+    lows = [to_x(jnp.concatenate([a[rows:], b[rows:]], axis=0)) for a, b in zip(own_y, root_y)]
+    state = near("root", [root_x, *root_y])
+
+    parent = expansion[0, group]
+    owners, helds = zip(*choices)
+    helds = after(state, *helds)
+    parent_rows = own
+    for owner, held in zip(owners, helds):
+        parent_rows = jnp.where(parent == owner, held, parent_rows)
+    (parent_rows,) = after(state, parent_rows)
+    kin_x, kin_y = to_x(parent_rows), [to_y(parent_rows, step) for step in steps]
+    groups, arrays = [], []
+    for step, top, low in zip(steps, tops, lows):
+        at = len(arrays)
+        groups.append(
+            members(at, "own", 1, step, (0,))
+            + members(at, "root", 1, step, (0,), 1)
+            + members(at + 1, "own", 1, step, (1,))
+            + members(at + 1, "root", 1, step, (1,), 1)
         )
-
-    def kin(*counts):
-        return tuple((array, b, ("kin", 0, 0, 0)) for array, count in counts for b in range(count))
-
-    run = functools.partial(attend, ny, rows, tables)
-    steps = range(1, ny)
-
-    every = lax.all_gather(segment, "leaf", axis=0, tiled=True)
-    from_x = to_x(local)
-    from_y = [to_y(local, step) for step in steps]
-    state = run([local], (members(0, 0, 0),), q_pair, None, False)
-    from_x, from_y, state[0] = lax.optimization_barrier((from_x, from_y, state[0]))
-    tops = [to_y(from_x[: 2 * rows], step) for step in steps]
-    lows = [to_x(array[2 * rows :]) for array in from_y]
-    near = [members(0, 1, 0, wanted=(kind,)) + members(1, 0, 1, wanted=(kind,)) for kind in kinds]
-    near += [members(step, 0, step) for step in steps if step > 1]
-    state = run([from_x, *from_y], tuple(near), None, state, False)
-
-    every, state[0] = lax.optimization_barrier((every, state[0]))
-    parent_rows = lax.dynamic_slice_in_dim(every, expansion[0, group] * 2 * rows, 2 * rows, 0)
-    parent_rows, state[0] = lax.optimization_barrier((parent_rows, state[0]))
-    kin_x = to_x(parent_rows)
-    kin_y = [to_y(parent_rows, step) for step in steps]
-    far, arrays = [], []
-    for step, top, low in zip(steps, tops, lows):
-        far.append(members(len(arrays), 1, step, (0,)) + members(len(arrays) + 1, 1, step, (1,)))
         arrays += [top, low]
-    state = run(arrays, tuple(far), None, state, False)
+    state = run([*arrays, parent_rows], (*groups, members(len(arrays), "kin")), None, state, False)
+
+    (kin_x,) = after(state, kin_x)
     tops = [to_y(kin_x[:rows], step) for step in steps]
     lows = [to_x(array[rows:]) for array in kin_y]
-    groups = [kin((0, 2), (1, 2), (2, 2))] + [kin((1 + step, 2)) for step in steps if step > 1]
-    state = run([parent_rows, kin_x, *kin_y], tuple(groups), None, state, False)
-    groups = tuple(kin((step - 1, 1), (ny + step - 2, 1)) for step in steps)
-    out_mine, out_other = run([*tops, *lows], groups, None, state, True)
+    groups = [members(0, "kin") + members(1, "kin")] + [members(step, "kin") for step in steps if step > 1]
+    state = run([kin_x, *kin_y], tuple(groups), None, state, False)
+    groups = [members(i, "kin", flips=(0,)) + members(len(tops) + i, "kin", flips=(1,)) for i in range(len(tops))]
+    out_mine, out_other = run([*tops, *lows], tuple(groups), None, state, True)
     out_got = to_core(out_other)
     return jnp.where(
         core == 0,

time: 118 us -> 121 us (1.025)
  the two profiles are of different devices: /device:TPU:0 before, /device:TPU:11 now
where the time goes in v4:
time: 121 us; the launch traced here: 120 us
  Pallas kernels  52.4 us (43%)
  local copies, waits for them, and re-layouts  29.5 us (24%)
  starting transfers between devices  26.1 us (22%)
  waiting for transfers between devices  5.06 us (4%)
  between operations  3.64 us (3%)
  other arithmetic  3.61 us (3%)
    pallas_call x6, Pallas kernels, attend(): pl.pallas_call(functools.partial(attend_kernel, ny, rows, len(arrays), gr...  52.4 us
    unnamed x40, local copies, waits for them, and re-layouts  25.9 us
    ppermute x2, starting transfers between devices, hop(): lax.ppermute(up, 'leaf', [(i, i + 1) for i in range(step - 1, leaves - 2)])  7.24 us
    ppermute x3, starting transfers between devices, hop(): lax.ppermute(down, 'leaf', [(i, i - 1) for i in range(1, leaves - step +...  6.68 us
    ppermute x3, starting transfers between devices, to_core(): lax.ppermute(array, 'ctx', [(index(x, y, k), index(x, y, k + 1)) for x, y...  5.07 us
    ppermute x3, waiting for transfers between devices, to_core(): lax.ppermute(array, 'ctx', [(index(x, y, k), index(x, y, k + 1)) for x, y...  5.02 us
    ppermute x5, starting transfers between devices, to_y(): lax.ppermute(array, 'ctx', [(index(x, y, k), index(x, y + step, k)) for x...  4.15 us
    ppermute x5, starting transfers between devices, to_x(): lax.ppermute(array, 'ctx', [(index(x, y, k), index(x + 1, y, k)) for x, y...  2.95 us
  transfers between devices with their start and end apart: 18, of which 2 were waited for; matrix products, arithmetic and copies ran while one was open for 2% of the time, Pallas kernels for 38%

profile of v4, /device:TPU:11, one launch (start us, length us, event | category | flops | bytes accessed | tf_op | source)
XLA Modules:
  0.0 120.3 jit_solution(5915390977285665108)
XLA Ops:
  0.0 2.8 %constant_dynamic-slice_fusion.2 = (bf16[128,4096]{1,0:T(8,128)(2,1)}, bf16[128,4096]{1,0:T(8,128)(2,1)S(1)}) fusion(bf16[128,8192]{1,0:T(8,128)(2,1)} %param.7, s32[]{:T(128)S(6)} %select_n.67, s32[]{:T(128)S(6)} %select_n.66), kind=kLoop, calls=%fused_computation.9 | loop fusion | bytes 4194312 | tf_op jit(solution)/shard_map/dynamic_slice | solution.py:204
  3.8 2.7 %collective-permute-done = bf16[256,1024]{1,0:T(8,128)(2,1)S(1)} collective-permute-done((bf16[256,1024]{1,0:T(8,128)(2,1)S(1)}, bf16[256,1024]{1,0:T(8,128)(2,1)S(1)}, u32[]{:S(2)}, u32[]{:S(2)}) %collective-permute-start) | collective-permute-done | bytes 524320 | tf_op jit(solution)/shard_map/ppermute | solution.py:213
  6.6 2.1 %collective-permute-start.1 = (bf16[256,1024]{1,0:T(8,128)(2,1)S(1)}, bf16[256,1024]{1,0:T(8,128)(2,1)}, u32[]{:S(2)}, u32[]{:S(2)}) collective-permute-start(bf16[256,1024]{1,0:T(8,128)(2,1)S(1)} %pad_maximum_fusion.refs_4_.refs_6_), channel_id=1, source_target_pairs={{8,0},{16,8},{24,16},{9,1},{17,9},{25,17},{10,2},{18,10},{26,18},{... | collective-permute-start | bytes 1572872 | tf_op jit(solution)/shard_map/ppermute | solution.py:245
  8.7 3.2 %collective-permute-start.2 = (bf16[256,1024]{1,0:T(8,128)(2,1)S(1)}, bf16[256,1024]{1,0:T(8,128)(2,1)}, u32[]{:S(2)}, u32[]{:S(2)}) collective-permute-start(bf16[256,1024]{1,0:T(8,128)(2,1)S(1)} %pad_maximum_fusion.refs_4_.refs_6_), channel_id=1, source_target_pairs={{0,8},{8,16},{1,9},{9,17},{2,10},{10,18},{3,11},{11,19},{4,12},{12... | collective-permute-start | bytes 1572872 | tf_op jit(solution)/shard_map/ppermute | solution.py:248
  12.2 1.2 %collective-permute-start.7 = (bf16[256,1024]{1,0:T(8,128)(2,1)S(1)}, bf16[256,1024]{1,0:T(8,128)(2,1)S(1)}, u32[]{:S(2)}, u32[]{:S(2)}) collective-permute-start(bf16[256,1024]{1,0:T(8,128)(2,1)S(1)} %pad_maximum_fusion.refs_4_.refs_6_), channel_id=1, source_target_pairs={{0,4},{1,5},{2,6},{3,7},{4,0},{5,1},{6,2},{7,3},{8,12},{9,13},{10,... | collective-permute-start | bytes 1572872 | tf_op jit(solution)/shard_map/ppermute | solution.py:219
  13.6 8.3 %shard_map.73 = (f32[8,128]{1,0:T(8,128)S(1)}, bf16[4,2,1024,256]{3,2,1,0:T(8,128)(2,1)S(1)}, f32[4,2,1024,256]{3,2,1,0:T(8,128)S(1)}, f32[4,2,1024,128]{3,2,1,0:T(8,128)S(1)}) custom-call(s32[2,4]{1,0:T(2,128)S(1)} %copy-done.12, s32[4]{0:T(128)S(1)} %copy-done.13, bf16[128,4096]{1,0:T(8,128)(2,1)S(1)} %get-tuple-element.90.refs_2_, ...), custom_call_target="tpu_custom_call" | custom-call | flops 4294967296 | bytes 4194304 | tf_op jit(solution)/shard_map/pallas_call | solution.py:180
  21.9 3.3 %copy-done = f32[4,2,1024,256]{3,2,1,0:T(8,128)} copy-done((f32[4,2,1024,256]{3,2,1,0:T(8,128)}, f32[4,2,1024,256]{3,2,1,0:T(8,128)S(1)}, u32[]{:S(2)}) %copy-start) | copy-done | bytes 8388632
  25.2 2.0 %copy-done.4 = bf16[4,2,1024,256]{3,2,1,0:T(8,128)(2,1)} copy-done((bf16[4,2,1024,256]{3,2,1,0:T(8,128)(2,1)}, bf16[4,2,1024,256]{3,2,1,0:T(8,128)(2,1)S(1)}, u32[]{:S(2)}) %copy-start.4) | copy-done | bytes 4194328
  27.2 1.9 %copy-done.8 = f32[4,2,1024,128]{3,2,1,0:T(8,128)} copy-done((f32[4,2,1024,128]{3,2,1,0:T(8,128)}, f32[4,2,1024,128]{3,2,1,0:T(8,128)S(1)}, u32[]{:S(2)}) %copy-start.8) | copy-done | bytes 4194328
  29.1 2.8 %collective-permute-start.4 = (bf16[256,1024]{1,0:T(8,128)(2,1)}, bf16[256,1024]{1,0:T(8,128)(2,1)}, u32[]{:S(2)}, u32[]{:S(2)}) collective-permute-start(bf16[256,1024]{1,0:T(8,128)(2,1)} %collective-permute-done.1), channel_id=1, source_target_pairs={{8,0},{16,8},{9,1},{17,9},{10,2},{18,10},{11,3},{19,11},{12,4},{20... | collective-permute-start | bytes 1572872 | tf_op jit(solution)/shard_map/ppermute | solution.py:245
  32.0 4.0 %collective-permute-start.5 = (bf16[256,1024]{1,0:T(8,128)(2,1)}, bf16[256,1024]{1,0:T(8,128)(2,1)}, u32[]{:S(2)}, u32[]{:S(2)}) collective-permute-start(bf16[256,1024]{1,0:T(8,128)(2,1)} %collective-permute-done.2), channel_id=1, source_target_pairs={{8,16},{9,17},{10,18},{11,19},{12,20},{13,21},{14,22},{15,23}} | collective-permute-start | bytes 1572872 | tf_op jit(solution)/shard_map/ppermute | solution.py:248
  36.3 1.2 %collective-permute-start.9 = (bf16[256,1024]{1,0:T(8,128)(2,1)S(1)}, bf16[256,1024]{1,0:T(8,128)(2,1)S(1)}, u32[]{:S(2)}, u32[]{:S(2)}) collective-permute-start(bf16[256,1024]{1,0:T(8,128)(2,1)S(1)} %pad_maximum_fusion.1.refs_5_.refs_7_), channel_id=1, source_target_pairs={{0,2},{1,3},{2,0},{3,1},{4,6},{5,7},{6,4},{7,5},{8,10},{9,11},{10,... | collective-permute-start | bytes 1572872 | tf_op jit(solution)/shard_map/ppermute | solution.py:216
  41.3 3.4 %copy-done.1 = f32[4,2,1024,256]{3,2,1,0:T(8,128)S(1)} copy-done((f32[4,2,1024,256]{3,2,1,0:T(8,128)S(1)}, f32[4,2,1024,256]{3,2,1,0:T(8,128)}, u32[]{:S(2)}) %copy-start.1) | copy-done | bytes 8388632
  44.7 2.2 %copy-done.5 = bf16[4,2,1024,256]{3,2,1,0:T(8,128)(2,1)S(1)} copy-done((bf16[4,2,1024,256]{3,2,1,0:T(8,128)(2,1)S(1)}, bf16[4,2,1024,256]{3,2,1,0:T(8,128)(2,1)}, u32[]{:S(2)}) %copy-start.5) | copy-done | bytes 4194328
  46.9 2.2 %copy-done.9 = f32[4,2,1024,128]{3,2,1,0:T(8,128)S(1)} copy-done((f32[4,2,1024,128]{3,2,1,0:T(8,128)S(1)}, f32[4,2,1024,128]{3,2,1,0:T(8,128)}, u32[]{:S(2)}) %copy-start.9) | copy-done | bytes 4194328
  49.1 8.8 %shard_map.74 = (f32[8,128]{1,0:T(8,128)S(1)}, bf16[4,2,1024,256]{3,2,1,0:T(8,128)(2,1)S(1)}, f32[4,2,1024,256]{3,2,1,0:T(8,128)S(1)}, f32[4,2,1024,128]{3,2,1,0:T(8,128)S(1)}) custom-call(s32[2,4]{1,0:T(2,128)S(1)} %copy-done.12, s32[4]{0:T(128)S(1)} %copy-done.13, ...), custom_call_target="tpu_custom_call", output_to_operand_aliasing={{1}: (7, {}), {2}: (8, {}), {3}: (9, {})} | custom-call | flops 4294967296 | bytes 4194304 | tf_op jit(solution)/shard_map/pallas_call | solution.py:180
  57.9 3.3 %copy-done.2 = f32[4,2,1024,256]{3,2,1,0:T(8,128)} copy-done((f32[4,2,1024,256]{3,2,1,0:T(8,128)}, f32[4,2,1024,256]{3,2,1,0:T(8,128)S(1)}, u32[]{:S(2)}) %copy-start.2) | copy-done | bytes 8388632
  61.2 1.9 %copy-done.10 = f32[4,2,1024,128]{3,2,1,0:T(8,128)} copy-done((f32[4,2,1024,128]{3,2,1,0:T(8,128)}, f32[4,2,1024,128]{3,2,1,0:T(8,128)S(1)}, u32[]{:S(2)}) %copy-start.10) | copy-done | bytes 4194328
  63.4 1.8 %collective-permute-start.8 = (bf16[256,1024]{1,0:T(8,128)(2,1)}, bf16[256,1024]{1,0:T(8,128)(2,1)S(1)}, u32[]{:S(2)}, u32[]{:S(2)}) collective-permute-start(bf16[256,1024]{1,0:T(8,128)(2,1)} %collective-permute-done.4), channel_id=1, source_target_pairs={{8,0},{9,1},{10,2},{11,3},{12,4},{13,5},{14,6},{15,7}} | collective-permute-start | bytes 1572872 | tf_op jit(solution)/shard_map/ppermute | solution.py:245
  65.2 1.5 %collective-permute-start.12 = (bf16[256,1024]{1,0:T(8,128)(2,1)S(1)}, bf16[256,1024]{1,0:T(8,128)(2,1)S(1)}, u32[]{:S(2)}, u32[]{:S(2)}) collective-permute-start(bf16[256,1024]{1,0:T(8,128)(2,1)S(1)} %pad_maximum_fusion.2), channel_id=1, source_target_pairs={{0,4},{1,5},{2,6},{3,7},{4,0},{5,1},{6,2},{7,3},{8,12},{9,13},{10,... | collective-permute-start | bytes 1572872 | tf_op jit(solution)/shard_map/ppermute | solution.py:219
  66.8 3.4 %copy-done.3 = f32[4,2,1024,256]{3,2,1,0:T(8,128)S(1)} copy-done((f32[4,2,1024,256]{3,2,1,0:T(8,128)S(1)}, f32[4,2,1024,256]{3,2,1,0:T(8,128)}, u32[]{:S(2)}) %copy-start.3) | copy-done | bytes 8388632
  70.2 2.2 %copy-done.7 = bf16[4,2,1024,256]{3,2,1,0:T(8,128)(2,1)S(1)} copy-done((bf16[4,2,1024,256]{3,2,1,0:T(8,128)(2,1)S(1)}, bf16[4,2,1024,256]{3,2,1,0:T(8,128)(2,1)}, u32[]{:S(2)}) %copy-start.7) | copy-done | bytes 4194328
  72.4 8.1 %shard_map.75 = (f32[8,128]{1,0:T(8,128)S(1)}, bf16[4,2,1024,256]{3,2,1,0:T(8,128)(2,1)S(1)}, f32[4,2,1024,256]{3,2,1,0:T(8,128)S(1)}, f32[4,2,1024,128]{3,2,1,0:T(8,128)S(1)}) custom-call(s32[2,4]{1,0:T(2,128)S(1)} %copy-done.12, s32[4]{0:T(128)S(1)} %copy-done.13, ...), custom_call_target="tpu_custom_call", output_to_operand_aliasing={{1}: (7, {}), {2}: (8, {}), {3}: (9, {})} | custom-call | flops 4294967296 | bytes 4194304 | tf_op jit(solution)/shard_map/pallas_call | solution.py:180
  80.5 1.6 %select_select_fusion.refs_4_.refs_7_ = bf16[256,1024]{1,0:T(8,128)(2,1)S(1)} fusion(bf16[256,1024]{1,0:T(8,128)(2,1)S(1)} %collective-permute-done.8, bf16[256,1024]{1,0:T(8,128)(2,1)} %collective-permute-done.5, bf16[256,1024]{1,0:T(8,128)(2,1)} %collective-permute-done.4, bf16[256,1024]{1,0:T(8,128)(2,1)} %collective-permute-done.2, ...), kind=kLoop, calls=%fused_computation.6 | loop fusion | flops 2883584 | bytes 3670021 | tf_op jit(solution)/shard_map/jit(_where)/select_n | solution.py:279
  82.5 1.1 collective-permute-start.15
  83.6 13.2 %shard_map.76 = (f32[8,128]{1,0:T(8,128)S(1)}, bf16[4,2,1024,256]{3,2,1,0:T(8,128)(2,1)S(1)}, f32[4,2,1024,256]{3,2,1,0:T(8,128)S(1)}, f32[4,2,1024,128]{3,2,1,0:T(8,128)S(1)}) custom-call(s32[2,4]{1,0:T(2,128)S(1)} %copy-done.12, s32[4]{0:T(128)S(1)} %copy-done.13, ...), custom_call_target="tpu_custom_call", output_to_operand_aliasing={{1}: (9, {}), {2}: (10, {}), {3}: (11, {})} | custom-call | flops 6442450944 | bytes 4194304 | tf_op jit(solution)/shard_map/pallas_call | solution.py:180
  97.0 0.9 collective-permute-start.16
  97.9 7.9 %shard_map.77 = (f32[8,128]{1,0:T(8,128)S(1)}, bf16[4,2,1024,256]{3,2,1,0:T(8,128)(2,1)S(1)}, f32[4,2,1024,256]{3,2,1,0:T(8,128)S(1)}, f32[4,2,1024,128]{3,2,1,0:T(8,128)S(1)}) custom-call(s32[2,4]{1,0:T(2,128)S(1)} %copy-done.12, s32[4]{0:T(128)S(1)} %copy-done.13, ...), custom_call_target="tpu_custom_call", output_to_operand_aliasing={{1}: (7, {}), {2}: (8, {}), {3}: (9, {})} | custom-call | flops 4294967296 | bytes 4194304 | tf_op jit(solution)/shard_map/pallas_call | solution.py:180
  105.8 6.1 %shard_map.78 = (bf16[128,4096]{1,0:T(8,128)(2,1)S(1)}, bf16[128,4096]{1,0:T(8,128)(2,1)S(1)}, bf16[4,2,1024,256]{3,2,1,0:T(8,128)(2,1)S(1)}, f32[4,2,1024,256]{3,2,1,0:T(8,128)S(1)}, f32[4,2,1024,128]{3,2,1,0:T(8,128)S(1)}) custom-call(s32[2,4]{1,0:T(2,128)S(1)} %copy-done.12, ...), custom_call_target="tpu_custom_call", output_to_operand_aliasing={{2}: (7, {}), {3}: (8, {}), {4}: (9, {})} | custom-call | flops 2147483648 | bytes 4194304 | tf_op jit(solution)/shard_map/pallas_call | solution.py:180
  111.9 4.3 %collective-permute-start.17 = (bf16[128,4096]{1,0:T(8,128)(2,1)S(1)}, bf16[128,4096]{1,0:T(8,128)(2,1)S(1)}, u32[]{:S(2)}, u32[]{:S(2)}) collective-permute-start(bf16[128,4096]{1,0:T(8,128)(2,1)S(1)} %get-tuple-element.88), channel_id=1, source_target_pairs={{0,1},{1,0},{2,3},{3,2},{4,5},{5,4},{6,7},{7,6},{8,9},{9,8},{10,11... | collective-permute-start | bytes 3145736 | tf_op jit(solution)/shard_map/ppermute | solution.py:213
  116.2 2.3 %collective-permute-done.17 = bf16[128,4096]{1,0:T(8,128)(2,1)S(1)} collective-permute-done((bf16[128,4096]{1,0:T(8,128)(2,1)S(1)}, bf16[128,4096]{1,0:T(8,128)(2,1)S(1)}, u32[]{:S(2)}, u32[]{:S(2)}) %collective-permute-start.17) | collective-permute-done | bytes 1048608 | tf_op jit(solution)/shard_map/ppermute | solution.py:213
  118.5 1.8 %maximum_select_fusion = bf16[128,8192]{1,0:T(8,128)(2,1)} fusion(bf16[128,4096]{1,0:T(8,128)(2,1)S(1)} %collective-permute-done.17, bf16[128,4096]{1,0:T(8,128)(2,1)S(1)} %get-tuple-element.87, pred[]{:T(512)S(6)} %eq.18), kind=kLoop, calls=%fused_computation | loop fusion | flops 9437184 | bytes 4194305 | tf_op jit(solution)/shard_map/jit(_where)/select_n | solution.py:302
  (68 shorter events, 3.2 us)
Async XLA Ops:
  0.0 3.5 %copy-start.17 = (bf16[128,1024]{1,0:T(8,128)(2,1)S(1)}, bf16[128,1024]{1,0:T(8,128)(2,1)}, u32[]{:S(2)}) copy-start(bf16[128,1024]{1,0:T(8,128)(2,1)} %param.8) | copy-start | bytes 786436
  0.0 3.5 %copy-start.16 = (bf16[128,1024]{1,0:T(8,128)(2,1)S(1)}, bf16[128,1024]{1,0:T(8,128)(2,1)}, u32[]{:S(2)}) copy-start(bf16[128,1024]{1,0:T(8,128)(2,1)} %param.9) | copy-start | bytes 786436
  0.0 3.5 %copy-start.19 = (bf16[128,1024]{1,0:T(8,128)(2,1)S(1)}, bf16[128,1024]{1,0:T(8,128)(2,1)}, u32[]{:S(2)}) copy-start(bf16[128,1024]{1,0:T(8,128)(2,1)} %param.10) | copy-start | bytes 786436
  0.0 3.5 %copy-start.18 = (bf16[128,1024]{1,0:T(8,128)(2,1)S(1)}, bf16[128,1024]{1,0:T(8,128)(2,1)}, u32[]{:S(2)}) copy-start(bf16[128,1024]{1,0:T(8,128)(2,1)} %param.11) | copy-start | bytes 786436
  2.8 10.7 %copy-start.12 = (s32[2,4]{1,0:T(2,128)S(1)}, s32[2,4]{1,0:T(2,128)}, u32[]{:S(2)}) copy-start(s32[2,4]{1,0:T(2,128)} %refs_0_.11) | copy-start | bytes 100
  2.8 10.7 %copy-start.13 = (s32[4]{0:T(128)S(1)}, s32[4]{0:T(128)}, u32[]{:S(2)}) copy-start(s32[4]{0:T(128)} %refs_1_.11) | copy-start | bytes 52
  2.8 10.7 %collective-permute-start.3 = (bf16[128,4096]{1,0:T(8,128)(2,1)}, bf16[128,4096]{1,0:T(8,128)(2,1)}, u32[]{:S(2)}, u32[]{:S(2)}) collective-permute-start(bf16[128,4096]{1,0:T(8,128)(2,1)} %get-tuple-element.89), channel_id=1, source_target_pairs={{0,1},{1,0},{2,3},{3,2},{4,5},{5,4},{6,7},{7,6},{8,9},{9,8},{10,11... | collective-permute-start | bytes 3145736 | tf_op jit(solution)/shard_map/ppermute | solution.py:213
  3.6 9.9 %copy-start.14 = (bf16[128,512]{1,0:T(8,128)(2,1)}, bf16[128,512]{1,0:T(8,128)(2,1)S(1)}, u32[]{:S(2)}) copy-start(bf16[128,512]{1,0:T(8,128)(2,1)S(1)} %get-tuple-element.104) | copy-start | bytes 393220
  3.7 2.8 %collective-permute-start = (bf16[256,1024]{1,0:T(8,128)(2,1)S(1)}, bf16[256,1024]{1,0:T(8,128)(2,1)S(1)}, u32[]{:S(2)}, u32[]{:S(2)}) collective-permute-start(bf16[256,1024]{1,0:T(8,128)(2,1)S(1)} %maximum_maximum_fusion), channel_id=1, source_target_pairs={{0,1},{1,0},{2,3},{3,2},{4,5},{5,4},{6,7},{7,6},{8,9},{9,8},{10,11... | collective-permute-start | bytes 1572872 | tf_op jit(solution)/shard_map/ppermute | solution.py:213
  6.6 22.5 %collective-permute-start.1 = (bf16[256,1024]{1,0:T(8,128)(2,1)S(1)}, bf16[256,1024]{1,0:T(8,128)(2,1)}, u32[]{:S(2)}, u32[]{:S(2)}) collective-permute-start(bf16[256,1024]{1,0:T(8,128)(2,1)S(1)} %pad_maximum_fusion.refs_4_.refs_6_), channel_id=1, source_target_pairs={{8,0},{16,8},{24,16},{9,1},{17,9},{25,17},{10,2},{18,10},{26,18},{... | collective-permute-start | bytes 1572872 | tf_op jit(solution)/shard_map/ppermute | solution.py:245
  8.7 20.4 %collective-permute-start.2 = (bf16[256,1024]{1,0:T(8,128)(2,1)S(1)}, bf16[256,1024]{1,0:T(8,128)(2,1)}, u32[]{:S(2)}, u32[]{:S(2)}) collective-permute-start(bf16[256,1024]{1,0:T(8,128)(2,1)S(1)} %pad_maximum_fusion.refs_4_.refs_6_), channel_id=1, source_target_pairs={{0,8},{8,16},{1,9},{9,17},{2,10},{10,18},{3,11},{11,19},{4,12},{12... | collective-permute-start | bytes 1572872 | tf_op jit(solution)/shard_map/ppermute | solution.py:248
  11.9 24.3 %collective-permute-start.6 = (bf16[256,1024]{1,0:T(8,128)(2,1)S(1)}, bf16[256,1024]{1,0:T(8,128)(2,1)S(1)}, u32[]{:S(2)}, u32[]{:S(2)}) collective-permute-start(bf16[256,1024]{1,0:T(8,128)(2,1)S(1)} %pad_maximum_fusion.refs_4_.refs_6_), channel_id=1, source_target_pairs={{0,2},{1,3},{2,0},{3,1},{4,6},{5,7},{6,4},{7,5},{8,10},{9,11},{10,... | collective-permute-start | bytes 1572872 | tf_op jit(solution)/shard_map/ppermute | solution.py:216
  12.2 29.0 %collective-permute-start.7 = (bf16[256,1024]{1,0:T(8,128)(2,1)S(1)}, bf16[256,1024]{1,0:T(8,128)(2,1)S(1)}, u32[]{:S(2)}, u32[]{:S(2)}) collective-permute-start(bf16[256,1024]{1,0:T(8,128)(2,1)S(1)} %pad_maximum_fusion.refs_4_.refs_6_), channel_id=1, source_target_pairs={{0,4},{1,5},{2,6},{3,7},{4,0},{5,1},{6,2},{7,3},{8,12},{9,13},{10,... | collective-permute-start | bytes 1572872 | tf_op jit(solution)/shard_map/ppermute | solution.py:219
  21.9 3.3 %copy-start = (f32[4,2,1024,256]{3,2,1,0:T(8,128)}, f32[4,2,1024,256]{3,2,1,0:T(8,128)S(1)}, u32[]{:S(2)}) copy-start(f32[4,2,1024,256]{3,2,1,0:T(8,128)S(1)} %get-tuple-element.52.refs_8_) | copy-start | bytes 25165828
  29.1 33.9 %collective-permute-start.4 = (bf16[256,1024]{1,0:T(8,128)(2,1)}, bf16[256,1024]{1,0:T(8,128)(2,1)}, u32[]{:S(2)}, u32[]{:S(2)}) collective-permute-start(bf16[256,1024]{1,0:T(8,128)(2,1)} %collective-permute-done.1), channel_id=1, source_target_pairs={{8,0},{16,8},{9,1},{17,9},{10,2},{18,10},{11,3},{19,11},{12,4},{20... | collective-permute-start | bytes 1572872 | tf_op jit(solution)/shard_map/ppermute | solution.py:245
  32.0 31.1 %collective-permute-start.5 = (bf16[256,1024]{1,0:T(8,128)(2,1)}, bf16[256,1024]{1,0:T(8,128)(2,1)}, u32[]{:S(2)}, u32[]{:S(2)}) collective-permute-start(bf16[256,1024]{1,0:T(8,128)(2,1)} %collective-permute-done.2), channel_id=1, source_target_pairs={{8,16},{9,17},{10,18},{11,19},{12,20},{13,21},{14,22},{15,23}} | collective-permute-start | bytes 1572872 | tf_op jit(solution)/shard_map/ppermute | solution.py:248
  36.0 27.1 %collective-permute-start.10 = (bf16[256,1024]{1,0:T(8,128)(2,1)S(1)}, bf16[256,1024]{1,0:T(8,128)(2,1)S(1)}, u32[]{:S(2)}, u32[]{:S(2)}) collective-permute-start(bf16[256,1024]{1,0:T(8,128)(2,1)S(1)} %pad_maximum_fusion.1.refs_5_.refs_7_), channel_id=1, source_target_pairs={{0,4},{1,5},{2,6},{3,7},{4,0},{5,1},{6,2},{7,3},{8,12},{9,13},{10,... | collective-permute-start | bytes 1572872 | tf_op jit(solution)/shard_map/ppermute | solution.py:219
  36.3 26.9 %collective-permute-start.9 = (bf16[256,1024]{1,0:T(8,128)(2,1)S(1)}, bf16[256,1024]{1,0:T(8,128)(2,1)S(1)}, u32[]{:S(2)}, u32[]{:S(2)}) collective-permute-start(bf16[256,1024]{1,0:T(8,128)(2,1)S(1)} %pad_maximum_fusion.1.refs_5_.refs_7_), channel_id=1, source_target_pairs={{0,2},{1,3},{2,0},{3,1},{4,6},{5,7},{6,4},{7,5},{8,10},{9,11},{10,... | collective-permute-start | bytes 1572872 | tf_op jit(solution)/shard_map/ppermute | solution.py:216
  41.3 3.4 %copy-start.1 = (f32[4,2,1024,256]{3,2,1,0:T(8,128)S(1)}, f32[4,2,1024,256]{3,2,1,0:T(8,128)}, u32[]{:S(2)}) copy-start(f32[4,2,1024,256]{3,2,1,0:T(8,128)} %copy-done) | copy-start | bytes 25165828
  57.9 3.3 %copy-start.2 = (f32[4,2,1024,256]{3,2,1,0:T(8,128)}, f32[4,2,1024,256]{3,2,1,0:T(8,128)S(1)}, u32[]{:S(2)}) copy-start(f32[4,2,1024,256]{3,2,1,0:T(8,128)S(1)} %get-tuple-element.61.refs_8_) | copy-start | bytes 25165828
  63.1 3.6 %copy-start.6 = (bf16[4,2,1024,256]{3,2,1,0:T(8,128)(2,1)}, bf16[4,2,1024,256]{3,2,1,0:T(8,128)(2,1)S(1)}, u32[]{:S(2)}) copy-start(bf16[4,2,1024,256]{3,2,1,0:T(8,128)(2,1)S(1)} %get-tuple-element.60.refs_7_) | copy-start | bytes 12582916
  63.1 3.7 %copy-start.11 = (f32[4,2,1024,128]{3,2,1,0:T(8,128)S(1)}, f32[4,2,1024,128]{3,2,1,0:T(8,128)}, u32[]{:S(2)}) copy-start(f32[4,2,1024,128]{3,2,1,0:T(8,128)} %copy-done.10) | copy-start | bytes 12582916
  63.2 20.4 %collective-permute-start.13 = (bf16[256,1024]{1,0:T(8,128)(2,1)S(1)}, bf16[256,1024]{1,0:T(8,128)(2,1)S(1)}, u32[]{:S(2)}, u32[]{:S(2)}) collective-permute-start(bf16[256,1024]{1,0:T(8,128)(2,1)S(1)} %pad_maximum_fusion.3), channel_id=1, source_target_pairs={{0,2},{1,3},{2,0},{3,1},{4,6},{5,7},{6,4},{7,5},{8,10},{9,11},{10,... | collective-permute-start | bytes 1572872 | tf_op jit(solution)/shard_map/ppermute | solution.py:216
  63.4 17.1 %collective-permute-start.8 = (bf16[256,1024]{1,0:T(8,128)(2,1)}, bf16[256,1024]{1,0:T(8,128)(2,1)S(1)}, u32[]{:S(2)}, u32[]{:S(2)}) collective-permute-start(bf16[256,1024]{1,0:T(8,128)(2,1)} %collective-permute-done.4), channel_id=1, source_target_pairs={{8,0},{9,1},{10,2},{11,3},{12,4},{13,5},{14,6},{15,7}} | collective-permute-start | bytes 1572872 | tf_op jit(solution)/shard_map/ppermute | solution.py:245
  65.2 18.4 %collective-permute-start.12 = (bf16[256,1024]{1,0:T(8,128)(2,1)S(1)}, bf16[256,1024]{1,0:T(8,128)(2,1)S(1)}, u32[]{:S(2)}, u32[]{:S(2)}) collective-permute-start(bf16[256,1024]{1,0:T(8,128)(2,1)S(1)} %pad_maximum_fusion.2), channel_id=1, source_target_pairs={{0,4},{1,5},{2,6},{3,7},{4,0},{5,1},{6,2},{7,3},{8,12},{9,13},{10,... | collective-permute-start | bytes 1572872 | tf_op jit(solution)/shard_map/ppermute | solution.py:219
  66.8 3.4 %copy-start.3 = (f32[4,2,1024,256]{3,2,1,0:T(8,128)S(1)}, f32[4,2,1024,256]{3,2,1,0:T(8,128)}, u32[]{:S(2)}) copy-start(f32[4,2,1024,256]{3,2,1,0:T(8,128)} %copy-done.2) | copy-start | bytes 25165828
  72.4 8.1 %copy-start.15 = (bf16[128,512]{1,0:T(8,128)(2,1)S(1)}, bf16[128,512]{1,0:T(8,128)(2,1)}, u32[]{:S(2)}) copy-start(bf16[128,512]{1,0:T(8,128)(2,1)} %copy-done.14) | copy-start | bytes 393220
  82.0 14.8 %collective-permute-start.11 = (bf16[256,1024]{1,0:T(8,128)(2,1)S(1)}, bf16[256,1024]{1,0:T(8,128)(2,1)S(1)}, u32[]{:S(2)}, u32[]{:S(2)}) collective-permute-start(bf16[256,1024]{1,0:T(8,128)(2,1)S(1)} %select_select_fusion.refs_4_.refs_7_), channel_id=1, source_target_pairs={{0,2},{1,3},{2,0},{3,1},{4,6},{5,7},{6,4},{7,5},{8,10},{9,11},{10,... | collective-permute-start | bytes 1572872 | tf_op jit(solution)/shard_map/ppermute | solution.py:216
  82.5 14.4 %collective-permute-start.15 = (bf16[256,1024]{1,0:T(8,128)(2,1)S(1)}, bf16[256,1024]{1,0:T(8,128)(2,1)S(1)}, u32[]{:S(2)}, u32[]{:S(2)}) collective-permute-start(bf16[256,1024]{1,0:T(8,128)(2,1)S(1)} %select_select_fusion.refs_4_.refs_7_), channel_id=1, source_target_pairs={{0,4},{1,5},{2,6},{3,7},{4,0},{5,1},{6,2},{7,3},{8,12},{9,13},{10,... | collective-permute-start | bytes 1572872 | tf_op jit(solution)/shard_map/ppermute | solution.py:219
  96.9 8.9 %collective-permute-start.14 = (bf16[128,1024]{1,0:T(8,128)(2,1)S(1)}, bf16[128,1024]{1,0:T(8,128)(2,1)S(1)}, u32[]{:S(2)}, u32[]{:S(2)}) collective-permute-start(bf16[128,1024]{1,0:T(8,128)(2,1)S(1)} %slice.30), channel_id=1, source_target_pairs={{0,4},{1,5},{2,6},{3,7},{4,0},{5,1},{6,2},{7,3},{8,12},{9,13},{10,... | collective-permute-start | bytes 786440 | tf_op jit(solution)/shard_map/ppermute | solution.py:219
  97.0 8.8 %collective-permute-start.16 = (bf16[128,1024]{1,0:T(8,128)(2,1)S(1)}, bf16[128,1024]{1,0:T(8,128)(2,1)S(1)}, u32[]{:S(2)}, u32[]{:S(2)}) collective-permute-start(bf16[128,1024]{1,0:T(8,128)(2,1)S(1)} %slice.34), channel_id=1, source_target_pairs={{0,2},{1,3},{2,0},{3,1},{4,6},{5,7},{6,4},{7,5},{8,10},{9,11},{10,... | collective-permute-start | bytes 786440 | tf_op jit(solution)/shard_map/ppermute | solution.py:216
  111.9 6.6 %collective-permute-start.17 = (bf16[128,4096]{1,0:T(8,128)(2,1)S(1)}, bf16[128,4096]{1,0:T(8,128)(2,1)S(1)}, u32[]{:S(2)}, u32[]{:S(2)}) collective-permute-start(bf16[128,4096]{1,0:T(8,128)(2,1)S(1)} %get-tuple-element.88), channel_id=1, source_target_pairs={{0,1},{1,0},{2,3},{3,2},{4,5},{5,4},{6,7},{7,6},{8,9},{9,8},{10,11... | collective-permute-start | bytes 3145736 | tf_op jit(solution)/shard_map/ppermute | solution.py:213
  (6 other events, 12.5 us)

commit v5 on v4

--- a/solution.py
+++ b/solution.py
@@ -15,25 +15,28 @@
 HALF_KV = KVH // 2
 NEG = -1e30
 Q_SCALE = math.log2(math.e) / math.sqrt(HD)
-ROW_BLOCK = 512
+ROW_BLOCK = 256
 
 
 def attend_kernel(ny, rows, arrays, groups, first, last, *refs):
     refs = list(refs)
     take = lambda count: [refs.pop(0) for _ in range(count)]
     exp_ref, off_ref = take(2)
-    raw = take(2) if first else None
+    raw = take(2) if first else take(1)
     key_refs = take(arrays)
     value_refs = take(arrays)
-    head = pl.program_id(0)
     if not first:
-        take(4)
+        take(1)
+        acc_in, stat_in = take(2)
     if last:
         outs = take(2)
+        acc_out, stat_out = take(2)
     else:
         take(1)[0][...] = jnp.zeros((8, HD), jnp.float32)
-    qs, accs, ms = take(3)
+        acc_out, stat_out = take(2)
+    qs = take(1)[0] if first else raw[0]
     stacked = GW * rows
+    lane = lax.broadcasted_iota(jnp.int32, (min(ROW_BLOCK, stacked), HD), 1)
 
     group = lax.axis_index("leaf")
     spot = lax.axis_index("ctx")
@@ -54,10 +57,10 @@
                 q = q_ref[:, g * HD : (g + 1) * HD].astype(jnp.float32) * Q_SCALE
                 high = q.astype(jnp.bfloat16)
                 low = (q - high.astype(jnp.float32)).astype(jnp.bfloat16)
-                qs[head, s, g * rows : (g + 1) * rows, :HD] = high
-                qs[head, s, g * rows : (g + 1) * rows, HD:] = low
-
-    def step(members, limits, masked, fresh):
+                qs[0, s, g * rows : (g + 1) * rows, :HD] = high
+                qs[0, s, g * rows : (g + 1) * rows, HD:] = low
+
+    def step(members, limits, masked, start):
         width = len(members) * rows
         cut = lambda refs: [refs[a][b * rows : (b + 1) * rows, :] for a, b, _ in members]
         keys = jnp.concatenate(cut(key_refs), axis=0)
@@ -69,7 +72,7 @@
 
         def score(s, here):
             return lax.dot_general(
-                qs[head, s, here, :], keys, (((1,), (1,)), ((), ())), preferred_element_type=jnp.float32
+                qs[0, s, here, :], keys, (((1,), (1,)), ((), ())), preferred_element_type=jnp.float32
             )
 
         def bias_of(s):
@@ -90,19 +93,23 @@
                 bias = bias_of(s)
                 scores = scores + jnp.concatenate([bias] * (size // rows), axis=0)
             new = jnp.max(scores, axis=1, keepdims=True)
-            if fresh:
+            if start == "new":
                 new = jnp.broadcast_to(new, (size, HD))
             else:
-                old = ms[head, s, here, :]
+                acc, stat = (acc_in, stat_in) if start == "in" else (acc_out, stat_out)
+                stats = stat[0, s, here, :]
+                old = jnp.broadcast_to(stats[:, :1], (size, HD))
+                total = jnp.broadcast_to(stats[:, HD - 1 :], (size, HD))
                 new = jnp.maximum(old, new)
             weights = jnp.exp2(scores - jnp.concatenate([new] * (width // HD), axis=1))
             update = jnp.dot(weights.astype(jnp.bfloat16), values, preferred_element_type=jnp.float32)
-            if fresh:
-                accs[head, s, here, :] = update
-            else:
+            update, share = update[:, :HD], update[:, HD:]
+            if start != "new":
                 shrink = jnp.exp2(old - new)
-                accs[head, s, here, :] = accs[head, s, here, :] * jnp.concatenate([shrink, shrink], axis=1) + update
-            ms[head, s, here, :] = new
+                update = acc[0, s, here, :] * shrink + update
+                share = total * shrink + share
+            acc_out[0, s, here, :] = update
+            stat_out[0, s, here, :] = jnp.where(lane < HD // 2, new, share)
 
     for number, members in enumerate(groups):
         limits = []
@@ -125,17 +132,26 @@
                 some = some | some_here
         kinds = {block[0] for _, _, block in members}
         if first and number == 0:
-            step(members, limits, True, True)
+            step(members, limits, True, "new")
             continue
-        pl.when(full)(functools.partial(step, members, limits, False, False))
-        if kinds != {"kin"}:
-            pl.when(jnp.logical_not(full) & some)(functools.partial(step, members, limits, True, False))
+        start = "in" if number == 0 else "out"
+        pl.when(full)(functools.partial(step, members, limits, False, start))
+        if kinds == {"kin"}:
+            some = full
+        else:
+            pl.when(jnp.logical_not(full) & some)(functools.partial(step, members, limits, True, start))
+        if number == 0:
+
+            @pl.when(jnp.logical_not(some))
+            def _():
+                acc_out[...] = acc_in[...]
+                stat_out[...] = stat_in[...]
 
     if last:
         for s in range(2):
             for g in range(GW):
                 here = slice(g * rows, (g + 1) * rows)
-                done = accs[head, s, here, :HD] / accs[head, s, here, HD:]
+                done = acc_out[0, s, here, :] / stat_out[0, s, here, HD - 1 :]
                 outs[s][:, g * HD : (g + 1) * HD] = done.astype(jnp.bfloat16)
 
 
@@ -143,39 +159,40 @@
     stacked = GW * rows
     first = state is None
     smem = pl.BlockSpec(memory_space=pltpu.SMEM)
-    held = pl.BlockSpec(memory_space=pltpu.VMEM)
     row_spec = pl.BlockSpec((rows, GW * HD), lambda h: (0, h))
-    kept = [
-        ((HALF_KV, 2, stacked, 2 * HD), jnp.bfloat16),
-        ((HALF_KV, 2, stacked, 2 * HD), jnp.float32),
-        ((HALF_KV, 2, stacked, HD), jnp.float32),
-    ]
+    q_spec = pl.BlockSpec((1, 2, stacked, 2 * HD), lambda h: (h, 0, 0, 0))
+    state_spec = pl.BlockSpec((1, 2, stacked, HD), lambda h: (h, 0, 0, 0))
+    scratch = []
     operands = [*tables]
     specs = [smem, smem]
     if first:
         operands += queries
         specs += [row_spec, row_spec]
+    else:
+        mark, *state, prepared = state
+        operands.append(pltpu.with_memory_space_constraint(prepared, pltpu.HBM))
+        specs.append(q_spec)
     for shift in (0, HALF_KV):
         for array in arrays:
             operands.append(array)
             specs.append(pl.BlockSpec((array.shape[0], HD), functools.partial(lambda s, h: (0, s + h), shift)))
-    aliases = {}
+    if not first:
+        operands.append(mark)
+        specs.append(pl.BlockSpec(memory_space=pl.ANY))
+        for array in state:
+            operands.append(pltpu.with_memory_space_constraint(array, pltpu.HBM))
+            specs.append(state_spec)
     if last:
         out_shape = [jax.ShapeDtypeStruct((rows, HALF_KV * GW * HD), jnp.bfloat16)] * 2
         out_specs = [row_spec, row_spec]
+        scratch = [pltpu.VMEM((1, 2, stacked, HD), jnp.float32)] * 2
     else:
         out_shape = [jax.ShapeDtypeStruct((8, HD), jnp.float32)]
-        out_specs = [pl.BlockSpec((8, HD), lambda h: (0, 0))]
-    if not first:
-        mark, *state = state
-        operands.append(mark)
-        specs.append(pl.BlockSpec(memory_space=pl.ANY))
-        for i, array in enumerate(state):
-            aliases[len(operands)] = len(out_shape) + i
-            operands.append(pltpu.with_memory_space_constraint(array, pltpu.VMEM))
-            specs.append(held)
-    out_shape += [pltpu.VMEM(shape, dtype) for shape, dtype in kept]
-    out_specs += [held] * 3
+        out_shape += [pltpu.HBM((HALF_KV, 2, stacked, HD), jnp.float32)] * 2
+        out_specs = [pl.BlockSpec((8, HD), lambda h: (0, 0)), state_spec, state_spec]
+    if first:
+        out_shape.append(pltpu.HBM((HALF_KV, 2, stacked, 2 * HD), jnp.bfloat16))
+        out_specs.append(q_spec)
     scores = HALF_KV * 2 * stacked * rows * sum(len(members) for members in groups)
     out = pl.pallas_call(
         functools.partial(attend_kernel, ny, rows, len(arrays), groups, first, last),
@@ -183,11 +200,11 @@
         in_specs=specs,
         out_specs=out_specs,
         out_shape=out_shape,
-        input_output_aliases=aliases,
+        scratch_shapes=scratch,
         compiler_params=pltpu.CompilerParams(vmem_limit_bytes=24 * 2**20),
         cost_estimate=pl.CostEstimate(flops=8 * scores * HD, bytes_accessed=4 * 2**20, transcendentals=scores),
     )(*operands)
-    return out[:2] if last else list(out)
+    return list(out) if first or last else [*out, prepared]
 
 
 def on_device(queries, seg_keys, seg_values, root_keys, root_values, expansion, root_offsets):

time: 121 us -> 128 us (1.058)
  the two profiles are of different devices: /device:TPU:11 before, /device:TPU:0 now
where the time goes in v5:
time: 128 us; the launch traced here: 125 us
  Pallas kernels  74.5 us (58%)
  starting transfers between devices  35.2 us (28%)
  waiting for transfers between devices  5.79 us (5%)
  local copies, waits for them, and re-layouts  3.62 us (3%)
  between operations  3.48 us (3%)
  other arithmetic  2.65 us (2%)
    pallas_call x6, Pallas kernels, attend(): pl.pallas_call(functools.partial(attend_kernel, ny, rows, len(arrays), gr...  74.5 us
    ppermute x5, starting transfers between devices, to_y(): lax.ppermute(array, 'ctx', [(index(x, y, k), index(x, y + step, k)) for x...  13 us
    ppermute x5, starting transfers between devices, to_x(): lax.ppermute(array, 'ctx', [(index(x, y, k), index(x + 1, y, k)) for x, y...  9.67 us
    ppermute x2, starting transfers between devices, hop(): lax.ppermute(up, 'leaf', [(i, i + 1) for i in range(step - 1, leaves - 2)])  7.77 us
    ppermute x3, waiting for transfers between devices, to_core(): lax.ppermute(array, 'ctx', [(index(x, y, k), index(x, y, k + 1)) for x, y...  5.38 us
    ppermute x3, starting transfers between devices, hop(): lax.ppermute(down, 'leaf', [(i, i - 1) for i in range(1, leaves - step +...  4.06 us
    dynamic_slice x1, local copies, waits for them, and re-layouts, halves(): lax.dynamic_slice_in_dim(array, (1 - core) * half, half, 1)  2.78 us
  transfers between devices with their start and end apart: 18, of which 4 were waited for; matrix products, arithmetic and copies ran while one was open for 1% of the time, Pallas kernels for 52%

profile of v5, /device:TPU:0, one launch (start us, length us, event | category | flops | bytes accessed | tf_op | source)
XLA Modules:
  0.0 125.3 jit_solution(2918285494171711126)
XLA Ops:
  0.0 2.8 %constant_dynamic-slice_fusion.9 = (bf16[128,4096]{1,0:T(8,128)(2,1)}, bf16[128,4096]{1,0:T(8,128)(2,1)S(1)}) fusion(bf16[128,8192]{1,0:T(8,128)(2,1)} %param.7, s32[]{:T(128)S(6)} %select_n.63, s32[]{:T(128)S(6)} %select_n.62), kind=kLoop, calls=%fused_computation.16 | loop fusion | bytes 4194312 | tf_op jit(solution)/shard_map/dynamic_slice | solution.py:221
  2.8 0.5 collective-permute-start
  3.5 0.1 collective-permute-start.1
  3.6 2.7 %collective-permute-done.1 = bf16[256,1024]{1,0:T(8,128)(2,1)S(1)} collective-permute-done((bf16[256,1024]{1,0:T(8,128)(2,1)S(1)}, bf16[256,1024]{1,0:T(8,128)(2,1)S(1)}, u32[]{:S(2)}, u32[]{:S(2)}) %collective-permute-start.1) | collective-permute-done | bytes 524320 | tf_op jit(solution)/shard_map/ppermute | solution.py:230
  6.4 1.3 %collective-permute-start.2 = (bf16[256,1024]{1,0:T(8,128)(2,1)S(1)}, bf16[256,1024]{1,0:T(8,128)(2,1)}, u32[]{:S(2)}, u32[]{:S(2)}) collective-permute-start(bf16[256,1024]{1,0:T(8,128)(2,1)S(1)} %pad_maximum_fusion.refs_4_.refs_6_), channel_id=1, source_target_pairs={{8,0},{16,8},{24,16},{9,1},{17,9},{25,17},{10,2},{18,10},{26,18},{... | collective-permute-start | bytes 1572872 | tf_op jit(solution)/shard_map/ppermute | solution.py:262
  7.7 6.3 %collective-permute-start.3 = (bf16[256,1024]{1,0:T(8,128)(2,1)S(1)}, bf16[256,1024]{1,0:T(8,128)(2,1)}, u32[]{:S(2)}, u32[]{:S(2)}) collective-permute-start(bf16[256,1024]{1,0:T(8,128)(2,1)S(1)} %pad_maximum_fusion.refs_4_.refs_6_), channel_id=1, source_target_pairs={{0,8},{8,16},{1,9},{9,17},{2,10},{10,18},{3,11},{11,19},{4,12},{12... | collective-permute-start | bytes 1572872 | tf_op jit(solution)/shard_map/ppermute | solution.py:265
  14.0 1.9 %collective-permute-start.6 = (bf16[256,1024]{1,0:T(8,128)(2,1)S(1)}, bf16[256,1024]{1,0:T(8,128)(2,1)S(1)}, u32[]{:S(2)}, u32[]{:S(2)}) collective-permute-start(bf16[256,1024]{1,0:T(8,128)(2,1)S(1)} %pad_maximum_fusion.refs_4_.refs_6_), channel_id=1, source_target_pairs={{0,2},{1,3},{2,0},{3,1},{4,6},{5,7},{6,4},{7,5},{8,10},{9,11},{10,... | collective-permute-start | bytes 1572872 | tf_op jit(solution)/shard_map/ppermute | solution.py:233
  15.9 1.5 %collective-permute-start.7 = (bf16[256,1024]{1,0:T(8,128)(2,1)S(1)}, bf16[256,1024]{1,0:T(8,128)(2,1)S(1)}, u32[]{:S(2)}, u32[]{:S(2)}) collective-permute-start(bf16[256,1024]{1,0:T(8,128)(2,1)S(1)} %pad_maximum_fusion.refs_4_.refs_6_), channel_id=1, source_target_pairs={{0,4},{1,5},{2,6},{3,7},{4,0},{5,1},{6,2},{7,3},{8,12},{9,13},{10,... | collective-permute-start | bytes 1572872 | tf_op jit(solution)/shard_map/ppermute | solution.py:236
  17.5 9.4 %shard_map.73 = (f32[8,128]{1,0:T(8,128)S(1)}, f32[4,2,1024,128]{3,2,1,0:T(8,128)}, f32[4,2,1024,128]{3,2,1,0:T(8,128)}, bf16[4,2,1024,256]{3,2,1,0:T(8,128)(2,1)}) custom-call(s32[2,4]{1,0:T(2,128)S(1)} %copy-done, s32[4]{0:T(128)S(1)} %copy-done.1, bf16[128,4096]{1,0:T(8,128)(2,1)S(1)} %get-tuple-element.82.refs_2_, ...), custom_call_target="tpu_custom_call" | custom-call | flops 4294967296 | bytes 4194304 | tf_op jit(solution)/shard_map/pallas_call | solution.py:197
  27.0 1.3 %collective-permute-start.4 = (bf16[256,1024]{1,0:T(8,128)(2,1)}, bf16[256,1024]{1,0:T(8,128)(2,1)}, u32[]{:S(2)}, u32[]{:S(2)}) collective-permute-start(bf16[256,1024]{1,0:T(8,128)(2,1)} %collective-permute-done.2), channel_id=1, source_target_pairs={{8,0},{16,8},{9,1},{17,9},{10,2},{18,10},{11,3},{19,11},{12,4},{20... | collective-permute-start | bytes 1572872 | tf_op jit(solution)/shard_map/ppermute | solution.py:262
  28.3 1.5 %collective-permute-start.5 = (bf16[256,1024]{1,0:T(8,128)(2,1)}, bf16[256,1024]{1,0:T(8,128)(2,1)}, u32[]{:S(2)}, u32[]{:S(2)}) collective-permute-start(bf16[256,1024]{1,0:T(8,128)(2,1)} %collective-permute-done.3), channel_id=1, source_target_pairs={{8,16},{9,17},{10,18},{11,19},{12,20},{13,21},{14,22},{15,23}} | collective-permute-start | bytes 1572872 | tf_op jit(solution)/shard_map/ppermute | solution.py:265
  29.8 0.5 collective-permute-start.10
  30.3 0.3 collective-permute-start.9
  30.6 0.6 constant_dynamic-slice_fusion
  34.4 8.0 %shard_map.74 = (f32[8,128]{1,0:T(8,128)S(1)}, f32[4,2,1024,128]{3,2,1,0:T(8,128)}, f32[4,2,1024,128]{3,2,1,0:T(8,128)}) custom-call(s32[2,4]{1,0:T(2,128)S(1)} %copy-done, s32[4]{0:T(128)S(1)} %copy-done.1, bf16[4,2,1024,256]{3,2,1,0:T(8,128)(2,1)} %get-tuple-element.43.refs_2_, bf16[256,1024]{1,0:T(8,128)(2,1)S(1)} %collective-permute-done.6.refs_3_.refs_5_, ...), custom_call_target="tpu_custom_call" | custom-call | flops 4294967296 | bytes 4194304 | tf_op jit(solution)/shard_map/pallas_call | solution.py:197
  42.4 0.2 collective-permute-done.10.refs_4_.refs_6_
  42.6 0.2 collective-permute-done.9.refs_3_.refs_5_
  42.9 5.3 %collective-permute-start.13 = (bf16[256,1024]{1,0:T(8,128)(2,1)S(1)}, bf16[256,1024]{1,0:T(8,128)(2,1)S(1)}, u32[]{:S(2)}, u32[]{:S(2)}) collective-permute-start(bf16[256,1024]{1,0:T(8,128)(2,1)S(1)} %pad_maximum_fusion.3), channel_id=1, source_target_pairs={{0,2},{1,3},{2,0},{3,1},{4,6},{5,7},{6,4},{7,5},{8,10},{9,11},{10,... | collective-permute-start | bytes 1572872 | tf_op jit(solution)/shard_map/ppermute | solution.py:233
  48.3 1.5 %collective-permute-start.8 = (bf16[256,1024]{1,0:T(8,128)(2,1)}, bf16[256,1024]{1,0:T(8,128)(2,1)S(1)}, u32[]{:S(2)}, u32[]{:S(2)}) collective-permute-start(bf16[256,1024]{1,0:T(8,128)(2,1)} %collective-permute-done.4), channel_id=1, source_target_pairs={{8,0},{9,1},{10,2},{11,3},{12,4},{13,5},{14,6},{15,7}} | collective-permute-start | bytes 1572872 | tf_op jit(solution)/shard_map/ppermute | solution.py:262
  49.8 4.9 %collective-permute-start.12 = (bf16[256,1024]{1,0:T(8,128)(2,1)S(1)}, bf16[256,1024]{1,0:T(8,128)(2,1)S(1)}, u32[]{:S(2)}, u32[]{:S(2)}) collective-permute-start(bf16[256,1024]{1,0:T(8,128)(2,1)S(1)} %pad_maximum_fusion.2), channel_id=1, source_target_pairs={{0,4},{1,5},{2,6},{3,7},{4,0},{5,1},{6,2},{7,3},{8,12},{9,13},{10,... | collective-permute-start | bytes 1572872 | tf_op jit(solution)/shard_map/ppermute | solution.py:236
  54.7 15.2 %shard_map.75 = (f32[8,128]{1,0:T(8,128)S(1)}, f32[4,2,1024,128]{3,2,1,0:T(8,128)}, f32[4,2,1024,128]{3,2,1,0:T(8,128)}) custom-call(s32[2,4]{1,0:T(2,128)S(1)} %copy-done, s32[4]{0:T(128)S(1)} %copy-done.1, bf16[4,2,1024,256]{3,2,1,0:T(8,128)(2,1)} %get-tuple-element.43.refs_2_, bf16[256,1024]{1,0:T(8,128)(2,1)S(1)} %collective-permute-done.9.refs_3_.refs_5_, ...), custom_call_target="tpu_custom_call" | custom-call | flops 4294967296 | bytes 4194304 | tf_op jit(solution)/shard_map/pallas_call | solution.py:197
  69.9 0.6 select_select_fusion.refs_5_.refs_8_
  70.6 0.1 collective-permute-start.11
  70.7 0.1 collective-permute-start.15
  70.8 17.2 %shard_map.76 = (f32[8,128]{1,0:T(8,128)S(1)}, f32[4,2,1024,128]{3,2,1,0:T(8,128)}, f32[4,2,1024,128]{3,2,1,0:T(8,128)}) custom-call(s32[2,4]{1,0:T(2,128)S(1)} %copy-done, s32[4]{0:T(128)S(1)} %copy-done.1, bf16[4,2,1024,256]{3,2,1,0:T(8,128)(2,1)} %get-tuple-element.43.refs_2_, bf16[256,1024]{1,0:T(8,128)(2,1)S(1)} %collective-permute-done.12.refs_3_.refs_6_, ...), custom_call_target="tpu_custom_call" | custom-call | flops 6442450944 | bytes 4194304 | tf_op jit(solution)/shard_map/pallas_call | solution.py:197
  88.0 6.0 %collective-permute-start.14 = (bf16[128,1024]{1,0:T(8,128)(2,1)S(1)}, bf16[128,1024]{1,0:T(8,128)(2,1)S(1)}, u32[]{:S(2)}, u32[]{:S(2)}) collective-permute-start(bf16[128,1024]{1,0:T(8,128)(2,1)S(1)} %slice.30), channel_id=1, source_target_pairs={{0,4},{1,5},{2,6},{3,7},{4,0},{5,1},{6,2},{7,3},{8,12},{9,13},{10,... | collective-permute-start | bytes 786440 | tf_op jit(solution)/shard_map/ppermute | solution.py:236
  94.1 2.0 %collective-permute-start.16 = (bf16[128,1024]{1,0:T(8,128)(2,1)S(1)}, bf16[128,1024]{1,0:T(8,128)(2,1)S(1)}, u32[]{:S(2)}, u32[]{:S(2)}) collective-permute-start(bf16[128,1024]{1,0:T(8,128)(2,1)S(1)} %slice.34), channel_id=1, source_target_pairs={{0,2},{1,3},{2,0},{3,1},{4,6},{5,7},{6,4},{7,5},{8,10},{9,11},{10,... | collective-permute-start | bytes 786440 | tf_op jit(solution)/shard_map/ppermute | solution.py:233
  96.1 15.1 %shard_map.77 = (f32[8,128]{1,0:T(8,128)S(1)}, f32[4,2,1024,128]{3,2,1,0:T(8,128)}, f32[4,2,1024,128]{3,2,1,0:T(8,128)}) custom-call(s32[2,4]{1,0:T(2,128)S(1)} %copy-done, s32[4]{0:T(128)S(1)} %copy-done.1, bf16[4,2,1024,256]{3,2,1,0:T(8,128)(2,1)} %get-tuple-element.43.refs_2_, bf16[256,1024]{1,0:T(8,128)(2,1)S(1)} %collective-permute-done.11.refs_3_.refs_5_, ...), custom_call_target="tpu_custom_call" | custom-call | flops 4294967296 | bytes 4194304 | tf_op jit(solution)/shard_map/pallas_call | solution.py:197
  111.2 9.6 %shard_map.78 = (bf16[128,4096]{1,0:T(8,128)(2,1)S(1)}, bf16[128,4096]{1,0:T(8,128)(2,1)S(1)}) custom-call(s32[2,4]{1,0:T(2,128)S(1)} %copy-done, s32[4]{0:T(128)S(1)} %copy-done.1, bf16[4,2,1024,256]{3,2,1,0:T(8,128)(2,1)} %get-tuple-element.43.refs_2_, bf16[128,1024]{1,0:T(8,128)(2,1)S(1)} %collective-permute-done.14.refs_3_.refs_5_, ...), custom_call_target="tpu_custom_call" | custom-call | flops 2147483648 | bytes 4194304 | tf_op jit(solution)/shard_map/pallas_call | solution.py:197
  120.7 0.1 collective-permute-start.17
  120.8 2.6 %collective-permute-done.17 = bf16[128,4096]{1,0:T(8,128)(2,1)S(1)} collective-permute-done((bf16[128,4096]{1,0:T(8,128)(2,1)S(1)}, bf16[128,4096]{1,0:T(8,128)(2,1)S(1)}, u32[]{:S(2)}, u32[]{:S(2)}) %collective-permute-start.17) | collective-permute-done | bytes 1048608 | tf_op jit(solution)/shard_map/ppermute | solution.py:230
  123.5 1.8 %maximum_select_fusion = bf16[128,8192]{1,0:T(8,128)(2,1)} fusion(bf16[128,4096]{1,0:T(8,128)(2,1)S(1)} %collective-permute-done.17, bf16[128,4096]{1,0:T(8,128)(2,1)S(1)} %get-tuple-element.79, pred[]{:T(512)S(6)} %eq.18), kind=kLoop, calls=%fused_computation | loop fusion | flops 9437184 | bytes 4194305 | tf_op jit(solution)/shard_map/jit(_where)/select_n | solution.py:319
  (44 shorter events, 0.5 us)
Async XLA Ops:
  0.0 3.3 %copy-start.5 = (bf16[128,1024]{1,0:T(8,128)(2,1)S(1)}, bf16[128,1024]{1,0:T(8,128)(2,1)}, u32[]{:S(2)}) copy-start(bf16[128,1024]{1,0:T(8,128)(2,1)} %param.10) | copy-start | bytes 786436
  0.0 3.3 %copy-start.4 = (bf16[128,1024]{1,0:T(8,128)(2,1)S(1)}, bf16[128,1024]{1,0:T(8,128)(2,1)}, u32[]{:S(2)}) copy-start(bf16[128,1024]{1,0:T(8,128)(2,1)} %param.11) | copy-start | bytes 786436
  0.0 3.3 %copy-start.7 = (bf16[128,1024]{1,0:T(8,128)(2,1)S(1)}, bf16[128,1024]{1,0:T(8,128)(2,1)}, u32[]{:S(2)}) copy-start(bf16[128,1024]{1,0:T(8,128)(2,1)} %param.8) | copy-start | bytes 786436
  0.0 3.3 %copy-start.6 = (bf16[128,1024]{1,0:T(8,128)(2,1)S(1)}, bf16[128,1024]{1,0:T(8,128)(2,1)}, u32[]{:S(2)}) copy-start(bf16[128,1024]{1,0:T(8,128)(2,1)} %param.9) | copy-start | bytes 786436
  2.8 14.7 %copy-start = (s32[2,4]{1,0:T(2,128)S(1)}, s32[2,4]{1,0:T(2,128)}, u32[]{:S(2)}) copy-start(s32[2,4]{1,0:T(2,128)} %refs_0_.11) | copy-start | bytes 100
  2.8 14.7 %copy-start.1 = (s32[4]{0:T(128)S(1)}, s32[4]{0:T(128)}, u32[]{:S(2)}) copy-start(s32[4]{0:T(128)} %refs_1_.11) | copy-start | bytes 52
  2.8 14.7 %collective-permute-start = (bf16[128,4096]{1,0:T(8,128)(2,1)}, bf16[128,4096]{1,0:T(8,128)(2,1)}, u32[]{:S(2)}, u32[]{:S(2)}) collective-permute-start(bf16[128,4096]{1,0:T(8,128)(2,1)} %get-tuple-element.81), channel_id=1, source_target_pairs={{0,1},{1,0},{2,3},{3,2},{4,5},{5,4},{6,7},{7,6},{8,9},{9,8},{10,11... | collective-permute-start | bytes 3145736 | tf_op jit(solution)/shard_map/ppermute | solution.py:230
  3.4 14.1 %copy-start.2 = (bf16[128,512]{1,0:T(8,128)(2,1)}, bf16[128,512]{1,0:T(8,128)(2,1)S(1)}, u32[]{:S(2)}) copy-start(bf16[128,512]{1,0:T(8,128)(2,1)S(1)} %get-tuple-element.96) | copy-start | bytes 393220
  3.5 2.8 %collective-permute-start.1 = (bf16[256,1024]{1,0:T(8,128)(2,1)S(1)}, bf16[256,1024]{1,0:T(8,128)(2,1)S(1)}, u32[]{:S(2)}, u32[]{:S(2)}) collective-permute-start(bf16[256,1024]{1,0:T(8,128)(2,1)S(1)} %maximum_maximum_fusion), channel_id=1, source_target_pairs={{0,1},{1,0},{2,3},{3,2},{4,5},{5,4},{6,7},{7,6},{8,9},{9,8},{10,11... | collective-permute-start | bytes 1572872 | tf_op jit(solution)/shard_map/ppermute | solution.py:230
  6.4 20.6 %collective-permute-start.2 = (bf16[256,1024]{1,0:T(8,128)(2,1)S(1)}, bf16[256,1024]{1,0:T(8,128)(2,1)}, u32[]{:S(2)}, u32[]{:S(2)}) collective-permute-start(bf16[256,1024]{1,0:T(8,128)(2,1)S(1)} %pad_maximum_fusion.refs_4_.refs_6_), channel_id=1, source_target_pairs={{8,0},{16,8},{24,16},{9,1},{17,9},{25,17},{10,2},{18,10},{26,18},{... | collective-permute-start | bytes 1572872 | tf_op jit(solution)/shard_map/ppermute | solution.py:262
  7.7 19.3 %collective-permute-start.3 = (bf16[256,1024]{1,0:T(8,128)(2,1)S(1)}, bf16[256,1024]{1,0:T(8,128)(2,1)}, u32[]{:S(2)}, u32[]{:S(2)}) collective-permute-start(bf16[256,1024]{1,0:T(8,128)(2,1)S(1)} %pad_maximum_fusion.refs_4_.refs_6_), channel_id=1, source_target_pairs={{0,8},{8,16},{1,9},{9,17},{2,10},{10,18},{3,11},{11,19},{4,12},{12... | collective-permute-start | bytes 1572872 | tf_op jit(solution)/shard_map/ppermute | solution.py:265
  14.0 16.3 %collective-permute-start.6 = (bf16[256,1024]{1,0:T(8,128)(2,1)S(1)}, bf16[256,1024]{1,0:T(8,128)(2,1)S(1)}, u32[]{:S(2)}, u32[]{:S(2)}) collective-permute-start(bf16[256,1024]{1,0:T(8,128)(2,1)S(1)} %pad_maximum_fusion.refs_4_.refs_6_), channel_id=1, source_target_pairs={{0,2},{1,3},{2,0},{3,1},{4,6},{5,7},{6,4},{7,5},{8,10},{9,11},{10,... | collective-permute-start | bytes 1572872 | tf_op jit(solution)/shard_map/ppermute | solution.py:233
  15.9 18.5 %collective-permute-start.7 = (bf16[256,1024]{1,0:T(8,128)(2,1)S(1)}, bf16[256,1024]{1,0:T(8,128)(2,1)S(1)}, u32[]{:S(2)}, u32[]{:S(2)}) collective-permute-start(bf16[256,1024]{1,0:T(8,128)(2,1)S(1)} %pad_maximum_fusion.refs_4_.refs_6_), channel_id=1, source_target_pairs={{0,4},{1,5},{2,6},{3,7},{4,0},{5,1},{6,2},{7,3},{8,12},{9,13},{10,... | collective-permute-start | bytes 1572872 | tf_op jit(solution)/shard_map/ppermute | solution.py:236
  27.0 15.5 %collective-permute-start.4 = (bf16[256,1024]{1,0:T(8,128)(2,1)}, bf16[256,1024]{1,0:T(8,128)(2,1)}, u32[]{:S(2)}, u32[]{:S(2)}) collective-permute-start(bf16[256,1024]{1,0:T(8,128)(2,1)} %collective-permute-done.2), channel_id=1, source_target_pairs={{8,0},{16,8},{9,1},{17,9},{10,2},{18,10},{11,3},{19,11},{12,4},{20... | collective-permute-start | bytes 1572872 | tf_op jit(solution)/shard_map/ppermute | solution.py:262
  28.3 14.2 %collective-permute-start.5 = (bf16[256,1024]{1,0:T(8,128)(2,1)}, bf16[256,1024]{1,0:T(8,128)(2,1)}, u32[]{:S(2)}, u32[]{:S(2)}) collective-permute-start(bf16[256,1024]{1,0:T(8,128)(2,1)} %collective-permute-done.3), channel_id=1, source_target_pairs={{8,16},{9,17},{10,18},{11,19},{12,20},{13,21},{14,22},{15,23}} | collective-permute-start | bytes 1572872 | tf_op jit(solution)/shard_map/ppermute | solution.py:265
  29.8 12.8 %collective-permute-start.10 = (bf16[256,1024]{1,0:T(8,128)(2,1)S(1)}, bf16[256,1024]{1,0:T(8,128)(2,1)S(1)}, u32[]{:S(2)}, u32[]{:S(2)}) collective-permute-start(bf16[256,1024]{1,0:T(8,128)(2,1)S(1)} %pad_maximum_fusion.1.refs_5_.refs_7_), channel_id=1, source_target_pairs={{0,4},{1,5},{2,6},{3,7},{4,0},{5,1},{6,2},{7,3},{8,12},{9,13},{10,... | collective-permute-start | bytes 1572872 | tf_op jit(solution)/shard_map/ppermute | solution.py:236
  30.3 12.6 %collective-permute-start.9 = (bf16[256,1024]{1,0:T(8,128)(2,1)S(1)}, bf16[256,1024]{1,0:T(8,128)(2,1)S(1)}, u32[]{:S(2)}, u32[]{:S(2)}) collective-permute-start(bf16[256,1024]{1,0:T(8,128)(2,1)S(1)} %pad_maximum_fusion.1.refs_5_.refs_7_), channel_id=1, source_target_pairs={{0,2},{1,3},{2,0},{3,1},{4,6},{5,7},{6,4},{7,5},{8,10},{9,11},{10,... | collective-permute-start | bytes 1572872 | tf_op jit(solution)/shard_map/ppermute | solution.py:233
  42.9 27.9 %collective-permute-start.13 = (bf16[256,1024]{1,0:T(8,128)(2,1)S(1)}, bf16[256,1024]{1,0:T(8,128)(2,1)S(1)}, u32[]{:S(2)}, u32[]{:S(2)}) collective-permute-start(bf16[256,1024]{1,0:T(8,128)(2,1)S(1)} %pad_maximum_fusion.3), channel_id=1, source_target_pairs={{0,2},{1,3},{2,0},{3,1},{4,6},{5,7},{6,4},{7,5},{8,10},{9,11},{10,... | collective-permute-start | bytes 1572872 | tf_op jit(solution)/shard_map/ppermute | solution.py:233
  48.3 21.6 %collective-permute-start.8 = (bf16[256,1024]{1,0:T(8,128)(2,1)}, bf16[256,1024]{1,0:T(8,128)(2,1)S(1)}, u32[]{:S(2)}, u32[]{:S(2)}) collective-permute-start(bf16[256,1024]{1,0:T(8,128)(2,1)} %collective-permute-done.4), channel_id=1, source_target_pairs={{8,0},{9,1},{10,2},{11,3},{12,4},{13,5},{14,6},{15,7}} | collective-permute-start | bytes 1572872 | tf_op jit(solution)/shard_map/ppermute | solution.py:262
  49.8 20.9 %collective-permute-start.12 = (bf16[256,1024]{1,0:T(8,128)(2,1)S(1)}, bf16[256,1024]{1,0:T(8,128)(2,1)S(1)}, u32[]{:S(2)}, u32[]{:S(2)}) collective-permute-start(bf16[256,1024]{1,0:T(8,128)(2,1)S(1)} %pad_maximum_fusion.2), channel_id=1, source_target_pairs={{0,4},{1,5},{2,6},{3,7},{4,0},{5,1},{6,2},{7,3},{8,12},{9,13},{10,... | collective-permute-start | bytes 1572872 | tf_op jit(solution)/shard_map/ppermute | solution.py:236
  54.7 15.2 %copy-start.3 = (bf16[128,512]{1,0:T(8,128)(2,1)S(1)}, bf16[128,512]{1,0:T(8,128)(2,1)}, u32[]{:S(2)}) copy-start(bf16[128,512]{1,0:T(8,128)(2,1)} %copy-done.2) | copy-start | bytes 393220
  70.6 17.4 %collective-permute-start.11 = (bf16[256,1024]{1,0:T(8,128)(2,1)S(1)}, bf16[256,1024]{1,0:T(8,128)(2,1)S(1)}, u32[]{:S(2)}, u32[]{:S(2)}) collective-permute-start(bf16[256,1024]{1,0:T(8,128)(2,1)S(1)} %select_select_fusion.refs_5_.refs_8_), channel_id=1, source_target_pairs={{0,2},{1,3},{2,0},{3,1},{4,6},{5,7},{6,4},{7,5},{8,10},{9,11},{10,... | collective-permute-start | bytes 1572872 | tf_op jit(solution)/shard_map/ppermute | solution.py:233
  70.7 23.4 %collective-permute-start.15 = (bf16[256,1024]{1,0:T(8,128)(2,1)S(1)}, bf16[256,1024]{1,0:T(8,128)(2,1)S(1)}, u32[]{:S(2)}, u32[]{:S(2)}) collective-permute-start(bf16[256,1024]{1,0:T(8,128)(2,1)S(1)} %select_select_fusion.refs_5_.refs_8_), channel_id=1, source_target_pairs={{0,4},{1,5},{2,6},{3,7},{4,0},{5,1},{6,2},{7,3},{8,12},{9,13},{10,... | collective-permute-start | bytes 1572872 | tf_op jit(solution)/shard_map/ppermute | solution.py:236
  88.0 23.1 %collective-permute-start.14 = (bf16[128,1024]{1,0:T(8,128)(2,1)S(1)}, bf16[128,1024]{1,0:T(8,128)(2,1)S(1)}, u32[]{:S(2)}, u32[]{:S(2)}) collective-permute-start(bf16[128,1024]{1,0:T(8,128)(2,1)S(1)} %slice.30), channel_id=1, source_target_pairs={{0,4},{1,5},{2,6},{3,7},{4,0},{5,1},{6,2},{7,3},{8,12},{9,13},{10,... | collective-permute-start | bytes 786440 | tf_op jit(solution)/shard_map/ppermute | solution.py:236
  94.1 17.1 %collective-permute-start.16 = (bf16[128,1024]{1,0:T(8,128)(2,1)S(1)}, bf16[128,1024]{1,0:T(8,128)(2,1)S(1)}, u32[]{:S(2)}, u32[]{:S(2)}) collective-permute-start(bf16[128,1024]{1,0:T(8,128)(2,1)S(1)} %slice.34), channel_id=1, source_target_pairs={{0,2},{1,3},{2,0},{3,1},{4,6},{5,7},{6,4},{7,5},{8,10},{9,11},{10,... | collective-permute-start | bytes 786440 | tf_op jit(solution)/shard_map/ppermute | solution.py:233
  120.7 2.7 %collective-permute-start.17 = (bf16[128,4096]{1,0:T(8,128)(2,1)S(1)}, bf16[128,4096]{1,0:T(8,128)(2,1)S(1)}, u32[]{:S(2)}, u32[]{:S(2)}) collective-permute-start(bf16[128,4096]{1,0:T(8,128)(2,1)S(1)} %get-tuple-element.80), channel_id=1, source_target_pairs={{0,1},{1,0},{2,3},{3,2},{4,5},{5,4},{6,7},{7,6},{8,9},{9,8},{10,11... | collective-permute-start | bytes 3145736 | tf_op jit(solution)/shard_map/ppermute | solution.py:230

commit v6 on v4

--- a/solution.py
+++ b/solution.py
@@ -15,24 +15,25 @@
 HALF_KV = KVH // 2
 NEG = -1e30
 Q_SCALE = math.log2(math.e) / math.sqrt(HD)
-ROW_BLOCK = 512
+ROW_BLOCK = 256
 
 
 def attend_kernel(ny, rows, arrays, groups, first, last, *refs):
     refs = list(refs)
     take = lambda count: [refs.pop(0) for _ in range(count)]
     exp_ref, off_ref = take(2)
-    raw = take(2) if first else None
+    raw = take(2 if first else 1)
     key_refs = take(arrays)
     value_refs = take(arrays)
     head = pl.program_id(0)
     if not first:
-        take(4)
+        take(2)
     if last:
         outs = take(2)
     else:
         take(1)[0][...] = jnp.zeros((8, HD), jnp.float32)
-    qs, accs, ms = take(3)
+    (held,) = take(1)
+    qs = take(1)[0] if first else raw[0]
     stacked = GW * rows
 
     group = lax.axis_index("leaf")
@@ -54,8 +55,8 @@
                 q = q_ref[:, g * HD : (g + 1) * HD].astype(jnp.float32) * Q_SCALE
                 high = q.astype(jnp.bfloat16)
                 low = (q - high.astype(jnp.float32)).astype(jnp.bfloat16)
-                qs[head, s, g * rows : (g + 1) * rows, :HD] = high
-                qs[head, s, g * rows : (g + 1) * rows, HD:] = low
+                qs[0, s, g * rows : (g + 1) * rows, :HD] = high
+                qs[0, s, g * rows : (g + 1) * rows, HD:] = low
 
     def step(members, limits, masked, fresh):
         width = len(members) * rows
@@ -69,7 +70,7 @@
 
         def score(s, here):
             return lax.dot_general(
-                qs[head, s, here, :], keys, (((1,), (1,)), ((), ())), preferred_element_type=jnp.float32
+                qs[0, s, here, :], keys, (((1,), (1,)), ((), ())), preferred_element_type=jnp.float32
             )
 
         def bias_of(s):
@@ -93,16 +94,17 @@
             if fresh:
                 new = jnp.broadcast_to(new, (size, HD))
             else:
-                old = ms[head, s, here, :]
+                old = held[head, s, here, 2 * HD :]
                 new = jnp.maximum(old, new)
             weights = jnp.exp2(scores - jnp.concatenate([new] * (width // HD), axis=1))
             update = jnp.dot(weights.astype(jnp.bfloat16), values, preferred_element_type=jnp.float32)
             if fresh:
-                accs[head, s, here, :] = update
+                held[head, s, here, : 2 * HD] = update
             else:
                 shrink = jnp.exp2(old - new)
-                accs[head, s, here, :] = accs[head, s, here, :] * jnp.concatenate([shrink, shrink], axis=1) + update
-            ms[head, s, here, :] = new
+                before = held[head, s, here, : 2 * HD] * jnp.concatenate([shrink, shrink], axis=1)
+                held[head, s, here, : 2 * HD] = before + update
+            held[head, s, here, 2 * HD :] = new
 
     for number, members in enumerate(groups):
         limits = []
@@ -135,26 +137,82 @@
         for s in range(2):
             for g in range(GW):
                 here = slice(g * rows, (g + 1) * rows)
-                done = accs[head, s, here, :HD] / accs[head, s, here, HD:]
+                done = held[head, s, here, :HD] / held[head, s, here, HD : 2 * HD]
                 outs[s][:, g * HD : (g + 1) * HD] = done.astype(jnp.bfloat16)
+
+
+WHOLE = pl.BlockSpec(memory_space=pltpu.VMEM)
+
+
+def fence(state, *values):
+    mark, held, prepared = state
+    *values, mark = lax.optimization_barrier((*values, mark))
+
+    def kernel(mark_ref, held_ref, out_ref, held_out_ref):
+        out_ref[...] = mark_ref[...]
+
+    mark, held = pl.pallas_call(
+        kernel,
+        in_specs=[WHOLE, WHOLE],
+        out_specs=[WHOLE, WHOLE],
+        out_shape=[jax.ShapeDtypeStruct(mark.shape, mark.dtype), pltpu.VMEM(held.shape, held.dtype)],
+        input_output_aliases={1: 1},
+        compiler_params=pltpu.CompilerParams(vmem_limit_bytes=4 * 2**20),
+    )(mark, pltpu.with_memory_space_constraint(held, pltpu.VMEM))
+    state[:] = [mark, held, prepared]
+    return values
+
+
+def pick(state, table, owners, arrays):
+    mark, held, prepared = state
+    count = len(arrays)
+
+    def kernel(table_ref, mark_ref, *refs):
+        out_ref, mark_out_ref, _, sem = refs[count + 1 :]
+        group = lax.axis_index("leaf")
+        parent = table_ref[0, group]
+        mark_out_ref[...] = mark_ref[...]
+        for owner, ref in zip(owners, refs):
+
+            @pl.when(parent == group + owner)
+            def _():
+                copy = pltpu.make_async_copy(ref, out_ref, sem)
+                copy.start()
+                copy.wait()
+
+    anywhere = pl.BlockSpec(memory_space=pl.ANY)
+    picked, mark, held = pl.pallas_call(
+        kernel,
+        in_specs=[pl.BlockSpec(memory_space=pltpu.SMEM), WHOLE] + [anywhere] * count + [WHOLE],
+        out_specs=[anywhere, WHOLE, WHOLE],
+        out_shape=[
+            jax.ShapeDtypeStruct(arrays[0].shape, arrays[0].dtype),
+            jax.ShapeDtypeStruct(mark.shape, mark.dtype),
+            pltpu.VMEM(held.shape, held.dtype),
+        ],
+        scratch_shapes=[pltpu.SemaphoreType.DMA(())],
+        input_output_aliases={count + 2: 2},
+        compiler_params=pltpu.CompilerParams(vmem_limit_bytes=4 * 2**20),
+    )(table, mark, *arrays, pltpu.with_memory_space_constraint(held, pltpu.VMEM))
+    state[:] = [mark, held, prepared]
+    return picked
 
 
 def attend(ny, rows, tables, arrays, groups, queries, state, last):
     stacked = GW * rows
     first = state is None
     smem = pl.BlockSpec(memory_space=pltpu.SMEM)
-    held = pl.BlockSpec(memory_space=pltpu.VMEM)
     row_spec = pl.BlockSpec((rows, GW * HD), lambda h: (0, h))
-    kept = [
-        ((HALF_KV, 2, stacked, 2 * HD), jnp.bfloat16),
-        ((HALF_KV, 2, stacked, 2 * HD), jnp.float32),
-        ((HALF_KV, 2, stacked, HD), jnp.float32),
-    ]
+    q_spec = pl.BlockSpec((1, 2, stacked, 2 * HD), lambda h: (h, 0, 0, 0))
     operands = [*tables]
     specs = [smem, smem]
     if first:
         operands += queries
         specs += [row_spec, row_spec]
+    else:
+        mark, state, prepared = state
+        operands.append(pltpu.with_memory_space_constraint(prepared, pltpu.HBM))
+        specs.append(q_spec)
     for shift in (0, HALF_KV):
         for array in arrays:
             operands.append(array)
@@ -167,15 +225,14 @@
         out_shape = [jax.ShapeDtypeStruct((8, HD), jnp.float32)]
         out_specs = [pl.BlockSpec((8, HD), lambda h: (0, 0))]
     if not first:
-        mark, *state = state
-        operands.append(mark)
-        specs.append(pl.BlockSpec(memory_space=pl.ANY))
-        for i, array in enumerate(state):
-            aliases[len(operands)] = len(out_shape) + i
-            operands.append(pltpu.with_memory_space_constraint(array, pltpu.VMEM))
-            specs.append(held)
-    out_shape += [pltpu.VMEM(shape, dtype) for shape, dtype in kept]
-    out_specs += [held] * 3
+        aliases = {len(operands) + 1: len(out_shape)}
+        operands += [mark, pltpu.with_memory_space_constraint(state, pltpu.VMEM)]
+        specs += [pl.BlockSpec(memory_space=pl.ANY), WHOLE]
+    out_shape.append(pltpu.VMEM((HALF_KV, 2, stacked, 3 * HD), jnp.float32))
+    out_specs.append(WHOLE)
+    if first:
+        out_shape.append(pltpu.HBM((HALF_KV, 2, stacked, 2 * HD), jnp.bfloat16))
+        out_specs.append(q_spec)
     scores = HALF_KV * 2 * stacked * rows * sum(len(members) for members in groups)
     out = pl.pallas_call(
         functools.partial(attend_kernel, ny, rows, len(arrays), groups, first, last),
@@ -187,7 +244,7 @@
         compiler_params=pltpu.CompilerParams(vmem_limit_bytes=24 * 2**20),
         cost_estimate=pl.CostEstimate(flops=8 * scores * HD, bytes_accessed=4 * 2**20, transcendentals=scores),
     )(*operands)
-    return out[:2] if last else list(out)
+    return out[:2] if last else list(out) if first else [*out, prepared]
 
 
 def on_device(queries, seg_keys, seg_values, root_keys, root_values, expansion, root_offsets):
@@ -243,10 +300,10 @@
 
     def hop(step, down, up):
         down = lax.ppermute(down, "leaf", [(i, i - 1) for i in range(1, leaves - step + 1)])
-        choices.append((group + step, down))
+        choices.append((step, down))
         if step < leaves - 1:
             up = lax.ppermute(up, "leaf", [(i, i + 1) for i in range(step - 1, leaves - 2)])
-            choices.append((group - step, up))
+            choices.append((-step, up))
         return down, up
 
     down, up = hop(1, own, own)
@@ -255,7 +312,8 @@
     state = run([own, root], (members(0, "own") + members(1, "root"),), q_pair, None, False)
 
     if leaves > 2:
-        down, up = hop(2, *after(state, down, up))
+        down, up = hop(2, *fence(state, down, up))
+    own_x, *own_y = after(state, own_x, *own_y)
 
     def near(kind, arrays):
         groups = [members(0, kind, 1) + members(1, kind, 0, 1)]
@@ -264,19 +322,15 @@
 
     state = near("own", [own_x, *own_y])
     for step in range(3, leaves):
-        down, up = hop(step, *after(state, down, up))
+        down, up = hop(step, *fence(state, down, up))
     own_x, root_x, *pairs = after(state, own_x, root_x, *own_y, *root_y)
     own_y, root_y = pairs[: ny - 1], pairs[ny - 1 :]
     tops = [to_y(jnp.concatenate([own_x[:rows], root_x[:rows]], axis=0), step) for step in steps]
     lows = [to_x(jnp.concatenate([a[rows:], b[rows:]], axis=0)) for a, b in zip(own_y, root_y)]
     state = near("root", [root_x, *root_y])
 
-    parent = expansion[0, group]
     owners, helds = zip(*choices)
-    helds = after(state, *helds)
-    parent_rows = own
-    for owner, held in zip(owners, helds):
-        parent_rows = jnp.where(parent == owner, held, parent_rows)
+    parent_rows = pick(state, expansion, (0, *owners), (own, *after(state, *helds)))
     (parent_rows,) = after(state, parent_rows)
     kin_x, kin_y = to_x(parent_rows), [to_y(parent_rows, step) for step in steps]
     groups, arrays = [], []

time: 121 us -> 98 us (0.81)
  the two profiles are of different devices: /device:TPU:11 before, /device:TPU:0 now
where the time goes in v6:
time: 98 us; the launch traced here: 97.5 us
  Pallas kernels  42.3 us (43%)
  starting transfers between devices  24.6 us (25%)
  waiting for transfers between devices  24.3 us (25%)
  local copies, waits for them, and re-layouts  4.03 us (4%)
  other arithmetic  2.01 us (2%)
    pallas_call x6, Pallas kernels, attend(): pl.pallas_call(functools.partial(attend_kernel, ny, rows, len(arrays), gr...  41.5 us
    ppermute x3, waiting for transfers between devices, hop(): lax.ppermute(down, 'leaf', [(i, i - 1) for i in range(1, leaves - step +...  15.3 us
    ppermute x5, starting transfers between devices, to_y(): lax.ppermute(array, 'ctx', [(index(x, y, k), index(x, y + step, k)) for x...  10.2 us
    ppermute x5, starting transfers between devices, to_x(): lax.ppermute(array, 'ctx', [(index(x, y, k), index(x + 1, y, k)) for x, y...  5.67 us
    ppermute x3, waiting for transfers between devices, to_core(): lax.ppermute(array, 'ctx', [(index(x, y, k), index(x, y, k + 1)) for x, y...  4.5 us
    ppermute x2, starting transfers between devices, hop(): lax.ppermute(up, 'leaf', [(i, i + 1) for i in range(step - 1, leaves - 2)])  4.2 us
    ppermute x3, starting transfers between devices, hop(): lax.ppermute(down, 'leaf', [(i, i - 1) for i in range(1, leaves - step +...  3.85 us
    ppermute x5, waiting for transfers between devices, to_x(): lax.ppermute(array, 'ctx', [(index(x, y, k), index(x + 1, y, k)) for x, y...  2.55 us
  transfers between devices with their start and end apart: 18, of which 10 were waited for; matrix products, arithmetic and copies ran while one was open for 2% of the time, Pallas kernels for 37%

profile of v6, /device:TPU:0, one launch (start us, length us, event | category | flops | bytes accessed | tf_op | source)
XLA Modules:
  0.0 97.5 jit_solution(10081549021290271469)
XLA Ops:
  0.0 1.7 %constant_dynamic-slice_fusion.8 = (bf16[128,4096]{1,0:T(8,128)(2,1)S(1)}, bf16[128,4096]{1,0:T(8,128)(2,1)S(1)}) fusion(bf16[128,8192]{1,0:T(8,128)(2,1)} %param.7, s32[]{:T(128)S(6)} %select_n.28, s32[]{:T(128)S(6)} %select_n.27), kind=kLoop, calls=%fused_computation.14 | loop fusion | bytes 4194312 | tf_op jit(solution)/shard_map/dynamic_slice | solution.py:261
  2.3 1.0 %constant_dynamic-slice_fusion.6 = (bf16[128,512]{1,0:T(8,128)(2,1)S(1)}, bf16[128,512]{1,0:T(8,128)(2,1)S(1)}, bf16[128,512]{1,0:T(8,128)(2,1)S(1)}, bf16[128,512]{1,0:T(8,128)(2,1)S(1)}) fusion(bf16[128,1024]{1,0:T(8,128)(2,1)S(1)} %copy-done.2, s32[]{:T(128)S(6)} %select_n.29, s32[]{:T(128)S(6)} %select_n.30, bf16[128,1024]{1,0:T(8,128)(2,1)} %param.8), kind=kLoop, calls=%fused_computation.12 | loop fusion | bytes 1048584 | tf_op jit(solution)/shard_map/dynamic_slice | solution.py:260
  3.3 1.1 %constant_dynamic-slice_fusion = (bf16[128,512]{1,0:T(8,128)(2,1)S(1)}, bf16[128,512]{1,0:T(8,128)(2,1)S(1)}, bf16[128,512]{1,0:T(8,128)(2,1)S(1)}, bf16[128,512]{1,0:T(8,128)(2,1)S(1)}) fusion(bf16[128,1024]{1,0:T(8,128)(2,1)} %param.11, s32[]{:T(128)S(6)} %select_n.29, s32[]{:T(128)S(6)} %select_n.30, bf16[128,1024]{1,0:T(8,128)(2,1)} %param.10), kind=kLoop, calls=%fused_computation.6 | loop fusion | bytes 1048584 | tf_op jit(solution)/shard_map/dynamic_slice | solution.py:260
  4.6 1.9 %collective-permute-done.1 = bf16[256,1024]{1,0:T(8,128)(2,1)S(1)} collective-permute-done((bf16[256,1024]{1,0:T(8,128)(2,1)S(1)}, bf16[256,1024]{1,0:T(8,128)(2,1)S(1)}, u32[]{:S(2)}, u32[]{:S(2)}) %collective-permute-start.1) | collective-permute-done | bytes 524320 | tf_op jit(solution)/shard_map/ppermute | solution.py:270
  6.6 2.7 %collective-permute-start.7 = (bf16[256,1024]{1,0:T(8,128)(2,1)S(1)}, bf16[256,1024]{1,0:T(8,128)(2,1)S(1)}, u32[]{:S(2)}, u32[]{:S(2)}) collective-permute-start(bf16[256,1024]{1,0:T(8,128)(2,1)S(1)} %pad_maximum_fusion.refs_4_.refs_6_.refs_0_), channel_id=1, source_target_pairs={{0,4},{1,5},{2,6},{3,7},{4,0},{5,1},{6,2},{7,3},{8,12},{9,13},{10,... | collective-permute-start | bytes 1572872 | tf_op jit(solution)/shard_map/ppermute | solution.py:276
  9.3 1.5 %collective-permute-start.6 = (bf16[256,1024]{1,0:T(8,128)(2,1)S(1)}, bf16[256,1024]{1,0:T(8,128)(2,1)S(1)}, u32[]{:S(2)}, u32[]{:S(2)}) collective-permute-start(bf16[256,1024]{1,0:T(8,128)(2,1)S(1)} %pad_maximum_fusion.refs_4_.refs_6_.refs_0_), channel_id=1, source_target_pairs={{0,2},{1,3},{2,0},{3,1},{4,6},{5,7},{6,4},{7,5},{8,10},{9,11},{10,... | collective-permute-start | bytes 1572872 | tf_op jit(solution)/shard_map/ppermute | solution.py:273
  10.8 3.5 %collective-permute-start.3 = (bf16[256,1024]{1,0:T(8,128)(2,1)S(1)}, bf16[256,1024]{1,0:T(8,128)(2,1)S(1)}, u32[]{:S(2)}, u32[]{:S(2)}) collective-permute-start(bf16[256,1024]{1,0:T(8,128)(2,1)S(1)} %pad_maximum_fusion.refs_4_.refs_6_.refs_0_), channel_id=1, source_target_pairs={{0,8},{8,16},{1,9},{9,17},{2,10},{10,18},{3,11},{11,19},{4,12},{12... | collective-permute-start | bytes 1572872 | tf_op jit(solution)/shard_map/ppermute | solution.py:305
  14.3 1.3 %collective-permute-start.2 = (bf16[256,1024]{1,0:T(8,128)(2,1)S(1)}, bf16[256,1024]{1,0:T(8,128)(2,1)S(1)}, u32[]{:S(2)}, u32[]{:S(2)}) collective-permute-start(bf16[256,1024]{1,0:T(8,128)(2,1)S(1)} %pad_maximum_fusion.refs_4_.refs_6_.refs_0_), channel_id=1, source_target_pairs={{8,0},{16,8},{24,16},{9,1},{17,9},{25,17},{10,2},{18,10},{26,18},{... | collective-permute-start | bytes 1572872 | tf_op jit(solution)/shard_map/ppermute | solution.py:302
  15.7 8.4 %shard_map.73 = (f32[8,128]{1,0:T(8,128)S(1)}, f32[4,2,1024,384]{3,2,1,0:T(8,128)S(1)}, bf16[4,2,1024,256]{3,2,1,0:T(8,128)(2,1)}) custom-call(s32[2,4]{1,0:T(2,128)S(1)} %copy-done, s32[4]{0:T(128)S(1)} %copy-done.1, bf16[128,4096]{1,0:T(8,128)(2,1)S(1)} %get-tuple-element.92.refs_2_, bf16[128,4096]{1,0:T(8,128)(2,1)S(1)} %collective-permute-done.refs_3_, ...), custom_call_target="tpu_custom_call" | custom-call | flops 4294967296 | bytes 4194304 | tf_op jit(solution)/shard_map/pallas_call | solution.py:237
  24.1 1.3 %collective-permute-done.3.refs_2_ = bf16[256,1024]{1,0:T(8,128)(2,1)S(1)} collective-permute-done((bf16[256,1024]{1,0:T(8,128)(2,1)S(1)}, bf16[256,1024]{1,0:T(8,128)(2,1)S(1)}, u32[]{:S(2)}, u32[]{:S(2)}) %collective-permute-start.3) | collective-permute-done | bytes 524320 | tf_op jit(solution)/shard_map/ppermute | solution.py:305
  25.4 4.1 %collective-permute-done.2.refs_1_ = bf16[256,1024]{1,0:T(8,128)(2,1)S(1)} collective-permute-done((bf16[256,1024]{1,0:T(8,128)(2,1)S(1)}, bf16[256,1024]{1,0:T(8,128)(2,1)S(1)}, u32[]{:S(2)}, u32[]{:S(2)}) %collective-permute-start.2) | collective-permute-done | bytes 524320 | tf_op jit(solution)/shard_map/ppermute | solution.py:302
  29.5 1.3 %collective-permute-start.4 = (bf16[256,1024]{1,0:T(8,128)(2,1)S(1)}, bf16[256,1024]{1,0:T(8,128)(2,1)S(1)}, u32[]{:S(2)}, u32[]{:S(2)}) collective-permute-start(bf16[256,1024]{1,0:T(8,128)(2,1)S(1)} %collective-permute-done.2.refs_1_), channel_id=1, source_target_pairs={{8,0},{16,8},{9,1},{17,9},{10,2},{18,10},{11,3},{19,11},{12,4},{20... | collective-permute-start | bytes 1572872 | tf_op jit(solution)/shard_map/ppermute | solution.py:302
  30.8 0.7 collective-permute-start.5
  31.5 0.6 collective-permute-start.10
  32.6 3.0 %shard_map.75 = (f32[8,128]{1,0:T(8,128)S(1)}, f32[4,2,1024,384]{3,2,1,0:T(8,128)S(1)}) custom-call(s32[2,4]{1,0:T(2,128)S(1)} %copy-done, s32[4]{0:T(128)S(1)} %copy-done.1, bf16[4,2,1024,256]{3,2,1,0:T(8,128)(2,1)} %get-tuple-element.48.refs_2_, bf16[256,1024]{1,0:T(8,128)(2,1)S(1)} %collective-permute-done.6.refs_3_.refs_5_, ...), custom_call_target="tpu_custom_call", output_to_operand_aliasing={{1}: (8, {})} | custom-call | flops 4294967296 | bytes 4194304 | tf_op jit(solution)/shard_map/pallas_call | solution.py:237
  35.7 8.1 %collective-permute-done.4.refs_3_ = bf16[256,1024]{1,0:T(8,128)(2,1)S(1)} collective-permute-done((bf16[256,1024]{1,0:T(8,128)(2,1)S(1)}, bf16[256,1024]{1,0:T(8,128)(2,1)S(1)}, u32[]{:S(2)}, u32[]{:S(2)}) %collective-permute-start.4) | collective-permute-done | bytes 524320 | tf_op jit(solution)/shard_map/ppermute | solution.py:302
  44.4 0.6 collective-permute-start.13
  45.0 1.3 %collective-permute-start.8 = (bf16[256,1024]{1,0:T(8,128)(2,1)S(1)}, bf16[256,1024]{1,0:T(8,128)(2,1)S(1)}, u32[]{:S(2)}, u32[]{:S(2)}) collective-permute-start(bf16[256,1024]{1,0:T(8,128)(2,1)S(1)} %collective-permute-done.4.refs_3_), channel_id=1, source_target_pairs={{8,0},{9,1},{10,2},{11,3},{12,4},{13,5},{14,6},{15,7}} | collective-permute-start | bytes 1572872 | tf_op jit(solution)/shard_map/ppermute | solution.py:302
  46.3 1.6 %collective-permute-start.12 = (bf16[256,1024]{1,0:T(8,128)(2,1)S(1)}, bf16[256,1024]{1,0:T(8,128)(2,1)S(1)}, u32[]{:S(2)}, u32[]{:S(2)}) collective-permute-start(bf16[256,1024]{1,0:T(8,128)(2,1)S(1)} %pad_maximum_fusion.2), channel_id=1, source_target_pairs={{0,4},{1,5},{2,6},{3,7},{4,0},{5,1},{6,2},{7,3},{8,12},{9,13},{10,... | collective-permute-start | bytes 1572872 | tf_op jit(solution)/shard_map/ppermute | solution.py:276
  47.9 9.0 %shard_map.77 = (f32[8,128]{1,0:T(8,128)S(1)}, f32[4,2,1024,384]{3,2,1,0:T(8,128)S(1)}) custom-call(s32[2,4]{1,0:T(2,128)S(1)} %copy-done, s32[4]{0:T(128)S(1)} %copy-done.1, bf16[4,2,1024,256]{3,2,1,0:T(8,128)(2,1)} %get-tuple-element.48.refs_2_, bf16[256,1024]{1,0:T(8,128)(2,1)S(1)} %collective-permute-done.9.refs_3_.refs_5_, ...), custom_call_target="tpu_custom_call", output_to_operand_aliasing={{1}: (8, {})} | custom-call | flops 4294967296 | bytes 4194304 | tf_op jit(solution)/shard_map/pallas_call | solution.py:237
  56.9 3.0 %collective-permute-done.8.refs_5_ = bf16[256,1024]{1,0:T(8,128)(2,1)S(1)} collective-permute-done((bf16[256,1024]{1,0:T(8,128)(2,1)S(1)}, bf16[256,1024]{1,0:T(8,128)(2,1)S(1)}, u32[]{:S(2)}, u32[]{:S(2)}) %collective-permute-start.8) | collective-permute-done | bytes 524320 | tf_op jit(solution)/shard_map/ppermute | solution.py:302
  59.9 0.8 shard_map.78
  60.7 1.5 %collective-permute-start.15 = (bf16[256,1024]{1,0:T(8,128)(2,1)S(1)}, bf16[256,1024]{1,0:T(8,128)(2,1)S(1)}, u32[]{:S(2)}, u32[]{:S(2)}) collective-permute-start(bf16[256,1024]{1,0:T(8,128)(2,1)S(1)} %get-tuple-element.78.refs_5_.refs_8_), channel_id=1, source_target_pairs={{0,4},{1,5},{2,6},{3,7},{4,0},{5,1},{6,2},{7,3},{8,12},{9,13},{10,... | collective-permute-start | bytes 1572872 | tf_op jit(solution)/shard_map/ppermute | solution.py:276
  62.2 1.5 %collective-permute-start.11 = (bf16[256,1024]{1,0:T(8,128)(2,1)S(1)}, bf16[256,1024]{1,0:T(8,128)(2,1)S(1)}, u32[]{:S(2)}, u32[]{:S(2)}) collective-permute-start(bf16[256,1024]{1,0:T(8,128)(2,1)S(1)} %get-tuple-element.78.refs_5_.refs_8_), channel_id=1, source_target_pairs={{0,2},{1,3},{2,0},{3,1},{4,6},{5,7},{6,4},{7,5},{8,10},{9,11},{10,... | collective-permute-start | bytes 1572872 | tf_op jit(solution)/shard_map/ppermute | solution.py:273
  63.7 6.1 %shard_map.79 = (f32[8,128]{1,0:T(8,128)S(1)}, f32[4,2,1024,384]{3,2,1,0:T(8,128)S(1)}) custom-call(s32[2,4]{1,0:T(2,128)S(1)} %copy-done, s32[4]{0:T(128)S(1)} %copy-done.1, bf16[4,2,1024,256]{3,2,1,0:T(8,128)(2,1)} %get-tuple-element.48.refs_2_, bf16[256,1024]{1,0:T(8,128)(2,1)S(1)} %collective-permute-done.12.refs_3_.refs_6_, ...), custom_call_target="tpu_custom_call", output_to_operand_aliasing={{1}: (10, {})} | custom-call | flops 6442450944 | bytes 4194304 | tf_op jit(solution)/shard_map/pallas_call | solution.py:237
  70.3 1.6 %collective-permute-start.16 = (bf16[128,1024]{1,0:T(8,128)(2,1)S(1)}, bf16[128,1024]{1,0:T(8,128)(2,1)S(1)}, u32[]{:S(2)}, u32[]{:S(2)}) collective-permute-start(bf16[128,1024]{1,0:T(8,128)(2,1)S(1)} %slice.34), channel_id=1, source_target_pairs={{0,2},{1,3},{2,0},{3,1},{4,6},{5,7},{6,4},{7,5},{8,10},{9,11},{10,... | collective-permute-start | bytes 786440 | tf_op jit(solution)/shard_map/ppermute | solution.py:273
  71.9 2.3 %collective-permute-done.11.refs_3_.refs_5_ = bf16[256,1024]{1,0:T(8,128)(2,1)S(1)} collective-permute-done((bf16[256,1024]{1,0:T(8,128)(2,1)S(1)}, bf16[256,1024]{1,0:T(8,128)(2,1)S(1)}, u32[]{:S(2)}, u32[]{:S(2)}) %collective-permute-start.11) | collective-permute-done | bytes 524320 | tf_op jit(solution)/shard_map/ppermute | solution.py:273
  74.2 3.7 %collective-permute-start.14 = (bf16[128,1024]{1,0:T(8,128)(2,1)S(1)}, bf16[128,1024]{1,0:T(8,128)(2,1)S(1)}, u32[]{:S(2)}, u32[]{:S(2)}) collective-permute-start(bf16[128,1024]{1,0:T(8,128)(2,1)S(1)} %slice.30), channel_id=1, source_target_pairs={{0,4},{1,5},{2,6},{3,7},{4,0},{5,1},{6,2},{7,3},{8,12},{9,13},{10,... | collective-permute-start | bytes 786440 | tf_op jit(solution)/shard_map/ppermute | solution.py:276
  78.0 8.5 %shard_map.80 = (f32[8,128]{1,0:T(8,128)S(1)}, f32[4,2,1024,384]{3,2,1,0:T(8,128)S(1)}) custom-call(s32[2,4]{1,0:T(2,128)S(1)} %copy-done, s32[4]{0:T(128)S(1)} %copy-done.1, bf16[4,2,1024,256]{3,2,1,0:T(8,128)(2,1)} %get-tuple-element.48.refs_2_, bf16[256,1024]{1,0:T(8,128)(2,1)S(1)} %collective-permute-done.11.refs_3_.refs_5_, ...), custom_call_target="tpu_custom_call", output_to_operand_aliasing={{1}: (8, {})} | custom-call | flops 4294967296 | bytes 4194304 | tf_op jit(solution)/shard_map/pallas_call | solution.py:237
  86.5 6.5 %shard_map.81 = (bf16[128,4096]{1,0:T(8,128)(2,1)S(1)}, bf16[128,4096]{1,0:T(8,128)(2,1)S(1)}, f32[4,2,1024,384]{3,2,1,0:T(8,128)S(1)}) custom-call(s32[2,4]{1,0:T(2,128)S(1)} %copy-done, s32[4]{0:T(128)S(1)} %copy-done.1, bf16[4,2,1024,256]{3,2,1,0:T(8,128)(2,1)} %get-tuple-element.48.refs_2_, ...), custom_call_target="tpu_custom_call", output_to_operand_aliasing={{2}: (8, {})} | custom-call | flops 2147483648 | bytes 4194304 | tf_op jit(solution)/shard_map/pallas_call | solution.py:237
  93.1 2.6 %collective-permute-done.17 = bf16[128,4096]{1,0:T(8,128)(2,1)S(1)} collective-permute-done((bf16[128,4096]{1,0:T(8,128)(2,1)S(1)}, bf16[128,4096]{1,0:T(8,128)(2,1)S(1)}, u32[]{:S(2)}, u32[]{:S(2)}) %collective-permute-start.17) | collective-permute-done | bytes 1048608 | tf_op jit(solution)/shard_map/ppermute | solution.py:270
  95.7 1.8 %maximum_select_fusion = bf16[128,8192]{1,0:T(8,128)(2,1)} fusion(bf16[128,4096]{1,0:T(8,128)(2,1)S(1)} %collective-permute-done.17, bf16[128,4096]{1,0:T(8,128)(2,1)S(1)} %get-tuple-element.89, pred[]{:T(512)S(6)} %eq.3), kind=kLoop, calls=%fused_computation | loop fusion | flops 9437184 | bytes 4194305 | tf_op jit(solution)/shard_map/jit(_where)/select_n | solution.py:356
  (35 shorter events, 2.5 us)
Async XLA Ops:
  0.0 2.3 %copy-start.2 = (bf16[128,1024]{1,0:T(8,128)(2,1)S(1)}, bf16[128,1024]{1,0:T(8,128)(2,1)}, u32[]{:S(2)}) copy-start(bf16[128,1024]{1,0:T(8,128)(2,1)} %param.9) | copy-start | bytes 786436
  1.7 13.9 %copy-start = (s32[2,4]{1,0:T(2,128)S(1)}, s32[2,4]{1,0:T(2,128)}, u32[]{:S(2)}) copy-start(s32[2,4]{1,0:T(2,128)} %refs_0_.11) | copy-start | bytes 100
  1.7 13.9 %copy-start.1 = (s32[4]{0:T(128)S(1)}, s32[4]{0:T(128)}, u32[]{:S(2)}) copy-start(s32[4]{0:T(128)} %refs_1_.11) | copy-start | bytes 52
  1.7 13.9 %collective-permute-start = (bf16[128,4096]{1,0:T(8,128)(2,1)S(1)}, bf16[128,4096]{1,0:T(8,128)(2,1)S(1)}, u32[]{:S(2)}, u32[]{:S(2)}) collective-permute-start(bf16[128,4096]{1,0:T(8,128)(2,1)S(1)} %get-tuple-element.91), channel_id=1, source_target_pairs={{0,1},{1,0},{2,3},{3,2},{4,5},{5,4},{6,7},{7,6},{8,9},{9,8},{10,11... | collective-permute-start | bytes 3145736 | tf_op jit(solution)/shard_map/ppermute | solution.py:270
  4.5 2.0 %collective-permute-start.1 = (bf16[256,1024]{1,0:T(8,128)(2,1)S(1)}, bf16[256,1024]{1,0:T(8,128)(2,1)S(1)}, u32[]{:S(2)}, u32[]{:S(2)}) collective-permute-start(bf16[256,1024]{1,0:T(8,128)(2,1)S(1)} %maximum_maximum_fusion), channel_id=1, source_target_pairs={{0,1},{1,0},{2,3},{3,2},{4,5},{5,4},{6,7},{7,6},{8,9},{9,8},{10,11... | collective-permute-start | bytes 1572872 | tf_op jit(solution)/shard_map/ppermute | solution.py:270
  6.6 25.5 %collective-permute-start.7 = (bf16[256,1024]{1,0:T(8,128)(2,1)S(1)}, bf16[256,1024]{1,0:T(8,128)(2,1)S(1)}, u32[]{:S(2)}, u32[]{:S(2)}) collective-permute-start(bf16[256,1024]{1,0:T(8,128)(2,1)S(1)} %pad_maximum_fusion.refs_4_.refs_6_.refs_0_), channel_id=1, source_target_pairs={{0,4},{1,5},{2,6},{3,7},{4,0},{5,1},{6,2},{7,3},{8,12},{9,13},{10,... | collective-permute-start | bytes 1572872 | tf_op jit(solution)/shard_map/ppermute | solution.py:276
  9.3 23.3 %collective-permute-start.6 = (bf16[256,1024]{1,0:T(8,128)(2,1)S(1)}, bf16[256,1024]{1,0:T(8,128)(2,1)S(1)}, u32[]{:S(2)}, u32[]{:S(2)}) collective-permute-start(bf16[256,1024]{1,0:T(8,128)(2,1)S(1)} %pad_maximum_fusion.refs_4_.refs_6_.refs_0_), channel_id=1, source_target_pairs={{0,2},{1,3},{2,0},{3,1},{4,6},{5,7},{6,4},{7,5},{8,10},{9,11},{10,... | collective-permute-start | bytes 1572872 | tf_op jit(solution)/shard_map/ppermute | solution.py:273
  10.8 14.6 %collective-permute-start.3 = (bf16[256,1024]{1,0:T(8,128)(2,1)S(1)}, bf16[256,1024]{1,0:T(8,128)(2,1)S(1)}, u32[]{:S(2)}, u32[]{:S(2)}) collective-permute-start(bf16[256,1024]{1,0:T(8,128)(2,1)S(1)} %pad_maximum_fusion.refs_4_.refs_6_.refs_0_), channel_id=1, source_target_pairs={{0,8},{8,16},{1,9},{9,17},{2,10},{10,18},{3,11},{11,19},{4,12},{12... | collective-permute-start | bytes 1572872 | tf_op jit(solution)/shard_map/ppermute | solution.py:305
  14.3 15.2 %collective-permute-start.2 = (bf16[256,1024]{1,0:T(8,128)(2,1)S(1)}, bf16[256,1024]{1,0:T(8,128)(2,1)S(1)}, u32[]{:S(2)}, u32[]{:S(2)}) collective-permute-start(bf16[256,1024]{1,0:T(8,128)(2,1)S(1)} %pad_maximum_fusion.refs_4_.refs_6_.refs_0_), channel_id=1, source_target_pairs={{8,0},{16,8},{24,16},{9,1},{17,9},{25,17},{10,2},{18,10},{26,18},{... | collective-permute-start | bytes 1572872 | tf_op jit(solution)/shard_map/ppermute | solution.py:302
  29.5 14.3 %collective-permute-start.4 = (bf16[256,1024]{1,0:T(8,128)(2,1)S(1)}, bf16[256,1024]{1,0:T(8,128)(2,1)S(1)}, u32[]{:S(2)}, u32[]{:S(2)}) collective-permute-start(bf16[256,1024]{1,0:T(8,128)(2,1)S(1)} %collective-permute-done.2.refs_1_), channel_id=1, source_target_pairs={{8,0},{16,8},{9,1},{17,9},{10,2},{18,10},{11,3},{19,11},{12,4},{20... | collective-permute-start | bytes 1572872 | tf_op jit(solution)/shard_map/ppermute | solution.py:302
  30.8 13.0 %collective-permute-start.5 = (bf16[256,1024]{1,0:T(8,128)(2,1)S(1)}, bf16[256,1024]{1,0:T(8,128)(2,1)S(1)}, u32[]{:S(2)}, u32[]{:S(2)}) collective-permute-start(bf16[256,1024]{1,0:T(8,128)(2,1)S(1)} %collective-permute-done.3.refs_2_), channel_id=1, source_target_pairs={{8,16},{9,17},{10,18},{11,19},{12,20},{13,21},{14,22},{15,23}} | collective-permute-start | bytes 1572872 | tf_op jit(solution)/shard_map/ppermute | solution.py:305
  31.5 12.5 %collective-permute-start.10 = (bf16[256,1024]{1,0:T(8,128)(2,1)S(1)}, bf16[256,1024]{1,0:T(8,128)(2,1)S(1)}, u32[]{:S(2)}, u32[]{:S(2)}) collective-permute-start(bf16[256,1024]{1,0:T(8,128)(2,1)S(1)} %pad_maximum_fusion.1.refs_5_.refs_7_), channel_id=1, source_target_pairs={{0,4},{1,5},{2,6},{3,7},{4,0},{5,1},{6,2},{7,3},{8,12},{9,13},{10,... | collective-permute-start | bytes 1572872 | tf_op jit(solution)/shard_map/ppermute | solution.py:276
  32.1 12.2 %collective-permute-start.9 = (bf16[256,1024]{1,0:T(8,128)(2,1)S(1)}, bf16[256,1024]{1,0:T(8,128)(2,1)S(1)}, u32[]{:S(2)}, u32[]{:S(2)}) collective-permute-start(bf16[256,1024]{1,0:T(8,128)(2,1)S(1)} %pad_maximum_fusion.1.refs_5_.refs_7_), channel_id=1, source_target_pairs={{0,2},{1,3},{2,0},{3,1},{4,6},{5,7},{6,4},{7,5},{8,10},{9,11},{10,... | collective-permute-start | bytes 1572872 | tf_op jit(solution)/shard_map/ppermute | solution.py:273
  44.4 19.3 %collective-permute-start.13 = (bf16[256,1024]{1,0:T(8,128)(2,1)S(1)}, bf16[256,1024]{1,0:T(8,128)(2,1)S(1)}, u32[]{:S(2)}, u32[]{:S(2)}) collective-permute-start(bf16[256,1024]{1,0:T(8,128)(2,1)S(1)} %pad_maximum_fusion.3), channel_id=1, source_target_pairs={{0,2},{1,3},{2,0},{3,1},{4,6},{5,7},{6,4},{7,5},{8,10},{9,11},{10,... | collective-permute-start | bytes 1572872 | tf_op jit(solution)/shard_map/ppermute | solution.py:273
  45.0 14.9 %collective-permute-start.8 = (bf16[256,1024]{1,0:T(8,128)(2,1)S(1)}, bf16[256,1024]{1,0:T(8,128)(2,1)S(1)}, u32[]{:S(2)}, u32[]{:S(2)}) collective-permute-start(bf16[256,1024]{1,0:T(8,128)(2,1)S(1)} %collective-permute-done.4.refs_3_), channel_id=1, source_target_pairs={{8,0},{9,1},{10,2},{11,3},{12,4},{13,5},{14,6},{15,7}} | collective-permute-start | bytes 1572872 | tf_op jit(solution)/shard_map/ppermute | solution.py:302
  46.3 17.4 %collective-permute-start.12 = (bf16[256,1024]{1,0:T(8,128)(2,1)S(1)}, bf16[256,1024]{1,0:T(8,128)(2,1)S(1)}, u32[]{:S(2)}, u32[]{:S(2)}) collective-permute-start(bf16[256,1024]{1,0:T(8,128)(2,1)S(1)} %pad_maximum_fusion.2), channel_id=1, source_target_pairs={{0,4},{1,5},{2,6},{3,7},{4,0},{5,1},{6,2},{7,3},{8,12},{9,13},{10,... | collective-permute-start | bytes 1572872 | tf_op jit(solution)/shard_map/ppermute | solution.py:276
  60.7 9.6 %collective-permute-start.15 = (bf16[256,1024]{1,0:T(8,128)(2,1)S(1)}, bf16[256,1024]{1,0:T(8,128)(2,1)S(1)}, u32[]{:S(2)}, u32[]{:S(2)}) collective-permute-start(bf16[256,1024]{1,0:T(8,128)(2,1)S(1)} %get-tuple-element.78.refs_5_.refs_8_), channel_id=1, source_target_pairs={{0,4},{1,5},{2,6},{3,7},{4,0},{5,1},{6,2},{7,3},{8,12},{9,13},{10,... | collective-permute-start | bytes 1572872 | tf_op jit(solution)/shard_map/ppermute | solution.py:276
  62.2 12.0 %collective-permute-start.11 = (bf16[256,1024]{1,0:T(8,128)(2,1)S(1)}, bf16[256,1024]{1,0:T(8,128)(2,1)S(1)}, u32[]{:S(2)}, u32[]{:S(2)}) collective-permute-start(bf16[256,1024]{1,0:T(8,128)(2,1)S(1)} %get-tuple-element.78.refs_5_.refs_8_), channel_id=1, source_target_pairs={{0,2},{1,3},{2,0},{3,1},{4,6},{5,7},{6,4},{7,5},{8,10},{9,11},{10,... | collective-permute-start | bytes 1572872 | tf_op jit(solution)/shard_map/ppermute | solution.py:273
  70.3 16.1 %collective-permute-start.16 = (bf16[128,1024]{1,0:T(8,128)(2,1)S(1)}, bf16[128,1024]{1,0:T(8,128)(2,1)S(1)}, u32[]{:S(2)}, u32[]{:S(2)}) collective-permute-start(bf16[128,1024]{1,0:T(8,128)(2,1)S(1)} %slice.34), channel_id=1, source_target_pairs={{0,2},{1,3},{2,0},{3,1},{4,6},{5,7},{6,4},{7,5},{8,10},{9,11},{10,... | collective-permute-start | bytes 786440 | tf_op jit(solution)/shard_map/ppermute | solution.py:273
  74.2 12.2 %collective-permute-start.14 = (bf16[128,1024]{1,0:T(8,128)(2,1)S(1)}, bf16[128,1024]{1,0:T(8,128)(2,1)S(1)}, u32[]{:S(2)}, u32[]{:S(2)}) collective-permute-start(bf16[128,1024]{1,0:T(8,128)(2,1)S(1)} %slice.30), channel_id=1, source_target_pairs={{0,4},{1,5},{2,6},{3,7},{4,0},{5,1},{6,2},{7,3},{8,12},{9,13},{10,... | collective-permute-start | bytes 786440 | tf_op jit(solution)/shard_map/ppermute | solution.py:276
  93.0 2.7 %collective-permute-start.17 = (bf16[128,4096]{1,0:T(8,128)(2,1)S(1)}, bf16[128,4096]{1,0:T(8,128)(2,1)S(1)}, u32[]{:S(2)}, u32[]{:S(2)}) collective-permute-start(bf16[128,4096]{1,0:T(8,128)(2,1)S(1)} %get-tuple-element.90), channel_id=1, source_target_pairs={{0,1},{1,0},{2,3},{3,2},{4,5},{5,4},{6,7},{7,6},{8,9},{9,8},{10,11... | collective-permute-start | bytes 3145736 | tf_op jit(solution)/shard_map/ppermute | solution.py:270

commit v7 on v6

--- a/solution.py
+++ b/solution.py
@@ -22,18 +22,17 @@
     refs = list(refs)
     take = lambda count: [refs.pop(0) for _ in range(count)]
     exp_ref, off_ref = take(2)
-    raw = take(2 if first else 1)
+    raw = take(2) if first else None
     key_refs = take(arrays)
     value_refs = take(arrays)
     head = pl.program_id(0)
     if not first:
-        take(2)
+        take(3)
     if last:
         outs = take(2)
     else:
         take(1)[0][...] = jnp.zeros((8, HD), jnp.float32)
-    (held,) = take(1)
-    qs = take(1)[0] if first else raw[0]
+    held, qs = take(2)
     stacked = GW * rows
 
     group = lax.axis_index("leaf")
@@ -55,8 +54,8 @@
                 q = q_ref[:, g * HD : (g + 1) * HD].astype(jnp.float32) * Q_SCALE
                 high = q.astype(jnp.bfloat16)
                 low = (q - high.astype(jnp.float32)).astype(jnp.bfloat16)
-                qs[0, s, g * rows : (g + 1) * rows, :HD] = high
-                qs[0, s, g * rows : (g + 1) * rows, HD:] = low
+                qs[head, s, g * rows : (g + 1) * rows, :HD] = high
+                qs[head, s, g * rows : (g + 1) * rows, HD:] = low
 
     def step(members, limits, masked, fresh):
         width = len(members) * rows
@@ -70,7 +69,7 @@
 
         def score(s, here):
             return lax.dot_general(
-                qs[0, s, here, :], keys, (((1,), (1,)), ((), ())), preferred_element_type=jnp.float32
+                qs[head, s, here, :], keys, (((1,), (1,)), ((), ())), preferred_element_type=jnp.float32
             )
 
         def bias_of(s):
@@ -144,58 +143,89 @@
 WHOLE = pl.BlockSpec(memory_space=pltpu.VMEM)
 
 
+def in_vmem(array):
+    return pltpu.with_memory_space_constraint(array, pltpu.VMEM)
+
+
 def fence(state, *values):
     mark, held, prepared = state
     *values, mark = lax.optimization_barrier((*values, mark))
 
-    def kernel(mark_ref, held_ref, out_ref, held_out_ref):
-        out_ref[...] = mark_ref[...]
-
-    mark, held = pl.pallas_call(
+    def kernel(mark_ref, *refs):
+        refs[2][...] = mark_ref[...]
+
+    state[:] = pl.pallas_call(
         kernel,
-        in_specs=[WHOLE, WHOLE],
-        out_specs=[WHOLE, WHOLE],
-        out_shape=[jax.ShapeDtypeStruct(mark.shape, mark.dtype), pltpu.VMEM(held.shape, held.dtype)],
-        input_output_aliases={1: 1},
+        in_specs=[WHOLE] * 3,
+        out_specs=[WHOLE] * 3,
+        out_shape=[
+            jax.ShapeDtypeStruct(mark.shape, mark.dtype),
+            pltpu.VMEM(held.shape, held.dtype),
+            pltpu.VMEM(prepared.shape, prepared.dtype),
+        ],
+        input_output_aliases={1: 1, 2: 2},
         compiler_params=pltpu.CompilerParams(vmem_limit_bytes=4 * 2**20),
-    )(mark, pltpu.with_memory_space_constraint(held, pltpu.VMEM))
-    state[:] = [mark, held, prepared]
+    )(mark, in_vmem(held), in_vmem(prepared))
     return values
 
 
-def pick(state, table, owners, arrays):
+def pick(state, table, leaves, arrays):
     mark, held, prepared = state
     count = len(arrays)
 
     def kernel(table_ref, mark_ref, *refs):
-        out_ref, mark_out_ref, _, sem = refs[count + 1 :]
+        out_ref, mark_out_ref, _, _, sem = refs[count + 2 :]
         group = lax.axis_index("leaf")
         parent = table_ref[0, group]
         mark_out_ref[...] = mark_ref[...]
-        for owner, ref in zip(owners, refs):
-
-            @pl.when(parent == group + owner)
+        for ahead, ref in enumerate(refs[:count]):
+
+            @pl.when(parent == lax.rem(group + ahead, leaves))
             def _():
                 copy = pltpu.make_async_copy(ref, out_ref, sem)
                 copy.start()
                 copy.wait()
 
     anywhere = pl.BlockSpec(memory_space=pl.ANY)
-    picked, mark, held = pl.pallas_call(
+    picked, *state[:] = pl.pallas_call(
         kernel,
-        in_specs=[pl.BlockSpec(memory_space=pltpu.SMEM), WHOLE] + [anywhere] * count + [WHOLE],
-        out_specs=[anywhere, WHOLE, WHOLE],
+        in_specs=[pl.BlockSpec(memory_space=pltpu.SMEM), WHOLE] + [anywhere] * count + [WHOLE] * 2,
+        out_specs=[anywhere, WHOLE, WHOLE, WHOLE],
         out_shape=[
             jax.ShapeDtypeStruct(arrays[0].shape, arrays[0].dtype),
             jax.ShapeDtypeStruct(mark.shape, mark.dtype),
             pltpu.VMEM(held.shape, held.dtype),
+            pltpu.VMEM(prepared.shape, prepared.dtype),
         ],
         scratch_shapes=[pltpu.SemaphoreType.DMA(())],
-        input_output_aliases={count + 2: 2},
+        input_output_aliases={count + 2: 2, count + 3: 3},
         compiler_params=pltpu.CompilerParams(vmem_limit_bytes=4 * 2**20),
-    )(table, mark, *arrays, pltpu.with_memory_space_constraint(held, pltpu.VMEM))
-    state[:] = [mark, held, prepared]
+    )(table, mark, *arrays, in_vmem(held), in_vmem(prepared))
     return picked
+
+
+def assemble(mine, got):
+    rows, half = mine.shape
+
+    def kernel(mine_ref, got_ref, out_ref, sems):
+        core = lax.rem(lax.axis_index("ctx"), 2)
+        copies = []
+        for i, (ref, place) in enumerate(((mine_ref, core), (got_ref, 1 - core))):
+            columns = pl.ds(pl.multiple_of(place * half, half), half)
+            copies.append(pltpu.make_async_copy(ref, out_ref.at[:, columns], sems.at[i]))
+            copies[i].start()
+        for copy in copies:
+            copy.wait()
+
+    anywhere = pl.BlockSpec(memory_space=pl.ANY)
+    return pl.pallas_call(
+        kernel,
+        in_specs=[anywhere] * 2,
+        out_specs=anywhere,
+        out_shape=jax.ShapeDtypeStruct((rows, 2 * half), mine.dtype),
+        scratch_shapes=[pltpu.SemaphoreType.DMA((2,))],
+        compiler_params=pltpu.CompilerParams(vmem_limit_bytes=4 * 2**20),
+    )(mine, got)
 
 
 def attend(ny, rows, tables, arrays, groups, queries, state, last):
@@ -203,7 +233,6 @@
     first = state is None
     smem = pl.BlockSpec(memory_space=pltpu.SMEM)
     row_spec = pl.BlockSpec((rows, GW * HD), lambda h: (0, h))
-    q_spec = pl.BlockSpec((1, 2, stacked, 2 * HD), lambda h: (h, 0, 0, 0))
     operands = [*tables]
     specs = [smem, smem]
     if first:
@@ -211,8 +240,6 @@
         specs += [row_spec, row_spec]
     else:
         mark, state, prepared = state
-        operands.append(pltpu.with_memory_space_constraint(prepared, pltpu.HBM))
-        specs.append(q_spec)
     for shift in (0, HALF_KV):
         for array in arrays:
             operands.append(array)
@@ -225,14 +252,12 @@
         out_shape = [jax.ShapeDtypeStruct((8, HD), jnp.float32)]
         out_specs = [pl.BlockSpec((8, HD), lambda h: (0, 0))]
     if not first:
-        aliases = {len(operands) + 1: len(out_shape)}
-        operands += [mark, pltpu.with_memory_space_constraint(state, pltpu.VMEM)]
-        specs += [pl.BlockSpec(memory_space=pl.ANY), WHOLE]
+        aliases = {len(operands) + 1 + i: len(out_shape) + i for i in range(2)}
+        operands += [mark, in_vmem(state), in_vmem(prepared)]
+        specs += [pl.BlockSpec(memory_space=pl.ANY), WHOLE, WHOLE]
     out_shape.append(pltpu.VMEM((HALF_KV, 2, stacked, 3 * HD), jnp.float32))
-    out_specs.append(WHOLE)
-    if first:
-        out_shape.append(pltpu.HBM((HALF_KV, 2, stacked, 2 * HD), jnp.bfloat16))
-        out_specs.append(q_spec)
+    out_shape.append(pltpu.VMEM((HALF_KV, 2, stacked, 2 * HD), jnp.bfloat16))
+    out_specs += [WHOLE, WHOLE]
     scores = HALF_KV * 2 * stacked * rows * sum(len(members) for members in groups)
     out = pl.pallas_call(
         functools.partial(attend_kernel, ny, rows, len(arrays), groups, first, last),
@@ -244,7 +269,7 @@
         compiler_params=pltpu.CompilerParams(vmem_limit_bytes=24 * 2**20),
         cost_estimate=pl.CostEstimate(flops=8 * scores * HD, bytes_accessed=4 * 2**20, transcendentals=scores),
     )(*operands)
-    return out[:2] if last else list(out) if first else [*out, prepared]
+    return out[:2] if last else list(out)
 
 
 def on_device(queries, seg_keys, seg_values, root_keys, root_values, expansion, root_offsets):
@@ -281,7 +306,9 @@
 
     own_mine, own_other = packed(seg_keys, seg_values)
     root_mine, root_other = packed(root_keys, root_values)
-    got = to_core(jnp.concatenate([own_other, root_other], axis=0))
+    sent = jnp.concatenate([own_other, root_other], axis=0)
+    got = to_core(sent)
+    queries, _ = lax.optimization_barrier((queries, sent))
     q_mine, q_other = halves(queries)
     q_pair = (q_mine, to_core(q_other))
     own = jnp.concatenate([own_mine, got[:rows]], axis=0)
@@ -296,54 +323,45 @@
         *values, state[0] = lax.optimization_barrier((*values, state[0]))
         return values
 
-    choices = []
-
-    def hop(step, down, up):
-        down = lax.ppermute(down, "leaf", [(i, i - 1) for i in range(1, leaves - step + 1)])
-        choices.append((step, down))
-        if step < leaves - 1:
-            up = lax.ppermute(up, "leaf", [(i, i + 1) for i in range(step - 1, leaves - 2)])
-            choices.append((-step, up))
-        return down, up
-
-    down, up = hop(1, own, own)
+    def hop(step, rows_held):
+        pairs = [(i, (i - 1) % leaves) for i in range(leaves)]
+        return lax.ppermute(rows_held, "leaf", pairs if step < leaves - 1 else pairs[1:])
+
+    ahead = [own]
+    if leaves > 1:
+        ahead.append(hop(1, own))
     own_x, own_y = to_x(own), [to_y(own, step) for step in steps]
     root_x, root_y = to_x(root), [to_y(root, step) for step in steps]
     state = run([own, root], (members(0, "own") + members(1, "root"),), q_pair, None, False)
-
-    if leaves > 2:
-        down, up = hop(2, *fence(state, down, up))
-    own_x, *own_y = after(state, own_x, *own_y)
 
     def near(kind, arrays):
         groups = [members(0, kind, 1) + members(1, kind, 0, 1)]
         groups += [members(step, kind, 0, step) for step in steps if step > 1]
         return run(arrays, tuple(groups), None, state, False)
 
+    if leaves > 2:
+        (held,) = fence(state, ahead[-1])
+        ahead[-1] = held
+        ahead.append(hop(2, held))
+    own_x, *own_y = after(state, own_x, *own_y)
+    own_far = [to_y(own_x, step) for step in steps]
     state = near("own", [own_x, *own_y])
     for step in range(3, leaves):
-        down, up = hop(step, *fence(state, down, up))
-    own_x, root_x, *pairs = after(state, own_x, root_x, *own_y, *root_y)
-    own_y, root_y = pairs[: ny - 1], pairs[ny - 1 :]
-    tops = [to_y(jnp.concatenate([own_x[:rows], root_x[:rows]], axis=0), step) for step in steps]
-    lows = [to_x(jnp.concatenate([a[rows:], b[rows:]], axis=0)) for a, b in zip(own_y, root_y)]
+        (held,) = fence(state, ahead[-1])
+        ahead[-1] = held
+        ahead.append(hop(step, held))
+    root_x, *root_y = after(state, root_x, *root_y)
+    root_far = [to_y(root_x, step) for step in steps]
     state = near("root", [root_x, *root_y])
 
-    owners, helds = zip(*choices)
-    parent_rows = pick(state, expansion, (0, *owners), (own, *after(state, *helds)))
+    parent_rows = pick(state, expansion, leaves, after(state, *ahead))
     (parent_rows,) = after(state, parent_rows)
     kin_x, kin_y = to_x(parent_rows), [to_y(parent_rows, step) for step in steps]
-    groups, arrays = [], []
-    for step, top, low in zip(steps, tops, lows):
-        at = len(arrays)
-        groups.append(
-            members(at, "own", 1, step, (0,))
-            + members(at, "root", 1, step, (0,), 1)
-            + members(at + 1, "own", 1, step, (1,))
-            + members(at + 1, "root", 1, step, (1,), 1)
-        )
-        arrays += [top, low]
-    state = run([*arrays, parent_rows], (*groups, members(len(arrays), "kin")), None, state, False)
+    far = [members(i, "own", 1, i + 1) + members(ny - 1 + i, "root", 1, i + 1) for i in range(ny - 1)]
+    far.append(members(2 * ny - 2, "kin"))
+    if ny == 2:
+        far = [far[0] + far[1]]
+    state = run([*own_far, *root_far, parent_rows], tuple(far), None, state, False)
 
     (kin_x,) = after(state, kin_x)
     tops = [to_y(kin_x[:rows], step) for step in steps]
@@ -352,12 +370,7 @@
     state = run([kin_x, *kin_y], tuple(groups), None, state, False)
     groups = [members(i, "kin", flips=(0,)) + members(len(tops) + i, "kin", flips=(1,)) for i in range(len(tops))]
     out_mine, out_other = run([*tops, *lows], tuple(groups), None, state, True)
-    out_got = to_core(out_other)
-    return jnp.where(
-        core == 0,
-        jnp.concatenate([out_mine, out_got], axis=1),
-        jnp.concatenate([out_got, out_mine], axis=1),
-    )
+    return assemble(out_mine, to_core(out_other))
 
 
 def solution(mesh):

time: 98 us -> 99 us (1.010)
  waiting for transfers between devices: 24.3 us -> 28.1 us
  Pallas kernels: 42.3 us -> 45.1 us
  starting transfers between devices: 24.6 us -> 22.4 us
  other arithmetic: 2.01 us -> 0.16 us
  local copies, waits for them, and re-layouts: 4.03 us -> 2.65 us
    ppermute x5 -> x6, waiting for transfers between devices: 0.65 us -> 10.7 us  [to_y(): lax.ppermute(array, 'ctx', [(index(x, y, k), index(x, y + step, k)) for x...]
    ppermute x5 -> x3, waiting for transfers between devices: 16.6 us -> 11.8 us  [hop(): lax.ppermute(rows_held, 'leaf', pairs if step < leaves - 1 else pairs[1:])]
    ppermute x5 -> x4, waiting for transfers between devices: 2.55 us -> 0.01 us  [to_x(): lax.ppermute(array, 'ctx', [(index(x, y, k), index(x + 1, y, k)) for x, y...]
    ppermute x5 -> x6, starting transfers between devices: 10.2 us -> 8.24 us  [to_y(): lax.ppermute(array, 'ctx', [(index(x, y, k), index(x, y + step, k)) for x...]
    select_n x1 -> x0, other arithmetic: 1.8 us -> none  [on_device(): jnp.where(core == 0, jnp.concatenate([out_mine, out_got], axis=1), jnp.co...]
    dynamic_slice x1, local copies, waits for them, and re-layouts: 1.72 us -> 0.15 us  [halves(): lax.dynamic_slice_in_dim(array, (1 - core) * half, half, 1)]
    pallas_call x6, Pallas kernels: 41.5 us -> 42.9 us  [attend(): pl.pallas_call(functools.partial(attend_kernel, ny, rows, len(arrays), gr...]
    pallas_call x2 -> x3, Pallas kernels: 0.01 us -> 1.33 us  [the longest x1 1.33 us: assemble(): pl.pallas_call(kernel, in_specs=[anywhere] * 2, out_specs=anywhere, out_s...]
  transfers between devices with their start and end apart: 18 -> 16, of which waited for: 10 -> 6; matrix products, arithmetic and copies ran while one was open for 2% -> 0% of each run, Pallas kernels for 37% -> 38%
where the time goes in v7:
time: 99 us; the launch traced here: 98.8 us
  Pallas kernels  45.1 us (46%)
  waiting for transfers between devices  28.1 us (28%)
  starting transfers between devices  22.4 us (23%)
  local copies, waits for them, and re-layouts  2.65 us (3%)
    pallas_call x6, Pallas kernels, attend(): pl.pallas_call(functools.partial(attend_kernel, ny, rows, len(arrays), gr...  42.9 us
    ppermute x3, waiting for transfers between devices, hop(): lax.ppermute(rows_held, 'leaf', pairs if step < leaves - 1 else pairs[1:])  11.8 us
    ppermute x6, waiting for transfers between devices, to_y(): lax.ppermute(array, 'ctx', [(index(x, y, k), index(x, y + step, k)) for x...  10.7 us
    ppermute x3, starting transfers between devices, hop(): lax.ppermute(rows_held, 'leaf', pairs if step < leaves - 1 else pairs[1:])  9.16 us
    ppermute x6, starting transfers between devices, to_y(): lax.ppermute(array, 'ctx', [(index(x, y, k), index(x, y + step, k)) for x...  8.24 us
    ppermute x3, waiting for transfers between devices, to_core(): lax.ppermute(array, 'ctx', [(index(x, y, k), index(x, y, k + 1)) for x, y...  5.61 us
    ppermute x4, starting transfers between devices, to_x(): lax.ppermute(array, 'ctx', [(index(x, y, k), index(x + 1, y, k)) for x, y...  4.37 us
    dynamic_slice x2, local copies, waits for them, and re-layouts, halves(): lax.dynamic_slice_in_dim(array, core * half, half, 1)  2.42 us
  transfers between devices with their start and end apart: 16, of which 6 were waited for; matrix products, arithmetic and copies ran while one was open for 0% of the time, Pallas kernels for 38%

profile of v7, /device:TPU:0, one launch (start us, length us, event | category | flops | bytes accessed | tf_op | source)
XLA Modules:
  0.0 98.8 jit_solution(14027648527065852541)
XLA Ops:
  0.0 1.3 %constant_dynamic-slice_fusion.8 = (bf16[128,512]{1,0:T(8,128)(2,1)S(1)}, bf16[128,512]{1,0:T(8,128)(2,1)S(1)}, bf16[128,512]{1,0:T(8,128)(2,1)S(1)}, bf16[128,512]{1,0:T(8,128)(2,1)S(1)}) fusion(bf16[128,1024]{1,0:T(8,128)(2,1)} %param.9, s32[]{:T(128)S(6)} %select_n.8, s32[]{:T(128)S(6)} %select_n.9, bf16[128,1024]{1,0:T(8,128)(2,1)} %param.8), kind=kLoop, calls=%fused_computation.11 | loop fusion | bytes 1048584 | tf_op jit(solution)/shard_map/dynamic_slice | solution.py:285
  1.3 1.1 %constant_dynamic-slice_fusion = (bf16[128,512]{1,0:T(8,128)(2,1)S(1)}, bf16[128,512]{1,0:T(8,128)(2,1)S(1)}, bf16[128,512]{1,0:T(8,128)(2,1)S(1)}, bf16[128,512]{1,0:T(8,128)(2,1)S(1)}) fusion(bf16[128,1024]{1,0:T(8,128)(2,1)} %param.11, s32[]{:T(128)S(6)} %select_n.8, s32[]{:T(128)S(6)} %select_n.9, bf16[128,1024]{1,0:T(8,128)(2,1)} %param.10), kind=kLoop, calls=%fused_computation.3 | loop fusion | bytes 1048584 | tf_op jit(solution)/shard_map/dynamic_slice | solution.py:285
  2.5 0.1 constant_dynamic-slice_fusion.2
  2.7 0.5 collective-permute-start.2
  3.2 0.1 collective-permute-start
  3.3 3.0 %collective-permute-done = bf16[256,1024]{1,0:T(8,128)(2,1)S(1)} collective-permute-done((bf16[256,1024]{1,0:T(8,128)(2,1)S(1)}, bf16[256,1024]{1,0:T(8,128)(2,1)S(1)}, u32[]{:S(2)}, u32[]{:S(2)}) %collective-permute-start) | collective-permute-done | bytes 524320 | tf_op jit(solution)/shard_map/ppermute | solution.py:295
  6.3 3.0 %collective-permute-start.5 = (bf16[256,1024]{1,0:T(8,128)(2,1)S(1)}, bf16[256,1024]{1,0:T(8,128)(2,1)S(1)}, u32[]{:S(2)}, u32[]{:S(2)}) collective-permute-start(bf16[256,1024]{1,0:T(8,128)(2,1)S(1)} %pad_maximum_fusion.refs_4_.refs_6_.refs_0_), channel_id=1, source_target_pairs={{0,4},{1,5},{2,6},{3,7},{4,0},{5,1},{6,2},{7,3},{8,12},{9,13},{10,... | collective-permute-start | bytes 1572872 | tf_op jit(solution)/shard_map/ppermute | solution.py:301
  9.3 1.5 %collective-permute-start.4 = (bf16[256,1024]{1,0:T(8,128)(2,1)S(1)}, bf16[256,1024]{1,0:T(8,128)(2,1)S(1)}, u32[]{:S(2)}, u32[]{:S(2)}) collective-permute-start(bf16[256,1024]{1,0:T(8,128)(2,1)S(1)} %pad_maximum_fusion.refs_4_.refs_6_.refs_0_), channel_id=1, source_target_pairs={{0,2},{1,3},{2,0},{3,1},{4,6},{5,7},{6,4},{7,5},{8,10},{9,11},{10,... | collective-permute-start | bytes 1572872 | tf_op jit(solution)/shard_map/ppermute | solution.py:298
  10.8 3.6 %collective-permute-start.1 = (bf16[256,1024]{1,0:T(8,128)(2,1)S(1)}, bf16[256,1024]{1,0:T(8,128)(2,1)S(1)}, u32[]{:S(2)}, u32[]{:S(2)}) collective-permute-start(bf16[256,1024]{1,0:T(8,128)(2,1)S(1)} %pad_maximum_fusion.refs_4_.refs_6_.refs_0_), channel_id=1, source_target_pairs={{0,24},{8,0},{16,8},{24,16},{1,25},{9,1},{17,9},{25,17},{2,26},{10... | collective-permute-start | bytes 1572872 | tf_op jit(solution)/shard_map/ppermute | solution.py:328
  14.5 7.8 %shard_map.73 = (f32[8,128]{1,0:T(8,128)S(1)}, f32[4,2,1024,384]{3,2,1,0:T(8,128)S(1)}, bf16[4,2,1024,256]{3,2,1,0:T(8,128)(2,1)S(1)}) custom-call(s32[2,4]{1,0:T(2,128)S(1)} %copy-done, s32[4]{0:T(128)S(1)} %copy-done.1, bf16[128,4096]{1,0:T(8,128)(2,1)S(1)} %get-tuple-element.100.refs_2_, bf16[128,4096]{1,0:T(8,128)(2,1)S(1)} %collective-permute-done.2.refs_3_, ...), custom_call_target="tpu_custom_call" | custom-call | flops 4294967296 | bytes 4194304 | tf_op jit(solution)/shard_map/pallas_call | solution.py:262
  22.3 3.0 %collective-permute-done.1.refs_1_ = bf16[256,1024]{1,0:T(8,128)(2,1)S(1)} collective-permute-done((bf16[256,1024]{1,0:T(8,128)(2,1)S(1)}, bf16[256,1024]{1,0:T(8,128)(2,1)S(1)}, u32[]{:S(2)}, u32[]{:S(2)}) %collective-permute-start.1) | collective-permute-done | bytes 524320 | tf_op jit(solution)/shard_map/ppermute | solution.py:328
  25.3 4.3 %collective-permute-start.3 = (bf16[256,1024]{1,0:T(8,128)(2,1)S(1)}, bf16[256,1024]{1,0:T(8,128)(2,1)S(1)}, u32[]{:S(2)}, u32[]{:S(2)}) collective-permute-start(bf16[256,1024]{1,0:T(8,128)(2,1)S(1)} %collective-permute-done.1.refs_1_), channel_id=1, source_target_pairs={{0,24},{8,0},{16,8},{24,16},{1,25},{9,1},{17,9},{25,17},{2,26},{10... | collective-permute-start | bytes 1572872 | tf_op jit(solution)/shard_map/ppermute | solution.py:328
  29.6 0.5 collective-permute-start.8
  30.1 0.5 collective-permute-start.7
  30.6 1.2 %shard_map.75 = (f32[8,128]{1,0:T(8,128)S(1)}, f32[4,2,1024,384]{3,2,1,0:T(8,128)S(1)}, bf16[4,2,1024,256]{3,2,1,0:T(8,128)(2,1)S(1)}) custom-call(s32[2,4]{1,0:T(2,128)S(1)} %copy-done, s32[4]{0:T(128)S(1)} %copy-done.1, bf16[256,1024]{1,0:T(8,128)(2,1)S(1)} %collective-permute-done.4.refs_2_.refs_4_, ...), custom_call_target="tpu_custom_call", output_to_operand_aliasing={{1}: (7, {}), {2}: (8, {})} | custom-call | flops 4294967296 | bytes 4194304 | tf_op jit(solution)/shard_map/pallas_call | solution.py:262
  31.9 7.7 %collective-permute-done.3.refs_2_ = bf16[256,1024]{1,0:T(8,128)(2,1)S(1)} collective-permute-done((bf16[256,1024]{1,0:T(8,128)(2,1)S(1)}, bf16[256,1024]{1,0:T(8,128)(2,1)S(1)}, u32[]{:S(2)}, u32[]{:S(2)}) %collective-permute-start.3) | collective-permute-done | bytes 524320 | tf_op jit(solution)/shard_map/ppermute | solution.py:328
  39.6 1.3 %collective-permute-start.6 = (bf16[256,1024]{1,0:T(8,128)(2,1)S(1)}, bf16[256,1024]{1,0:T(8,128)(2,1)S(1)}, u32[]{:S(2)}, u32[]{:S(2)}) collective-permute-start(bf16[256,1024]{1,0:T(8,128)(2,1)S(1)} %collective-permute-done.3.refs_2_), channel_id=1, source_target_pairs={{8,0},{16,8},{24,16},{9,1},{17,9},{25,17},{10,2},{18,10},{26,18},{... | collective-permute-start | bytes 1572872 | tf_op jit(solution)/shard_map/ppermute | solution.py:328
  40.9 1.6 %collective-permute-start.10 = (bf16[256,1024]{1,0:T(8,128)(2,1)S(1)}, bf16[256,1024]{1,0:T(8,128)(2,1)S(1)}, u32[]{:S(2)}, u32[]{:S(2)}) collective-permute-start(bf16[256,1024]{1,0:T(8,128)(2,1)S(1)} %collective-permute-done.4.refs_2_.refs_4_), channel_id=1, source_target_pairs={{0,4},{1,5},{2,6},{3,7},{4,0},{5,1},{6,2},{7,3},{8,12},{9,13},{10,... | collective-permute-start | bytes 1572872 | tf_op jit(solution)/shard_map/ppermute | solution.py:301
  42.5 1.1 %collective-permute-start.11 = (bf16[256,1024]{1,0:T(8,128)(2,1)S(1)}, bf16[256,1024]{1,0:T(8,128)(2,1)S(1)}, u32[]{:S(2)}, u32[]{:S(2)}) collective-permute-start(bf16[256,1024]{1,0:T(8,128)(2,1)S(1)} %collective-permute-done.7.refs_2_.refs_4_), channel_id=1, source_target_pairs={{0,4},{1,5},{2,6},{3,7},{4,0},{5,1},{6,2},{7,3},{8,12},{9,13},{10,... | collective-permute-start | bytes 1572872 | tf_op jit(solution)/shard_map/ppermute | solution.py:301
  43.5 8.5 %shard_map.77 = (f32[8,128]{1,0:T(8,128)S(1)}, f32[4,2,1024,384]{3,2,1,0:T(8,128)S(1)}, bf16[4,2,1024,256]{3,2,1,0:T(8,128)(2,1)S(1)}) custom-call(s32[2,4]{1,0:T(2,128)S(1)} %copy-done, s32[4]{0:T(128)S(1)} %copy-done.1, bf16[256,1024]{1,0:T(8,128)(2,1)S(1)} %collective-permute-done.7.refs_2_.refs_4_, ...), custom_call_target="tpu_custom_call", output_to_operand_aliasing={{1}: (7, {}), {2}: (8, {})} | custom-call | flops 4294967296 | bytes 4194304 | tf_op jit(solution)/shard_map/pallas_call | solution.py:262
  52.1 1.0 %collective-permute-done.6.refs_3_ = bf16[256,1024]{1,0:T(8,128)(2,1)S(1)} collective-permute-done((bf16[256,1024]{1,0:T(8,128)(2,1)S(1)}, bf16[256,1024]{1,0:T(8,128)(2,1)S(1)}, u32[]{:S(2)}, u32[]{:S(2)}) %collective-permute-start.6) | collective-permute-done | bytes 524320 | tf_op jit(solution)/shard_map/ppermute | solution.py:328
  53.1 0.8 shard_map.78
  53.9 1.7 %collective-permute-start.13 = (bf16[256,1024]{1,0:T(8,128)(2,1)S(1)}, bf16[256,1024]{1,0:T(8,128)(2,1)S(1)}, u32[]{:S(2)}, u32[]{:S(2)}) collective-permute-start(bf16[256,1024]{1,0:T(8,128)(2,1)S(1)} %get-tuple-element.85.refs_4_.refs_7_), channel_id=1, source_target_pairs={{0,4},{1,5},{2,6},{3,7},{4,0},{5,1},{6,2},{7,3},{8,12},{9,13},{10,... | collective-permute-start | bytes 1572872 | tf_op jit(solution)/shard_map/ppermute | solution.py:301
  55.5 0.8 collective-permute-start.9
  56.3 10.7 %collective-permute-done.11.refs_3_.refs_6_ = bf16[256,1024]{1,0:T(8,128)(2,1)S(1)} collective-permute-done((bf16[256,1024]{1,0:T(8,128)(2,1)S(1)}, bf16[256,1024]{1,0:T(8,128)(2,1)S(1)}, u32[]{:S(2)}, u32[]{:S(2)}) %collective-permute-start.11) | collective-permute-done | bytes 524320 | tf_op jit(solution)/shard_map/ppermute | solution.py:301
  67.1 11.5 %shard_map.79 = (f32[8,128]{1,0:T(8,128)S(1)}, f32[4,2,1024,384]{3,2,1,0:T(8,128)S(1)}, bf16[4,2,1024,256]{3,2,1,0:T(8,128)(2,1)S(1)}) custom-call(s32[2,4]{1,0:T(2,128)S(1)} %copy-done, s32[4]{0:T(128)S(1)} %copy-done.1, bf16[256,1024]{1,0:T(8,128)(2,1)S(1)} %collective-permute-done.10.refs_2_.refs_5_, ...), custom_call_target="tpu_custom_call", output_to_operand_aliasing={{1}: (9, {}), {2}: (10, {})} | custom-call | flops 6442450944 | bytes 4194304 | tf_op jit(solution)/shard_map/pallas_call | solution.py:262
  78.6 1.6 %collective-permute-start.14 = (bf16[128,1024]{1,0:T(8,128)(2,1)S(1)}, bf16[128,1024]{1,0:T(8,128)(2,1)S(1)}, u32[]{:S(2)}, u32[]{:S(2)}) collective-permute-start(bf16[128,1024]{1,0:T(8,128)(2,1)S(1)} %slice.18), channel_id=1, source_target_pairs={{0,2},{1,3},{2,0},{3,1},{4,6},{5,7},{6,4},{7,5},{8,10},{9,11},{10,... | collective-permute-start | bytes 786440 | tf_op jit(solution)/shard_map/ppermute | solution.py:298
  80.2 0.5 collective-permute-start.12
  80.6 8.0 %shard_map.80 = (f32[8,128]{1,0:T(8,128)S(1)}, f32[4,2,1024,384]{3,2,1,0:T(8,128)S(1)}, bf16[4,2,1024,256]{3,2,1,0:T(8,128)(2,1)S(1)}) custom-call(s32[2,4]{1,0:T(2,128)S(1)} %copy-done, s32[4]{0:T(128)S(1)} %copy-done.1, bf16[256,1024]{1,0:T(8,128)(2,1)S(1)} %collective-permute-done.9.refs_2_.refs_4_, ...), custom_call_target="tpu_custom_call", output_to_operand_aliasing={{1}: (7, {}), {2}: (8, {})} | custom-call | flops 4294967296 | bytes 4194304 | tf_op jit(solution)/shard_map/pallas_call | solution.py:262
  88.7 5.9 %shard_map.81 = (bf16[128,4096]{1,0:T(8,128)(2,1)S(1)}, bf16[128,4096]{1,0:T(8,128)(2,1)S(1)}, f32[4,2,1024,384]{3,2,1,0:T(8,128)S(1)}, bf16[4,2,1024,256]{3,2,1,0:T(8,128)(2,1)S(1)}) custom-call(s32[2,4]{1,0:T(2,128)S(1)} %copy-done, s32[4]{0:T(128)S(1)} %copy-done.1, ...), custom_call_target="tpu_custom_call", output_to_operand_aliasing={{2}: (7, {}), {3}: (8, {})} | custom-call | flops 2147483648 | bytes 4194304 | tf_op jit(solution)/shard_map/pallas_call | solution.py:262
  94.7 2.6 %collective-permute-done.15.got_ref = bf16[128,4096]{1,0:T(8,128)(2,1)S(1)} collective-permute-done((bf16[128,4096]{1,0:T(8,128)(2,1)S(1)}, bf16[128,4096]{1,0:T(8,128)(2,1)S(1)}, u32[]{:S(2)}, u32[]{:S(2)}) %collective-permute-start.15) | collective-permute-done | bytes 1048608 | tf_op jit(solution)/shard_map/ppermute | solution.py:295
  97.3 1.3 %shard_map.82 = bf16[128,8192]{1,0:T(8,128)(2,1)} custom-call(bf16[128,4096]{1,0:T(8,128)(2,1)S(1)} %get-tuple-element.97.mine_ref, bf16[128,4096]{1,0:T(8,128)(2,1)S(1)} %collective-permute-done.15.got_ref), custom_call_target="tpu_custom_call" | custom-call | tf_op jit(solution)/shard_map/pallas_call | solution.py:221
  (25 shorter events, 0.3 us)
Async XLA Ops:
  0.0 2.5 %copy-start.2 = (bf16[128,8192]{1,0:T(8,128)(2,1)S(1)}, bf16[128,8192]{1,0:T(8,128)(2,1)}, u32[]{:S(2)}) copy-start(bf16[128,8192]{1,0:T(8,128)(2,1)} %param.7) | copy-start | bytes 6291460
  2.4 12.0 %copy-start = (s32[2,4]{1,0:T(2,128)S(1)}, s32[2,4]{1,0:T(2,128)}, u32[]{:S(2)}) copy-start(s32[2,4]{1,0:T(2,128)} %refs_0_.11) | copy-start | bytes 100
  2.4 12.0 %copy-start.1 = (s32[4]{0:T(128)S(1)}, s32[4]{0:T(128)}, u32[]{:S(2)}) copy-start(s32[4]{0:T(128)} %refs_1_.11) | copy-start | bytes 52
  2.7 11.8 %collective-permute-start.2 = (bf16[128,4096]{1,0:T(8,128)(2,1)S(1)}, bf16[128,4096]{1,0:T(8,128)(2,1)S(1)}, u32[]{:S(2)}, u32[]{:S(2)}) collective-permute-start(bf16[128,4096]{1,0:T(8,128)(2,1)S(1)} %get-tuple-element.99), channel_id=1, source_target_pairs={{0,1},{1,0},{2,3},{3,2},{4,5},{5,4},{6,7},{7,6},{8,9},{9,8},{10,11... | collective-permute-start | bytes 3145736 | tf_op jit(solution)/shard_map/ppermute | solution.py:295
  3.2 3.0 %collective-permute-start = (bf16[256,1024]{1,0:T(8,128)(2,1)S(1)}, bf16[256,1024]{1,0:T(8,128)(2,1)S(1)}, u32[]{:S(2)}, u32[]{:S(2)}) collective-permute-start(bf16[256,1024]{1,0:T(8,128)(2,1)S(1)} %maximum_maximum_fusion), channel_id=1, source_target_pairs={{0,1},{1,0},{2,3},{3,2},{4,5},{5,4},{6,7},{7,6},{8,9},{9,8},{10,11... | collective-permute-start | bytes 1572872 | tf_op jit(solution)/shard_map/ppermute | solution.py:295
  6.3 24.3 %collective-permute-start.5 = (bf16[256,1024]{1,0:T(8,128)(2,1)S(1)}, bf16[256,1024]{1,0:T(8,128)(2,1)S(1)}, u32[]{:S(2)}, u32[]{:S(2)}) collective-permute-start(bf16[256,1024]{1,0:T(8,128)(2,1)S(1)} %pad_maximum_fusion.refs_4_.refs_6_.refs_0_), channel_id=1, source_target_pairs={{0,4},{1,5},{2,6},{3,7},{4,0},{5,1},{6,2},{7,3},{8,12},{9,13},{10,... | collective-permute-start | bytes 1572872 | tf_op jit(solution)/shard_map/ppermute | solution.py:301
  9.3 21.3 %collective-permute-start.4 = (bf16[256,1024]{1,0:T(8,128)(2,1)S(1)}, bf16[256,1024]{1,0:T(8,128)(2,1)S(1)}, u32[]{:S(2)}, u32[]{:S(2)}) collective-permute-start(bf16[256,1024]{1,0:T(8,128)(2,1)S(1)} %pad_maximum_fusion.refs_4_.refs_6_.refs_0_), channel_id=1, source_target_pairs={{0,2},{1,3},{2,0},{3,1},{4,6},{5,7},{6,4},{7,5},{8,10},{9,11},{10,... | collective-permute-start | bytes 1572872 | tf_op jit(solution)/shard_map/ppermute | solution.py:298
  10.8 14.5 %collective-permute-start.1 = (bf16[256,1024]{1,0:T(8,128)(2,1)S(1)}, bf16[256,1024]{1,0:T(8,128)(2,1)S(1)}, u32[]{:S(2)}, u32[]{:S(2)}) collective-permute-start(bf16[256,1024]{1,0:T(8,128)(2,1)S(1)} %pad_maximum_fusion.refs_4_.refs_6_.refs_0_), channel_id=1, source_target_pairs={{0,24},{8,0},{16,8},{24,16},{1,25},{9,1},{17,9},{25,17},{2,26},{10... | collective-permute-start | bytes 1572872 | tf_op jit(solution)/shard_map/ppermute | solution.py:328
  25.3 14.3 %collective-permute-start.3 = (bf16[256,1024]{1,0:T(8,128)(2,1)S(1)}, bf16[256,1024]{1,0:T(8,128)(2,1)S(1)}, u32[]{:S(2)}, u32[]{:S(2)}) collective-permute-start(bf16[256,1024]{1,0:T(8,128)(2,1)S(1)} %collective-permute-done.1.refs_1_), channel_id=1, source_target_pairs={{0,24},{8,0},{16,8},{24,16},{1,25},{9,1},{17,9},{25,17},{2,26},{10... | collective-permute-start | bytes 1572872 | tf_op jit(solution)/shard_map/ppermute | solution.py:328
  29.6 12.9 %collective-permute-start.8 = (bf16[256,1024]{1,0:T(8,128)(2,1)S(1)}, bf16[256,1024]{1,0:T(8,128)(2,1)S(1)}, u32[]{:S(2)}, u32[]{:S(2)}) collective-permute-start(bf16[256,1024]{1,0:T(8,128)(2,1)S(1)} %pad_maximum_fusion.1.refs_5_.refs_7_), channel_id=1, source_target_pairs={{0,4},{1,5},{2,6},{3,7},{4,0},{5,1},{6,2},{7,3},{8,12},{9,13},{10,... | collective-permute-start | bytes 1572872 | tf_op jit(solution)/shard_map/ppermute | solution.py:301
  30.1 12.4 %collective-permute-start.7 = (bf16[256,1024]{1,0:T(8,128)(2,1)S(1)}, bf16[256,1024]{1,0:T(8,128)(2,1)S(1)}, u32[]{:S(2)}, u32[]{:S(2)}) collective-permute-start(bf16[256,1024]{1,0:T(8,128)(2,1)S(1)} %pad_maximum_fusion.1.refs_5_.refs_7_), channel_id=1, source_target_pairs={{0,2},{1,3},{2,0},{3,1},{4,6},{5,7},{6,4},{7,5},{8,10},{9,11},{10,... | collective-permute-start | bytes 1572872 | tf_op jit(solution)/shard_map/ppermute | solution.py:298
  39.6 13.5 %collective-permute-start.6 = (bf16[256,1024]{1,0:T(8,128)(2,1)S(1)}, bf16[256,1024]{1,0:T(8,128)(2,1)S(1)}, u32[]{:S(2)}, u32[]{:S(2)}) collective-permute-start(bf16[256,1024]{1,0:T(8,128)(2,1)S(1)} %collective-permute-done.3.refs_2_), channel_id=1, source_target_pairs={{8,0},{16,8},{24,16},{9,1},{17,9},{25,17},{10,2},{18,10},{26,18},{... | collective-permute-start | bytes 1572872 | tf_op jit(solution)/shard_map/ppermute | solution.py:328
  40.9 15.4 %collective-permute-start.10 = (bf16[256,1024]{1,0:T(8,128)(2,1)S(1)}, bf16[256,1024]{1,0:T(8,128)(2,1)S(1)}, u32[]{:S(2)}, u32[]{:S(2)}) collective-permute-start(bf16[256,1024]{1,0:T(8,128)(2,1)S(1)} %collective-permute-done.4.refs_2_.refs_4_), channel_id=1, source_target_pairs={{0,4},{1,5},{2,6},{3,7},{4,0},{5,1},{6,2},{7,3},{8,12},{9,13},{10,... | collective-permute-start | bytes 1572872 | tf_op jit(solution)/shard_map/ppermute | solution.py:301
  42.5 24.6 %collective-permute-start.11 = (bf16[256,1024]{1,0:T(8,128)(2,1)S(1)}, bf16[256,1024]{1,0:T(8,128)(2,1)S(1)}, u32[]{:S(2)}, u32[]{:S(2)}) collective-permute-start(bf16[256,1024]{1,0:T(8,128)(2,1)S(1)} %collective-permute-done.7.refs_2_.refs_4_), channel_id=1, source_target_pairs={{0,4},{1,5},{2,6},{3,7},{4,0},{5,1},{6,2},{7,3},{8,12},{9,13},{10,... | collective-permute-start | bytes 1572872 | tf_op jit(solution)/shard_map/ppermute | solution.py:301
  53.9 24.7 %collective-permute-start.13 = (bf16[256,1024]{1,0:T(8,128)(2,1)S(1)}, bf16[256,1024]{1,0:T(8,128)(2,1)S(1)}, u32[]{:S(2)}, u32[]{:S(2)}) collective-permute-start(bf16[256,1024]{1,0:T(8,128)(2,1)S(1)} %get-tuple-element.85.refs_4_.refs_7_), channel_id=1, source_target_pairs={{0,4},{1,5},{2,6},{3,7},{4,0},{5,1},{6,2},{7,3},{8,12},{9,13},{10,... | collective-permute-start | bytes 1572872 | tf_op jit(solution)/shard_map/ppermute | solution.py:301
  55.5 24.6 %collective-permute-start.9 = (bf16[256,1024]{1,0:T(8,128)(2,1)S(1)}, bf16[256,1024]{1,0:T(8,128)(2,1)S(1)}, u32[]{:S(2)}, u32[]{:S(2)}) collective-permute-start(bf16[256,1024]{1,0:T(8,128)(2,1)S(1)} %get-tuple-element.85.refs_4_.refs_7_), channel_id=1, source_target_pairs={{0,2},{1,3},{2,0},{3,1},{4,6},{5,7},{6,4},{7,5},{8,10},{9,11},{10,... | collective-permute-start | bytes 1572872 | tf_op jit(solution)/shard_map/ppermute | solution.py:298
  78.6 10.1 %collective-permute-start.14 = (bf16[128,1024]{1,0:T(8,128)(2,1)S(1)}, bf16[128,1024]{1,0:T(8,128)(2,1)S(1)}, u32[]{:S(2)}, u32[]{:S(2)}) collective-permute-start(bf16[128,1024]{1,0:T(8,128)(2,1)S(1)} %slice.18), channel_id=1, source_target_pairs={{0,2},{1,3},{2,0},{3,1},{4,6},{5,7},{6,4},{7,5},{8,10},{9,11},{10,... | collective-permute-start | bytes 786440 | tf_op jit(solution)/shard_map/ppermute | solution.py:298
  80.2 8.5 %collective-permute-start.12 = (bf16[128,1024]{1,0:T(8,128)(2,1)S(1)}, bf16[128,1024]{1,0:T(8,128)(2,1)S(1)}, u32[]{:S(2)}, u32[]{:S(2)}) collective-permute-start(bf16[128,1024]{1,0:T(8,128)(2,1)S(1)} %slice.14), channel_id=1, source_target_pairs={{0,4},{1,5},{2,6},{3,7},{4,0},{5,1},{6,2},{7,3},{8,12},{9,13},{10,... | collective-permute-start | bytes 786440 | tf_op jit(solution)/shard_map/ppermute | solution.py:301
  94.6 2.7 %collective-permute-start.15 = (bf16[128,4096]{1,0:T(8,128)(2,1)S(1)}, bf16[128,4096]{1,0:T(8,128)(2,1)S(1)}, u32[]{:S(2)}, u32[]{:S(2)}) collective-permute-start(bf16[128,4096]{1,0:T(8,128)(2,1)S(1)} %get-tuple-element.98), channel_id=1, source_target_pairs={{0,1},{1,0},{2,3},{3,2},{4,5},{5,4},{6,7},{7,6},{8,9},{9,8},{10,11... | collective-permute-start | bytes 3145736 | tf_op jit(solution)/shard_map/ppermute | solution.py:295

commit v8 on v7

--- a/solution.py
+++ b/solution.py
@@ -307,10 +307,8 @@
     own_mine, own_other = packed(seg_keys, seg_values)
     root_mine, root_other = packed(root_keys, root_values)
     sent = jnp.concatenate([own_other, root_other], axis=0)
-    got = to_core(sent)
-    queries, _ = lax.optimization_barrier((queries, sent))
+    queries, got = lax.optimization_barrier((queries, to_core(sent)))
     q_mine, q_other = halves(queries)
-    q_pair = (q_mine, to_core(q_other))
     own = jnp.concatenate([own_mine, got[:rows]], axis=0)
     root = jnp.concatenate([root_mine, got[rows:]], axis=0)
     run = functools.partial(attend, ny, rows, (expansion, root_offsets))
@@ -330,14 +328,15 @@
     ahead = [own]
     if leaves > 1:
         ahead.append(hop(1, own))
+    own, root, q_other = lax.optimization_barrier((own, root, q_other))
+    q_pair = (q_mine, to_core(q_other))
     own_x, own_y = to_x(own), [to_y(own, step) for step in steps]
     root_x, root_y = to_x(root), [to_y(root, step) for step in steps]
     state = run([own, root], (members(0, "own") + members(1, "root"),), q_pair, None, False)
 
-    def near(kind, arrays):
+    def near(kind):
         groups = [members(0, kind, 1) + members(1, kind, 0, 1)]
-        groups += [members(step, kind, 0, step) for step in steps if step > 1]
-        return run(arrays, tuple(groups), None, state, False)
+        return groups + [members(step, kind, 0, step) for step in steps if step > 1]
 
     if leaves > 2:
         (held,) = fence(state, ahead[-1])
@@ -345,23 +344,24 @@
         ahead.append(hop(2, held))
     own_x, *own_y = after(state, own_x, *own_y)
     own_far = [to_y(own_x, step) for step in steps]
-    state = near("own", [own_x, *own_y])
+    state = run([own_x, *own_y], tuple(near("own")), None, state, False)
     for step in range(3, leaves):
         (held,) = fence(state, ahead[-1])
         ahead[-1] = held
         ahead.append(hop(step, held))
     root_x, *root_y = after(state, root_x, *root_y)
     root_far = [to_y(root_x, step) for step in steps]
-    state = near("root", [root_x, *root_y])
+    groups = near("root")
+    groups[0] += members(ny, "own", 1, 1)
+    groups += [members(ny - 1 + step, "own", 1, step) for step in steps if step > 1]
+    state = run([root_x, *root_y, *own_far], tuple(groups), None, state, False)
 
     parent_rows = pick(state, expansion, leaves, after(state, *ahead))
     (parent_rows,) = after(state, parent_rows)
     kin_x, kin_y = to_x(parent_rows), [to_y(parent_rows, step) for step in steps]
-    far = [members(i, "own", 1, i + 1) + members(ny - 1 + i, "root", 1, i + 1) for i in range(ny - 1)]
-    far.append(members(2 * ny - 2, "kin"))
-    if ny == 2:
-        far = [far[0] + far[1]]
-    state = run([*own_far, *root_far, parent_rows], tuple(far), None, state, False)
+    groups = [members(0, "kin") + members(1, "root", 1, 1)]
+    groups += [members(step, "root", 1, step) for step in steps if step > 1]
+    state = run([parent_rows, *root_far], tuple(groups), None, state, False)
 
     (kin_x,) = after(state, kin_x)
     tops = [to_y(kin_x[:rows], step) for step in steps]

time: 99 us -> 97.4 us (0.984)
  Pallas kernels: 45.1 us -> 33 us
  starting transfers between devices: 22.4 us -> 33.4 us
  waiting for transfers between devices: 28.1 us -> 26.1 us
    pallas_call x6, Pallas kernels: 42.9 us -> 30.8 us  [attend(): pl.pallas_call(functools.partial(attend_kernel, ny, rows, len(arrays), gr...]
    ppermute x6, starting transfers between devices: 8.24 us -> 16 us  [to_y(): lax.ppermute(array, 'ctx', [(index(x, y, k), index(x, y + step, k)) for x...]
    ppermute x3, waiting for transfers between devices: 11.8 us -> 8.26 us  [hop(): lax.ppermute(rows_held, 'leaf', pairs if step < leaves - 1 else pairs[1:])]
    ppermute x4, starting transfers between devices: 4.37 us -> 6.1 us  [to_x(): lax.ppermute(array, 'ctx', [(index(x, y, k), index(x + 1, y, k)) for x, y...]
    ppermute x6, waiting for transfers between devices: 10.7 us -> 12.4 us  [to_y(): lax.ppermute(array, 'ctx', [(index(x, y, k), index(x, y + step, k)) for x...]
    ppermute x3, waiting for transfers between devices: 5.61 us -> 4.19 us  [to_core(): lax.ppermute(array, 'ctx', [(index(x, y, k), index(x, y, k + 1)) for x, y...]
    ppermute x4, waiting for transfers between devices: 0.01 us -> 1.25 us  [to_x(): lax.ppermute(array, 'ctx', [(index(x, y, k), index(x + 1, y, k)) for x, y...]
    ppermute x3, starting transfers between devices: 9.16 us -> 10.3 us  [hop(): lax.ppermute(rows_held, 'leaf', pairs if step < leaves - 1 else pairs[1:])]
  transfers between devices with their start and end apart: 16 -> 16, of which waited for: 6 -> 8; matrix products, arithmetic and copies ran while one was open for 0% -> 0% of each run, Pallas kernels for 38% -> 27%
where the time goes in v8:
time: 97.4 us; the launch traced here: 97.2 us
  starting transfers between devices  33.4 us (34%)
  Pallas kernels  33 us (34%)
  waiting for transfers between devices  26.1 us (27%)
  local copies, waits for them, and re-layouts  3.31 us (3%)
  other arithmetic  1.04 us (1%)
    pallas_call x6, Pallas kernels, attend(): pl.pallas_call(functools.partial(attend_kernel, ny, rows, len(arrays), gr...  30.8 us
    ppermute x6, starting transfers between devices, to_y(): lax.ppermute(array, 'ctx', [(index(x, y, k), index(x, y + step, k)) for x...  16 us
    ppermute x6, waiting for transfers between devices, to_y(): lax.ppermute(array, 'ctx', [(index(x, y, k), index(x, y + step, k)) for x...  12.4 us
    ppermute x3, starting transfers between devices, hop(): lax.ppermute(rows_held, 'leaf', pairs if step < leaves - 1 else pairs[1:])  10.3 us
    ppermute x3, waiting for transfers between devices, hop(): lax.ppermute(rows_held, 'leaf', pairs if step < leaves - 1 else pairs[1:])  8.26 us
    ppermute x4, starting transfers between devices, to_x(): lax.ppermute(array, 'ctx', [(index(x, y, k), index(x + 1, y, k)) for x, y...  6.1 us
    ppermute x3, waiting for transfers between devices, to_core(): lax.ppermute(array, 'ctx', [(index(x, y, k), index(x, y, k + 1)) for x, y...  4.19 us
    dynamic_slice x2, local copies, waits for them, and re-layouts, halves(): lax.dynamic_slice_in_dim(array, core * half, half, 1)  3.07 us
  transfers between devices with their start and end apart: 16, of which 8 were waited for; matrix products, arithmetic and copies ran while one was open for 0% of the time, Pallas kernels for 27%

profile of v8, /device:TPU:0, one launch (start us, length us, event | category | flops | bytes accessed | tf_op | source)
XLA Modules:
  0.0 97.2 jit_solution(365612713675035442)
XLA Ops:
  0.0 1.3 %constant_dynamic-slice_fusion.8 = (bf16[128,512]{1,0:T(8,128)(2,1)S(1)}, bf16[128,512]{1,0:T(8,128)(2,1)S(1)}, bf16[128,512]{1,0:T(8,128)(2,1)S(1)}, bf16[128,512]{1,0:T(8,128)(2,1)S(1)}) fusion(bf16[128,1024]{1,0:T(8,128)(2,1)} %param.9, s32[]{:T(128)S(6)} %select_n.8, s32[]{:T(128)S(6)} %select_n.9, bf16[128,1024]{1,0:T(8,128)(2,1)} %param.8), kind=kLoop, calls=%fused_computation.11 | loop fusion | bytes 1048584 | tf_op jit(solution)/shard_map/dynamic_slice | solution.py:285
  1.3 1.8 %constant_dynamic-slice_fusion.1 = (bf16[128,512]{1,0:T(8,128)(2,1)S(1)}, bf16[128,512]{1,0:T(8,128)(2,1)S(1)}, bf16[128,512]{1,0:T(8,128)(2,1)S(1)}, bf16[128,512]{1,0:T(8,128)(2,1)}) fusion(bf16[128,1024]{1,0:T(8,128)(2,1)} %param.11, s32[]{:T(128)S(6)} %select_n.8, s32[]{:T(128)S(6)} %select_n.9, bf16[128,1024]{1,0:T(8,128)(2,1)} %param.10), kind=kLoop, calls=%fused_computation.4 | loop fusion | bytes 1048584 | tf_op jit(solution)/shard_map/dynamic_slice | solution.py:285
  3.7 1.5 %collective-permute-done = bf16[256,1024]{1,0:T(8,128)(2,1)S(1)} collective-permute-done((bf16[256,1024]{1,0:T(8,128)(2,1)S(1)}, bf16[256,1024]{1,0:T(8,128)(2,1)S(1)}, u32[]{:S(2)}, u32[]{:S(2)}) %collective-permute-start) | collective-permute-done | bytes 524320 | tf_op jit(solution)/shard_map/ppermute | solution.py:295
  5.2 0.9 pad_maximum_fusion.1.refs_5_.refs_7_
  6.9 4.7 %collective-permute-start.1 = (bf16[256,1024]{1,0:T(8,128)(2,1)S(1)}, bf16[256,1024]{1,0:T(8,128)(2,1)S(1)}, u32[]{:S(2)}, u32[]{:S(2)}) collective-permute-start(bf16[256,1024]{1,0:T(8,128)(2,1)S(1)} %pad_maximum_fusion.refs_4_.refs_6_.refs_0_), channel_id=1, source_target_pairs={{0,24},{8,0},{16,8},{24,16},{1,25},{9,1},{17,9},{25,17},{2,26},{10... | collective-permute-start | bytes 1572872 | tf_op jit(solution)/shard_map/ppermute | solution.py:326
  11.6 1.5 %collective-permute-start.5 = (bf16[256,1024]{1,0:T(8,128)(2,1)S(1)}, bf16[256,1024]{1,0:T(8,128)(2,1)S(1)}, u32[]{:S(2)}, u32[]{:S(2)}) collective-permute-start(bf16[256,1024]{1,0:T(8,128)(2,1)S(1)} %pad_maximum_fusion.refs_4_.refs_6_.refs_0_), channel_id=1, source_target_pairs={{0,4},{1,5},{2,6},{3,7},{4,0},{5,1},{6,2},{7,3},{8,12},{9,13},{10,... | collective-permute-start | bytes 1572872 | tf_op jit(solution)/shard_map/ppermute | solution.py:301
  13.1 1.5 %collective-permute-start.4 = (bf16[256,1024]{1,0:T(8,128)(2,1)S(1)}, bf16[256,1024]{1,0:T(8,128)(2,1)S(1)}, u32[]{:S(2)}, u32[]{:S(2)}) collective-permute-start(bf16[256,1024]{1,0:T(8,128)(2,1)S(1)} %pad_maximum_fusion.refs_4_.refs_6_.refs_0_), channel_id=1, source_target_pairs={{0,2},{1,3},{2,0},{3,1},{4,6},{5,7},{6,4},{7,5},{8,10},{9,11},{10,... | collective-permute-start | bytes 1572872 | tf_op jit(solution)/shard_map/ppermute | solution.py:298
  14.6 7.5 %shard_map.73 = (f32[8,128]{1,0:T(8,128)S(1)}, f32[4,2,1024,384]{3,2,1,0:T(8,128)S(1)}, bf16[4,2,1024,256]{3,2,1,0:T(8,128)(2,1)S(1)}) custom-call(s32[2,4]{1,0:T(2,128)S(1)} %copy-done, s32[4]{0:T(128)S(1)} %copy-done.1, bf16[128,4096]{1,0:T(8,128)(2,1)S(1)} %get-tuple-element.108.refs_2_, bf16[128,4096]{1,0:T(8,128)(2,1)S(1)} %collective-permute-done.2.refs_3_, ...), custom_call_target="tpu_custom_call" | custom-call | flops 4294967296 | bytes 4194304 | tf_op jit(solution)/shard_map/pallas_call | solution.py:262
  22.1 1.2 %collective-permute-done.1.refs_1_ = bf16[256,1024]{1,0:T(8,128)(2,1)S(1)} collective-permute-done((bf16[256,1024]{1,0:T(8,128)(2,1)S(1)}, bf16[256,1024]{1,0:T(8,128)(2,1)S(1)}, u32[]{:S(2)}, u32[]{:S(2)}) %collective-permute-start.1) | collective-permute-done | bytes 524320 | tf_op jit(solution)/shard_map/ppermute | solution.py:326
  23.3 4.3 %collective-permute-start.3 = (bf16[256,1024]{1,0:T(8,128)(2,1)S(1)}, bf16[256,1024]{1,0:T(8,128)(2,1)S(1)}, u32[]{:S(2)}, u32[]{:S(2)}) collective-permute-start(bf16[256,1024]{1,0:T(8,128)(2,1)S(1)} %collective-permute-done.1.refs_1_), channel_id=1, source_target_pairs={{0,24},{8,0},{16,8},{24,16},{1,25},{9,1},{17,9},{25,17},{2,26},{10... | collective-permute-start | bytes 1572872 | tf_op jit(solution)/shard_map/ppermute | solution.py:326
  27.6 1.5 %collective-permute-start.8 = (bf16[256,1024]{1,0:T(8,128)(2,1)S(1)}, bf16[256,1024]{1,0:T(8,128)(2,1)S(1)}, u32[]{:S(2)}, u32[]{:S(2)}) collective-permute-start(bf16[256,1024]{1,0:T(8,128)(2,1)S(1)} %pad_maximum_fusion.1.refs_5_.refs_7_), channel_id=1, source_target_pairs={{0,4},{1,5},{2,6},{3,7},{4,0},{5,1},{6,2},{7,3},{8,12},{9,13},{10,... | collective-permute-start | bytes 1572872 | tf_op jit(solution)/shard_map/ppermute | solution.py:301
  29.1 1.5 %collective-permute-start.7 = (bf16[256,1024]{1,0:T(8,128)(2,1)S(1)}, bf16[256,1024]{1,0:T(8,128)(2,1)S(1)}, u32[]{:S(2)}, u32[]{:S(2)}) collective-permute-start(bf16[256,1024]{1,0:T(8,128)(2,1)S(1)} %pad_maximum_fusion.1.refs_5_.refs_7_), channel_id=1, source_target_pairs={{0,2},{1,3},{2,0},{3,1},{4,6},{5,7},{6,4},{7,5},{8,10},{9,11},{10,... | collective-permute-start | bytes 1572872 | tf_op jit(solution)/shard_map/ppermute | solution.py:298
  30.6 0.6 collective-permute-start.9
  31.2 1.2 %shard_map.75 = (f32[8,128]{1,0:T(8,128)S(1)}, f32[4,2,1024,384]{3,2,1,0:T(8,128)S(1)}, bf16[4,2,1024,256]{3,2,1,0:T(8,128)(2,1)S(1)}) custom-call(s32[2,4]{1,0:T(2,128)S(1)} %copy-done, s32[4]{0:T(128)S(1)} %copy-done.1, bf16[256,1024]{1,0:T(8,128)(2,1)S(1)} %collective-permute-done.4.refs_2_.refs_4_, ...), custom_call_target="tpu_custom_call", output_to_operand_aliasing={{1}: (7, {}), {2}: (8, {})} | custom-call | flops 4294967296 | bytes 4194304 | tf_op jit(solution)/shard_map/pallas_call | solution.py:262
  32.4 6.1 %collective-permute-done.3.refs_2_ = bf16[256,1024]{1,0:T(8,128)(2,1)S(1)} collective-permute-done((bf16[256,1024]{1,0:T(8,128)(2,1)S(1)}, bf16[256,1024]{1,0:T(8,128)(2,1)S(1)}, u32[]{:S(2)}, u32[]{:S(2)}) %collective-permute-start.3) | collective-permute-done | bytes 524320 | tf_op jit(solution)/shard_map/ppermute | solution.py:326
  38.5 4.0 %collective-permute-done.8.refs_3_.refs_6_ = bf16[256,1024]{1,0:T(8,128)(2,1)S(1)} collective-permute-done((bf16[256,1024]{1,0:T(8,128)(2,1)S(1)}, bf16[256,1024]{1,0:T(8,128)(2,1)S(1)}, u32[]{:S(2)}, u32[]{:S(2)}) %collective-permute-start.8) | collective-permute-done | bytes 524320 | tf_op jit(solution)/shard_map/ppermute | solution.py:301
  42.5 1.5 %collective-permute-start.11 = (bf16[256,1024]{1,0:T(8,128)(2,1)S(1)}, bf16[256,1024]{1,0:T(8,128)(2,1)S(1)}, u32[]{:S(2)}, u32[]{:S(2)}) collective-permute-start(bf16[256,1024]{1,0:T(8,128)(2,1)S(1)} %collective-permute-done.7.refs_2_.refs_5_), channel_id=1, source_target_pairs={{0,4},{1,5},{2,6},{3,7},{4,0},{5,1},{6,2},{7,3},{8,12},{9,13},{10,... | collective-permute-start | bytes 1572872 | tf_op jit(solution)/shard_map/ppermute | solution.py:301
  44.0 1.3 %collective-permute-start.6 = (bf16[256,1024]{1,0:T(8,128)(2,1)S(1)}, bf16[256,1024]{1,0:T(8,128)(2,1)S(1)}, u32[]{:S(2)}, u32[]{:S(2)}) collective-permute-start(bf16[256,1024]{1,0:T(8,128)(2,1)S(1)} %collective-permute-done.3.refs_2_), channel_id=1, source_target_pairs={{8,0},{16,8},{24,16},{9,1},{17,9},{25,17},{10,2},{18,10},{26,18},{... | collective-permute-start | bytes 1572872 | tf_op jit(solution)/shard_map/ppermute | solution.py:326
  45.3 8.4 %collective-permute-done.9.refs_4_.refs_7_ = bf16[256,1024]{1,0:T(8,128)(2,1)S(1)} collective-permute-done((bf16[256,1024]{1,0:T(8,128)(2,1)S(1)}, bf16[256,1024]{1,0:T(8,128)(2,1)S(1)}, u32[]{:S(2)}, u32[]{:S(2)}) %collective-permute-start.9) | collective-permute-done | bytes 524320 | tf_op jit(solution)/shard_map/ppermute | solution.py:301
  53.7 1.4 %shard_map.77 = (f32[8,128]{1,0:T(8,128)S(1)}, f32[4,2,1024,384]{3,2,1,0:T(8,128)S(1)}, bf16[4,2,1024,256]{3,2,1,0:T(8,128)(2,1)S(1)}) custom-call(s32[2,4]{1,0:T(2,128)S(1)} %copy-done, s32[4]{0:T(128)S(1)} %copy-done.1, bf16[256,1024]{1,0:T(8,128)(2,1)S(1)} %collective-permute-done.7.refs_2_.refs_5_, ...), custom_call_target="tpu_custom_call", output_to_operand_aliasing={{1}: (9, {}), {2}: (10, {})} | custom-call | flops 6442450944 | bytes 4194304 | tf_op jit(solution)/shard_map/pallas_call | solution.py:262
  55.0 1.0 collective-permute-done.6.refs_3_
  56.0 0.8 shard_map.78
  56.8 9.7 %collective-permute-start.13 = (bf16[256,1024]{1,0:T(8,128)(2,1)S(1)}, bf16[256,1024]{1,0:T(8,128)(2,1)S(1)}, u32[]{:S(2)}, u32[]{:S(2)}) collective-permute-start(bf16[256,1024]{1,0:T(8,128)(2,1)S(1)} %get-tuple-element.93.refs_2_.refs_4_), channel_id=1, source_target_pairs={{0,4},{1,5},{2,6},{3,7},{4,0},{5,1},{6,2},{7,3},{8,12},{9,13},{10,... | collective-permute-start | bytes 1572872 | tf_op jit(solution)/shard_map/ppermute | solution.py:301
  66.6 1.5 %collective-permute-start.10 = (bf16[256,1024]{1,0:T(8,128)(2,1)S(1)}, bf16[256,1024]{1,0:T(8,128)(2,1)S(1)}, u32[]{:S(2)}, u32[]{:S(2)}) collective-permute-start(bf16[256,1024]{1,0:T(8,128)(2,1)S(1)} %get-tuple-element.93.refs_2_.refs_4_), channel_id=1, source_target_pairs={{0,2},{1,3},{2,0},{3,1},{4,6},{5,7},{6,4},{7,5},{8,10},{9,11},{10,... | collective-permute-start | bytes 1572872 | tf_op jit(solution)/shard_map/ppermute | solution.py:298
  68.1 7.8 %shard_map.79 = (f32[8,128]{1,0:T(8,128)S(1)}, f32[4,2,1024,384]{3,2,1,0:T(8,128)S(1)}, bf16[4,2,1024,256]{3,2,1,0:T(8,128)(2,1)S(1)}) custom-call(s32[2,4]{1,0:T(2,128)S(1)} %copy-done, s32[4]{0:T(128)S(1)} %copy-done.1, bf16[256,1024]{1,0:T(8,128)(2,1)S(1)} %get-tuple-element.93.refs_2_.refs_4_, ...), custom_call_target="tpu_custom_call", output_to_operand_aliasing={{1}: (7, {}), {2}: (8, {})} | custom-call | flops 4294967296 | bytes 4194304 | tf_op jit(solution)/shard_map/pallas_call | solution.py:262
  75.9 1.6 %collective-permute-start.14 = (bf16[128,1024]{1,0:T(8,128)(2,1)S(1)}, bf16[128,1024]{1,0:T(8,128)(2,1)S(1)}, u32[]{:S(2)}, u32[]{:S(2)}) collective-permute-start(bf16[128,1024]{1,0:T(8,128)(2,1)S(1)} %slice.16), channel_id=1, source_target_pairs={{0,2},{1,3},{2,0},{3,1},{4,6},{5,7},{6,4},{7,5},{8,10},{9,11},{10,... | collective-permute-start | bytes 786440 | tf_op jit(solution)/shard_map/ppermute | solution.py:298
  77.5 1.2 %collective-permute-done.10.refs_2_.refs_4_ = bf16[256,1024]{1,0:T(8,128)(2,1)S(1)} collective-permute-done((bf16[256,1024]{1,0:T(8,128)(2,1)S(1)}, bf16[256,1024]{1,0:T(8,128)(2,1)S(1)}, u32[]{:S(2)}, u32[]{:S(2)}) %collective-permute-start.10) | collective-permute-done | bytes 524320 | tf_op jit(solution)/shard_map/ppermute | solution.py:298
  78.8 1.1 %collective-permute-start.12 = (bf16[128,1024]{1,0:T(8,128)(2,1)S(1)}, bf16[128,1024]{1,0:T(8,128)(2,1)S(1)}, u32[]{:S(2)}, u32[]{:S(2)}) collective-permute-start(bf16[128,1024]{1,0:T(8,128)(2,1)S(1)} %slice.14), channel_id=1, source_target_pairs={{0,4},{1,5},{2,6},{3,7},{4,0},{5,1},{6,2},{7,3},{8,12},{9,13},{10,... | collective-permute-start | bytes 786440 | tf_op jit(solution)/shard_map/ppermute | solution.py:301
  79.9 7.5 %shard_map.80 = (f32[8,128]{1,0:T(8,128)S(1)}, f32[4,2,1024,384]{3,2,1,0:T(8,128)S(1)}, bf16[4,2,1024,256]{3,2,1,0:T(8,128)(2,1)S(1)}) custom-call(s32[2,4]{1,0:T(2,128)S(1)} %copy-done, s32[4]{0:T(128)S(1)} %copy-done.1, bf16[256,1024]{1,0:T(8,128)(2,1)S(1)} %collective-permute-done.10.refs_2_.refs_4_, ...), custom_call_target="tpu_custom_call", output_to_operand_aliasing={{1}: (7, {}), {2}: (8, {})} | custom-call | flops 4294967296 | bytes 4194304 | tf_op jit(solution)/shard_map/pallas_call | solution.py:262
  87.4 5.6 %shard_map.81 = (bf16[128,4096]{1,0:T(8,128)(2,1)S(1)}, bf16[128,4096]{1,0:T(8,128)(2,1)S(1)}, f32[4,2,1024,384]{3,2,1,0:T(8,128)S(1)}, bf16[4,2,1024,256]{3,2,1,0:T(8,128)(2,1)S(1)}) custom-call(s32[2,4]{1,0:T(2,128)S(1)} %copy-done, s32[4]{0:T(128)S(1)} %copy-done.1, ...), custom_call_target="tpu_custom_call", output_to_operand_aliasing={{2}: (7, {}), {3}: (8, {})} | custom-call | flops 2147483648 | bytes 4194304 | tf_op jit(solution)/shard_map/pallas_call | solution.py:262
  93.0 2.6 %collective-permute-done.15.got_ref = bf16[128,4096]{1,0:T(8,128)(2,1)S(1)} collective-permute-done((bf16[128,4096]{1,0:T(8,128)(2,1)S(1)}, bf16[128,4096]{1,0:T(8,128)(2,1)S(1)}, u32[]{:S(2)}, u32[]{:S(2)}) %collective-permute-start.15) | collective-permute-done | bytes 1048608 | tf_op jit(solution)/shard_map/ppermute | solution.py:295
  95.7 1.3 %shard_map.82 = bf16[128,8192]{1,0:T(8,128)(2,1)} custom-call(bf16[128,4096]{1,0:T(8,128)(2,1)S(1)} %get-tuple-element.105.mine_ref, bf16[128,4096]{1,0:T(8,128)(2,1)S(1)} %collective-permute-done.15.got_ref), custom_call_target="tpu_custom_call" | custom-call | tf_op jit(solution)/shard_map/pallas_call | solution.py:221
  (25 shorter events, 1.4 us)
Async XLA Ops:
  0.0 6.2 %copy-start.2 = (bf16[128,8192]{1,0:T(8,128)(2,1)S(1)}, bf16[128,8192]{1,0:T(8,128)(2,1)}, u32[]{:S(2)}) copy-start(bf16[128,8192]{1,0:T(8,128)(2,1)} %param.7) | copy-start | bytes 6291460
  3.1 11.5 %copy-start = (s32[2,4]{1,0:T(2,128)S(1)}, s32[2,4]{1,0:T(2,128)}, u32[]{:S(2)}) copy-start(s32[2,4]{1,0:T(2,128)} %refs_0_.11) | copy-start | bytes 100
  3.1 11.5 %copy-start.1 = (s32[4]{0:T(128)S(1)}, s32[4]{0:T(128)}, u32[]{:S(2)}) copy-start(s32[4]{0:T(128)} %refs_1_.11) | copy-start | bytes 52
  3.1 2.1 %collective-permute-start = (bf16[256,1024]{1,0:T(8,128)(2,1)S(1)}, bf16[256,1024]{1,0:T(8,128)(2,1)S(1)}, u32[]{:S(2)}, u32[]{:S(2)}) collective-permute-start(bf16[256,1024]{1,0:T(8,128)(2,1)S(1)} %maximum_maximum_fusion), channel_id=1, source_target_pairs={{0,1},{1,0},{2,3},{3,2},{4,5},{5,4},{6,7},{7,6},{8,9},{9,8},{10,11... | collective-permute-start | bytes 1572872 | tf_op jit(solution)/shard_map/ppermute | solution.py:295
  6.4 8.2 %collective-permute-start.2 = (bf16[128,4096]{1,0:T(8,128)(2,1)S(1)}, bf16[128,4096]{1,0:T(8,128)(2,1)S(1)}, u32[]{:S(2)}, u32[]{:S(2)}) collective-permute-start(bf16[128,4096]{1,0:T(8,128)(2,1)S(1)} %get-tuple-element.58), channel_id=1, source_target_pairs={{0,1},{1,0},{2,3},{3,2},{4,5},{5,4},{6,7},{7,6},{8,9},{9,8},{10,11... | collective-permute-start | bytes 3145736 | tf_op jit(solution)/shard_map/ppermute | solution.py:295
  6.9 16.5 %collective-permute-start.1 = (bf16[256,1024]{1,0:T(8,128)(2,1)S(1)}, bf16[256,1024]{1,0:T(8,128)(2,1)S(1)}, u32[]{:S(2)}, u32[]{:S(2)}) collective-permute-start(bf16[256,1024]{1,0:T(8,128)(2,1)S(1)} %pad_maximum_fusion.refs_4_.refs_6_.refs_0_), channel_id=1, source_target_pairs={{0,24},{8,0},{16,8},{24,16},{1,25},{9,1},{17,9},{25,17},{2,26},{10... | collective-permute-start | bytes 1572872 | tf_op jit(solution)/shard_map/ppermute | solution.py:326
  11.6 19.0 %collective-permute-start.5 = (bf16[256,1024]{1,0:T(8,128)(2,1)S(1)}, bf16[256,1024]{1,0:T(8,128)(2,1)S(1)}, u32[]{:S(2)}, u32[]{:S(2)}) collective-permute-start(bf16[256,1024]{1,0:T(8,128)(2,1)S(1)} %pad_maximum_fusion.refs_4_.refs_6_.refs_0_), channel_id=1, source_target_pairs={{0,4},{1,5},{2,6},{3,7},{4,0},{5,1},{6,2},{7,3},{8,12},{9,13},{10,... | collective-permute-start | bytes 1572872 | tf_op jit(solution)/shard_map/ppermute | solution.py:301
  13.1 17.5 %collective-permute-start.4 = (bf16[256,1024]{1,0:T(8,128)(2,1)S(1)}, bf16[256,1024]{1,0:T(8,128)(2,1)S(1)}, u32[]{:S(2)}, u32[]{:S(2)}) collective-permute-start(bf16[256,1024]{1,0:T(8,128)(2,1)S(1)} %pad_maximum_fusion.refs_4_.refs_6_.refs_0_), channel_id=1, source_target_pairs={{0,2},{1,3},{2,0},{3,1},{4,6},{5,7},{6,4},{7,5},{8,10},{9,11},{10,... | collective-permute-start | bytes 1572872 | tf_op jit(solution)/shard_map/ppermute | solution.py:298
  23.3 15.2 %collective-permute-start.3 = (bf16[256,1024]{1,0:T(8,128)(2,1)S(1)}, bf16[256,1024]{1,0:T(8,128)(2,1)S(1)}, u32[]{:S(2)}, u32[]{:S(2)}) collective-permute-start(bf16[256,1024]{1,0:T(8,128)(2,1)S(1)} %collective-permute-done.1.refs_1_), channel_id=1, source_target_pairs={{0,24},{8,0},{16,8},{24,16},{1,25},{9,1},{17,9},{25,17},{2,26},{10... | collective-permute-start | bytes 1572872 | tf_op jit(solution)/shard_map/ppermute | solution.py:326
  27.6 14.9 %collective-permute-start.8 = (bf16[256,1024]{1,0:T(8,128)(2,1)S(1)}, bf16[256,1024]{1,0:T(8,128)(2,1)S(1)}, u32[]{:S(2)}, u32[]{:S(2)}) collective-permute-start(bf16[256,1024]{1,0:T(8,128)(2,1)S(1)} %pad_maximum_fusion.1.refs_5_.refs_7_), channel_id=1, source_target_pairs={{0,4},{1,5},{2,6},{3,7},{4,0},{5,1},{6,2},{7,3},{8,12},{9,13},{10,... | collective-permute-start | bytes 1572872 | tf_op jit(solution)/shard_map/ppermute | solution.py:301
  29.1 13.3 %collective-permute-start.7 = (bf16[256,1024]{1,0:T(8,128)(2,1)S(1)}, bf16[256,1024]{1,0:T(8,128)(2,1)S(1)}, u32[]{:S(2)}, u32[]{:S(2)}) collective-permute-start(bf16[256,1024]{1,0:T(8,128)(2,1)S(1)} %pad_maximum_fusion.1.refs_5_.refs_7_), channel_id=1, source_target_pairs={{0,2},{1,3},{2,0},{3,1},{4,6},{5,7},{6,4},{7,5},{8,10},{9,11},{10,... | collective-permute-start | bytes 1572872 | tf_op jit(solution)/shard_map/ppermute | solution.py:298
  30.6 23.1 %collective-permute-start.9 = (bf16[256,1024]{1,0:T(8,128)(2,1)S(1)}, bf16[256,1024]{1,0:T(8,128)(2,1)S(1)}, u32[]{:S(2)}, u32[]{:S(2)}) collective-permute-start(bf16[256,1024]{1,0:T(8,128)(2,1)S(1)} %collective-permute-done.4.refs_2_.refs_4_), channel_id=1, source_target_pairs={{0,4},{1,5},{2,6},{3,7},{4,0},{5,1},{6,2},{7,3},{8,12},{9,13},{10,... | collective-permute-start | bytes 1572872 | tf_op jit(solution)/shard_map/ppermute | solution.py:301
  42.5 25.6 %collective-permute-start.11 = (bf16[256,1024]{1,0:T(8,128)(2,1)S(1)}, bf16[256,1024]{1,0:T(8,128)(2,1)S(1)}, u32[]{:S(2)}, u32[]{:S(2)}) collective-permute-start(bf16[256,1024]{1,0:T(8,128)(2,1)S(1)} %collective-permute-done.7.refs_2_.refs_5_), channel_id=1, source_target_pairs={{0,4},{1,5},{2,6},{3,7},{4,0},{5,1},{6,2},{7,3},{8,12},{9,13},{10,... | collective-permute-start | bytes 1572872 | tf_op jit(solution)/shard_map/ppermute | solution.py:301
  44.0 12.0 %collective-permute-start.6 = (bf16[256,1024]{1,0:T(8,128)(2,1)S(1)}, bf16[256,1024]{1,0:T(8,128)(2,1)S(1)}, u32[]{:S(2)}, u32[]{:S(2)}) collective-permute-start(bf16[256,1024]{1,0:T(8,128)(2,1)S(1)} %collective-permute-done.3.refs_2_), channel_id=1, source_target_pairs={{8,0},{16,8},{24,16},{9,1},{17,9},{25,17},{10,2},{18,10},{26,18},{... | collective-permute-start | bytes 1572872 | tf_op jit(solution)/shard_map/ppermute | solution.py:326
  56.8 19.0 %collective-permute-start.13 = (bf16[256,1024]{1,0:T(8,128)(2,1)S(1)}, bf16[256,1024]{1,0:T(8,128)(2,1)S(1)}, u32[]{:S(2)}, u32[]{:S(2)}) collective-permute-start(bf16[256,1024]{1,0:T(8,128)(2,1)S(1)} %get-tuple-element.93.refs_2_.refs_4_), channel_id=1, source_target_pairs={{0,4},{1,5},{2,6},{3,7},{4,0},{5,1},{6,2},{7,3},{8,12},{9,13},{10,... | collective-permute-start | bytes 1572872 | tf_op jit(solution)/shard_map/ppermute | solution.py:301
  66.6 12.2 %collective-permute-start.10 = (bf16[256,1024]{1,0:T(8,128)(2,1)S(1)}, bf16[256,1024]{1,0:T(8,128)(2,1)S(1)}, u32[]{:S(2)}, u32[]{:S(2)}) collective-permute-start(bf16[256,1024]{1,0:T(8,128)(2,1)S(1)} %get-tuple-element.93.refs_2_.refs_4_), channel_id=1, source_target_pairs={{0,2},{1,3},{2,0},{3,1},{4,6},{5,7},{6,4},{7,5},{8,10},{9,11},{10,... | collective-permute-start | bytes 1572872 | tf_op jit(solution)/shard_map/ppermute | solution.py:298
  75.9 11.5 %collective-permute-start.14 = (bf16[128,1024]{1,0:T(8,128)(2,1)S(1)}, bf16[128,1024]{1,0:T(8,128)(2,1)S(1)}, u32[]{:S(2)}, u32[]{:S(2)}) collective-permute-start(bf16[128,1024]{1,0:T(8,128)(2,1)S(1)} %slice.16), channel_id=1, source_target_pairs={{0,2},{1,3},{2,0},{3,1},{4,6},{5,7},{6,4},{7,5},{8,10},{9,11},{10,... | collective-permute-start | bytes 786440 | tf_op jit(solution)/shard_map/ppermute | solution.py:298
  78.8 8.6 %collective-permute-start.12 = (bf16[128,1024]{1,0:T(8,128)(2,1)S(1)}, bf16[128,1024]{1,0:T(8,128)(2,1)S(1)}, u32[]{:S(2)}, u32[]{:S(2)}) collective-permute-start(bf16[128,1024]{1,0:T(8,128)(2,1)S(1)} %slice.14), channel_id=1, source_target_pairs={{0,4},{1,5},{2,6},{3,7},{4,0},{5,1},{6,2},{7,3},{8,12},{9,13},{10,... | collective-permute-start | bytes 786440 | tf_op jit(solution)/shard_map/ppermute | solution.py:301
  93.0 2.7 %collective-permute-start.15 = (bf16[128,4096]{1,0:T(8,128)(2,1)S(1)}, bf16[128,4096]{1,0:T(8,128)(2,1)S(1)}, u32[]{:S(2)}, u32[]{:S(2)}) collective-permute-start(bf16[128,4096]{1,0:T(8,128)(2,1)S(1)} %get-tuple-element.106), channel_id=1, source_target_pairs={{0,1},{1,0},{2,3},{3,2},{4,5},{5,4},{6,7},{7,6},{8,9},{9,8},{10,11... | collective-permute-start | bytes 3145736 | tf_op jit(solution)/shard_map/ppermute | solution.py:295

commit v9 on v8

--- a/solution.py
+++ b/solution.py
@@ -14,7 +14,7 @@
 GW = HQ // KVH
 HALF_KV = KVH // 2
 NEG = -1e30
-Q_SCALE = math.log2(math.e) / math.sqrt(HD)
+EXP_SCALE = math.log2(math.e) / math.sqrt(HD)
 ROW_BLOCK = 256
 
 
@@ -51,17 +51,12 @@
     if first:
         for s, q_ref in enumerate(raw):
             for g in range(GW):
-                q = q_ref[:, g * HD : (g + 1) * HD].astype(jnp.float32) * Q_SCALE
-                high = q.astype(jnp.bfloat16)
-                low = (q - high.astype(jnp.float32)).astype(jnp.bfloat16)
-                qs[head, s, g * rows : (g + 1) * rows, :HD] = high
-                qs[head, s, g * rows : (g + 1) * rows, HD:] = low
+                qs[head, s, g * rows : (g + 1) * rows, :] = q_ref[:, g * HD : (g + 1) * HD]
 
     def step(members, limits, masked, fresh):
         width = len(members) * rows
         cut = lambda refs: [refs[a][b * rows : (b + 1) * rows, :] for a, b, _ in members]
         keys = jnp.concatenate(cut(key_refs), axis=0)
-        keys = jnp.concatenate([keys, keys], axis=1)
         values = jnp.concatenate(cut(value_refs), axis=0)
         values = jnp.concatenate([values, jnp.ones_like(values)], axis=1)
         size = min(ROW_BLOCK, stacked)
@@ -95,12 +90,12 @@
             else:
                 old = held[head, s, here, 2 * HD :]
                 new = jnp.maximum(old, new)
-            weights = jnp.exp2(scores - jnp.concatenate([new] * (width // HD), axis=1))
+            weights = jnp.exp2((scores - jnp.concatenate([new] * (width // HD), axis=1)) * EXP_SCALE)
             update = jnp.dot(weights.astype(jnp.bfloat16), values, preferred_element_type=jnp.float32)
             if fresh:
                 held[head, s, here, : 2 * HD] = update
             else:
-                shrink = jnp.exp2(old - new)
+                shrink = jnp.exp2((old - new) * EXP_SCALE)
                 before = held[head, s, here, : 2 * HD] * jnp.concatenate([shrink, shrink], axis=1)
                 held[head, s, here, : 2 * HD] = before + update
             held[head, s, here, 2 * HD :] = new
@@ -256,7 +251,7 @@
         operands += [mark, in_vmem(state), in_vmem(prepared)]
         specs += [pl.BlockSpec(memory_space=pl.ANY), WHOLE, WHOLE]
     out_shape.append(pltpu.VMEM((HALF_KV, 2, stacked, 3 * HD), jnp.float32))
-    out_shape.append(pltpu.VMEM((HALF_KV, 2, stacked, 2 * HD), jnp.bfloat16))
+    out_shape.append(pltpu.VMEM((HALF_KV, 2, stacked, HD), jnp.bfloat16))
     out_specs += [WHOLE, WHOLE]
     scores = HALF_KV * 2 * stacked * rows * sum(len(members) for members in groups)
     out = pl.pallas_call(
@@ -343,25 +338,22 @@
         ahead[-1] = held
         ahead.append(hop(2, held))
     own_x, *own_y = after(state, own_x, *own_y)
-    own_far = [to_y(own_x, step) for step in steps]
     state = run([own_x, *own_y], tuple(near("own")), None, state, False)
     for step in range(3, leaves):
         (held,) = fence(state, ahead[-1])
         ahead[-1] = held
         ahead.append(hop(step, held))
-    root_x, *root_y = after(state, root_x, *root_y)
-    root_far = [to_y(root_x, step) for step in steps]
-    groups = near("root")
-    groups[0] += members(ny, "own", 1, 1)
-    groups += [members(ny - 1 + step, "own", 1, step) for step in steps if step > 1]
-    state = run([root_x, *root_y, *own_far], tuple(groups), None, state, False)
+    own_x, root_x, *root_y = after(state, own_x, root_x, *root_y)
+    own_far = [to_y(own_x, step) for step in steps]
+    root_far = [to_x(array) for array in root_y]
+    state = run([root_x, *root_y], tuple(near("root")), None, state, False)
 
     parent_rows = pick(state, expansion, leaves, after(state, *ahead))
     (parent_rows,) = after(state, parent_rows)
     kin_x, kin_y = to_x(parent_rows), [to_y(parent_rows, step) for step in steps]
-    groups = [members(0, "kin") + members(1, "root", 1, 1)]
-    groups += [members(step, "root", 1, step) for step in steps if step > 1]
-    state = run([parent_rows, *root_far], tuple(groups), None, state, False)
+    groups = [members(i, "own", 1, i + 1) + members(ny - 1 + i, "root", 1, i + 1) for i in range(ny - 1)]
+    groups[0] += members(2 * ny - 2, "kin")
+    state = run([*own_far, *root_far, parent_rows], tuple(groups), None, state, False)
 
     (kin_x,) = after(state, kin_x)
     tops = [to_y(kin_x[:rows], step) for step in steps]

time: 97.4 us -> 86.9 us (0.89)
  starting transfers between devices: 33.4 us -> 23.3 us
  waiting for transfers between devices: 26.1 us -> 22 us
  Pallas kernels: 33 us -> 36.7 us
    ppermute x6 -> x5, waiting for transfers between devices: 12.4 us -> 0.91 us  [to_y(): lax.ppermute(array, 'ctx', [(index(x, y, k), index(x, y + step, k)) for x...]
    ppermute x6 -> x5, starting transfers between devices: 16 us -> 5.43 us  [to_y(): lax.ppermute(array, 'ctx', [(index(x, y, k), index(x, y + step, k)) for x...]
    ppermute x3, waiting for transfers between devices: 8.26 us -> 15.7 us  [hop(): lax.ppermute(rows_held, 'leaf', pairs if step < leaves - 1 else pairs[1:])]
    pallas_call x6, Pallas kernels: 30.8 us -> 34.6 us  [attend(): pl.pallas_call(functools.partial(attend_kernel, ny, rows, len(arrays), gr...]
    ppermute x4 -> x5, starting transfers between devices: 6.1 us -> 6.57 us  [to_x(): lax.ppermute(array, 'ctx', [(index(x, y, k), index(x + 1, y, k)) for x, y...]
  transfers between devices with their start and end apart: 16 -> 16, of which waited for: 8 -> 7; matrix products, arithmetic and copies ran while one was open for 0% -> 0% of each run, Pallas kernels for 27% -> 34%
where the time goes in v9:
time: 86.9 us; the launch traced here: 86.7 us
  Pallas kernels  36.7 us (42%)
  starting transfers between devices  23.3 us (27%)
  waiting for transfers between devices  22 us (25%)
  local copies, waits for them, and re-layouts  3.15 us (4%)
  other arithmetic  1.04 us (1%)
    pallas_call x6, Pallas kernels, attend(): pl.pallas_call(functools.partial(attend_kernel, ny, rows, len(arrays), gr...  34.6 us
    ppermute x3, waiting for transfers between devices, hop(): lax.ppermute(rows_held, 'leaf', pairs if step < leaves - 1 else pairs[1:])  15.7 us
    ppermute x3, starting transfers between devices, hop(): lax.ppermute(rows_held, 'leaf', pairs if step < leaves - 1 else pairs[1:])  10.3 us
    ppermute x5, starting transfers between devices, to_x(): lax.ppermute(array, 'ctx', [(index(x, y, k), index(x + 1, y, k)) for x, y...  6.57 us
    ppermute x5, starting transfers between devices, to_y(): lax.ppermute(array, 'ctx', [(index(x, y, k), index(x, y + step, k)) for x...  5.43 us
    ppermute x3, waiting for transfers between devices, to_core(): lax.ppermute(array, 'ctx', [(index(x, y, k), index(x, y, k + 1)) for x, y...  4.19 us
    dynamic_slice x2, local copies, waits for them, and re-layouts, halves(): lax.dynamic_slice_in_dim(array, core * half, half, 1)  2.92 us
  transfers between devices with their start and end apart: 16, of which 7 were waited for; matrix products, arithmetic and copies ran while one was open for 0% of the time, Pallas kernels for 34%

profile of v9, /device:TPU:0, one launch (start us, length us, event | category | flops | bytes accessed | tf_op | source)
XLA Modules:
  0.0 86.7 jit_solution(1815060324671057993)
XLA Ops:
  0.0 1.1 %constant_dynamic-slice_fusion.8 = (bf16[128,512]{1,0:T(8,128)(2,1)S(1)}, bf16[128,512]{1,0:T(8,128)(2,1)S(1)}, bf16[128,512]{1,0:T(8,128)(2,1)S(1)}, bf16[128,512]{1,0:T(8,128)(2,1)S(1)}) fusion(bf16[128,1024]{1,0:T(8,128)(2,1)} %param.9, s32[]{:T(128)S(6)} %select_n.8, s32[]{:T(128)S(6)} %select_n.9, bf16[128,1024]{1,0:T(8,128)(2,1)} %param.8), kind=kLoop, calls=%fused_computation.11 | loop fusion | bytes 1048584 | tf_op jit(solution)/shard_map/dynamic_slice | solution.py:280
  1.1 1.8 %constant_dynamic-slice_fusion.1 = (bf16[128,512]{1,0:T(8,128)(2,1)S(1)}, bf16[128,512]{1,0:T(8,128)(2,1)S(1)}, bf16[128,512]{1,0:T(8,128)(2,1)S(1)}, bf16[128,512]{1,0:T(8,128)(2,1)}) fusion(bf16[128,1024]{1,0:T(8,128)(2,1)} %param.11, s32[]{:T(128)S(6)} %select_n.8, s32[]{:T(128)S(6)} %select_n.9, bf16[128,1024]{1,0:T(8,128)(2,1)} %param.10), kind=kLoop, calls=%fused_computation.4 | loop fusion | bytes 1048584 | tf_op jit(solution)/shard_map/dynamic_slice | solution.py:280
  3.0 0.5 collective-permute-start
  3.5 1.5 %collective-permute-done = bf16[256,1024]{1,0:T(8,128)(2,1)S(1)} collective-permute-done((bf16[256,1024]{1,0:T(8,128)(2,1)S(1)}, bf16[256,1024]{1,0:T(8,128)(2,1)S(1)}, u32[]{:S(2)}, u32[]{:S(2)}) %collective-permute-start) | collective-permute-done | bytes 524320 | tf_op jit(solution)/shard_map/ppermute | solution.py:290
  5.1 0.9 %pad_maximum_fusion.1.refs_5_.refs_7_ = bf16[256,1024]{1,0:T(8,128)(2,1)S(1)} fusion(bf16[128,1024]{1,0:T(8,128)(2,1)S(1)} %get-tuple-element.111, bf16[128,512]{1,0:T(8,128)(2,1)S(1)} %get-tuple-element.115, bf16[128,512]{1,0:T(8,128)(2,1)} %get-tuple-element.122), kind=kLoop, calls=%fused_computation.2 | loop fusion | flops 1572864 | bytes 1048576 | tf_op jit(solution)/shard_map/concatenate | solution.py:308
  6.3 0.4 collective-permute-start.2
  6.7 4.7 %collective-permute-start.1 = (bf16[256,1024]{1,0:T(8,128)(2,1)S(1)}, bf16[256,1024]{1,0:T(8,128)(2,1)S(1)}, u32[]{:S(2)}, u32[]{:S(2)}) collective-permute-start(bf16[256,1024]{1,0:T(8,128)(2,1)S(1)} %pad_maximum_fusion.refs_4_.refs_6_.refs_0_), channel_id=1, source_target_pairs={{0,24},{8,0},{16,8},{24,16},{1,25},{9,1},{17,9},{25,17},{2,26},{10... | collective-permute-start | bytes 1572872 | tf_op jit(solution)/shard_map/ppermute | solution.py:321
  11.5 1.5 %collective-permute-start.5 = (bf16[256,1024]{1,0:T(8,128)(2,1)S(1)}, bf16[256,1024]{1,0:T(8,128)(2,1)S(1)}, u32[]{:S(2)}, u32[]{:S(2)}) collective-permute-start(bf16[256,1024]{1,0:T(8,128)(2,1)S(1)} %pad_maximum_fusion.refs_4_.refs_6_.refs_0_), channel_id=1, source_target_pairs={{0,4},{1,5},{2,6},{3,7},{4,0},{5,1},{6,2},{7,3},{8,12},{9,13},{10,... | collective-permute-start | bytes 1572872 | tf_op jit(solution)/shard_map/ppermute | solution.py:296
  13.0 1.5 %collective-permute-start.4 = (bf16[256,1024]{1,0:T(8,128)(2,1)S(1)}, bf16[256,1024]{1,0:T(8,128)(2,1)S(1)}, u32[]{:S(2)}, u32[]{:S(2)}) collective-permute-start(bf16[256,1024]{1,0:T(8,128)(2,1)S(1)} %pad_maximum_fusion.refs_4_.refs_6_.refs_0_), channel_id=1, source_target_pairs={{0,2},{1,3},{2,0},{3,1},{4,6},{5,7},{6,4},{7,5},{8,10},{9,11},{10,... | collective-permute-start | bytes 1572872 | tf_op jit(solution)/shard_map/ppermute | solution.py:293
  14.5 7.4 %shard_map.73 = (f32[8,128]{1,0:T(8,128)S(1)}, f32[4,2,1024,384]{3,2,1,0:T(8,128)S(1)}, bf16[4,2,1024,128]{3,2,1,0:T(8,128)(2,1)S(1)}) custom-call(s32[2,4]{1,0:T(2,128)S(1)} %copy-done, s32[4]{0:T(128)S(1)} %copy-done.1, bf16[128,4096]{1,0:T(8,128)(2,1)S(1)} %get-tuple-element.110.refs_2_, bf16[128,4096]{1,0:T(8,128)(2,1)S(1)} %collective-permute-done.2.refs_3_, ...), custom_call_target="tpu_custom_call" | custom-call | flops 4294967296 | bytes 4194304 | tf_op jit(solution)/shard_map/pallas_call | solution.py:257
  21.9 1.3 %collective-permute-done.1.refs_1_ = bf16[256,1024]{1,0:T(8,128)(2,1)S(1)} collective-permute-done((bf16[256,1024]{1,0:T(8,128)(2,1)S(1)}, bf16[256,1024]{1,0:T(8,128)(2,1)S(1)}, u32[]{:S(2)}, u32[]{:S(2)}) %collective-permute-start.1) | collective-permute-done | bytes 524320 | tf_op jit(solution)/shard_map/ppermute | solution.py:321
  23.2 4.3 %collective-permute-start.3 = (bf16[256,1024]{1,0:T(8,128)(2,1)S(1)}, bf16[256,1024]{1,0:T(8,128)(2,1)S(1)}, u32[]{:S(2)}, u32[]{:S(2)}) collective-permute-start(bf16[256,1024]{1,0:T(8,128)(2,1)S(1)} %collective-permute-done.1.refs_1_), channel_id=1, source_target_pairs={{0,24},{8,0},{16,8},{24,16},{1,25},{9,1},{17,9},{25,17},{2,26},{10... | collective-permute-start | bytes 1572872 | tf_op jit(solution)/shard_map/ppermute | solution.py:321
  27.4 1.5 %collective-permute-start.8 = (bf16[256,1024]{1,0:T(8,128)(2,1)S(1)}, bf16[256,1024]{1,0:T(8,128)(2,1)S(1)}, u32[]{:S(2)}, u32[]{:S(2)}) collective-permute-start(bf16[256,1024]{1,0:T(8,128)(2,1)S(1)} %pad_maximum_fusion.1.refs_5_.refs_7_), channel_id=1, source_target_pairs={{0,4},{1,5},{2,6},{3,7},{4,0},{5,1},{6,2},{7,3},{8,12},{9,13},{10,... | collective-permute-start | bytes 1572872 | tf_op jit(solution)/shard_map/ppermute | solution.py:296
  29.0 1.5 %collective-permute-start.7 = (bf16[256,1024]{1,0:T(8,128)(2,1)S(1)}, bf16[256,1024]{1,0:T(8,128)(2,1)S(1)}, u32[]{:S(2)}, u32[]{:S(2)}) collective-permute-start(bf16[256,1024]{1,0:T(8,128)(2,1)S(1)} %pad_maximum_fusion.1.refs_5_.refs_7_), channel_id=1, source_target_pairs={{0,2},{1,3},{2,0},{3,1},{4,6},{5,7},{6,4},{7,5},{8,10},{9,11},{10,... | collective-permute-start | bytes 1572872 | tf_op jit(solution)/shard_map/ppermute | solution.py:293
  30.5 1.2 %shard_map.75 = (f32[8,128]{1,0:T(8,128)S(1)}, f32[4,2,1024,384]{3,2,1,0:T(8,128)S(1)}, bf16[4,2,1024,128]{3,2,1,0:T(8,128)(2,1)S(1)}) custom-call(s32[2,4]{1,0:T(2,128)S(1)} %copy-done, s32[4]{0:T(128)S(1)} %copy-done.1, bf16[256,1024]{1,0:T(8,128)(2,1)S(1)} %collective-permute-done.4.refs_2_.refs_4_, ...), custom_call_target="tpu_custom_call", output_to_operand_aliasing={{1}: (7, {}), {2}: (8, {})} | custom-call | flops 4294967296 | bytes 4194304 | tf_op jit(solution)/shard_map/pallas_call | solution.py:257
  31.7 6.7 %collective-permute-done.3.refs_2_ = bf16[256,1024]{1,0:T(8,128)(2,1)S(1)} collective-permute-done((bf16[256,1024]{1,0:T(8,128)(2,1)S(1)}, bf16[256,1024]{1,0:T(8,128)(2,1)S(1)}, u32[]{:S(2)}, u32[]{:S(2)}) %collective-permute-start.3) | collective-permute-done | bytes 524320 | tf_op jit(solution)/shard_map/ppermute | solution.py:321
  38.4 1.3 %collective-permute-start.6 = (bf16[256,1024]{1,0:T(8,128)(2,1)S(1)}, bf16[256,1024]{1,0:T(8,128)(2,1)S(1)}, u32[]{:S(2)}, u32[]{:S(2)}) collective-permute-start(bf16[256,1024]{1,0:T(8,128)(2,1)S(1)} %collective-permute-done.3.refs_2_), channel_id=1, source_target_pairs={{8,0},{16,8},{24,16},{9,1},{17,9},{25,17},{10,2},{18,10},{26,18},{... | collective-permute-start | bytes 1572872 | tf_op jit(solution)/shard_map/ppermute | solution.py:321
  39.7 0.9 %collective-permute-done.8.refs_3_.refs_5_ = bf16[256,1024]{1,0:T(8,128)(2,1)S(1)} collective-permute-done((bf16[256,1024]{1,0:T(8,128)(2,1)S(1)}, bf16[256,1024]{1,0:T(8,128)(2,1)S(1)}, u32[]{:S(2)}, u32[]{:S(2)}) %collective-permute-start.8) | collective-permute-done | bytes 524320 | tf_op jit(solution)/shard_map/ppermute | solution.py:296
  40.6 1.2 %collective-permute-done.7.refs_2_.refs_4_ = bf16[256,1024]{1,0:T(8,128)(2,1)S(1)} collective-permute-done((bf16[256,1024]{1,0:T(8,128)(2,1)S(1)}, bf16[256,1024]{1,0:T(8,128)(2,1)S(1)}, u32[]{:S(2)}, u32[]{:S(2)}) %collective-permute-start.7) | collective-permute-done | bytes 524320 | tf_op jit(solution)/shard_map/ppermute | solution.py:293
  41.8 0.5 collective-permute-start.10
  42.3 1.5 %collective-permute-start.11 = (bf16[256,1024]{1,0:T(8,128)(2,1)S(1)}, bf16[256,1024]{1,0:T(8,128)(2,1)S(1)}, u32[]{:S(2)}, u32[]{:S(2)}) collective-permute-start(bf16[256,1024]{1,0:T(8,128)(2,1)S(1)} %collective-permute-done.8.refs_3_.refs_5_), channel_id=1, source_target_pairs={{0,2},{1,3},{2,0},{3,1},{4,6},{5,7},{6,4},{7,5},{8,10},{9,11},{10,... | collective-permute-start | bytes 1572872 | tf_op jit(solution)/shard_map/ppermute | solution.py:293
  43.8 1.2 %shard_map.77 = (f32[8,128]{1,0:T(8,128)S(1)}, f32[4,2,1024,384]{3,2,1,0:T(8,128)S(1)}, bf16[4,2,1024,128]{3,2,1,0:T(8,128)(2,1)S(1)}) custom-call(s32[2,4]{1,0:T(2,128)S(1)} %copy-done, s32[4]{0:T(128)S(1)} %copy-done.1, bf16[256,1024]{1,0:T(8,128)(2,1)S(1)} %collective-permute-done.7.refs_2_.refs_4_, ...), custom_call_target="tpu_custom_call", output_to_operand_aliasing={{1}: (7, {}), {2}: (8, {})} | custom-call | flops 4294967296 | bytes 4194304 | tf_op jit(solution)/shard_map/pallas_call | solution.py:257
  45.0 7.8 %collective-permute-done.6.refs_3_ = bf16[256,1024]{1,0:T(8,128)(2,1)S(1)} collective-permute-done((bf16[256,1024]{1,0:T(8,128)(2,1)S(1)}, bf16[256,1024]{1,0:T(8,128)(2,1)S(1)}, u32[]{:S(2)}, u32[]{:S(2)}) %collective-permute-start.6) | collective-permute-done | bytes 524320 | tf_op jit(solution)/shard_map/ppermute | solution.py:321
  52.7 0.8 shard_map.78
  53.5 1.6 %collective-permute-start.13 = (bf16[256,1024]{1,0:T(8,128)(2,1)S(1)}, bf16[256,1024]{1,0:T(8,128)(2,1)S(1)}, u32[]{:S(2)}, u32[]{:S(2)}) collective-permute-start(bf16[256,1024]{1,0:T(8,128)(2,1)S(1)} %get-tuple-element.94.refs_4_.refs_7_), channel_id=1, source_target_pairs={{0,4},{1,5},{2,6},{3,7},{4,0},{5,1},{6,2},{7,3},{8,12},{9,13},{10,... | collective-permute-start | bytes 1572872 | tf_op jit(solution)/shard_map/ppermute | solution.py:296
  55.1 1.5 %collective-permute-start.9 = (bf16[256,1024]{1,0:T(8,128)(2,1)S(1)}, bf16[256,1024]{1,0:T(8,128)(2,1)S(1)}, u32[]{:S(2)}, u32[]{:S(2)}) collective-permute-start(bf16[256,1024]{1,0:T(8,128)(2,1)S(1)} %get-tuple-element.94.refs_4_.refs_7_), channel_id=1, source_target_pairs={{0,2},{1,3},{2,0},{3,1},{4,6},{5,7},{6,4},{7,5},{8,10},{9,11},{10,... | collective-permute-start | bytes 1572872 | tf_op jit(solution)/shard_map/ppermute | solution.py:293
  56.6 11.1 %shard_map.79 = (f32[8,128]{1,0:T(8,128)S(1)}, f32[4,2,1024,384]{3,2,1,0:T(8,128)S(1)}, bf16[4,2,1024,128]{3,2,1,0:T(8,128)(2,1)S(1)}) custom-call(s32[2,4]{1,0:T(2,128)S(1)} %copy-done, s32[4]{0:T(128)S(1)} %copy-done.1, bf16[256,1024]{1,0:T(8,128)(2,1)S(1)} %collective-permute-done.10.refs_2_.refs_5_, ...), custom_call_target="tpu_custom_call", output_to_operand_aliasing={{1}: (9, {}), {2}: (10, {})} | custom-call | flops 6442450944 | bytes 4194304 | tf_op jit(solution)/shard_map/pallas_call | solution.py:257
  67.8 0.6 collective-permute-start.14
  68.7 7.7 %shard_map.80 = (f32[8,128]{1,0:T(8,128)S(1)}, f32[4,2,1024,384]{3,2,1,0:T(8,128)S(1)}, bf16[4,2,1024,128]{3,2,1,0:T(8,128)(2,1)S(1)}) custom-call(s32[2,4]{1,0:T(2,128)S(1)} %copy-done, s32[4]{0:T(128)S(1)} %copy-done.1, bf16[256,1024]{1,0:T(8,128)(2,1)S(1)} %collective-permute-done.9.refs_2_.refs_4_, ...), custom_call_target="tpu_custom_call", output_to_operand_aliasing={{1}: (7, {}), {2}: (8, {})} | custom-call | flops 4294967296 | bytes 4194304 | tf_op jit(solution)/shard_map/pallas_call | solution.py:257
  76.4 6.0 %shard_map.81 = (bf16[128,4096]{1,0:T(8,128)(2,1)S(1)}, bf16[128,4096]{1,0:T(8,128)(2,1)S(1)}, f32[4,2,1024,384]{3,2,1,0:T(8,128)S(1)}, bf16[4,2,1024,128]{3,2,1,0:T(8,128)(2,1)S(1)}) custom-call(s32[2,4]{1,0:T(2,128)S(1)} %copy-done, s32[4]{0:T(128)S(1)} %copy-done.1, ...), custom_call_target="tpu_custom_call", output_to_operand_aliasing={{2}: (7, {}), {3}: (8, {})} | custom-call | flops 2147483648 | bytes 4194304 | tf_op jit(solution)/shard_map/pallas_call | solution.py:257
  82.5 2.6 %collective-permute-done.15.got_ref = bf16[128,4096]{1,0:T(8,128)(2,1)S(1)} collective-permute-done((bf16[128,4096]{1,0:T(8,128)(2,1)S(1)}, bf16[128,4096]{1,0:T(8,128)(2,1)S(1)}, u32[]{:S(2)}, u32[]{:S(2)}) %collective-permute-start.15) | collective-permute-done | bytes 1048608 | tf_op jit(solution)/shard_map/ppermute | solution.py:290
  85.2 1.3 %shard_map.82 = bf16[128,8192]{1,0:T(8,128)(2,1)} custom-call(bf16[128,4096]{1,0:T(8,128)(2,1)S(1)} %get-tuple-element.107.mine_ref, bf16[128,4096]{1,0:T(8,128)(2,1)S(1)} %collective-permute-done.15.got_ref), custom_call_target="tpu_custom_call" | custom-call | tf_op jit(solution)/shard_map/pallas_call | solution.py:216
  (25 shorter events, 0.7 us)
Async XLA Ops:
  2.9 3.2 %copy-start.2 = (bf16[128,8192]{1,0:T(8,128)(2,1)S(1)}, bf16[128,8192]{1,0:T(8,128)(2,1)}, u32[]{:S(2)}) copy-start(bf16[128,8192]{1,0:T(8,128)(2,1)} %param.7) | copy-start | bytes 6291460
  3.0 2.1 %collective-permute-start = (bf16[256,1024]{1,0:T(8,128)(2,1)S(1)}, bf16[256,1024]{1,0:T(8,128)(2,1)S(1)}, u32[]{:S(2)}, u32[]{:S(2)}) collective-permute-start(bf16[256,1024]{1,0:T(8,128)(2,1)S(1)} %maximum_maximum_fusion), channel_id=1, source_target_pairs={{0,1},{1,0},{2,3},{3,2},{4,5},{5,4},{6,7},{7,6},{8,9},{9,8},{10,11... | collective-permute-start | bytes 1572872 | tf_op jit(solution)/shard_map/ppermute | solution.py:290
  6.1 8.4 %copy-start = (s32[2,4]{1,0:T(2,128)S(1)}, s32[2,4]{1,0:T(2,128)}, u32[]{:S(2)}) copy-start(s32[2,4]{1,0:T(2,128)} %refs_0_.11) | copy-start | bytes 100
  6.1 8.4 %copy-start.1 = (s32[4]{0:T(128)S(1)}, s32[4]{0:T(128)}, u32[]{:S(2)}) copy-start(s32[4]{0:T(128)} %refs_1_.11) | copy-start | bytes 52
  6.3 8.2 %collective-permute-start.2 = (bf16[128,4096]{1,0:T(8,128)(2,1)S(1)}, bf16[128,4096]{1,0:T(8,128)(2,1)S(1)}, u32[]{:S(2)}, u32[]{:S(2)}) collective-permute-start(bf16[128,4096]{1,0:T(8,128)(2,1)S(1)} %get-tuple-element.59), channel_id=1, source_target_pairs={{0,1},{1,0},{2,3},{3,2},{4,5},{5,4},{6,7},{7,6},{8,9},{9,8},{10,11... | collective-permute-start | bytes 3145736 | tf_op jit(solution)/shard_map/ppermute | solution.py:290
  6.7 16.5 %collective-permute-start.1 = (bf16[256,1024]{1,0:T(8,128)(2,1)S(1)}, bf16[256,1024]{1,0:T(8,128)(2,1)S(1)}, u32[]{:S(2)}, u32[]{:S(2)}) collective-permute-start(bf16[256,1024]{1,0:T(8,128)(2,1)S(1)} %pad_maximum_fusion.refs_4_.refs_6_.refs_0_), channel_id=1, source_target_pairs={{0,24},{8,0},{16,8},{24,16},{1,25},{9,1},{17,9},{25,17},{2,26},{10... | collective-permute-start | bytes 1572872 | tf_op jit(solution)/shard_map/ppermute | solution.py:321
  11.5 19.0 %collective-permute-start.5 = (bf16[256,1024]{1,0:T(8,128)(2,1)S(1)}, bf16[256,1024]{1,0:T(8,128)(2,1)S(1)}, u32[]{:S(2)}, u32[]{:S(2)}) collective-permute-start(bf16[256,1024]{1,0:T(8,128)(2,1)S(1)} %pad_maximum_fusion.refs_4_.refs_6_.refs_0_), channel_id=1, source_target_pairs={{0,4},{1,5},{2,6},{3,7},{4,0},{5,1},{6,2},{7,3},{8,12},{9,13},{10,... | collective-permute-start | bytes 1572872 | tf_op jit(solution)/shard_map/ppermute | solution.py:296
  13.0 17.5 %collective-permute-start.4 = (bf16[256,1024]{1,0:T(8,128)(2,1)S(1)}, bf16[256,1024]{1,0:T(8,128)(2,1)S(1)}, u32[]{:S(2)}, u32[]{:S(2)}) collective-permute-start(bf16[256,1024]{1,0:T(8,128)(2,1)S(1)} %pad_maximum_fusion.refs_4_.refs_6_.refs_0_), channel_id=1, source_target_pairs={{0,2},{1,3},{2,0},{3,1},{4,6},{5,7},{6,4},{7,5},{8,10},{9,11},{10,... | collective-permute-start | bytes 1572872 | tf_op jit(solution)/shard_map/ppermute | solution.py:293
  23.2 15.2 %collective-permute-start.3 = (bf16[256,1024]{1,0:T(8,128)(2,1)S(1)}, bf16[256,1024]{1,0:T(8,128)(2,1)S(1)}, u32[]{:S(2)}, u32[]{:S(2)}) collective-permute-start(bf16[256,1024]{1,0:T(8,128)(2,1)S(1)} %collective-permute-done.1.refs_1_), channel_id=1, source_target_pairs={{0,24},{8,0},{16,8},{24,16},{1,25},{9,1},{17,9},{25,17},{2,26},{10... | collective-permute-start | bytes 1572872 | tf_op jit(solution)/shard_map/ppermute | solution.py:321
  27.4 13.1 %collective-permute-start.8 = (bf16[256,1024]{1,0:T(8,128)(2,1)S(1)}, bf16[256,1024]{1,0:T(8,128)(2,1)S(1)}, u32[]{:S(2)}, u32[]{:S(2)}) collective-permute-start(bf16[256,1024]{1,0:T(8,128)(2,1)S(1)} %pad_maximum_fusion.1.refs_5_.refs_7_), channel_id=1, source_target_pairs={{0,4},{1,5},{2,6},{3,7},{4,0},{5,1},{6,2},{7,3},{8,12},{9,13},{10,... | collective-permute-start | bytes 1572872 | tf_op jit(solution)/shard_map/ppermute | solution.py:296
  29.0 12.8 %collective-permute-start.7 = (bf16[256,1024]{1,0:T(8,128)(2,1)S(1)}, bf16[256,1024]{1,0:T(8,128)(2,1)S(1)}, u32[]{:S(2)}, u32[]{:S(2)}) collective-permute-start(bf16[256,1024]{1,0:T(8,128)(2,1)S(1)} %pad_maximum_fusion.1.refs_5_.refs_7_), channel_id=1, source_target_pairs={{0,2},{1,3},{2,0},{3,1},{4,6},{5,7},{6,4},{7,5},{8,10},{9,11},{10,... | collective-permute-start | bytes 1572872 | tf_op jit(solution)/shard_map/ppermute | solution.py:293
  38.4 14.4 %collective-permute-start.6 = (bf16[256,1024]{1,0:T(8,128)(2,1)S(1)}, bf16[256,1024]{1,0:T(8,128)(2,1)S(1)}, u32[]{:S(2)}, u32[]{:S(2)}) collective-permute-start(bf16[256,1024]{1,0:T(8,128)(2,1)S(1)} %collective-permute-done.3.refs_2_), channel_id=1, source_target_pairs={{8,0},{16,8},{24,16},{9,1},{17,9},{25,17},{10,2},{18,10},{26,18},{... | collective-permute-start | bytes 1572872 | tf_op jit(solution)/shard_map/ppermute | solution.py:321
  41.8 14.8 %collective-permute-start.10 = (bf16[256,1024]{1,0:T(8,128)(2,1)S(1)}, bf16[256,1024]{1,0:T(8,128)(2,1)S(1)}, u32[]{:S(2)}, u32[]{:S(2)}) collective-permute-start(bf16[256,1024]{1,0:T(8,128)(2,1)S(1)} %collective-permute-done.4.refs_2_.refs_4_), channel_id=1, source_target_pairs={{0,4},{1,5},{2,6},{3,7},{4,0},{5,1},{6,2},{7,3},{8,12},{9,13},{10,... | collective-permute-start | bytes 1572872 | tf_op jit(solution)/shard_map/ppermute | solution.py:296
  42.3 14.3 %collective-permute-start.11 = (bf16[256,1024]{1,0:T(8,128)(2,1)S(1)}, bf16[256,1024]{1,0:T(8,128)(2,1)S(1)}, u32[]{:S(2)}, u32[]{:S(2)}) collective-permute-start(bf16[256,1024]{1,0:T(8,128)(2,1)S(1)} %collective-permute-done.8.refs_3_.refs_5_), channel_id=1, source_target_pairs={{0,2},{1,3},{2,0},{3,1},{4,6},{5,7},{6,4},{7,5},{8,10},{9,11},{10,... | collective-permute-start | bytes 1572872 | tf_op jit(solution)/shard_map/ppermute | solution.py:293
  53.5 14.2 %collective-permute-start.13 = (bf16[256,1024]{1,0:T(8,128)(2,1)S(1)}, bf16[256,1024]{1,0:T(8,128)(2,1)S(1)}, u32[]{:S(2)}, u32[]{:S(2)}) collective-permute-start(bf16[256,1024]{1,0:T(8,128)(2,1)S(1)} %get-tuple-element.94.refs_4_.refs_7_), channel_id=1, source_target_pairs={{0,4},{1,5},{2,6},{3,7},{4,0},{5,1},{6,2},{7,3},{8,12},{9,13},{10,... | collective-permute-start | bytes 1572872 | tf_op jit(solution)/shard_map/ppermute | solution.py:296
  55.1 13.2 %collective-permute-start.9 = (bf16[256,1024]{1,0:T(8,128)(2,1)S(1)}, bf16[256,1024]{1,0:T(8,128)(2,1)S(1)}, u32[]{:S(2)}, u32[]{:S(2)}) collective-permute-start(bf16[256,1024]{1,0:T(8,128)(2,1)S(1)} %get-tuple-element.94.refs_4_.refs_7_), channel_id=1, source_target_pairs={{0,2},{1,3},{2,0},{3,1},{4,6},{5,7},{6,4},{7,5},{8,10},{9,11},{10,... | collective-permute-start | bytes 1572872 | tf_op jit(solution)/shard_map/ppermute | solution.py:293
  67.8 8.6 %collective-permute-start.14 = (bf16[128,1024]{1,0:T(8,128)(2,1)S(1)}, bf16[128,1024]{1,0:T(8,128)(2,1)S(1)}, u32[]{:S(2)}, u32[]{:S(2)}) collective-permute-start(bf16[128,1024]{1,0:T(8,128)(2,1)S(1)} %slice.16), channel_id=1, source_target_pairs={{0,2},{1,3},{2,0},{3,1},{4,6},{5,7},{6,4},{7,5},{8,10},{9,11},{10,... | collective-permute-start | bytes 786440 | tf_op jit(solution)/shard_map/ppermute | solution.py:293
  68.4 8.0 %collective-permute-start.12 = (bf16[128,1024]{1,0:T(8,128)(2,1)S(1)}, bf16[128,1024]{1,0:T(8,128)(2,1)S(1)}, u32[]{:S(2)}, u32[]{:S(2)}) collective-permute-start(bf16[128,1024]{1,0:T(8,128)(2,1)S(1)} %slice.14), channel_id=1, source_target_pairs={{0,4},{1,5},{2,6},{3,7},{4,0},{5,1},{6,2},{7,3},{8,12},{9,13},{10,... | collective-permute-start | bytes 786440 | tf_op jit(solution)/shard_map/ppermute | solution.py:296
  82.4 2.7 %collective-permute-start.15 = (bf16[128,4096]{1,0:T(8,128)(2,1)S(1)}, bf16[128,4096]{1,0:T(8,128)(2,1)S(1)}, u32[]{:S(2)}, u32[]{:S(2)}) collective-permute-start(bf16[128,4096]{1,0:T(8,128)(2,1)S(1)} %get-tuple-element.108), channel_id=1, source_target_pairs={{0,1},{1,0},{2,3},{3,2},{4,5},{5,4},{6,7},{7,6},{8,9},{9,8},{10,11... | collective-permute-start | bytes 3145736 | tf_op jit(solution)/shard_map/ppermute | solution.py:290

commit v10 on v9

--- a/solution.py
+++ b/solution.py
@@ -15,7 +15,7 @@
 HALF_KV = KVH // 2
 NEG = -1e30
 EXP_SCALE = math.log2(math.e) / math.sqrt(HD)
-ROW_BLOCK = 256
+ROW_BLOCK = 128
 
 
 def attend_kernel(ny, rows, arrays, groups, first, last, *refs):
@@ -164,18 +164,17 @@
     return values
 
 
-def pick(state, table, leaves, arrays):
+def pick(state, table, choose, arrays):
     mark, held, prepared = state
     count = len(arrays)
 
     def kernel(table_ref, mark_ref, *refs):
         out_ref, mark_out_ref, _, _, sem = refs[count + 2 :]
-        group = lax.axis_index("leaf")
-        parent = table_ref[0, group]
         mark_out_ref[...] = mark_ref[...]
-        for ahead, ref in enumerate(refs[:count]):
-
-            @pl.when(parent == lax.rem(group + ahead, leaves))
+        chosen = choose(table_ref, lax.axis_index("leaf"))
+        for i, ref in enumerate(refs[:count]):
+
+            @pl.when(chosen == i)
             def _():
                 copy = pltpu.make_async_copy(ref, out_ref, sem)
                 copy.start()
@@ -197,6 +196,36 @@
         compiler_params=pltpu.CompilerParams(vmem_limit_bytes=4 * 2**20),
     )(table, mark, *arrays, in_vmem(held), in_vmem(prepared))
     return picked
+
+
+def pack(*arrays):
+    rows, width = arrays[0].shape
+    half = width // 2
+
+    def kernel(*refs):
+        *in_refs, mine_ref, other_ref, sems = refs
+        core = lax.rem(lax.axis_index("ctx"), 2)
+        copies = []
+        for out_ref, place in ((other_ref, 1 - core), (mine_ref, core)):
+            columns = pl.ds(pl.multiple_of(place * half, half), half)
+            for i, ref in enumerate(in_refs):
+                target = out_ref.at[pl.ds(i // 2 * rows, rows), pl.ds(i % 2 * half, half)]
+                copies.append(pltpu.make_async_copy(ref.at[:, columns], target, sems.at[len(copies)]))
+        for copy in copies:
+            copy.start()
+        for copy in copies:
+            copy.wait()
+
+    anywhere = pl.BlockSpec(memory_space=pl.ANY)
+    packed = jax.ShapeDtypeStruct((len(arrays) // 2 * rows, width), arrays[0].dtype)
+    return pl.pallas_call(
+        kernel,
+        in_specs=[anywhere] * len(arrays),
+        out_specs=[anywhere] * 2,
+        out_shape=[packed] * 2,
+        scratch_shapes=[pltpu.SemaphoreType.DMA((2 * len(arrays),))],
+        compiler_params=pltpu.CompilerParams(vmem_limit_bytes=4 * 2**20),
+    )(*(pltpu.with_memory_space_constraint(array, pltpu.HBM) for array in arrays))
 
 
 def assemble(mine, got):
@@ -295,17 +324,11 @@
     def to_y(array, step):
         return lax.ppermute(array, "ctx", [(index(x, y, k), index(x, y + step, k)) for x, y, k in places])
 
-    def packed(keys, values):
-        (key_mine, key_other), (value_mine, value_other) = halves(keys), halves(values)
-        return jnp.concatenate([key_mine, value_mine], axis=1), jnp.concatenate([key_other, value_other], axis=1)
-
-    own_mine, own_other = packed(seg_keys, seg_values)
-    root_mine, root_other = packed(root_keys, root_values)
-    sent = jnp.concatenate([own_other, root_other], axis=0)
+    mine, sent = pack(seg_keys, seg_values, root_keys, root_values)
     queries, got = lax.optimization_barrier((queries, to_core(sent)))
     q_mine, q_other = halves(queries)
-    own = jnp.concatenate([own_mine, got[:rows]], axis=0)
-    root = jnp.concatenate([root_mine, got[rows:]], axis=0)
+    own = jnp.concatenate([mine[:rows], got[:rows]], axis=0)
+    root = jnp.concatenate([mine[rows:], got[rows:]], axis=0)
     run = functools.partial(attend, ny, rows, (expansion, root_offsets))
     steps = range(1, ny)
 
@@ -320,35 +343,53 @@
         pairs = [(i, (i - 1) % leaves) for i in range(leaves)]
         return lax.ppermute(rows_held, "leaf", pairs if step < leaves - 1 else pairs[1:])
 
+    direct = leaves == 4
     ahead = [own]
-    if leaves > 1:
+    if direct:
+        for pairs in (((1, 0), (2, 1), (3, 2)), ((0, 2), (3, 1)), ((0, 1), (1, 2))):
+            ahead.append(lax.ppermute(own, "leaf", pairs))
+    elif leaves > 1:
         ahead.append(hop(1, own))
-    own, root, q_other = lax.optimization_barrier((own, root, q_other))
-    q_pair = (q_mine, to_core(q_other))
+    own, q_got = lax.optimization_barrier((own, to_core(q_other)))
+    q_pair = (q_mine, q_got)
     own_x, own_y = to_x(own), [to_y(own, step) for step in steps]
+    state = run([own, root], (members(0, "own") + members(1, "root"),), q_pair, None, False)
+
+    (root,) = after(state, root)
     root_x, root_y = to_x(root), [to_y(root, step) for step in steps]
-    state = run([own, root], (members(0, "own") + members(1, "root"),), q_pair, None, False)
 
     def near(kind):
         groups = [members(0, kind, 1) + members(1, kind, 0, 1)]
         return groups + [members(step, kind, 0, step) for step in steps if step > 1]
 
-    if leaves > 2:
+    if leaves > 2 and not direct:
         (held,) = fence(state, ahead[-1])
         ahead[-1] = held
         ahead.append(hop(2, held))
     own_x, *own_y = after(state, own_x, *own_y)
     state = run([own_x, *own_y], tuple(near("own")), None, state, False)
-    for step in range(3, leaves):
-        (held,) = fence(state, ahead[-1])
-        ahead[-1] = held
-        ahead.append(hop(step, held))
+    if direct:
+        ahead = after(state, *ahead)
+        relay = pick(state, expansion, lambda table, g: jnp.where(table[0, 0] == 3, 1, 0), ahead[1:3])
+        ahead.append(lax.ppermute(relay, "leaf", [(1, 0)]))
+    else:
+        for step in range(3, leaves):
+            (held,) = fence(state, ahead[-1])
+            ahead[-1] = held
+            ahead.append(hop(step, held))
     own_x, root_x, *root_y = after(state, own_x, root_x, *root_y)
     own_far = [to_y(own_x, step) for step in steps]
     root_far = [to_x(array) for array in root_y]
     state = run([root_x, *root_y], tuple(near("root")), None, state, False)
 
-    parent_rows = pick(state, expansion, leaves, after(state, *ahead))
+    def choose(table, g):
+        offset = table[0, g] - g
+        if not direct:
+            return lax.rem(offset + leaves, leaves)
+        far_one = jnp.where(g == 0, 4, 2)
+        return jnp.where(offset == 0, 0, jnp.where(offset == 1, 1, jnp.where(offset == -1, 3, far_one)))
+
+    parent_rows = pick(state, expansion, choose, after(state, *ahead))
     (parent_rows,) = after(state, parent_rows)
     kin_x, kin_y = to_x(parent_rows), [to_y(parent_rows, step) for step in steps]
     groups = [members(i, "own", 1, i + 1) + members(ny - 1 + i, "root", 1, i + 1) for i in range(ny - 1)]

time: 86.9 us -> 89.6 us (1.031)
  Pallas kernels: 36.7 us -> 45.4 us
  waiting for transfers between devices: 22 us -> 17.9 us
  local copies, waits for them, and re-layouts: 3.15 us -> 1.79 us
  other arithmetic: 1.04 us -> 0.07 us
    ppermute x3 -> x4, waiting for transfers between devices: 15.7 us -> 2.94 us  [the longest x1 1.8 us: on_device(): ahead.append(lax.ppermute(relay, 'leaf', [(1, 0)]))]
    ppermute x5, waiting for transfers between devices: 0.91 us -> 9.49 us  [to_y(): lax.ppermute(array, 'ctx', [(index(x, y, k), index(x, y + step, k)) for x...]
    pallas_call x6, Pallas kernels: 34.6 us -> 41.3 us  [attend(): pl.pallas_call(functools.partial(attend_kernel, ny, rows, len(arrays), gr...]
    pallas_call x2 -> x1, Pallas kernels: 0.01 us -> 1.35 us  [pack(): pl.pallas_call(kernel, in_specs=[anywhere] * len(arrays), out_specs=[anyw...]
    ppermute x5, starting transfers between devices: 5.43 us -> 6.68 us  [to_y(): lax.ppermute(array, 'ctx', [(index(x, y, k), index(x, y + step, k)) for x...]
    dynamic_slice x2 -> x1, local copies, waits for them, and re-layouts: 2.92 us -> 1.68 us  [halves(): lax.dynamic_slice_in_dim(array, core * half, half, 1)]
    concatenate x3 -> x2, other arithmetic: 1.04 us -> 0.07 us  [the longest x1 0.04 us: on_device(): own = jnp.concatenate([mine[:rows], got[:rows]], axis=0)]
    ppermute x3 -> x4, starting transfers between devices: 10.3 us -> 9.55 us  [the longest x3 8.26 us: on_device(): ahead.append(lax.ppermute(own, 'leaf', pairs))]
  transfers between devices with their start and end apart: 16 -> 17, of which waited for: 7 -> 7; matrix products, arithmetic and copies ran while one was open for 0% -> 0% of each run, Pallas kernels for 34% -> 41%
where the time goes in v10:
time: 89.6 us; the launch traced here: 89.3 us
  Pallas kernels  45.4 us (51%)
  starting transfers between devices  23.8 us (27%)
  waiting for transfers between devices  17.9 us (20%)
  local copies, waits for them, and re-layouts  1.79 us (2%)
    pallas_call x6, Pallas kernels, attend(): pl.pallas_call(functools.partial(attend_kernel, ny, rows, len(arrays), gr...  41.3 us
    ppermute x5, waiting for transfers between devices, to_y(): lax.ppermute(array, 'ctx', [(index(x, y, k), index(x, y + step, k)) for x...  9.49 us
    ppermute x3, starting transfers between devices, on_device(): ahead.append(lax.ppermute(own, 'leaf', pairs))  8.26 us
    ppermute x5, starting transfers between devices, to_y(): lax.ppermute(array, 'ctx', [(index(x, y, k), index(x, y + step, k)) for x...  6.68 us
    ppermute x5, starting transfers between devices, to_x(): lax.ppermute(array, 'ctx', [(index(x, y, k), index(x + 1, y, k)) for x, y...  6.57 us
    ppermute x3, waiting for transfers between devices, to_core(): lax.ppermute(array, 'ctx', [(index(x, y, k), index(x, y, k + 1)) for x, y...  4.19 us
    ppermute x1, waiting for transfers between devices, on_device(): ahead.append(lax.ppermute(relay, 'leaf', [(1, 0)]))  1.8 us
  transfers between devices with their start and end apart: 17, of which 7 were waited for; matrix products, arithmetic and copies ran while one was open for 0% of the time, Pallas kernels for 41%

profile of v10, /device:TPU:0, one launch (start us, length us, event | category | flops | bytes accessed | tf_op | source)
XLA Modules:
  0.0 89.3 jit_solution(9984120157873254407)
XLA Ops:
  0.0 1.3 %shard_map.73 = (bf16[256,1024]{1,0:T(8,128)(2,1)S(1)}, bf16[256,1024]{1,0:T(8,128)(2,1)S(1)}) custom-call(bf16[128,1024]{1,0:T(8,128)(2,1)} %refs_0_.7, bf16[128,1024]{1,0:T(8,128)(2,1)} %refs_1_.7, bf16[128,1024]{1,0:T(8,128)(2,1)} %refs_2_.1, bf16[128,1024]{1,0:T(8,128)(2,1)} %refs_3_.1), custom_call_target="tpu_custom_call" | custom-call | tf_op jit(solution)/shard_map/pallas_call | solution.py:221
  1.4 0.5 collective-permute-start
  1.9 1.5 %collective-permute-done = bf16[256,1024]{1,0:T(8,128)(2,1)S(1)} collective-permute-done((bf16[256,1024]{1,0:T(8,128)(2,1)S(1)}, bf16[256,1024]{1,0:T(8,128)(2,1)S(1)}, u32[]{:S(2)}, u32[]{:S(2)}) %collective-permute-start) | collective-permute-done | bytes 524320 | tf_op jit(solution)/shard_map/ppermute | solution.py:319
  3.4 1.7 %constant_dynamic-slice_fusion = (bf16[128,4096]{1,0:T(8,128)(2,1)S(1)}, bf16[128,4096]{1,0:T(8,128)(2,1)S(1)}) fusion(bf16[128,8192]{1,0:T(8,128)(2,1)} %param.7, s32[]{:T(128)S(6)} %select_n.7, s32[]{:T(128)S(6)} %select_n.6), kind=kLoop, calls=%fused_computation.2 | loop fusion | bytes 4194312 | tf_op jit(solution)/shard_map/dynamic_slice | solution.py:309
  5.7 4.7 %collective-permute-start.3 = (bf16[256,1024]{1,0:T(8,128)(2,1)S(1)}, bf16[256,1024]{1,0:T(8,128)(2,1)S(1)}, u32[]{:S(2)}, u32[]{:S(2)}) collective-permute-start(bf16[256,1024]{1,0:T(8,128)(2,1)S(1)} %pad_maximum_fusion.refs_4_.refs_6_.refs_0_), channel_id=1, source_target_pairs={{0,8},{8,16},{1,9},{9,17},{2,10},{10,18},{3,11},{11,19},{4,12},{12... | collective-permute-start | bytes 1572872 | tf_op jit(solution)/shard_map/ppermute | solution.py:350
  10.3 2.3 %collective-permute-start.2 = (bf16[256,1024]{1,0:T(8,128)(2,1)S(1)}, bf16[256,1024]{1,0:T(8,128)(2,1)S(1)}, u32[]{:S(2)}, u32[]{:S(2)}) collective-permute-start(bf16[256,1024]{1,0:T(8,128)(2,1)S(1)} %pad_maximum_fusion.refs_4_.refs_6_.refs_0_), channel_id=1, source_target_pairs={{0,16},{24,8},{1,17},{25,9},{2,18},{26,10},{3,19},{27,11},{4,20},{... | collective-permute-start | bytes 1572872 | tf_op jit(solution)/shard_map/ppermute | solution.py:350
  12.6 1.3 %collective-permute-start.1 = (bf16[256,1024]{1,0:T(8,128)(2,1)S(1)}, bf16[256,1024]{1,0:T(8,128)(2,1)S(1)}, u32[]{:S(2)}, u32[]{:S(2)}) collective-permute-start(bf16[256,1024]{1,0:T(8,128)(2,1)S(1)} %pad_maximum_fusion.refs_4_.refs_6_.refs_0_), channel_id=1, source_target_pairs={{8,0},{16,8},{24,16},{9,1},{17,9},{25,17},{10,2},{18,10},{26,18},{... | collective-permute-start | bytes 1572872 | tf_op jit(solution)/shard_map/ppermute | solution.py:350
  14.0 1.6 %collective-permute-start.6 = (bf16[256,1024]{1,0:T(8,128)(2,1)S(1)}, bf16[256,1024]{1,0:T(8,128)(2,1)S(1)}, u32[]{:S(2)}, u32[]{:S(2)}) collective-permute-start(bf16[256,1024]{1,0:T(8,128)(2,1)S(1)} %pad_maximum_fusion.refs_4_.refs_6_.refs_0_), channel_id=1, source_target_pairs={{0,4},{1,5},{2,6},{3,7},{4,0},{5,1},{6,2},{7,3},{8,12},{9,13},{10,... | collective-permute-start | bytes 1572872 | tf_op jit(solution)/shard_map/ppermute | solution.py:325
  15.5 1.5 %collective-permute-start.5 = (bf16[256,1024]{1,0:T(8,128)(2,1)S(1)}, bf16[256,1024]{1,0:T(8,128)(2,1)S(1)}, u32[]{:S(2)}, u32[]{:S(2)}) collective-permute-start(bf16[256,1024]{1,0:T(8,128)(2,1)S(1)} %pad_maximum_fusion.refs_4_.refs_6_.refs_0_), channel_id=1, source_target_pairs={{0,2},{1,3},{2,0},{3,1},{4,6},{5,7},{6,4},{7,5},{8,10},{9,11},{10,... | collective-permute-start | bytes 1572872 | tf_op jit(solution)/shard_map/ppermute | solution.py:322
  17.1 7.2 %shard_map.74 = (f32[8,128]{1,0:T(8,128)S(1)}, f32[4,2,1024,384]{3,2,1,0:T(8,128)S(1)}, bf16[4,2,1024,128]{3,2,1,0:T(8,128)(2,1)S(1)}) custom-call(s32[2,4]{1,0:T(2,128)S(1)} %copy-done, s32[4]{0:T(128)S(1)} %copy-done.1, bf16[128,4096]{1,0:T(8,128)(2,1)S(1)} %get-tuple-element.115.refs_2_, bf16[128,4096]{1,0:T(8,128)(2,1)S(1)} %collective-permute-done.4.refs_3_, ...), custom_call_target="tpu_custom_call" | custom-call | flops 4294967296 | bytes 4194304 | tf_op jit(solution)/shard_map/pallas_call | solution.py:286
  24.3 3.7 %collective-permute-done.6.refs_3_.refs_5_ = bf16[256,1024]{1,0:T(8,128)(2,1)S(1)} collective-permute-done((bf16[256,1024]{1,0:T(8,128)(2,1)S(1)}, bf16[256,1024]{1,0:T(8,128)(2,1)S(1)}, u32[]{:S(2)}, u32[]{:S(2)}) %collective-permute-start.6) | collective-permute-done | bytes 524320 | tf_op jit(solution)/shard_map/ppermute | solution.py:325
  27.9 1.5 %collective-permute-start.9 = (bf16[256,1024]{1,0:T(8,128)(2,1)S(1)}, bf16[256,1024]{1,0:T(8,128)(2,1)S(1)}, u32[]{:S(2)}, u32[]{:S(2)}) collective-permute-start(bf16[256,1024]{1,0:T(8,128)(2,1)S(1)} %pad_maximum_fusion.1.refs_5_.refs_7_), channel_id=1, source_target_pairs={{0,4},{1,5},{2,6},{3,7},{4,0},{5,1},{6,2},{7,3},{8,12},{9,13},{10,... | collective-permute-start | bytes 1572872 | tf_op jit(solution)/shard_map/ppermute | solution.py:325
  29.5 1.5 %collective-permute-start.8 = (bf16[256,1024]{1,0:T(8,128)(2,1)S(1)}, bf16[256,1024]{1,0:T(8,128)(2,1)S(1)}, u32[]{:S(2)}, u32[]{:S(2)}) collective-permute-start(bf16[256,1024]{1,0:T(8,128)(2,1)S(1)} %pad_maximum_fusion.1.refs_5_.refs_7_), channel_id=1, source_target_pairs={{0,2},{1,3},{2,0},{3,1},{4,6},{5,7},{6,4},{7,5},{8,10},{9,11},{10,... | collective-permute-start | bytes 1572872 | tf_op jit(solution)/shard_map/ppermute | solution.py:322
  30.9 1.2 %shard_map.75 = (f32[8,128]{1,0:T(8,128)S(1)}, f32[4,2,1024,384]{3,2,1,0:T(8,128)S(1)}, bf16[4,2,1024,128]{3,2,1,0:T(8,128)(2,1)S(1)}) custom-call(s32[2,4]{1,0:T(2,128)S(1)} %copy-done, s32[4]{0:T(128)S(1)} %copy-done.1, bf16[256,1024]{1,0:T(8,128)(2,1)S(1)} %collective-permute-done.5.refs_2_.refs_4_, ...), custom_call_target="tpu_custom_call", output_to_operand_aliasing={{1}: (7, {}), {2}: (8, {})} | custom-call | flops 4294967296 | bytes 4194304 | tf_op jit(solution)/shard_map/pallas_call | solution.py:286
  32.1 1.1 %collective-permute-done.2.refs_1_.refs_2_ = bf16[256,1024]{1,0:T(8,128)(2,1)S(1)} collective-permute-done((bf16[256,1024]{1,0:T(8,128)(2,1)S(1)}, bf16[256,1024]{1,0:T(8,128)(2,1)S(1)}, u32[]{:S(2)}, u32[]{:S(2)}) %collective-permute-start.2) | collective-permute-done | bytes 524320 | tf_op jit(solution)/shard_map/ppermute | solution.py:350
  33.3 0.6 shard_map.76
  33.9 1.3 %collective-permute-start.7 = (bf16[256,1024]{1,0:T(8,128)(2,1)S(1)}, bf16[256,1024]{1,0:T(8,128)(2,1)S(1)}, u32[]{:S(2)}, u32[]{:S(2)}) collective-permute-start(bf16[256,1024]{1,0:T(8,128)(2,1)S(1)} %get-tuple-element.81), channel_id=1, source_target_pairs={{8,0},{9,1},{10,2},{11,3},{12,4},{13,5},{14,6},{15,7}} | collective-permute-start | bytes 1572872 | tf_op jit(solution)/shard_map/ppermute | solution.py:374
  35.2 5.8 %collective-permute-done.9.refs_3_.refs_5_ = bf16[256,1024]{1,0:T(8,128)(2,1)S(1)} collective-permute-done((bf16[256,1024]{1,0:T(8,128)(2,1)S(1)}, bf16[256,1024]{1,0:T(8,128)(2,1)S(1)}, u32[]{:S(2)}, u32[]{:S(2)}) %collective-permute-start.9) | collective-permute-done | bytes 524320 | tf_op jit(solution)/shard_map/ppermute | solution.py:325
  41.0 1.2 %collective-permute-done.8.refs_2_.refs_4_ = bf16[256,1024]{1,0:T(8,128)(2,1)S(1)} collective-permute-done((bf16[256,1024]{1,0:T(8,128)(2,1)S(1)}, bf16[256,1024]{1,0:T(8,128)(2,1)S(1)}, u32[]{:S(2)}, u32[]{:S(2)}) %collective-permute-start.8) | collective-permute-done | bytes 524320 | tf_op jit(solution)/shard_map/ppermute | solution.py:322
  42.7 1.5 %collective-permute-start.12 = (bf16[256,1024]{1,0:T(8,128)(2,1)S(1)}, bf16[256,1024]{1,0:T(8,128)(2,1)S(1)}, u32[]{:S(2)}, u32[]{:S(2)}) collective-permute-start(bf16[256,1024]{1,0:T(8,128)(2,1)S(1)} %collective-permute-done.9.refs_3_.refs_5_), channel_id=1, source_target_pairs={{0,2},{1,3},{2,0},{3,1},{4,6},{5,7},{6,4},{7,5},{8,10},{9,11},{10,... | collective-permute-start | bytes 1572872 | tf_op jit(solution)/shard_map/ppermute | solution.py:322
  44.2 7.8 %shard_map.77 = (f32[8,128]{1,0:T(8,128)S(1)}, f32[4,2,1024,384]{3,2,1,0:T(8,128)S(1)}, bf16[4,2,1024,128]{3,2,1,0:T(8,128)(2,1)S(1)}) custom-call(s32[2,4]{1,0:T(2,128)S(1)} %copy-done, s32[4]{0:T(128)S(1)} %copy-done.1, bf16[256,1024]{1,0:T(8,128)(2,1)S(1)} %collective-permute-done.8.refs_2_.refs_4_, ...), custom_call_target="tpu_custom_call", output_to_operand_aliasing={{1}: (7, {}), {2}: (8, {})} | custom-call | flops 4294967296 | bytes 4194304 | tf_op jit(solution)/shard_map/pallas_call | solution.py:286
  52.0 1.8 %collective-permute-done.7.refs_4_ = bf16[256,1024]{1,0:T(8,128)(2,1)S(1)} collective-permute-done((bf16[256,1024]{1,0:T(8,128)(2,1)S(1)}, bf16[256,1024]{1,0:T(8,128)(2,1)S(1)}, u32[]{:S(2)}, u32[]{:S(2)}) %collective-permute-start.7) | collective-permute-done | bytes 524320 | tf_op jit(solution)/shard_map/ppermute | solution.py:374
  53.8 0.8 shard_map.78
  54.6 1.6 %collective-permute-start.14 = (bf16[256,1024]{1,0:T(8,128)(2,1)S(1)}, bf16[256,1024]{1,0:T(8,128)(2,1)S(1)}, u32[]{:S(2)}, u32[]{:S(2)}) collective-permute-start(bf16[256,1024]{1,0:T(8,128)(2,1)S(1)} %get-tuple-element.100.refs_4_.refs_7_), channel_id=1, source_target_pairs={{0,4},{1,5},{2,6},{3,7},{4,0},{5,1},{6,2},{7,3},{8,12},{9,13},{10,... | collective-permute-start | bytes 1572872 | tf_op jit(solution)/shard_map/ppermute | solution.py:325
  56.2 1.5 %collective-permute-start.10 = (bf16[256,1024]{1,0:T(8,128)(2,1)S(1)}, bf16[256,1024]{1,0:T(8,128)(2,1)S(1)}, u32[]{:S(2)}, u32[]{:S(2)}) collective-permute-start(bf16[256,1024]{1,0:T(8,128)(2,1)S(1)} %get-tuple-element.100.refs_4_.refs_7_), channel_id=1, source_target_pairs={{0,2},{1,3},{2,0},{3,1},{4,6},{5,7},{6,4},{7,5},{8,10},{9,11},{10,... | collective-permute-start | bytes 1572872 | tf_op jit(solution)/shard_map/ppermute | solution.py:322
  57.7 11.3 %shard_map.79 = (f32[8,128]{1,0:T(8,128)S(1)}, f32[4,2,1024,384]{3,2,1,0:T(8,128)S(1)}, bf16[4,2,1024,128]{3,2,1,0:T(8,128)(2,1)S(1)}) custom-call(s32[2,4]{1,0:T(2,128)S(1)} %copy-done, s32[4]{0:T(128)S(1)} %copy-done.1, bf16[256,1024]{1,0:T(8,128)(2,1)S(1)} %collective-permute-done.11.refs_2_.refs_5_, ...), custom_call_target="tpu_custom_call", output_to_operand_aliasing={{1}: (9, {}), {2}: (10, {})} | custom-call | flops 6442450944 | bytes 4194304 | tf_op jit(solution)/shard_map/pallas_call | solution.py:286
  69.1 0.6 collective-permute-start.15
  69.7 1.5 %collective-permute-start.13 = (bf16[128,1024]{1,0:T(8,128)(2,1)S(1)}, bf16[128,1024]{1,0:T(8,128)(2,1)S(1)}, u32[]{:S(2)}, u32[]{:S(2)}) collective-permute-start(bf16[128,1024]{1,0:T(8,128)(2,1)S(1)} %slice.22), channel_id=1, source_target_pairs={{0,4},{1,5},{2,6},{3,7},{4,0},{5,1},{6,2},{7,3},{8,12},{9,13},{10,... | collective-permute-start | bytes 786440 | tf_op jit(solution)/shard_map/ppermute | solution.py:325
  71.2 7.8 %shard_map.80 = (f32[8,128]{1,0:T(8,128)S(1)}, f32[4,2,1024,384]{3,2,1,0:T(8,128)S(1)}, bf16[4,2,1024,128]{3,2,1,0:T(8,128)(2,1)S(1)}) custom-call(s32[2,4]{1,0:T(2,128)S(1)} %copy-done, s32[4]{0:T(128)S(1)} %copy-done.1, bf16[256,1024]{1,0:T(8,128)(2,1)S(1)} %collective-permute-done.10.refs_2_.refs_4_, ...), custom_call_target="tpu_custom_call", output_to_operand_aliasing={{1}: (7, {}), {2}: (8, {})} | custom-call | flops 4294967296 | bytes 4194304 | tf_op jit(solution)/shard_map/pallas_call | solution.py:286
  79.1 6.0 %shard_map.81 = (bf16[128,4096]{1,0:T(8,128)(2,1)S(1)}, bf16[128,4096]{1,0:T(8,128)(2,1)S(1)}, f32[4,2,1024,384]{3,2,1,0:T(8,128)S(1)}, bf16[4,2,1024,128]{3,2,1,0:T(8,128)(2,1)S(1)}) custom-call(s32[2,4]{1,0:T(2,128)S(1)} %copy-done, s32[4]{0:T(128)S(1)} %copy-done.1, ...), custom_call_target="tpu_custom_call", output_to_operand_aliasing={{2}: (7, {}), {3}: (8, {})} | custom-call | flops 2147483648 | bytes 4194304 | tf_op jit(solution)/shard_map/pallas_call | solution.py:286
  85.2 2.6 %collective-permute-done.16.got_ref = bf16[128,4096]{1,0:T(8,128)(2,1)S(1)} collective-permute-done((bf16[128,4096]{1,0:T(8,128)(2,1)S(1)}, bf16[128,4096]{1,0:T(8,128)(2,1)S(1)}, u32[]{:S(2)}, u32[]{:S(2)}) %collective-permute-start.16) | collective-permute-done | bytes 1048608 | tf_op jit(solution)/shard_map/ppermute | solution.py:319
  87.8 1.3 %shard_map.82 = bf16[128,8192]{1,0:T(8,128)(2,1)} custom-call(bf16[128,4096]{1,0:T(8,128)(2,1)S(1)} %get-tuple-element.113.mine_ref, bf16[128,4096]{1,0:T(8,128)(2,1)S(1)} %collective-permute-done.16.got_ref), custom_call_target="tpu_custom_call" | custom-call | tf_op jit(solution)/shard_map/pallas_call | solution.py:245
  (23 shorter events, 1.2 us)
Async XLA Ops:
  1.4 2.1 %collective-permute-start = (bf16[256,1024]{1,0:T(8,128)(2,1)S(1)}, bf16[256,1024]{1,0:T(8,128)(2,1)S(1)}, u32[]{:S(2)}, u32[]{:S(2)}) collective-permute-start(bf16[256,1024]{1,0:T(8,128)(2,1)S(1)} %get-tuple-element.61), channel_id=1, source_target_pairs={{0,1},{1,0},{2,3},{3,2},{4,5},{5,4},{6,7},{7,6},{8,9},{9,8},{10,11... | collective-permute-start | bytes 1572872 | tf_op jit(solution)/shard_map/ppermute | solution.py:319
  5.1 8.9 %collective-permute-start.4 = (bf16[128,4096]{1,0:T(8,128)(2,1)S(1)}, bf16[128,4096]{1,0:T(8,128)(2,1)S(1)}, u32[]{:S(2)}, u32[]{:S(2)}) collective-permute-start(bf16[128,4096]{1,0:T(8,128)(2,1)S(1)} %get-tuple-element.116), channel_id=1, source_target_pairs={{0,1},{1,0},{2,3},{3,2},{4,5},{5,4},{6,7},{7,6},{8,9},{9,8},{10,11... | collective-permute-start | bytes 3145736 | tf_op jit(solution)/shard_map/ppermute | solution.py:319
  5.5 11.5 %copy-start = (s32[2,4]{1,0:T(2,128)S(1)}, s32[2,4]{1,0:T(2,128)}, u32[]{:S(2)}) copy-start(s32[2,4]{1,0:T(2,128)} %refs_0_.13) | copy-start | bytes 100
  5.5 11.5 %copy-start.1 = (s32[4]{0:T(128)S(1)}, s32[4]{0:T(128)}, u32[]{:S(2)}) copy-start(s32[4]{0:T(128)} %refs_1_.13) | copy-start | bytes 52
  5.7 26.5 %collective-permute-start.3 = (bf16[256,1024]{1,0:T(8,128)(2,1)S(1)}, bf16[256,1024]{1,0:T(8,128)(2,1)S(1)}, u32[]{:S(2)}, u32[]{:S(2)}) collective-permute-start(bf16[256,1024]{1,0:T(8,128)(2,1)S(1)} %pad_maximum_fusion.refs_4_.refs_6_.refs_0_), channel_id=1, source_target_pairs={{0,8},{8,16},{1,9},{9,17},{2,10},{10,18},{3,11},{11,19},{4,12},{12... | collective-permute-start | bytes 1572872 | tf_op jit(solution)/shard_map/ppermute | solution.py:350
  10.3 22.9 %collective-permute-start.2 = (bf16[256,1024]{1,0:T(8,128)(2,1)S(1)}, bf16[256,1024]{1,0:T(8,128)(2,1)S(1)}, u32[]{:S(2)}, u32[]{:S(2)}) collective-permute-start(bf16[256,1024]{1,0:T(8,128)(2,1)S(1)} %pad_maximum_fusion.refs_4_.refs_6_.refs_0_), channel_id=1, source_target_pairs={{0,16},{24,8},{1,17},{25,9},{2,18},{26,10},{3,19},{27,11},{4,20},{... | collective-permute-start | bytes 1572872 | tf_op jit(solution)/shard_map/ppermute | solution.py:350
  12.6 20.6 %collective-permute-start.1 = (bf16[256,1024]{1,0:T(8,128)(2,1)S(1)}, bf16[256,1024]{1,0:T(8,128)(2,1)S(1)}, u32[]{:S(2)}, u32[]{:S(2)}) collective-permute-start(bf16[256,1024]{1,0:T(8,128)(2,1)S(1)} %pad_maximum_fusion.refs_4_.refs_6_.refs_0_), channel_id=1, source_target_pairs={{8,0},{16,8},{24,16},{9,1},{17,9},{25,17},{10,2},{18,10},{26,18},{... | collective-permute-start | bytes 1572872 | tf_op jit(solution)/shard_map/ppermute | solution.py:350
  14.0 14.0 %collective-permute-start.6 = (bf16[256,1024]{1,0:T(8,128)(2,1)S(1)}, bf16[256,1024]{1,0:T(8,128)(2,1)S(1)}, u32[]{:S(2)}, u32[]{:S(2)}) collective-permute-start(bf16[256,1024]{1,0:T(8,128)(2,1)S(1)} %pad_maximum_fusion.refs_4_.refs_6_.refs_0_), channel_id=1, source_target_pairs={{0,4},{1,5},{2,6},{3,7},{4,0},{5,1},{6,2},{7,3},{8,12},{9,13},{10,... | collective-permute-start | bytes 1572872 | tf_op jit(solution)/shard_map/ppermute | solution.py:325
  15.5 13.9 %collective-permute-start.5 = (bf16[256,1024]{1,0:T(8,128)(2,1)S(1)}, bf16[256,1024]{1,0:T(8,128)(2,1)S(1)}, u32[]{:S(2)}, u32[]{:S(2)}) collective-permute-start(bf16[256,1024]{1,0:T(8,128)(2,1)S(1)} %pad_maximum_fusion.refs_4_.refs_6_.refs_0_), channel_id=1, source_target_pairs={{0,2},{1,3},{2,0},{3,1},{4,6},{5,7},{6,4},{7,5},{8,10},{9,11},{10,... | collective-permute-start | bytes 1572872 | tf_op jit(solution)/shard_map/ppermute | solution.py:322
  27.9 13.1 %collective-permute-start.9 = (bf16[256,1024]{1,0:T(8,128)(2,1)S(1)}, bf16[256,1024]{1,0:T(8,128)(2,1)S(1)}, u32[]{:S(2)}, u32[]{:S(2)}) collective-permute-start(bf16[256,1024]{1,0:T(8,128)(2,1)S(1)} %pad_maximum_fusion.1.refs_5_.refs_7_), channel_id=1, source_target_pairs={{0,4},{1,5},{2,6},{3,7},{4,0},{5,1},{6,2},{7,3},{8,12},{9,13},{10,... | collective-permute-start | bytes 1572872 | tf_op jit(solution)/shard_map/ppermute | solution.py:325
  29.5 12.8 %collective-permute-start.8 = (bf16[256,1024]{1,0:T(8,128)(2,1)S(1)}, bf16[256,1024]{1,0:T(8,128)(2,1)S(1)}, u32[]{:S(2)}, u32[]{:S(2)}) collective-permute-start(bf16[256,1024]{1,0:T(8,128)(2,1)S(1)} %pad_maximum_fusion.1.refs_5_.refs_7_), channel_id=1, source_target_pairs={{0,2},{1,3},{2,0},{3,1},{4,6},{5,7},{6,4},{7,5},{8,10},{9,11},{10,... | collective-permute-start | bytes 1572872 | tf_op jit(solution)/shard_map/ppermute | solution.py:322
  33.9 19.9 %collective-permute-start.7 = (bf16[256,1024]{1,0:T(8,128)(2,1)S(1)}, bf16[256,1024]{1,0:T(8,128)(2,1)S(1)}, u32[]{:S(2)}, u32[]{:S(2)}) collective-permute-start(bf16[256,1024]{1,0:T(8,128)(2,1)S(1)} %get-tuple-element.81), channel_id=1, source_target_pairs={{8,0},{9,1},{10,2},{11,3},{12,4},{13,5},{14,6},{15,7}} | collective-permute-start | bytes 1572872 | tf_op jit(solution)/shard_map/ppermute | solution.py:374
  42.2 15.5 %collective-permute-start.11 = (bf16[256,1024]{1,0:T(8,128)(2,1)S(1)}, bf16[256,1024]{1,0:T(8,128)(2,1)S(1)}, u32[]{:S(2)}, u32[]{:S(2)}) collective-permute-start(bf16[256,1024]{1,0:T(8,128)(2,1)S(1)} %collective-permute-done.5.refs_2_.refs_4_), channel_id=1, source_target_pairs={{0,4},{1,5},{2,6},{3,7},{4,0},{5,1},{6,2},{7,3},{8,12},{9,13},{10,... | collective-permute-start | bytes 1572872 | tf_op jit(solution)/shard_map/ppermute | solution.py:325
  42.7 15.0 %collective-permute-start.12 = (bf16[256,1024]{1,0:T(8,128)(2,1)S(1)}, bf16[256,1024]{1,0:T(8,128)(2,1)S(1)}, u32[]{:S(2)}, u32[]{:S(2)}) collective-permute-start(bf16[256,1024]{1,0:T(8,128)(2,1)S(1)} %collective-permute-done.9.refs_3_.refs_5_), channel_id=1, source_target_pairs={{0,2},{1,3},{2,0},{3,1},{4,6},{5,7},{6,4},{7,5},{8,10},{9,11},{10,... | collective-permute-start | bytes 1572872 | tf_op jit(solution)/shard_map/ppermute | solution.py:322
  54.6 14.4 %collective-permute-start.14 = (bf16[256,1024]{1,0:T(8,128)(2,1)S(1)}, bf16[256,1024]{1,0:T(8,128)(2,1)S(1)}, u32[]{:S(2)}, u32[]{:S(2)}) collective-permute-start(bf16[256,1024]{1,0:T(8,128)(2,1)S(1)} %get-tuple-element.100.refs_4_.refs_7_), channel_id=1, source_target_pairs={{0,4},{1,5},{2,6},{3,7},{4,0},{5,1},{6,2},{7,3},{8,12},{9,13},{10,... | collective-permute-start | bytes 1572872 | tf_op jit(solution)/shard_map/ppermute | solution.py:325
  56.2 13.5 %collective-permute-start.10 = (bf16[256,1024]{1,0:T(8,128)(2,1)S(1)}, bf16[256,1024]{1,0:T(8,128)(2,1)S(1)}, u32[]{:S(2)}, u32[]{:S(2)}) collective-permute-start(bf16[256,1024]{1,0:T(8,128)(2,1)S(1)} %get-tuple-element.100.refs_4_.refs_7_), channel_id=1, source_target_pairs={{0,2},{1,3},{2,0},{3,1},{4,6},{5,7},{6,4},{7,5},{8,10},{9,11},{10,... | collective-permute-start | bytes 1572872 | tf_op jit(solution)/shard_map/ppermute | solution.py:322
  69.1 10.0 %collective-permute-start.15 = (bf16[128,1024]{1,0:T(8,128)(2,1)S(1)}, bf16[128,1024]{1,0:T(8,128)(2,1)S(1)}, u32[]{:S(2)}, u32[]{:S(2)}) collective-permute-start(bf16[128,1024]{1,0:T(8,128)(2,1)S(1)} %slice.24), channel_id=1, source_target_pairs={{0,2},{1,3},{2,0},{3,1},{4,6},{5,7},{6,4},{7,5},{8,10},{9,11},{10,... | collective-permute-start | bytes 786440 | tf_op jit(solution)/shard_map/ppermute | solution.py:322
  69.7 9.3 %collective-permute-start.13 = (bf16[128,1024]{1,0:T(8,128)(2,1)S(1)}, bf16[128,1024]{1,0:T(8,128)(2,1)S(1)}, u32[]{:S(2)}, u32[]{:S(2)}) collective-permute-start(bf16[128,1024]{1,0:T(8,128)(2,1)S(1)} %slice.22), channel_id=1, source_target_pairs={{0,4},{1,5},{2,6},{3,7},{4,0},{5,1},{6,2},{7,3},{8,12},{9,13},{10,... | collective-permute-start | bytes 786440 | tf_op jit(solution)/shard_map/ppermute | solution.py:325
  85.1 2.7 %collective-permute-start.16 = (bf16[128,4096]{1,0:T(8,128)(2,1)S(1)}, bf16[128,4096]{1,0:T(8,128)(2,1)S(1)}, u32[]{:S(2)}, u32[]{:S(2)}) collective-permute-start(bf16[128,4096]{1,0:T(8,128)(2,1)S(1)} %get-tuple-element.114), channel_id=1, source_target_pairs={{0,1},{1,0},{2,3},{3,2},{4,5},{5,4},{6,7},{7,6},{8,9},{9,8},{10,11... | collective-permute-start | bytes 3145736 | tf_op jit(solution)/shard_map/ppermute | solution.py:319

commit v11 on v10

--- a/solution.py
+++ b/solution.py
@@ -15,7 +15,8 @@
 HALF_KV = KVH // 2
 NEG = -1e30
 EXP_SCALE = math.log2(math.e) / math.sqrt(HD)
-ROW_BLOCK = 128
+ROW_BLOCK = 256
+KEY_CHUNK = 256
 
 
 def attend_kernel(ny, rows, arrays, groups, first, last, *refs):
@@ -62,36 +63,50 @@
         size = min(ROW_BLOCK, stacked)
         todo = [(s, slice(base, base + size)) for s in range(2) for base in range(0, stacked, size)]
 
-        def score(s, here):
-            return lax.dot_general(
-                qs[head, s, here, :], keys, (((1,), (1,)), ((), ())), preferred_element_type=jnp.float32
+        chunks = [slice(c, min(c + KEY_CHUNK, width)) for c in range(0, width, KEY_CHUNK)]
+        biases = {}
+
+        def bias_of(s):
+            if s not in biases:
+                column = lax.broadcasted_iota(jnp.int32, (rows, rows), 1)
+                line = lax.broadcasted_iota(jnp.int32, (rows, rows), 0)
+                allowed = []
+                for (_, _, block), limit in zip(members, limits[s]):
+                    ahead = column - line if block[0] == "own" else column
+                    allowed.append(jnp.where(ahead < limit, 0.0, NEG))
+                biases[s] = jnp.concatenate(allowed, axis=1)
+            return biases[s]
+
+        def score(item, chunk):
+            s, here = item
+            found = lax.dot_general(
+                qs[head, s, here, :], keys[chunk], (((1,), (1,)), ((), ())), preferred_element_type=jnp.float32
             )
-
-        def bias_of(s):
-            column = lax.broadcasted_iota(jnp.int32, (rows, rows), 1)
-            line = lax.broadcasted_iota(jnp.int32, (rows, rows), 0)
-            allowed = []
-            for (_, _, block), limit in zip(members, limits[s]):
-                ahead = column - line if block[0] == "own" else column
-                allowed.append(jnp.where(ahead < limit, 0.0, NEG))
-            return jnp.concatenate(allowed, axis=1)
-
-        following = score(*todo[0])
+            if masked:
+                found = found + jnp.concatenate([bias_of(s)[:, chunk]] * (size // rows), axis=0)
+            return found
+
+        def peak_of(scores):
+            parts = [part[:, c : c + HD] for part in scores for c in range(0, part.shape[1], HD)]
+            return jnp.max(functools.reduce(jnp.maximum, parts), axis=1, keepdims=True)
+
+        scores = [score(todo[0], chunk) for chunk in chunks]
+        peak = peak_of(scores)
         for at, (s, here) in enumerate(todo):
-            scores = following
-            if at + 1 < len(todo):
-                following = score(*todo[at + 1])
-            if masked:
-                bias = bias_of(s)
-                scores = scores + jnp.concatenate([bias] * (size // rows), axis=0)
-            new = jnp.max(scores, axis=1, keepdims=True)
             if fresh:
-                new = jnp.broadcast_to(new, (size, HD))
+                new = jnp.broadcast_to(peak, (size, HD))
             else:
                 old = held[head, s, here, 2 * HD :]
-                new = jnp.maximum(old, new)
-            weights = jnp.exp2((scores - jnp.concatenate([new] * (width // HD), axis=1)) * EXP_SCALE)
-            update = jnp.dot(weights.astype(jnp.bfloat16), values, preferred_element_type=jnp.float32)
+                new = jnp.maximum(old, peak)
+            following, weights = [], []
+            for i, chunk in enumerate(chunks):
+                if at + 1 < len(todo):
+                    following.append(score(todo[at + 1], chunk))
+                shifted = scores[i] - jnp.concatenate([new] * (scores[i].shape[1] // HD), axis=1)
+                weights.append(jnp.exp2(shifted * EXP_SCALE).astype(jnp.bfloat16))
+            update = jnp.dot(jnp.concatenate(weights, axis=1), values, preferred_element_type=jnp.float32)
+            if following:
+                scores, peak = following, peak_of(following)
             if fresh:
                 held[head, s, here, : 2 * HD] = update
             else:
@@ -198,7 +213,7 @@
     return picked
 
 
-def pack(*arrays):
+def pack(beside, *arrays):
     rows, width = arrays[0].shape
     half = width // 2
 
@@ -209,7 +224,7 @@
         for out_ref, place in ((other_ref, 1 - core), (mine_ref, core)):
             columns = pl.ds(pl.multiple_of(place * half, half), half)
             for i, ref in enumerate(in_refs):
-                target = out_ref.at[pl.ds(i // 2 * rows, rows), pl.ds(i % 2 * half, half)]
+                target = out_ref.at[pl.ds(i // beside * rows, rows), pl.ds(i % beside * half, half)]
                 copies.append(pltpu.make_async_copy(ref.at[:, columns], target, sems.at[len(copies)]))
         for copy in copies:
             copy.start()
@@ -217,7 +232,7 @@
             copy.wait()
 
     anywhere = pl.BlockSpec(memory_space=pl.ANY)
-    packed = jax.ShapeDtypeStruct((len(arrays) // 2 * rows, width), arrays[0].dtype)
+    packed = jax.ShapeDtypeStruct((len(arrays) // beside * rows, beside * half), arrays[0].dtype)
     return pl.pallas_call(
         kernel,
         in_specs=[anywhere] * len(arrays),
@@ -301,15 +316,6 @@
     ny = spots // 4
     rows = queries.shape[0]
     group = lax.axis_index("leaf")
-    core = lax.rem(lax.axis_index("ctx"), 2)
-
-    def halves(array):
-        half = array.shape[1] // 2
-        return (
-            lax.dynamic_slice_in_dim(array, core * half, half, 1),
-            lax.dynamic_slice_in_dim(array, (1 - core) * half, half, 1),
-        )
-
     def index(x, y, k):
         return ((y % ny) * 2 + x % 2) * 2 + k % 2
 
@@ -324,9 +330,10 @@
     def to_y(array, step):
         return lax.ppermute(array, "ctx", [(index(x, y, k), index(x, y + step, k)) for x, y, k in places])
 
-    mine, sent = pack(seg_keys, seg_values, root_keys, root_values)
-    queries, got = lax.optimization_barrier((queries, to_core(sent)))
-    q_mine, q_other = halves(queries)
+    mine, sent = pack(2, seg_keys, seg_values, root_keys, root_values)
+    queries, sent = lax.optimization_barrier((queries, sent))
+    q_mine, q_other = pack(1, queries)
+    q_other, got = lax.optimization_barrier((q_other, to_core(sent)))
     own = jnp.concatenate([mine[:rows], got[:rows]], axis=0)
     root = jnp.concatenate([mine[rows:], got[rows:]], axis=0)
     run = functools.partial(attend, ny, rows, (expansion, root_offsets))
@@ -343,6 +350,9 @@
         pairs = [(i, (i - 1) % leaves) for i in range(leaves)]
         return lax.ppermute(rows_held, "leaf", pairs if step < leaves - 1 else pairs[1:])
 
+    own_x, own_y = to_x(own), [to_y(own, step) for step in steps]
+    own, q_got = lax.optimization_barrier((own, to_core(q_other)))
+    q_pair = (q_mine, q_got)
     direct = leaves == 4
     ahead = [own]
     if direct:
@@ -350,9 +360,6 @@
             ahead.append(lax.ppermute(own, "leaf", pairs))
     elif leaves > 1:
         ahead.append(hop(1, own))
-    own, q_got = lax.optimization_barrier((own, to_core(q_other)))
-    q_pair = (q_mine, q_got)
-    own_x, own_y = to_x(own), [to_y(own, step) for step in steps]
     state = run([own, root], (members(0, "own") + members(1, "root"),), q_pair, None, False)
 
     (root,) = after(state, root)

time: 89.6 us -> 90 us (level)
  waiting for transfers between devices: 17.9 us -> 26 us
  Pallas kernels: 45.4 us -> 39.8 us
  local copies, waits for them, and re-layouts: 1.79 us -> 0.12 us
    ppermute x1, waiting for transfers between devices: 1.8 us -> 14.4 us  [on_device(): ahead.append(lax.ppermute(relay, 'leaf', [(1, 0)]))]
    ppermute x5, waiting for transfers between devices: 9.49 us -> 0.1 us  [to_y(): lax.ppermute(array, 'ctx', [(index(x, y, k), index(x, y + step, k)) for x...]
    pallas_call x6, Pallas kernels: 41.3 us -> 34.1 us  [attend(): pl.pallas_call(functools.partial(attend_kernel, ny, rows, len(arrays), gr...]
    ppermute x3, waiting for transfers between devices: 1.14 us -> 7.9 us  [on_device(): ahead.append(lax.ppermute(own, 'leaf', pairs))]
    dynamic_slice x1 -> x0, local copies, waits for them, and re-layouts: 1.68 us -> none  [halves(): lax.dynamic_slice_in_dim(array, core * half, half, 1)]
    pallas_call x1 -> x2, Pallas kernels: 1.35 us -> 2.9 us  [pack(): pl.pallas_call(kernel, in_specs=[anywhere] * len(arrays), out_specs=[anyw...]
    ppermute x3, waiting for transfers between devices: 4.19 us -> 2.65 us  [to_core(): lax.ppermute(array, 'ctx', [(index(x, y, k), index(x, y, k + 1)) for x, y...]
    ppermute x3, starting transfers between devices: 8.26 us -> 7.11 us  [on_device(): ahead.append(lax.ppermute(own, 'leaf', pairs))]
  transfers between devices with their start and end apart: 17 -> 17, of which waited for: 7 -> 5; matrix products, arithmetic and copies ran while one was open for 0% -> 0% of each run, Pallas kernels for 41% -> 35%
where the time goes in v11:
time: 90 us; the launch traced here: 89.7 us
  Pallas kernels  39.8 us (44%)
  waiting for transfers between devices  26 us (29%)
  starting transfers between devices  23.3 us (26%)
    pallas_call x6, Pallas kernels, attend(): pl.pallas_call(functools.partial(attend_kernel, ny, rows, len(arrays), gr...  34.1 us
    ppermute x1, waiting for transfers between devices, on_device(): ahead.append(lax.ppermute(relay, 'leaf', [(1, 0)]))  14.4 us
    ppermute x3, waiting for transfers between devices, on_device(): ahead.append(lax.ppermute(own, 'leaf', pairs))  7.9 us
    ppermute x5, starting transfers between devices, to_y(): lax.ppermute(array, 'ctx', [(index(x, y, k), index(x, y + step, k)) for x...  7.23 us
    ppermute x3, starting transfers between devices, on_device(): ahead.append(lax.ppermute(own, 'leaf', pairs))  7.11 us
    ppermute x5, starting transfers between devices, to_x(): lax.ppermute(array, 'ctx', [(index(x, y, k), index(x + 1, y, k)) for x, y...  6.75 us
    pallas_call x2, Pallas kernels, pack(): pl.pallas_call(kernel, in_specs=[anywhere] * len(arrays), out_specs=[anyw...  2.9 us
    ppermute x3, waiting for transfers between devices, to_core(): lax.ppermute(array, 'ctx', [(index(x, y, k), index(x, y, k + 1)) for x, y...  2.65 us
  transfers between devices with their start and end apart: 17, of which 5 were waited for; matrix products, arithmetic and copies ran while one was open for 0% of the time, Pallas kernels for 35%

profile of v11, /device:TPU:0, one launch (start us, length us, event | category | flops | bytes accessed | tf_op | source)
XLA Modules:
  0.0 89.7 jit_solution(824709418316389511)
XLA Ops:
  0.0 1.3 %shard_map.73 = (bf16[256,1024]{1,0:T(8,128)(2,1)S(1)}, bf16[256,1024]{1,0:T(8,128)(2,1)S(1)}) custom-call(bf16[128,1024]{1,0:T(8,128)(2,1)} %refs_0_.7, bf16[128,1024]{1,0:T(8,128)(2,1)} %refs_1_.7, bf16[128,1024]{1,0:T(8,128)(2,1)} %refs_2_.1, bf16[128,1024]{1,0:T(8,128)(2,1)} %refs_3_.1), custom_call_target="tpu_custom_call" | custom-call | tf_op jit(solution)/shard_map/pallas_call | solution.py:236
  1.4 0.5 collective-permute-start
  1.9 1.6 %shard_map.74 = (bf16[128,4096]{1,0:T(8,128)(2,1)S(1)}, bf16[128,4096]{1,0:T(8,128)(2,1)S(1)}) custom-call(bf16[128,8192]{1,0:T(8,128)(2,1)} %refs_0_.8), custom_call_target="tpu_custom_call" | custom-call | tf_op jit(solution)/shard_map/pallas_call | solution.py:236
  3.5 0.3 collective-permute-start.1
  3.9 2.8 %collective-permute-start.6 = (bf16[256,1024]{1,0:T(8,128)(2,1)S(1)}, bf16[256,1024]{1,0:T(8,128)(2,1)S(1)}, u32[]{:S(2)}, u32[]{:S(2)}) collective-permute-start(bf16[256,1024]{1,0:T(8,128)(2,1)S(1)} %pad_maximum_fusion.refs_4_.refs_6_.refs_0_), channel_id=1, source_target_pairs={{0,4},{1,5},{2,6},{3,7},{4,0},{5,1},{6,2},{7,3},{8,12},{9,13},{10,... | collective-permute-start | bytes 1572872 | tf_op jit(solution)/shard_map/ppermute | solution.py:331
  6.7 1.5 %collective-permute-start.5 = (bf16[256,1024]{1,0:T(8,128)(2,1)S(1)}, bf16[256,1024]{1,0:T(8,128)(2,1)S(1)}, u32[]{:S(2)}, u32[]{:S(2)}) collective-permute-start(bf16[256,1024]{1,0:T(8,128)(2,1)S(1)} %pad_maximum_fusion.refs_4_.refs_6_.refs_0_), channel_id=1, source_target_pairs={{0,2},{1,3},{2,0},{3,1},{4,6},{5,7},{6,4},{7,5},{8,10},{9,11},{10,... | collective-permute-start | bytes 1572872 | tf_op jit(solution)/shard_map/ppermute | solution.py:328
  8.3 3.5 %collective-permute-start.4 = (bf16[256,1024]{1,0:T(8,128)(2,1)S(1)}, bf16[256,1024]{1,0:T(8,128)(2,1)S(1)}, u32[]{:S(2)}, u32[]{:S(2)}) collective-permute-start(bf16[256,1024]{1,0:T(8,128)(2,1)S(1)} %pad_maximum_fusion.refs_4_.refs_6_.refs_0_), channel_id=1, source_target_pairs={{0,8},{8,16},{1,9},{9,17},{2,10},{10,18},{3,11},{11,19},{4,12},{12... | collective-permute-start | bytes 1572872 | tf_op jit(solution)/shard_map/ppermute | solution.py:360
  11.8 2.3 %collective-permute-start.3 = (bf16[256,1024]{1,0:T(8,128)(2,1)S(1)}, bf16[256,1024]{1,0:T(8,128)(2,1)S(1)}, u32[]{:S(2)}, u32[]{:S(2)}) collective-permute-start(bf16[256,1024]{1,0:T(8,128)(2,1)S(1)} %pad_maximum_fusion.refs_4_.refs_6_.refs_0_), channel_id=1, source_target_pairs={{0,16},{24,8},{1,17},{25,9},{2,18},{26,10},{3,19},{27,11},{4,20},{... | collective-permute-start | bytes 1572872 | tf_op jit(solution)/shard_map/ppermute | solution.py:360
  14.1 1.3 %collective-permute-start.2 = (bf16[256,1024]{1,0:T(8,128)(2,1)S(1)}, bf16[256,1024]{1,0:T(8,128)(2,1)S(1)}, u32[]{:S(2)}, u32[]{:S(2)}) collective-permute-start(bf16[256,1024]{1,0:T(8,128)(2,1)S(1)} %pad_maximum_fusion.refs_4_.refs_6_.refs_0_), channel_id=1, source_target_pairs={{8,0},{16,8},{24,16},{9,1},{17,9},{25,17},{10,2},{18,10},{26,18},{... | collective-permute-start | bytes 1572872 | tf_op jit(solution)/shard_map/ppermute | solution.py:360
  15.4 7.3 %shard_map.75 = (f32[8,128]{1,0:T(8,128)S(1)}, f32[4,2,1024,384]{3,2,1,0:T(8,128)S(1)}, bf16[4,2,1024,128]{3,2,1,0:T(8,128)(2,1)S(1)}) custom-call(s32[2,4]{1,0:T(2,128)S(1)} %copy-done, s32[4]{0:T(128)S(1)} %copy-done.1, bf16[128,4096]{1,0:T(8,128)(2,1)S(1)} %get-tuple-element.72.refs_2_, bf16[128,4096]{1,0:T(8,128)(2,1)S(1)} %collective-permute-done.1.refs_3_, ...), custom_call_target="tpu_custom_call" | custom-call | flops 4294967296 | bytes 4194304 | tf_op jit(solution)/shard_map/pallas_call | solution.py:301
  22.8 0.7 collective-permute-start.9
  23.5 1.5 %collective-permute-start.8 = (bf16[256,1024]{1,0:T(8,128)(2,1)S(1)}, bf16[256,1024]{1,0:T(8,128)(2,1)S(1)}, u32[]{:S(2)}, u32[]{:S(2)}) collective-permute-start(bf16[256,1024]{1,0:T(8,128)(2,1)S(1)} %pad_maximum_fusion.1.refs_5_.refs_7_), channel_id=1, source_target_pairs={{0,2},{1,3},{2,0},{3,1},{4,6},{5,7},{6,4},{7,5},{8,10},{9,11},{10,... | collective-permute-start | bytes 1572872 | tf_op jit(solution)/shard_map/ppermute | solution.py:328
  25.0 1.2 %shard_map.76 = (f32[8,128]{1,0:T(8,128)S(1)}, f32[4,2,1024,384]{3,2,1,0:T(8,128)S(1)}, bf16[4,2,1024,128]{3,2,1,0:T(8,128)(2,1)S(1)}) custom-call(s32[2,4]{1,0:T(2,128)S(1)} %copy-done, s32[4]{0:T(128)S(1)} %copy-done.1, bf16[256,1024]{1,0:T(8,128)(2,1)S(1)} %collective-permute-done.5.refs_2_.refs_4_, ...), custom_call_target="tpu_custom_call", output_to_operand_aliasing={{1}: (7, {}), {2}: (8, {})} | custom-call | flops 4294967296 | bytes 4194304 | tf_op jit(solution)/shard_map/pallas_call | solution.py:301
  26.2 7.9 %collective-permute-done.3.refs_1_.refs_2_ = bf16[256,1024]{1,0:T(8,128)(2,1)S(1)} collective-permute-done((bf16[256,1024]{1,0:T(8,128)(2,1)S(1)}, bf16[256,1024]{1,0:T(8,128)(2,1)S(1)}, u32[]{:S(2)}, u32[]{:S(2)}) %collective-permute-start.3) | collective-permute-done | bytes 524320 | tf_op jit(solution)/shard_map/ppermute | solution.py:360
  34.1 0.6 shard_map.77
  34.7 1.3 %collective-permute-start.7 = (bf16[256,1024]{1,0:T(8,128)(2,1)S(1)}, bf16[256,1024]{1,0:T(8,128)(2,1)S(1)}, u32[]{:S(2)}, u32[]{:S(2)}) collective-permute-start(bf16[256,1024]{1,0:T(8,128)(2,1)S(1)} %get-tuple-element.89), channel_id=1, source_target_pairs={{8,0},{9,1},{10,2},{11,3},{12,4},{13,5},{14,6},{15,7}} | collective-permute-start | bytes 1572872 | tf_op jit(solution)/shard_map/ppermute | solution.py:381
  36.0 0.1 collective-permute-done.9.refs_3_.refs_5_
  36.1 0.9 %collective-permute-done.8.refs_2_.refs_4_ = bf16[256,1024]{1,0:T(8,128)(2,1)S(1)} collective-permute-done((bf16[256,1024]{1,0:T(8,128)(2,1)S(1)}, bf16[256,1024]{1,0:T(8,128)(2,1)S(1)}, u32[]{:S(2)}, u32[]{:S(2)}) %collective-permute-start.8) | collective-permute-done | bytes 524320 | tf_op jit(solution)/shard_map/ppermute | solution.py:328
  37.0 0.8 collective-permute-start.11
  37.8 1.2 %collective-permute-start.12 = (bf16[256,1024]{1,0:T(8,128)(2,1)S(1)}, bf16[256,1024]{1,0:T(8,128)(2,1)S(1)}, u32[]{:S(2)}, u32[]{:S(2)}) collective-permute-start(bf16[256,1024]{1,0:T(8,128)(2,1)S(1)} %collective-permute-done.9.refs_3_.refs_5_), channel_id=1, source_target_pairs={{0,2},{1,3},{2,0},{3,1},{4,6},{5,7},{6,4},{7,5},{8,10},{9,11},{10,... | collective-permute-start | bytes 1572872 | tf_op jit(solution)/shard_map/ppermute | solution.py:328
  39.0 1.2 %shard_map.78 = (f32[8,128]{1,0:T(8,128)S(1)}, f32[4,2,1024,384]{3,2,1,0:T(8,128)S(1)}, bf16[4,2,1024,128]{3,2,1,0:T(8,128)(2,1)S(1)}) custom-call(s32[2,4]{1,0:T(2,128)S(1)} %copy-done, s32[4]{0:T(128)S(1)} %copy-done.1, bf16[256,1024]{1,0:T(8,128)(2,1)S(1)} %collective-permute-done.8.refs_2_.refs_4_, ...), custom_call_target="tpu_custom_call", output_to_operand_aliasing={{1}: (7, {}), {2}: (8, {})} | custom-call | flops 4294967296 | bytes 4194304 | tf_op jit(solution)/shard_map/pallas_call | solution.py:301
  40.2 14.4 %collective-permute-done.7.refs_4_ = bf16[256,1024]{1,0:T(8,128)(2,1)S(1)} collective-permute-done((bf16[256,1024]{1,0:T(8,128)(2,1)S(1)}, bf16[256,1024]{1,0:T(8,128)(2,1)S(1)}, u32[]{:S(2)}, u32[]{:S(2)}) %collective-permute-start.7) | collective-permute-done | bytes 524320 | tf_op jit(solution)/shard_map/ppermute | solution.py:381
  54.6 0.8 shard_map.79
  55.4 1.3 %collective-permute-start.14 = (bf16[256,1024]{1,0:T(8,128)(2,1)S(1)}, bf16[256,1024]{1,0:T(8,128)(2,1)S(1)}, u32[]{:S(2)}, u32[]{:S(2)}) collective-permute-start(bf16[256,1024]{1,0:T(8,128)(2,1)S(1)} %get-tuple-element.108.refs_4_.refs_7_), channel_id=1, source_target_pairs={{0,4},{1,5},{2,6},{3,7},{4,0},{5,1},{6,2},{7,3},{8,12},{9,13},{10,... | collective-permute-start | bytes 1572872 | tf_op jit(solution)/shard_map/ppermute | solution.py:331
  56.7 1.5 %collective-permute-start.10 = (bf16[256,1024]{1,0:T(8,128)(2,1)S(1)}, bf16[256,1024]{1,0:T(8,128)(2,1)S(1)}, u32[]{:S(2)}, u32[]{:S(2)}) collective-permute-start(bf16[256,1024]{1,0:T(8,128)(2,1)S(1)} %get-tuple-element.108.refs_4_.refs_7_), channel_id=1, source_target_pairs={{0,2},{1,3},{2,0},{3,1},{4,6},{5,7},{6,4},{7,5},{8,10},{9,11},{10,... | collective-permute-start | bytes 1572872 | tf_op jit(solution)/shard_map/ppermute | solution.py:328
  58.2 10.7 %shard_map.80 = (f32[8,128]{1,0:T(8,128)S(1)}, f32[4,2,1024,384]{3,2,1,0:T(8,128)S(1)}, bf16[4,2,1024,128]{3,2,1,0:T(8,128)(2,1)S(1)}) custom-call(s32[2,4]{1,0:T(2,128)S(1)} %copy-done, s32[4]{0:T(128)S(1)} %copy-done.1, bf16[256,1024]{1,0:T(8,128)(2,1)S(1)} %collective-permute-done.11.refs_2_.refs_5_, ...), custom_call_target="tpu_custom_call", output_to_operand_aliasing={{1}: (9, {}), {2}: (10, {})} | custom-call | flops 6442450944 | bytes 4194304 | tf_op jit(solution)/shard_map/pallas_call | solution.py:301
  69.0 1.1 %collective-permute-start.15 = (bf16[128,1024]{1,0:T(8,128)(2,1)S(1)}, bf16[128,1024]{1,0:T(8,128)(2,1)S(1)}, u32[]{:S(2)}, u32[]{:S(2)}) collective-permute-start(bf16[128,1024]{1,0:T(8,128)(2,1)S(1)} %slice.24), channel_id=1, source_target_pairs={{0,2},{1,3},{2,0},{3,1},{4,6},{5,7},{6,4},{7,5},{8,10},{9,11},{10,... | collective-permute-start | bytes 786440 | tf_op jit(solution)/shard_map/ppermute | solution.py:328
  70.1 1.6 %collective-permute-start.13 = (bf16[128,1024]{1,0:T(8,128)(2,1)S(1)}, bf16[128,1024]{1,0:T(8,128)(2,1)S(1)}, u32[]{:S(2)}, u32[]{:S(2)}) collective-permute-start(bf16[128,1024]{1,0:T(8,128)(2,1)S(1)} %slice.22), channel_id=1, source_target_pairs={{0,4},{1,5},{2,6},{3,7},{4,0},{5,1},{6,2},{7,3},{8,12},{9,13},{10,... | collective-permute-start | bytes 786440 | tf_op jit(solution)/shard_map/ppermute | solution.py:331
  71.7 7.7 %shard_map.81 = (f32[8,128]{1,0:T(8,128)S(1)}, f32[4,2,1024,384]{3,2,1,0:T(8,128)S(1)}, bf16[4,2,1024,128]{3,2,1,0:T(8,128)(2,1)S(1)}) custom-call(s32[2,4]{1,0:T(2,128)S(1)} %copy-done, s32[4]{0:T(128)S(1)} %copy-done.1, bf16[256,1024]{1,0:T(8,128)(2,1)S(1)} %collective-permute-done.10.refs_2_.refs_4_, ...), custom_call_target="tpu_custom_call", output_to_operand_aliasing={{1}: (7, {}), {2}: (8, {})} | custom-call | flops 4294967296 | bytes 4194304 | tf_op jit(solution)/shard_map/pallas_call | solution.py:301
  79.5 6.0 %shard_map.82 = (bf16[128,4096]{1,0:T(8,128)(2,1)S(1)}, bf16[128,4096]{1,0:T(8,128)(2,1)S(1)}, f32[4,2,1024,384]{3,2,1,0:T(8,128)S(1)}, bf16[4,2,1024,128]{3,2,1,0:T(8,128)(2,1)S(1)}) custom-call(s32[2,4]{1,0:T(2,128)S(1)} %copy-done, s32[4]{0:T(128)S(1)} %copy-done.1, ...), custom_call_target="tpu_custom_call", output_to_operand_aliasing={{2}: (7, {}), {3}: (8, {})} | custom-call | flops 2147483648 | bytes 4194304 | tf_op jit(solution)/shard_map/pallas_call | solution.py:301
  85.6 2.6 %collective-permute-done.16.got_ref = bf16[128,4096]{1,0:T(8,128)(2,1)S(1)} collective-permute-done((bf16[128,4096]{1,0:T(8,128)(2,1)S(1)}, bf16[128,4096]{1,0:T(8,128)(2,1)S(1)}, u32[]{:S(2)}, u32[]{:S(2)}) %collective-permute-start.16) | collective-permute-done | bytes 1048608 | tf_op jit(solution)/shard_map/ppermute | solution.py:325
  88.2 1.3 %shard_map.83 = bf16[128,8192]{1,0:T(8,128)(2,1)} custom-call(bf16[128,4096]{1,0:T(8,128)(2,1)S(1)} %get-tuple-element.121.mine_ref, bf16[128,4096]{1,0:T(8,128)(2,1)S(1)} %collective-permute-done.16.got_ref), custom_call_target="tpu_custom_call" | custom-call | tf_op jit(solution)/shard_map/pallas_call | solution.py:260
  (23 shorter events, 0.3 us)
Async XLA Ops:
  1.4 2.1 %collective-permute-start = (bf16[256,1024]{1,0:T(8,128)(2,1)S(1)}, bf16[256,1024]{1,0:T(8,128)(2,1)S(1)}, u32[]{:S(2)}, u32[]{:S(2)}) collective-permute-start(bf16[256,1024]{1,0:T(8,128)(2,1)S(1)} %get-tuple-element.68), channel_id=1, source_target_pairs={{0,1},{1,0},{2,3},{3,2},{4,5},{5,4},{6,7},{7,6},{8,9},{9,8},{10,11... | collective-permute-start | bytes 1572872 | tf_op jit(solution)/shard_map/ppermute | solution.py:325
  3.5 4.8 %collective-permute-start.1 = (bf16[128,4096]{1,0:T(8,128)(2,1)S(1)}, bf16[128,4096]{1,0:T(8,128)(2,1)S(1)}, u32[]{:S(2)}, u32[]{:S(2)}) collective-permute-start(bf16[128,4096]{1,0:T(8,128)(2,1)S(1)} %get-tuple-element.70), channel_id=1, source_target_pairs={{0,1},{1,0},{2,3},{3,2},{4,5},{5,4},{6,7},{7,6},{8,9},{9,8},{10,11... | collective-permute-start | bytes 3145736 | tf_op jit(solution)/shard_map/ppermute | solution.py:325
  3.8 11.6 %copy-start = (s32[2,4]{1,0:T(2,128)S(1)}, s32[2,4]{1,0:T(2,128)}, u32[]{:S(2)}) copy-start(s32[2,4]{1,0:T(2,128)} %refs_0_.14) | copy-start | bytes 100
  3.8 11.6 %copy-start.1 = (s32[4]{0:T(128)S(1)}, s32[4]{0:T(128)}, u32[]{:S(2)}) copy-start(s32[4]{0:T(128)} %refs_1_.13) | copy-start | bytes 52
  3.9 18.8 %collective-permute-start.6 = (bf16[256,1024]{1,0:T(8,128)(2,1)S(1)}, bf16[256,1024]{1,0:T(8,128)(2,1)S(1)}, u32[]{:S(2)}, u32[]{:S(2)}) collective-permute-start(bf16[256,1024]{1,0:T(8,128)(2,1)S(1)} %pad_maximum_fusion.refs_4_.refs_6_.refs_0_), channel_id=1, source_target_pairs={{0,4},{1,5},{2,6},{3,7},{4,0},{5,1},{6,2},{7,3},{8,12},{9,13},{10,... | collective-permute-start | bytes 1572872 | tf_op jit(solution)/shard_map/ppermute | solution.py:331
  6.7 16.8 %collective-permute-start.5 = (bf16[256,1024]{1,0:T(8,128)(2,1)S(1)}, bf16[256,1024]{1,0:T(8,128)(2,1)S(1)}, u32[]{:S(2)}, u32[]{:S(2)}) collective-permute-start(bf16[256,1024]{1,0:T(8,128)(2,1)S(1)} %pad_maximum_fusion.refs_4_.refs_6_.refs_0_), channel_id=1, source_target_pairs={{0,2},{1,3},{2,0},{3,1},{4,6},{5,7},{6,4},{7,5},{8,10},{9,11},{10,... | collective-permute-start | bytes 1572872 | tf_op jit(solution)/shard_map/ppermute | solution.py:328
  8.3 17.9 %collective-permute-start.4 = (bf16[256,1024]{1,0:T(8,128)(2,1)S(1)}, bf16[256,1024]{1,0:T(8,128)(2,1)S(1)}, u32[]{:S(2)}, u32[]{:S(2)}) collective-permute-start(bf16[256,1024]{1,0:T(8,128)(2,1)S(1)} %pad_maximum_fusion.refs_4_.refs_6_.refs_0_), channel_id=1, source_target_pairs={{0,8},{8,16},{1,9},{9,17},{2,10},{10,18},{3,11},{11,19},{4,12},{12... | collective-permute-start | bytes 1572872 | tf_op jit(solution)/shard_map/ppermute | solution.py:360
  11.8 22.3 %collective-permute-start.3 = (bf16[256,1024]{1,0:T(8,128)(2,1)S(1)}, bf16[256,1024]{1,0:T(8,128)(2,1)S(1)}, u32[]{:S(2)}, u32[]{:S(2)}) collective-permute-start(bf16[256,1024]{1,0:T(8,128)(2,1)S(1)} %pad_maximum_fusion.refs_4_.refs_6_.refs_0_), channel_id=1, source_target_pairs={{0,16},{24,8},{1,17},{25,9},{2,18},{26,10},{3,19},{27,11},{4,20},{... | collective-permute-start | bytes 1572872 | tf_op jit(solution)/shard_map/ppermute | solution.py:360
  14.1 20.0 %collective-permute-start.2 = (bf16[256,1024]{1,0:T(8,128)(2,1)S(1)}, bf16[256,1024]{1,0:T(8,128)(2,1)S(1)}, u32[]{:S(2)}, u32[]{:S(2)}) collective-permute-start(bf16[256,1024]{1,0:T(8,128)(2,1)S(1)} %pad_maximum_fusion.refs_4_.refs_6_.refs_0_), channel_id=1, source_target_pairs={{8,0},{16,8},{24,16},{9,1},{17,9},{25,17},{10,2},{18,10},{26,18},{... | collective-permute-start | bytes 1572872 | tf_op jit(solution)/shard_map/ppermute | solution.py:360
  22.8 13.3 %collective-permute-start.9 = (bf16[256,1024]{1,0:T(8,128)(2,1)S(1)}, bf16[256,1024]{1,0:T(8,128)(2,1)S(1)}, u32[]{:S(2)}, u32[]{:S(2)}) collective-permute-start(bf16[256,1024]{1,0:T(8,128)(2,1)S(1)} %pad_maximum_fusion.1.refs_5_.refs_7_), channel_id=1, source_target_pairs={{0,4},{1,5},{2,6},{3,7},{4,0},{5,1},{6,2},{7,3},{8,12},{9,13},{10,... | collective-permute-start | bytes 1572872 | tf_op jit(solution)/shard_map/ppermute | solution.py:331
  23.5 13.5 %collective-permute-start.8 = (bf16[256,1024]{1,0:T(8,128)(2,1)S(1)}, bf16[256,1024]{1,0:T(8,128)(2,1)S(1)}, u32[]{:S(2)}, u32[]{:S(2)}) collective-permute-start(bf16[256,1024]{1,0:T(8,128)(2,1)S(1)} %pad_maximum_fusion.1.refs_5_.refs_7_), channel_id=1, source_target_pairs={{0,2},{1,3},{2,0},{3,1},{4,6},{5,7},{6,4},{7,5},{8,10},{9,11},{10,... | collective-permute-start | bytes 1572872 | tf_op jit(solution)/shard_map/ppermute | solution.py:328
  34.7 19.9 %collective-permute-start.7 = (bf16[256,1024]{1,0:T(8,128)(2,1)S(1)}, bf16[256,1024]{1,0:T(8,128)(2,1)S(1)}, u32[]{:S(2)}, u32[]{:S(2)}) collective-permute-start(bf16[256,1024]{1,0:T(8,128)(2,1)S(1)} %get-tuple-element.89), channel_id=1, source_target_pairs={{8,0},{9,1},{10,2},{11,3},{12,4},{13,5},{14,6},{15,7}} | collective-permute-start | bytes 1572872 | tf_op jit(solution)/shard_map/ppermute | solution.py:381
  37.0 21.2 %collective-permute-start.11 = (bf16[256,1024]{1,0:T(8,128)(2,1)S(1)}, bf16[256,1024]{1,0:T(8,128)(2,1)S(1)}, u32[]{:S(2)}, u32[]{:S(2)}) collective-permute-start(bf16[256,1024]{1,0:T(8,128)(2,1)S(1)} %collective-permute-done.5.refs_2_.refs_4_), channel_id=1, source_target_pairs={{0,4},{1,5},{2,6},{3,7},{4,0},{5,1},{6,2},{7,3},{8,12},{9,13},{10,... | collective-permute-start | bytes 1572872 | tf_op jit(solution)/shard_map/ppermute | solution.py:331
  37.8 20.4 %collective-permute-start.12 = (bf16[256,1024]{1,0:T(8,128)(2,1)S(1)}, bf16[256,1024]{1,0:T(8,128)(2,1)S(1)}, u32[]{:S(2)}, u32[]{:S(2)}) collective-permute-start(bf16[256,1024]{1,0:T(8,128)(2,1)S(1)} %collective-permute-done.9.refs_3_.refs_5_), channel_id=1, source_target_pairs={{0,2},{1,3},{2,0},{3,1},{4,6},{5,7},{6,4},{7,5},{8,10},{9,11},{10,... | collective-permute-start | bytes 1572872 | tf_op jit(solution)/shard_map/ppermute | solution.py:328
  55.4 13.5 %collective-permute-start.14 = (bf16[256,1024]{1,0:T(8,128)(2,1)S(1)}, bf16[256,1024]{1,0:T(8,128)(2,1)S(1)}, u32[]{:S(2)}, u32[]{:S(2)}) collective-permute-start(bf16[256,1024]{1,0:T(8,128)(2,1)S(1)} %get-tuple-element.108.refs_4_.refs_7_), channel_id=1, source_target_pairs={{0,4},{1,5},{2,6},{3,7},{4,0},{5,1},{6,2},{7,3},{8,12},{9,13},{10,... | collective-permute-start | bytes 1572872 | tf_op jit(solution)/shard_map/ppermute | solution.py:331
  56.7 13.4 %collective-permute-start.10 = (bf16[256,1024]{1,0:T(8,128)(2,1)S(1)}, bf16[256,1024]{1,0:T(8,128)(2,1)S(1)}, u32[]{:S(2)}, u32[]{:S(2)}) collective-permute-start(bf16[256,1024]{1,0:T(8,128)(2,1)S(1)} %get-tuple-element.108.refs_4_.refs_7_), channel_id=1, source_target_pairs={{0,2},{1,3},{2,0},{3,1},{4,6},{5,7},{6,4},{7,5},{8,10},{9,11},{10,... | collective-permute-start | bytes 1572872 | tf_op jit(solution)/shard_map/ppermute | solution.py:328
  69.0 10.5 %collective-permute-start.15 = (bf16[128,1024]{1,0:T(8,128)(2,1)S(1)}, bf16[128,1024]{1,0:T(8,128)(2,1)S(1)}, u32[]{:S(2)}, u32[]{:S(2)}) collective-permute-start(bf16[128,1024]{1,0:T(8,128)(2,1)S(1)} %slice.24), channel_id=1, source_target_pairs={{0,2},{1,3},{2,0},{3,1},{4,6},{5,7},{6,4},{7,5},{8,10},{9,11},{10,... | collective-permute-start | bytes 786440 | tf_op jit(solution)/shard_map/ppermute | solution.py:328
  70.1 9.4 %collective-permute-start.13 = (bf16[128,1024]{1,0:T(8,128)(2,1)S(1)}, bf16[128,1024]{1,0:T(8,128)(2,1)S(1)}, u32[]{:S(2)}, u32[]{:S(2)}) collective-permute-start(bf16[128,1024]{1,0:T(8,128)(2,1)S(1)} %slice.22), channel_id=1, source_target_pairs={{0,4},{1,5},{2,6},{3,7},{4,0},{5,1},{6,2},{7,3},{8,12},{9,13},{10,... | collective-permute-start | bytes 786440 | tf_op jit(solution)/shard_map/ppermute | solution.py:331
  85.5 2.7 %collective-permute-start.16 = (bf16[128,4096]{1,0:T(8,128)(2,1)S(1)}, bf16[128,4096]{1,0:T(8,128)(2,1)S(1)}, u32[]{:S(2)}, u32[]{:S(2)}) collective-permute-start(bf16[128,4096]{1,0:T(8,128)(2,1)S(1)} %get-tuple-element.122), channel_id=1, source_target_pairs={{0,1},{1,0},{2,3},{3,2},{4,5},{5,4},{6,7},{7,6},{8,9},{9,8},{10,11... | collective-permute-start | bytes 3145736 | tf_op jit(solution)/shard_map/ppermute | solution.py:325

commit v12 on v11

--- a/solution.py
+++ b/solution.py
@@ -350,19 +350,21 @@
         pairs = [(i, (i - 1) % leaves) for i in range(leaves)]
         return lax.ppermute(rows_held, "leaf", pairs if step < leaves - 1 else pairs[1:])
 
-    own_x, own_y = to_x(own), [to_y(own, step) for step in steps]
-    own, q_got = lax.optimization_barrier((own, to_core(q_other)))
-    q_pair = (q_mine, q_got)
     direct = leaves == 4
     ahead = [own]
     if direct:
-        for pairs in (((1, 0), (2, 1), (3, 2)), ((0, 2), (3, 1)), ((0, 1), (1, 2))):
+        for pairs in (((1, 0), (2, 1), (3, 2)), ((0, 2), (3, 1))):
             ahead.append(lax.ppermute(own, "leaf", pairs))
     elif leaves > 1:
         ahead.append(hop(1, own))
+    own, q_got = lax.optimization_barrier((own, to_core(q_other)))
+    q_pair = (q_mine, q_got)
+    own_x, own_y = to_x(own), [to_y(own, step) for step in steps]
     state = run([own, root], (members(0, "own") + members(1, "root"),), q_pair, None, False)
 
-    (root,) = after(state, root)
+    root, sent_up = after(state, root, own)
+    if direct:
+        before = lax.ppermute(sent_up, "leaf", ((0, 1), (1, 2)))
     root_x, root_y = to_x(root), [to_y(root, step) for step in steps]
 
     def near(kind):
@@ -377,8 +379,8 @@
     state = run([own_x, *own_y], tuple(near("own")), None, state, False)
     if direct:
         ahead = after(state, *ahead)
-        relay = pick(state, expansion, lambda table, g: jnp.where(table[0, 0] == 3, 1, 0), ahead[1:3])
-        ahead.append(lax.ppermute(relay, "leaf", [(1, 0)]))
+        relay = pick(state, expansion, lambda table, g: jnp.where(table[0, 0] == 3, 1, 0), ahead[1:])
+        ahead += [before, lax.ppermute(relay, "leaf", [(1, 0)])]
     else:
         for step in range(3, leaves):
             (held,) = fence(state, ahead[-1])

time: 90 us -> 87.2 us (0.969)
  waiting for transfers between devices: 26 us -> 9.24 us
  starting transfers between devices: 23.3 us -> 30.6 us
  Pallas kernels: 39.8 us -> 46.6 us
    ppermute x1 -> x2, waiting for transfers between devices: 14.4 us -> 0.01 us  [the longest x1 0.01 us: on_device(): before = lax.ppermute(sent_up, 'leaf', ((0, 1), (1, 2)))]
    ppermute x3 -> x2, waiting for transfers between devices: 7.9 us -> 0.01 us  [on_device(): ahead.append(lax.ppermute(own, 'leaf', pairs))]
    pallas_call x6, Pallas kernels: 34.1 us -> 40.9 us  [attend(): pl.pallas_call(functools.partial(attend_kernel, ny, rows, len(arrays), gr...]
    ppermute x5, waiting for transfers between devices: 0.1 us -> 4.83 us  [to_y(): lax.ppermute(array, 'ctx', [(index(x, y, k), index(x, y + step, k)) for x...]
    ppermute x1 -> x2, starting transfers between devices: 1.29 us -> 5.9 us  [the longest x1 4.61 us: on_device(): before = lax.ppermute(sent_up, 'leaf', ((0, 1), (1, 2)))]
    ppermute x5, starting transfers between devices: 7.23 us -> 11.1 us  [to_y(): lax.ppermute(array, 'ctx', [(index(x, y, k), index(x, y + step, k)) for x...]
    ppermute x5, starting transfers between devices: 6.75 us -> 5.59 us  [to_x(): lax.ppermute(array, 'ctx', [(index(x, y, k), index(x + 1, y, k)) for x, y...]
    ppermute x3 -> x2, starting transfers between devices: 7.11 us -> 7.05 us  [on_device(): ahead.append(lax.ppermute(own, 'leaf', pairs))]
  transfers between devices with their start and end apart: 17 -> 17, of which waited for: 5 -> 4; matrix products, arithmetic and copies ran while one was open for 0% -> 0% of each run, Pallas kernels for 35% -> 44%
where the time goes in v12:
time: 87.2 us; the launch traced here: 87 us
  Pallas kernels  46.6 us (53%)
  starting transfers between devices  30.6 us (35%)
  waiting for transfers between devices  9.24 us (11%)
    pallas_call x6, Pallas kernels, attend(): pl.pallas_call(functools.partial(attend_kernel, ny, rows, len(arrays), gr...  40.9 us
    ppermute x5, starting transfers between devices, to_y(): lax.ppermute(array, 'ctx', [(index(x, y, k), index(x, y + step, k)) for x...  11.1 us
    ppermute x2, starting transfers between devices, on_device(): ahead.append(lax.ppermute(own, 'leaf', pairs))  7.05 us
    ppermute x5, starting transfers between devices, to_x(): lax.ppermute(array, 'ctx', [(index(x, y, k), index(x + 1, y, k)) for x, y...  5.59 us
    ppermute x5, waiting for transfers between devices, to_y(): lax.ppermute(array, 'ctx', [(index(x, y, k), index(x, y + step, k)) for x...  4.83 us
    ppermute x1, starting transfers between devices, on_device(): before = lax.ppermute(sent_up, 'leaf', ((0, 1), (1, 2)))  4.61 us
    pallas_call x2, Pallas kernels, pack(): pl.pallas_call(kernel, in_specs=[anywhere] * len(arrays), out_specs=[anyw...  2.9 us
    ppermute x3, waiting for transfers between devices, to_core(): lax.ppermute(array, 'ctx', [(index(x, y, k), index(x, y, k + 1)) for x, y...  2.65 us
  transfers between devices with their start and end apart: 17, of which 4 were waited for; matrix products, arithmetic and copies ran while one was open for 0% of the time, Pallas kernels for 44%

profile of v12, /device:TPU:0, one launch (start us, length us, event | category | flops | bytes accessed | tf_op | source)
XLA Modules:
  0.0 87.0 jit_solution(4278609784372319714)
XLA Ops:
  0.0 1.3 %shard_map.73 = (bf16[256,1024]{1,0:T(8,128)(2,1)S(1)}, bf16[256,1024]{1,0:T(8,128)(2,1)S(1)}) custom-call(bf16[128,1024]{1,0:T(8,128)(2,1)} %refs_0_.7, bf16[128,1024]{1,0:T(8,128)(2,1)} %refs_1_.7, bf16[128,1024]{1,0:T(8,128)(2,1)} %refs_2_.1, bf16[128,1024]{1,0:T(8,128)(2,1)} %refs_3_.1), custom_call_target="tpu_custom_call" | custom-call | tf_op jit(solution)/shard_map/pallas_call | solution.py:236
  1.4 0.5 collective-permute-start
  1.9 1.6 %shard_map.74 = (bf16[128,4096]{1,0:T(8,128)(2,1)S(1)}, bf16[128,4096]{1,0:T(8,128)(2,1)S(1)}) custom-call(bf16[128,8192]{1,0:T(8,128)(2,1)} %refs_0_.8), custom_call_target="tpu_custom_call" | custom-call | tf_op jit(solution)/shard_map/pallas_call | solution.py:236
  3.5 0.3 collective-permute-start.3
  3.9 5.8 %collective-permute-start.2 = (bf16[256,1024]{1,0:T(8,128)(2,1)S(1)}, bf16[256,1024]{1,0:T(8,128)(2,1)S(1)}, u32[]{:S(2)}, u32[]{:S(2)}) collective-permute-start(bf16[256,1024]{1,0:T(8,128)(2,1)S(1)} %pad_maximum_fusion.refs_4_.refs_6_.refs_0_), channel_id=1, source_target_pairs={{0,16},{24,8},{1,17},{25,9},{2,18},{26,10},{3,19},{27,11},{4,20},{... | collective-permute-start | bytes 1572872 | tf_op jit(solution)/shard_map/ppermute | solution.py:357
  9.7 1.3 %collective-permute-start.1 = (bf16[256,1024]{1,0:T(8,128)(2,1)S(1)}, bf16[256,1024]{1,0:T(8,128)(2,1)S(1)}, u32[]{:S(2)}, u32[]{:S(2)}) collective-permute-start(bf16[256,1024]{1,0:T(8,128)(2,1)S(1)} %pad_maximum_fusion.refs_4_.refs_6_.refs_0_), channel_id=1, source_target_pairs={{8,0},{16,8},{24,16},{9,1},{17,9},{25,17},{10,2},{18,10},{26,18},{... | collective-permute-start | bytes 1572872 | tf_op jit(solution)/shard_map/ppermute | solution.py:357
  11.0 1.6 %collective-permute-start.5 = (bf16[256,1024]{1,0:T(8,128)(2,1)S(1)}, bf16[256,1024]{1,0:T(8,128)(2,1)S(1)}, u32[]{:S(2)}, u32[]{:S(2)}) collective-permute-start(bf16[256,1024]{1,0:T(8,128)(2,1)S(1)} %pad_maximum_fusion.refs_4_.refs_6_.refs_0_), channel_id=1, source_target_pairs={{0,4},{1,5},{2,6},{3,7},{4,0},{5,1},{6,2},{7,3},{8,12},{9,13},{10,... | collective-permute-start | bytes 1572872 | tf_op jit(solution)/shard_map/ppermute | solution.py:331
  12.6 1.5 %collective-permute-start.4 = (bf16[256,1024]{1,0:T(8,128)(2,1)S(1)}, bf16[256,1024]{1,0:T(8,128)(2,1)S(1)}, u32[]{:S(2)}, u32[]{:S(2)}) collective-permute-start(bf16[256,1024]{1,0:T(8,128)(2,1)S(1)} %pad_maximum_fusion.refs_4_.refs_6_.refs_0_), channel_id=1, source_target_pairs={{0,2},{1,3},{2,0},{3,1},{4,6},{5,7},{6,4},{7,5},{8,10},{9,11},{10,... | collective-permute-start | bytes 1572872 | tf_op jit(solution)/shard_map/ppermute | solution.py:328
  14.1 7.3 %shard_map.75 = (f32[8,128]{1,0:T(8,128)S(1)}, f32[4,2,1024,384]{3,2,1,0:T(8,128)S(1)}, bf16[4,2,1024,128]{3,2,1,0:T(8,128)(2,1)S(1)}) custom-call(s32[2,4]{1,0:T(2,128)S(1)} %copy-done, s32[4]{0:T(128)S(1)} %copy-done.1, bf16[128,4096]{1,0:T(8,128)(2,1)S(1)} %get-tuple-element.72.refs_2_, bf16[128,4096]{1,0:T(8,128)(2,1)S(1)} %collective-permute-done.3.refs_3_, ...), custom_call_target="tpu_custom_call" | custom-call | flops 4294967296 | bytes 4194304 | tf_op jit(solution)/shard_map/pallas_call | solution.py:301
  21.5 0.6 collective-permute-start.9
  22.0 3.8 %collective-permute-done.5.refs_3_.refs_5_ = bf16[256,1024]{1,0:T(8,128)(2,1)S(1)} collective-permute-done((bf16[256,1024]{1,0:T(8,128)(2,1)S(1)}, bf16[256,1024]{1,0:T(8,128)(2,1)S(1)}, u32[]{:S(2)}, u32[]{:S(2)}) %collective-permute-start.5) | collective-permute-done | bytes 524320 | tf_op jit(solution)/shard_map/ppermute | solution.py:331
  25.9 1.5 %collective-permute-start.8 = (bf16[256,1024]{1,0:T(8,128)(2,1)S(1)}, bf16[256,1024]{1,0:T(8,128)(2,1)S(1)}, u32[]{:S(2)}, u32[]{:S(2)}) collective-permute-start(bf16[256,1024]{1,0:T(8,128)(2,1)S(1)} %pad_maximum_fusion.1.refs_5_.refs_7_), channel_id=1, source_target_pairs={{0,2},{1,3},{2,0},{3,1},{4,6},{5,7},{6,4},{7,5},{8,10},{9,11},{10,... | collective-permute-start | bytes 1572872 | tf_op jit(solution)/shard_map/ppermute | solution.py:328
  27.3 4.6 %collective-permute-start.6 = (bf16[256,1024]{1,0:T(8,128)(2,1)S(1)}, bf16[256,1024]{1,0:T(8,128)(2,1)S(1)}, u32[]{:S(2)}, u32[]{:S(2)}) collective-permute-start(bf16[256,1024]{1,0:T(8,128)(2,1)S(1)} %pad_maximum_fusion.refs_4_.refs_6_.refs_0_), channel_id=1, source_target_pairs={{0,8},{8,16},{1,9},{9,17},{2,10},{10,18},{3,11},{11,19},{4,12},{12... | collective-permute-start | bytes 1572872 | tf_op jit(solution)/shard_map/ppermute | solution.py:367
  32.0 1.2 %shard_map.76 = (f32[8,128]{1,0:T(8,128)S(1)}, f32[4,2,1024,384]{3,2,1,0:T(8,128)S(1)}, bf16[4,2,1024,128]{3,2,1,0:T(8,128)(2,1)S(1)}) custom-call(s32[2,4]{1,0:T(2,128)S(1)} %copy-done, s32[4]{0:T(128)S(1)} %copy-done.1, bf16[256,1024]{1,0:T(8,128)(2,1)S(1)} %collective-permute-done.4.refs_2_.refs_4_, ...), custom_call_target="tpu_custom_call", output_to_operand_aliasing={{1}: (7, {}), {2}: (8, {})} | custom-call | flops 4294967296 | bytes 4194304 | tf_op jit(solution)/shard_map/pallas_call | solution.py:301
  33.2 0.6 shard_map.77
  33.8 1.3 %collective-permute-start.7 = (bf16[256,1024]{1,0:T(8,128)(2,1)S(1)}, bf16[256,1024]{1,0:T(8,128)(2,1)S(1)}, u32[]{:S(2)}, u32[]{:S(2)}) collective-permute-start(bf16[256,1024]{1,0:T(8,128)(2,1)S(1)} %get-tuple-element.89), channel_id=1, source_target_pairs={{8,0},{9,1},{10,2},{11,3},{12,4},{13,5},{14,6},{15,7}} | collective-permute-start | bytes 1572872 | tf_op jit(solution)/shard_map/ppermute | solution.py:383
  35.1 1.0 %collective-permute-done.9.refs_3_.refs_5_ = bf16[256,1024]{1,0:T(8,128)(2,1)S(1)} collective-permute-done((bf16[256,1024]{1,0:T(8,128)(2,1)S(1)}, bf16[256,1024]{1,0:T(8,128)(2,1)S(1)}, u32[]{:S(2)}, u32[]{:S(2)}) %collective-permute-start.9) | collective-permute-done | bytes 524320 | tf_op jit(solution)/shard_map/ppermute | solution.py:331
  36.1 1.7 %collective-permute-done.8.refs_2_.refs_4_ = bf16[256,1024]{1,0:T(8,128)(2,1)S(1)} collective-permute-done((bf16[256,1024]{1,0:T(8,128)(2,1)S(1)}, bf16[256,1024]{1,0:T(8,128)(2,1)S(1)}, u32[]{:S(2)}, u32[]{:S(2)}) %collective-permute-start.8) | collective-permute-done | bytes 524320 | tf_op jit(solution)/shard_map/ppermute | solution.py:328
  37.8 5.6 %collective-permute-start.11 = (bf16[256,1024]{1,0:T(8,128)(2,1)S(1)}, bf16[256,1024]{1,0:T(8,128)(2,1)S(1)}, u32[]{:S(2)}, u32[]{:S(2)}) collective-permute-start(bf16[256,1024]{1,0:T(8,128)(2,1)S(1)} %collective-permute-done.4.refs_2_.refs_4_), channel_id=1, source_target_pairs={{0,4},{1,5},{2,6},{3,7},{4,0},{5,1},{6,2},{7,3},{8,12},{9,13},{10,... | collective-permute-start | bytes 1572872 | tf_op jit(solution)/shard_map/ppermute | solution.py:331
  43.5 0.5 collective-permute-start.12
  44.0 7.9 %shard_map.78 = (f32[8,128]{1,0:T(8,128)S(1)}, f32[4,2,1024,384]{3,2,1,0:T(8,128)S(1)}, bf16[4,2,1024,128]{3,2,1,0:T(8,128)(2,1)S(1)}) custom-call(s32[2,4]{1,0:T(2,128)S(1)} %copy-done, s32[4]{0:T(128)S(1)} %copy-done.1, bf16[256,1024]{1,0:T(8,128)(2,1)S(1)} %collective-permute-done.8.refs_2_.refs_4_, ...), custom_call_target="tpu_custom_call", output_to_operand_aliasing={{1}: (7, {}), {2}: (8, {})} | custom-call | flops 4294967296 | bytes 4194304 | tf_op jit(solution)/shard_map/pallas_call | solution.py:301
  51.9 0.8 shard_map.79
  52.7 2.9 %collective-permute-start.14 = (bf16[256,1024]{1,0:T(8,128)(2,1)S(1)}, bf16[256,1024]{1,0:T(8,128)(2,1)S(1)}, u32[]{:S(2)}, u32[]{:S(2)}) collective-permute-start(bf16[256,1024]{1,0:T(8,128)(2,1)S(1)} %get-tuple-element.108.refs_4_.refs_7_), channel_id=1, source_target_pairs={{0,4},{1,5},{2,6},{3,7},{4,0},{5,1},{6,2},{7,3},{8,12},{9,13},{10,... | collective-permute-start | bytes 1572872 | tf_op jit(solution)/shard_map/ppermute | solution.py:331
  55.7 0.5 collective-permute-start.10
  56.2 10.7 %shard_map.80 = (f32[8,128]{1,0:T(8,128)S(1)}, f32[4,2,1024,384]{3,2,1,0:T(8,128)S(1)}, bf16[4,2,1024,128]{3,2,1,0:T(8,128)(2,1)S(1)}) custom-call(s32[2,4]{1,0:T(2,128)S(1)} %copy-done, s32[4]{0:T(128)S(1)} %copy-done.1, bf16[256,1024]{1,0:T(8,128)(2,1)S(1)} %collective-permute-done.11.refs_2_.refs_5_, ...), custom_call_target="tpu_custom_call", output_to_operand_aliasing={{1}: (9, {}), {2}: (10, {})} | custom-call | flops 6442450944 | bytes 4194304 | tf_op jit(solution)/shard_map/pallas_call | solution.py:301
  67.0 1.6 %collective-permute-start.15 = (bf16[128,1024]{1,0:T(8,128)(2,1)S(1)}, bf16[128,1024]{1,0:T(8,128)(2,1)S(1)}, u32[]{:S(2)}, u32[]{:S(2)}) collective-permute-start(bf16[128,1024]{1,0:T(8,128)(2,1)S(1)} %slice.24), channel_id=1, source_target_pairs={{0,2},{1,3},{2,0},{3,1},{4,6},{5,7},{6,4},{7,5},{8,10},{9,11},{10,... | collective-permute-start | bytes 786440 | tf_op jit(solution)/shard_map/ppermute | solution.py:328
  68.6 0.4 collective-permute-start.13
  68.9 7.8 %shard_map.81 = (f32[8,128]{1,0:T(8,128)S(1)}, f32[4,2,1024,384]{3,2,1,0:T(8,128)S(1)}, bf16[4,2,1024,128]{3,2,1,0:T(8,128)(2,1)S(1)}) custom-call(s32[2,4]{1,0:T(2,128)S(1)} %copy-done, s32[4]{0:T(128)S(1)} %copy-done.1, bf16[256,1024]{1,0:T(8,128)(2,1)S(1)} %collective-permute-done.10.refs_2_.refs_4_, ...), custom_call_target="tpu_custom_call", output_to_operand_aliasing={{1}: (7, {}), {2}: (8, {})} | custom-call | flops 4294967296 | bytes 4194304 | tf_op jit(solution)/shard_map/pallas_call | solution.py:301
  76.7 6.0 %shard_map.82 = (bf16[128,4096]{1,0:T(8,128)(2,1)S(1)}, bf16[128,4096]{1,0:T(8,128)(2,1)S(1)}, f32[4,2,1024,384]{3,2,1,0:T(8,128)S(1)}, bf16[4,2,1024,128]{3,2,1,0:T(8,128)(2,1)S(1)}) custom-call(s32[2,4]{1,0:T(2,128)S(1)} %copy-done, s32[4]{0:T(128)S(1)} %copy-done.1, ...), custom_call_target="tpu_custom_call", output_to_operand_aliasing={{2}: (7, {}), {3}: (8, {})} | custom-call | flops 2147483648 | bytes 4194304 | tf_op jit(solution)/shard_map/pallas_call | solution.py:301
  82.7 0.1 collective-permute-start.16
  82.8 2.6 %collective-permute-done.16.got_ref = bf16[128,4096]{1,0:T(8,128)(2,1)S(1)} collective-permute-done((bf16[128,4096]{1,0:T(8,128)(2,1)S(1)}, bf16[128,4096]{1,0:T(8,128)(2,1)S(1)}, u32[]{:S(2)}, u32[]{:S(2)}) %collective-permute-start.16) | collective-permute-done | bytes 1048608 | tf_op jit(solution)/shard_map/ppermute | solution.py:325
  85.5 1.3 %shard_map.83 = bf16[128,8192]{1,0:T(8,128)(2,1)} custom-call(bf16[128,4096]{1,0:T(8,128)(2,1)S(1)} %get-tuple-element.121.mine_ref, bf16[128,4096]{1,0:T(8,128)(2,1)S(1)} %collective-permute-done.16.got_ref), custom_call_target="tpu_custom_call" | custom-call | tf_op jit(solution)/shard_map/pallas_call | solution.py:260
  (23 shorter events, 0.2 us)
Async XLA Ops:
  1.4 2.1 %collective-permute-start = (bf16[256,1024]{1,0:T(8,128)(2,1)S(1)}, bf16[256,1024]{1,0:T(8,128)(2,1)S(1)}, u32[]{:S(2)}, u32[]{:S(2)}) collective-permute-start(bf16[256,1024]{1,0:T(8,128)(2,1)S(1)} %get-tuple-element.68), channel_id=1, source_target_pairs={{0,1},{1,0},{2,3},{3,2},{4,5},{5,4},{6,7},{7,6},{8,9},{9,8},{10,11... | collective-permute-start | bytes 1572872 | tf_op jit(solution)/shard_map/ppermute | solution.py:325
  3.5 7.5 %collective-permute-start.3 = (bf16[128,4096]{1,0:T(8,128)(2,1)S(1)}, bf16[128,4096]{1,0:T(8,128)(2,1)S(1)}, u32[]{:S(2)}, u32[]{:S(2)}) collective-permute-start(bf16[128,4096]{1,0:T(8,128)(2,1)S(1)} %get-tuple-element.70), channel_id=1, source_target_pairs={{0,1},{1,0},{2,3},{3,2},{4,5},{5,4},{6,7},{7,6},{8,9},{9,8},{10,11... | collective-permute-start | bytes 3145736 | tf_op jit(solution)/shard_map/ppermute | solution.py:325
  3.8 10.3 %copy-start = (s32[2,4]{1,0:T(2,128)S(1)}, s32[2,4]{1,0:T(2,128)}, u32[]{:S(2)}) copy-start(s32[2,4]{1,0:T(2,128)} %refs_0_.14) | copy-start | bytes 100
  3.8 10.3 %copy-start.1 = (s32[4]{0:T(128)S(1)}, s32[4]{0:T(128)}, u32[]{:S(2)}) copy-start(s32[4]{0:T(128)} %refs_1_.13) | copy-start | bytes 52
  3.9 29.3 %collective-permute-start.2 = (bf16[256,1024]{1,0:T(8,128)(2,1)S(1)}, bf16[256,1024]{1,0:T(8,128)(2,1)S(1)}, u32[]{:S(2)}, u32[]{:S(2)}) collective-permute-start(bf16[256,1024]{1,0:T(8,128)(2,1)S(1)} %pad_maximum_fusion.refs_4_.refs_6_.refs_0_), channel_id=1, source_target_pairs={{0,16},{24,8},{1,17},{25,9},{2,18},{26,10},{3,19},{27,11},{4,20},{... | collective-permute-start | bytes 1572872 | tf_op jit(solution)/shard_map/ppermute | solution.py:357
  9.7 23.5 %collective-permute-start.1 = (bf16[256,1024]{1,0:T(8,128)(2,1)S(1)}, bf16[256,1024]{1,0:T(8,128)(2,1)S(1)}, u32[]{:S(2)}, u32[]{:S(2)}) collective-permute-start(bf16[256,1024]{1,0:T(8,128)(2,1)S(1)} %pad_maximum_fusion.refs_4_.refs_6_.refs_0_), channel_id=1, source_target_pairs={{8,0},{16,8},{24,16},{9,1},{17,9},{25,17},{10,2},{18,10},{26,18},{... | collective-permute-start | bytes 1572872 | tf_op jit(solution)/shard_map/ppermute | solution.py:357
  11.0 14.9 %collective-permute-start.5 = (bf16[256,1024]{1,0:T(8,128)(2,1)S(1)}, bf16[256,1024]{1,0:T(8,128)(2,1)S(1)}, u32[]{:S(2)}, u32[]{:S(2)}) collective-permute-start(bf16[256,1024]{1,0:T(8,128)(2,1)S(1)} %pad_maximum_fusion.refs_4_.refs_6_.refs_0_), channel_id=1, source_target_pairs={{0,4},{1,5},{2,6},{3,7},{4,0},{5,1},{6,2},{7,3},{8,12},{9,13},{10,... | collective-permute-start | bytes 1572872 | tf_op jit(solution)/shard_map/ppermute | solution.py:331
  12.6 14.8 %collective-permute-start.4 = (bf16[256,1024]{1,0:T(8,128)(2,1)S(1)}, bf16[256,1024]{1,0:T(8,128)(2,1)S(1)}, u32[]{:S(2)}, u32[]{:S(2)}) collective-permute-start(bf16[256,1024]{1,0:T(8,128)(2,1)S(1)} %pad_maximum_fusion.refs_4_.refs_6_.refs_0_), channel_id=1, source_target_pairs={{0,2},{1,3},{2,0},{3,1},{4,6},{5,7},{6,4},{7,5},{8,10},{9,11},{10,... | collective-permute-start | bytes 1572872 | tf_op jit(solution)/shard_map/ppermute | solution.py:328
  21.5 14.7 %collective-permute-start.9 = (bf16[256,1024]{1,0:T(8,128)(2,1)S(1)}, bf16[256,1024]{1,0:T(8,128)(2,1)S(1)}, u32[]{:S(2)}, u32[]{:S(2)}) collective-permute-start(bf16[256,1024]{1,0:T(8,128)(2,1)S(1)} %pad_maximum_fusion.1.refs_5_.refs_7_), channel_id=1, source_target_pairs={{0,4},{1,5},{2,6},{3,7},{4,0},{5,1},{6,2},{7,3},{8,12},{9,13},{10,... | collective-permute-start | bytes 1572872 | tf_op jit(solution)/shard_map/ppermute | solution.py:331
  25.9 12.0 %collective-permute-start.8 = (bf16[256,1024]{1,0:T(8,128)(2,1)S(1)}, bf16[256,1024]{1,0:T(8,128)(2,1)S(1)}, u32[]{:S(2)}, u32[]{:S(2)}) collective-permute-start(bf16[256,1024]{1,0:T(8,128)(2,1)S(1)} %pad_maximum_fusion.1.refs_5_.refs_7_), channel_id=1, source_target_pairs={{0,2},{1,3},{2,0},{3,1},{4,6},{5,7},{6,4},{7,5},{8,10},{9,11},{10,... | collective-permute-start | bytes 1572872 | tf_op jit(solution)/shard_map/ppermute | solution.py:328
  27.3 24.5 %collective-permute-start.6 = (bf16[256,1024]{1,0:T(8,128)(2,1)S(1)}, bf16[256,1024]{1,0:T(8,128)(2,1)S(1)}, u32[]{:S(2)}, u32[]{:S(2)}) collective-permute-start(bf16[256,1024]{1,0:T(8,128)(2,1)S(1)} %pad_maximum_fusion.refs_4_.refs_6_.refs_0_), channel_id=1, source_target_pairs={{0,8},{8,16},{1,9},{9,17},{2,10},{10,18},{3,11},{11,19},{4,12},{12... | collective-permute-start | bytes 1572872 | tf_op jit(solution)/shard_map/ppermute | solution.py:367
  33.8 18.1 %collective-permute-start.7 = (bf16[256,1024]{1,0:T(8,128)(2,1)S(1)}, bf16[256,1024]{1,0:T(8,128)(2,1)S(1)}, u32[]{:S(2)}, u32[]{:S(2)}) collective-permute-start(bf16[256,1024]{1,0:T(8,128)(2,1)S(1)} %get-tuple-element.89), channel_id=1, source_target_pairs={{8,0},{9,1},{10,2},{11,3},{12,4},{13,5},{14,6},{15,7}} | collective-permute-start | bytes 1572872 | tf_op jit(solution)/shard_map/ppermute | solution.py:383
  37.8 18.3 %collective-permute-start.11 = (bf16[256,1024]{1,0:T(8,128)(2,1)S(1)}, bf16[256,1024]{1,0:T(8,128)(2,1)S(1)}, u32[]{:S(2)}, u32[]{:S(2)}) collective-permute-start(bf16[256,1024]{1,0:T(8,128)(2,1)S(1)} %collective-permute-done.4.refs_2_.refs_4_), channel_id=1, source_target_pairs={{0,4},{1,5},{2,6},{3,7},{4,0},{5,1},{6,2},{7,3},{8,12},{9,13},{10,... | collective-permute-start | bytes 1572872 | tf_op jit(solution)/shard_map/ppermute | solution.py:331
  43.5 12.7 %collective-permute-start.12 = (bf16[256,1024]{1,0:T(8,128)(2,1)S(1)}, bf16[256,1024]{1,0:T(8,128)(2,1)S(1)}, u32[]{:S(2)}, u32[]{:S(2)}) collective-permute-start(bf16[256,1024]{1,0:T(8,128)(2,1)S(1)} %collective-permute-done.9.refs_3_.refs_5_), channel_id=1, source_target_pairs={{0,2},{1,3},{2,0},{3,1},{4,6},{5,7},{6,4},{7,5},{8,10},{9,11},{10,... | collective-permute-start | bytes 1572872 | tf_op jit(solution)/shard_map/ppermute | solution.py:328
  52.7 14.2 %collective-permute-start.14 = (bf16[256,1024]{1,0:T(8,128)(2,1)S(1)}, bf16[256,1024]{1,0:T(8,128)(2,1)S(1)}, u32[]{:S(2)}, u32[]{:S(2)}) collective-permute-start(bf16[256,1024]{1,0:T(8,128)(2,1)S(1)} %get-tuple-element.108.refs_4_.refs_7_), channel_id=1, source_target_pairs={{0,4},{1,5},{2,6},{3,7},{4,0},{5,1},{6,2},{7,3},{8,12},{9,13},{10,... | collective-permute-start | bytes 1572872 | tf_op jit(solution)/shard_map/ppermute | solution.py:331
  55.7 12.9 %collective-permute-start.10 = (bf16[256,1024]{1,0:T(8,128)(2,1)S(1)}, bf16[256,1024]{1,0:T(8,128)(2,1)S(1)}, u32[]{:S(2)}, u32[]{:S(2)}) collective-permute-start(bf16[256,1024]{1,0:T(8,128)(2,1)S(1)} %get-tuple-element.108.refs_4_.refs_7_), channel_id=1, source_target_pairs={{0,2},{1,3},{2,0},{3,1},{4,6},{5,7},{6,4},{7,5},{8,10},{9,11},{10,... | collective-permute-start | bytes 1572872 | tf_op jit(solution)/shard_map/ppermute | solution.py:328
  67.0 9.7 %collective-permute-start.15 = (bf16[128,1024]{1,0:T(8,128)(2,1)S(1)}, bf16[128,1024]{1,0:T(8,128)(2,1)S(1)}, u32[]{:S(2)}, u32[]{:S(2)}) collective-permute-start(bf16[128,1024]{1,0:T(8,128)(2,1)S(1)} %slice.24), channel_id=1, source_target_pairs={{0,2},{1,3},{2,0},{3,1},{4,6},{5,7},{6,4},{7,5},{8,10},{9,11},{10,... | collective-permute-start | bytes 786440 | tf_op jit(solution)/shard_map/ppermute | solution.py:328
  68.6 8.2 %collective-permute-start.13 = (bf16[128,1024]{1,0:T(8,128)(2,1)S(1)}, bf16[128,1024]{1,0:T(8,128)(2,1)S(1)}, u32[]{:S(2)}, u32[]{:S(2)}) collective-permute-start(bf16[128,1024]{1,0:T(8,128)(2,1)S(1)} %slice.22), channel_id=1, source_target_pairs={{0,4},{1,5},{2,6},{3,7},{4,0},{5,1},{6,2},{7,3},{8,12},{9,13},{10,... | collective-permute-start | bytes 786440 | tf_op jit(solution)/shard_map/ppermute | solution.py:331
  82.7 2.7 %collective-permute-start.16 = (bf16[128,4096]{1,0:T(8,128)(2,1)S(1)}, bf16[128,4096]{1,0:T(8,128)(2,1)S(1)}, u32[]{:S(2)}, u32[]{:S(2)}) collective-permute-start(bf16[128,4096]{1,0:T(8,128)(2,1)S(1)} %get-tuple-element.122), channel_id=1, source_target_pairs={{0,1},{1,0},{2,3},{3,2},{4,5},{5,4},{6,7},{7,6},{8,9},{9,8},{10,11... | collective-permute-start | bytes 3145736 | tf_op jit(solution)/shard_map/ppermute | solution.py:325

commit v13 on v12

--- a/solution.py
+++ b/solution.py
@@ -350,6 +350,9 @@
         pairs = [(i, (i - 1) % leaves) for i in range(leaves)]
         return lax.ppermute(rows_held, "leaf", pairs if step < leaves - 1 else pairs[1:])
 
+    own_x, own_y = to_x(own), [to_y(own, step) for step in steps]
+    own, q_got = lax.optimization_barrier((own, to_core(q_other)))
+    q_pair = (q_mine, q_got)
     direct = leaves == 4
     ahead = [own]
     if direct:
@@ -357,9 +360,6 @@
             ahead.append(lax.ppermute(own, "leaf", pairs))
     elif leaves > 1:
         ahead.append(hop(1, own))
-    own, q_got = lax.optimization_barrier((own, to_core(q_other)))
-    q_pair = (q_mine, q_got)
-    own_x, own_y = to_x(own), [to_y(own, step) for step in steps]
     state = run([own, root], (members(0, "own") + members(1, "root"),), q_pair, None, False)
 
     root, sent_up = after(state, root, own)

time: 87.2 us -> 86.1 us (0.987)
  starting transfers between devices: 30.6 us -> 28.3 us
  waiting for transfers between devices: 9.24 us -> 10.6 us
    ppermute x1, waiting for transfers between devices: 0.01 us -> 3.6 us  [on_device(): ahead += [before, lax.ppermute(relay, 'leaf', [(1, 0)])]]
    ppermute x5, starting transfers between devices: 11.1 us -> 9.27 us  [to_y(): lax.ppermute(array, 'ctx', [(index(x, y, k), index(x, y + step, k)) for x...]
    ppermute x5, waiting for transfers between devices: 4.83 us -> 3.37 us  [to_y(): lax.ppermute(array, 'ctx', [(index(x, y, k), index(x, y + step, k)) for x...]
    ppermute x2, starting transfers between devices: 7.05 us -> 5.82 us  [on_device(): ahead.append(lax.ppermute(own, 'leaf', pairs))]
where the time goes in v13:
time: 86.1 us; the launch traced here: 85.8 us
  Pallas kernels  46.4 us (54%)
  starting transfers between devices  28.3 us (33%)
  waiting for transfers between devices  10.6 us (12%)
    pallas_call x6, Pallas kernels, attend(): pl.pallas_call(functools.partial(attend_kernel, ny, rows, len(arrays), gr...  40.7 us
    ppermute x5, starting transfers between devices, to_y(): lax.ppermute(array, 'ctx', [(index(x, y, k), index(x, y + step, k)) for x...  9.27 us
    ppermute x5, starting transfers between devices, to_x(): lax.ppermute(array, 'ctx', [(index(x, y, k), index(x + 1, y, k)) for x, y...  6.44 us
    ppermute x2, starting transfers between devices, on_device(): ahead.append(lax.ppermute(own, 'leaf', pairs))  5.82 us
    ppermute x1, starting transfers between devices, on_device(): before = lax.ppermute(sent_up, 'leaf', ((0, 1), (1, 2)))  4.56 us
    ppermute x1, waiting for transfers between devices, on_device(): ahead += [before, lax.ppermute(relay, 'leaf', [(1, 0)])]  3.6 us
    ppermute x5, waiting for transfers between devices, to_y(): lax.ppermute(array, 'ctx', [(index(x, y, k), index(x, y + step, k)) for x...  3.37 us
    pallas_call x2, Pallas kernels, pack(): pl.pallas_call(kernel, in_specs=[anywhere] * len(arrays), out_specs=[anyw...  2.9 us
  transfers between devices with their start and end apart: 17, of which 4 were waited for; matrix products, arithmetic and copies ran while one was open for 0% of the time, Pallas kernels for 44%

profile of v13, /device:TPU:0, one launch (start us, length us, event | category | flops | bytes accessed | tf_op | source)
XLA Modules:
  0.0 85.8 jit_solution(8578908759146869041)
XLA Ops:
  0.0 1.3 %shard_map.73 = (bf16[256,1024]{1,0:T(8,128)(2,1)S(1)}, bf16[256,1024]{1,0:T(8,128)(2,1)S(1)}) custom-call(bf16[128,1024]{1,0:T(8,128)(2,1)} %refs_0_.7, bf16[128,1024]{1,0:T(8,128)(2,1)} %refs_1_.7, bf16[128,1024]{1,0:T(8,128)(2,1)} %refs_2_.1, bf16[128,1024]{1,0:T(8,128)(2,1)} %refs_3_.1), custom_call_target="tpu_custom_call" | custom-call | tf_op jit(solution)/shard_map/pallas_call | solution.py:236
  1.4 0.5 collective-permute-start
  1.9 1.6 %shard_map.74 = (bf16[128,4096]{1,0:T(8,128)(2,1)S(1)}, bf16[128,4096]{1,0:T(8,128)(2,1)S(1)}) custom-call(bf16[128,8192]{1,0:T(8,128)(2,1)} %refs_0_.8), custom_call_target="tpu_custom_call" | custom-call | tf_op jit(solution)/shard_map/pallas_call | solution.py:236
  3.5 0.3 collective-permute-start.1
  3.9 2.8 %collective-permute-start.5 = (bf16[256,1024]{1,0:T(8,128)(2,1)S(1)}, bf16[256,1024]{1,0:T(8,128)(2,1)S(1)}, u32[]{:S(2)}, u32[]{:S(2)}) collective-permute-start(bf16[256,1024]{1,0:T(8,128)(2,1)S(1)} %pad_maximum_fusion.refs_4_.refs_6_.refs_0_), channel_id=1, source_target_pairs={{0,4},{1,5},{2,6},{3,7},{4,0},{5,1},{6,2},{7,3},{8,12},{9,13},{10,... | collective-permute-start | bytes 1572872 | tf_op jit(solution)/shard_map/ppermute | solution.py:331
  6.7 1.5 %collective-permute-start.4 = (bf16[256,1024]{1,0:T(8,128)(2,1)S(1)}, bf16[256,1024]{1,0:T(8,128)(2,1)S(1)}, u32[]{:S(2)}, u32[]{:S(2)}) collective-permute-start(bf16[256,1024]{1,0:T(8,128)(2,1)S(1)} %pad_maximum_fusion.refs_4_.refs_6_.refs_0_), channel_id=1, source_target_pairs={{0,2},{1,3},{2,0},{3,1},{4,6},{5,7},{6,4},{7,5},{8,10},{9,11},{10,... | collective-permute-start | bytes 1572872 | tf_op jit(solution)/shard_map/ppermute | solution.py:328
  8.3 4.5 %collective-permute-start.3 = (bf16[256,1024]{1,0:T(8,128)(2,1)S(1)}, bf16[256,1024]{1,0:T(8,128)(2,1)S(1)}, u32[]{:S(2)}, u32[]{:S(2)}) collective-permute-start(bf16[256,1024]{1,0:T(8,128)(2,1)S(1)} %pad_maximum_fusion.refs_4_.refs_6_.refs_0_), channel_id=1, source_target_pairs={{0,16},{24,8},{1,17},{25,9},{2,18},{26,10},{3,19},{27,11},{4,20},{... | collective-permute-start | bytes 1572872 | tf_op jit(solution)/shard_map/ppermute | solution.py:360
  12.8 1.3 %collective-permute-start.2 = (bf16[256,1024]{1,0:T(8,128)(2,1)S(1)}, bf16[256,1024]{1,0:T(8,128)(2,1)S(1)}, u32[]{:S(2)}, u32[]{:S(2)}) collective-permute-start(bf16[256,1024]{1,0:T(8,128)(2,1)S(1)} %pad_maximum_fusion.refs_4_.refs_6_.refs_0_), channel_id=1, source_target_pairs={{8,0},{16,8},{24,16},{9,1},{17,9},{25,17},{10,2},{18,10},{26,18},{... | collective-permute-start | bytes 1572872 | tf_op jit(solution)/shard_map/ppermute | solution.py:360
  14.1 7.3 %shard_map.75 = (f32[8,128]{1,0:T(8,128)S(1)}, f32[4,2,1024,384]{3,2,1,0:T(8,128)S(1)}, bf16[4,2,1024,128]{3,2,1,0:T(8,128)(2,1)S(1)}) custom-call(s32[2,4]{1,0:T(2,128)S(1)} %copy-done, s32[4]{0:T(128)S(1)} %copy-done.1, bf16[128,4096]{1,0:T(8,128)(2,1)S(1)} %get-tuple-element.72.refs_2_, bf16[128,4096]{1,0:T(8,128)(2,1)S(1)} %collective-permute-done.1.refs_3_, ...), custom_call_target="tpu_custom_call" | custom-call | flops 4294967296 | bytes 4194304 | tf_op jit(solution)/shard_map/pallas_call | solution.py:301
  21.5 0.7 collective-permute-start.9
  22.2 1.5 %collective-permute-start.8 = (bf16[256,1024]{1,0:T(8,128)(2,1)S(1)}, bf16[256,1024]{1,0:T(8,128)(2,1)S(1)}, u32[]{:S(2)}, u32[]{:S(2)}) collective-permute-start(bf16[256,1024]{1,0:T(8,128)(2,1)S(1)} %pad_maximum_fusion.1.refs_5_.refs_7_), channel_id=1, source_target_pairs={{0,2},{1,3},{2,0},{3,1},{4,6},{5,7},{6,4},{7,5},{8,10},{9,11},{10,... | collective-permute-start | bytes 1572872 | tf_op jit(solution)/shard_map/ppermute | solution.py:328
  23.7 4.6 %collective-permute-start.6 = (bf16[256,1024]{1,0:T(8,128)(2,1)S(1)}, bf16[256,1024]{1,0:T(8,128)(2,1)S(1)}, u32[]{:S(2)}, u32[]{:S(2)}) collective-permute-start(bf16[256,1024]{1,0:T(8,128)(2,1)S(1)} %pad_maximum_fusion.refs_4_.refs_6_.refs_0_), channel_id=1, source_target_pairs={{0,8},{8,16},{1,9},{9,17},{2,10},{10,18},{3,11},{11,19},{4,12},{12... | collective-permute-start | bytes 1572872 | tf_op jit(solution)/shard_map/ppermute | solution.py:367
  28.3 1.2 %shard_map.76 = (f32[8,128]{1,0:T(8,128)S(1)}, f32[4,2,1024,384]{3,2,1,0:T(8,128)S(1)}, bf16[4,2,1024,128]{3,2,1,0:T(8,128)(2,1)S(1)}) custom-call(s32[2,4]{1,0:T(2,128)S(1)} %copy-done, s32[4]{0:T(128)S(1)} %copy-done.1, bf16[256,1024]{1,0:T(8,128)(2,1)S(1)} %collective-permute-done.4.refs_2_.refs_4_, ...), custom_call_target="tpu_custom_call", output_to_operand_aliasing={{1}: (7, {}), {2}: (8, {})} | custom-call | flops 4294967296 | bytes 4194304 | tf_op jit(solution)/shard_map/pallas_call | solution.py:301
  29.5 0.6 shard_map.77
  30.1 1.3 %collective-permute-start.7 = (bf16[256,1024]{1,0:T(8,128)(2,1)S(1)}, bf16[256,1024]{1,0:T(8,128)(2,1)S(1)}, u32[]{:S(2)}, u32[]{:S(2)}) collective-permute-start(bf16[256,1024]{1,0:T(8,128)(2,1)S(1)} %get-tuple-element.89), channel_id=1, source_target_pairs={{8,0},{9,1},{10,2},{11,3},{12,4},{13,5},{14,6},{15,7}} | collective-permute-start | bytes 1572872 | tf_op jit(solution)/shard_map/ppermute | solution.py:383
  31.4 3.4 %collective-permute-done.9.refs_3_.refs_5_ = bf16[256,1024]{1,0:T(8,128)(2,1)S(1)} collective-permute-done((bf16[256,1024]{1,0:T(8,128)(2,1)S(1)}, bf16[256,1024]{1,0:T(8,128)(2,1)S(1)}, u32[]{:S(2)}, u32[]{:S(2)}) %collective-permute-start.9) | collective-permute-done | bytes 524320 | tf_op jit(solution)/shard_map/ppermute | solution.py:331
  34.8 0.9 %collective-permute-done.8.refs_2_.refs_4_ = bf16[256,1024]{1,0:T(8,128)(2,1)S(1)} collective-permute-done((bf16[256,1024]{1,0:T(8,128)(2,1)S(1)}, bf16[256,1024]{1,0:T(8,128)(2,1)S(1)}, u32[]{:S(2)}, u32[]{:S(2)}) %collective-permute-start.8) | collective-permute-done | bytes 524320 | tf_op jit(solution)/shard_map/ppermute | solution.py:328
  35.7 3.0 %collective-permute-start.11 = (bf16[256,1024]{1,0:T(8,128)(2,1)S(1)}, bf16[256,1024]{1,0:T(8,128)(2,1)S(1)}, u32[]{:S(2)}, u32[]{:S(2)}) collective-permute-start(bf16[256,1024]{1,0:T(8,128)(2,1)S(1)} %collective-permute-done.4.refs_2_.refs_4_), channel_id=1, source_target_pairs={{0,4},{1,5},{2,6},{3,7},{4,0},{5,1},{6,2},{7,3},{8,12},{9,13},{10,... | collective-permute-start | bytes 1572872 | tf_op jit(solution)/shard_map/ppermute | solution.py:331
  38.8 1.4 %collective-permute-start.12 = (bf16[256,1024]{1,0:T(8,128)(2,1)S(1)}, bf16[256,1024]{1,0:T(8,128)(2,1)S(1)}, u32[]{:S(2)}, u32[]{:S(2)}) collective-permute-start(bf16[256,1024]{1,0:T(8,128)(2,1)S(1)} %collective-permute-done.9.refs_3_.refs_5_), channel_id=1, source_target_pairs={{0,2},{1,3},{2,0},{3,1},{4,6},{5,7},{6,4},{7,5},{8,10},{9,11},{10,... | collective-permute-start | bytes 1572872 | tf_op jit(solution)/shard_map/ppermute | solution.py:328
  40.1 7.7 %shard_map.78 = (f32[8,128]{1,0:T(8,128)S(1)}, f32[4,2,1024,384]{3,2,1,0:T(8,128)S(1)}, bf16[4,2,1024,128]{3,2,1,0:T(8,128)(2,1)S(1)}) custom-call(s32[2,4]{1,0:T(2,128)S(1)} %copy-done, s32[4]{0:T(128)S(1)} %copy-done.1, bf16[256,1024]{1,0:T(8,128)(2,1)S(1)} %collective-permute-done.8.refs_2_.refs_4_, ...), custom_call_target="tpu_custom_call", output_to_operand_aliasing={{1}: (7, {}), {2}: (8, {})} | custom-call | flops 4294967296 | bytes 4194304 | tf_op jit(solution)/shard_map/pallas_call | solution.py:301
  47.8 3.6 %collective-permute-done.7.refs_4_ = bf16[256,1024]{1,0:T(8,128)(2,1)S(1)} collective-permute-done((bf16[256,1024]{1,0:T(8,128)(2,1)S(1)}, bf16[256,1024]{1,0:T(8,128)(2,1)S(1)}, u32[]{:S(2)}, u32[]{:S(2)}) %collective-permute-start.7) | collective-permute-done | bytes 524320 | tf_op jit(solution)/shard_map/ppermute | solution.py:383
  51.4 0.8 shard_map.79
  52.2 1.3 %collective-permute-start.14 = (bf16[256,1024]{1,0:T(8,128)(2,1)S(1)}, bf16[256,1024]{1,0:T(8,128)(2,1)S(1)}, u32[]{:S(2)}, u32[]{:S(2)}) collective-permute-start(bf16[256,1024]{1,0:T(8,128)(2,1)S(1)} %get-tuple-element.108.refs_4_.refs_7_), channel_id=1, source_target_pairs={{0,4},{1,5},{2,6},{3,7},{4,0},{5,1},{6,2},{7,3},{8,12},{9,13},{10,... | collective-permute-start | bytes 1572872 | tf_op jit(solution)/shard_map/ppermute | solution.py:331
  53.5 1.5 %collective-permute-start.10 = (bf16[256,1024]{1,0:T(8,128)(2,1)S(1)}, bf16[256,1024]{1,0:T(8,128)(2,1)S(1)}, u32[]{:S(2)}, u32[]{:S(2)}) collective-permute-start(bf16[256,1024]{1,0:T(8,128)(2,1)S(1)} %get-tuple-element.108.refs_4_.refs_7_), channel_id=1, source_target_pairs={{0,2},{1,3},{2,0},{3,1},{4,6},{5,7},{6,4},{7,5},{8,10},{9,11},{10,... | collective-permute-start | bytes 1572872 | tf_op jit(solution)/shard_map/ppermute | solution.py:328
  55.0 10.7 %shard_map.80 = (f32[8,128]{1,0:T(8,128)S(1)}, f32[4,2,1024,384]{3,2,1,0:T(8,128)S(1)}, bf16[4,2,1024,128]{3,2,1,0:T(8,128)(2,1)S(1)}) custom-call(s32[2,4]{1,0:T(2,128)S(1)} %copy-done, s32[4]{0:T(128)S(1)} %copy-done.1, bf16[256,1024]{1,0:T(8,128)(2,1)S(1)} %collective-permute-done.11.refs_2_.refs_5_, ...), custom_call_target="tpu_custom_call", output_to_operand_aliasing={{1}: (9, {}), {2}: (10, {})} | custom-call | flops 6442450944 | bytes 4194304 | tf_op jit(solution)/shard_map/pallas_call | solution.py:301
  65.8 0.6 collective-permute-start.15
  66.4 1.4 %collective-permute-start.13 = (bf16[128,1024]{1,0:T(8,128)(2,1)S(1)}, bf16[128,1024]{1,0:T(8,128)(2,1)S(1)}, u32[]{:S(2)}, u32[]{:S(2)}) collective-permute-start(bf16[128,1024]{1,0:T(8,128)(2,1)S(1)} %slice.22), channel_id=1, source_target_pairs={{0,4},{1,5},{2,6},{3,7},{4,0},{5,1},{6,2},{7,3},{8,12},{9,13},{10,... | collective-permute-start | bytes 786440 | tf_op jit(solution)/shard_map/ppermute | solution.py:331
  67.8 7.8 %shard_map.81 = (f32[8,128]{1,0:T(8,128)S(1)}, f32[4,2,1024,384]{3,2,1,0:T(8,128)S(1)}, bf16[4,2,1024,128]{3,2,1,0:T(8,128)(2,1)S(1)}) custom-call(s32[2,4]{1,0:T(2,128)S(1)} %copy-done, s32[4]{0:T(128)S(1)} %copy-done.1, bf16[256,1024]{1,0:T(8,128)(2,1)S(1)} %collective-permute-done.10.refs_2_.refs_4_, ...), custom_call_target="tpu_custom_call", output_to_operand_aliasing={{1}: (7, {}), {2}: (8, {})} | custom-call | flops 4294967296 | bytes 4194304 | tf_op jit(solution)/shard_map/pallas_call | solution.py:301
  75.6 6.0 %shard_map.82 = (bf16[128,4096]{1,0:T(8,128)(2,1)S(1)}, bf16[128,4096]{1,0:T(8,128)(2,1)S(1)}, f32[4,2,1024,384]{3,2,1,0:T(8,128)S(1)}, bf16[4,2,1024,128]{3,2,1,0:T(8,128)(2,1)S(1)}) custom-call(s32[2,4]{1,0:T(2,128)S(1)} %copy-done, s32[4]{0:T(128)S(1)} %copy-done.1, ...), custom_call_target="tpu_custom_call", output_to_operand_aliasing={{2}: (7, {}), {3}: (8, {})} | custom-call | flops 2147483648 | bytes 4194304 | tf_op jit(solution)/shard_map/pallas_call | solution.py:301
  81.6 0.1 collective-permute-start.16
  81.7 2.6 %collective-permute-done.16.got_ref = bf16[128,4096]{1,0:T(8,128)(2,1)S(1)} collective-permute-done((bf16[128,4096]{1,0:T(8,128)(2,1)S(1)}, bf16[128,4096]{1,0:T(8,128)(2,1)S(1)}, u32[]{:S(2)}, u32[]{:S(2)}) %collective-permute-start.16) | collective-permute-done | bytes 1048608 | tf_op jit(solution)/shard_map/ppermute | solution.py:325
  84.3 1.3 %shard_map.83 = bf16[128,8192]{1,0:T(8,128)(2,1)} custom-call(bf16[128,4096]{1,0:T(8,128)(2,1)S(1)} %get-tuple-element.121.mine_ref, bf16[128,4096]{1,0:T(8,128)(2,1)S(1)} %collective-permute-done.16.got_ref), custom_call_target="tpu_custom_call" | custom-call | tf_op jit(solution)/shard_map/pallas_call | solution.py:260
  (23 shorter events, 0.2 us)
Async XLA Ops:
  1.4 2.1 %collective-permute-start = (bf16[256,1024]{1,0:T(8,128)(2,1)S(1)}, bf16[256,1024]{1,0:T(8,128)(2,1)S(1)}, u32[]{:S(2)}, u32[]{:S(2)}) collective-permute-start(bf16[256,1024]{1,0:T(8,128)(2,1)S(1)} %get-tuple-element.68), channel_id=1, source_target_pairs={{0,1},{1,0},{2,3},{3,2},{4,5},{5,4},{6,7},{7,6},{8,9},{9,8},{10,11... | collective-permute-start | bytes 1572872 | tf_op jit(solution)/shard_map/ppermute | solution.py:325
  3.5 4.8 %collective-permute-start.1 = (bf16[128,4096]{1,0:T(8,128)(2,1)S(1)}, bf16[128,4096]{1,0:T(8,128)(2,1)S(1)}, u32[]{:S(2)}, u32[]{:S(2)}) collective-permute-start(bf16[128,4096]{1,0:T(8,128)(2,1)S(1)} %get-tuple-element.70), channel_id=1, source_target_pairs={{0,1},{1,0},{2,3},{3,2},{4,5},{5,4},{6,7},{7,6},{8,9},{9,8},{10,11... | collective-permute-start | bytes 3145736 | tf_op jit(solution)/shard_map/ppermute | solution.py:325
  3.8 10.3 %copy-start = (s32[2,4]{1,0:T(2,128)S(1)}, s32[2,4]{1,0:T(2,128)}, u32[]{:S(2)}) copy-start(s32[2,4]{1,0:T(2,128)} %refs_0_.14) | copy-start | bytes 100
  3.8 10.3 %copy-start.1 = (s32[4]{0:T(128)S(1)}, s32[4]{0:T(128)}, u32[]{:S(2)}) copy-start(s32[4]{0:T(128)} %refs_1_.13) | copy-start | bytes 52
  3.9 18.3 %collective-permute-start.5 = (bf16[256,1024]{1,0:T(8,128)(2,1)S(1)}, bf16[256,1024]{1,0:T(8,128)(2,1)S(1)}, u32[]{:S(2)}, u32[]{:S(2)}) collective-permute-start(bf16[256,1024]{1,0:T(8,128)(2,1)S(1)} %pad_maximum_fusion.refs_4_.refs_6_.refs_0_), channel_id=1, source_target_pairs={{0,4},{1,5},{2,6},{3,7},{4,0},{5,1},{6,2},{7,3},{8,12},{9,13},{10,... | collective-permute-start | bytes 1572872 | tf_op jit(solution)/shard_map/ppermute | solution.py:331
  6.7 17.0 %collective-permute-start.4 = (bf16[256,1024]{1,0:T(8,128)(2,1)S(1)}, bf16[256,1024]{1,0:T(8,128)(2,1)S(1)}, u32[]{:S(2)}, u32[]{:S(2)}) collective-permute-start(bf16[256,1024]{1,0:T(8,128)(2,1)S(1)} %pad_maximum_fusion.refs_4_.refs_6_.refs_0_), channel_id=1, source_target_pairs={{0,2},{1,3},{2,0},{3,1},{4,6},{5,7},{6,4},{7,5},{8,10},{9,11},{10,... | collective-permute-start | bytes 1572872 | tf_op jit(solution)/shard_map/ppermute | solution.py:328
  8.3 21.2 %collective-permute-start.3 = (bf16[256,1024]{1,0:T(8,128)(2,1)S(1)}, bf16[256,1024]{1,0:T(8,128)(2,1)S(1)}, u32[]{:S(2)}, u32[]{:S(2)}) collective-permute-start(bf16[256,1024]{1,0:T(8,128)(2,1)S(1)} %pad_maximum_fusion.refs_4_.refs_6_.refs_0_), channel_id=1, source_target_pairs={{0,16},{24,8},{1,17},{25,9},{2,18},{26,10},{3,19},{27,11},{4,20},{... | collective-permute-start | bytes 1572872 | tf_op jit(solution)/shard_map/ppermute | solution.py:360
  12.8 16.7 %collective-permute-start.2 = (bf16[256,1024]{1,0:T(8,128)(2,1)S(1)}, bf16[256,1024]{1,0:T(8,128)(2,1)S(1)}, u32[]{:S(2)}, u32[]{:S(2)}) collective-permute-start(bf16[256,1024]{1,0:T(8,128)(2,1)S(1)} %pad_maximum_fusion.refs_4_.refs_6_.refs_0_), channel_id=1, source_target_pairs={{8,0},{16,8},{24,16},{9,1},{17,9},{25,17},{10,2},{18,10},{26,18},{... | collective-permute-start | bytes 1572872 | tf_op jit(solution)/shard_map/ppermute | solution.py:360
  21.5 13.3 %collective-permute-start.9 = (bf16[256,1024]{1,0:T(8,128)(2,1)S(1)}, bf16[256,1024]{1,0:T(8,128)(2,1)S(1)}, u32[]{:S(2)}, u32[]{:S(2)}) collective-permute-start(bf16[256,1024]{1,0:T(8,128)(2,1)S(1)} %pad_maximum_fusion.1.refs_5_.refs_7_), channel_id=1, source_target_pairs={{0,4},{1,5},{2,6},{3,7},{4,0},{5,1},{6,2},{7,3},{8,12},{9,13},{10,... | collective-permute-start | bytes 1572872 | tf_op jit(solution)/shard_map/ppermute | solution.py:331
  22.2 13.5 %collective-permute-start.8 = (bf16[256,1024]{1,0:T(8,128)(2,1)S(1)}, bf16[256,1024]{1,0:T(8,128)(2,1)S(1)}, u32[]{:S(2)}, u32[]{:S(2)}) collective-permute-start(bf16[256,1024]{1,0:T(8,128)(2,1)S(1)} %pad_maximum_fusion.1.refs_5_.refs_7_), channel_id=1, source_target_pairs={{0,2},{1,3},{2,0},{3,1},{4,6},{5,7},{6,4},{7,5},{8,10},{9,11},{10,... | collective-permute-start | bytes 1572872 | tf_op jit(solution)/shard_map/ppermute | solution.py:328
  23.7 24.1 %collective-permute-start.6 = (bf16[256,1024]{1,0:T(8,128)(2,1)S(1)}, bf16[256,1024]{1,0:T(8,128)(2,1)S(1)}, u32[]{:S(2)}, u32[]{:S(2)}) collective-permute-start(bf16[256,1024]{1,0:T(8,128)(2,1)S(1)} %pad_maximum_fusion.refs_4_.refs_6_.refs_0_), channel_id=1, source_target_pairs={{0,8},{8,16},{1,9},{9,17},{2,10},{10,18},{3,11},{11,19},{4,12},{12... | collective-permute-start | bytes 1572872 | tf_op jit(solution)/shard_map/ppermute | solution.py:367
  30.1 21.3 %collective-permute-start.7 = (bf16[256,1024]{1,0:T(8,128)(2,1)S(1)}, bf16[256,1024]{1,0:T(8,128)(2,1)S(1)}, u32[]{:S(2)}, u32[]{:S(2)}) collective-permute-start(bf16[256,1024]{1,0:T(8,128)(2,1)S(1)} %get-tuple-element.89), channel_id=1, source_target_pairs={{8,0},{9,1},{10,2},{11,3},{12,4},{13,5},{14,6},{15,7}} | collective-permute-start | bytes 1572872 | tf_op jit(solution)/shard_map/ppermute | solution.py:383
  35.7 19.3 %collective-permute-start.11 = (bf16[256,1024]{1,0:T(8,128)(2,1)S(1)}, bf16[256,1024]{1,0:T(8,128)(2,1)S(1)}, u32[]{:S(2)}, u32[]{:S(2)}) collective-permute-start(bf16[256,1024]{1,0:T(8,128)(2,1)S(1)} %collective-permute-done.4.refs_2_.refs_4_), channel_id=1, source_target_pairs={{0,4},{1,5},{2,6},{3,7},{4,0},{5,1},{6,2},{7,3},{8,12},{9,13},{10,... | collective-permute-start | bytes 1572872 | tf_op jit(solution)/shard_map/ppermute | solution.py:331
  38.8 16.3 %collective-permute-start.12 = (bf16[256,1024]{1,0:T(8,128)(2,1)S(1)}, bf16[256,1024]{1,0:T(8,128)(2,1)S(1)}, u32[]{:S(2)}, u32[]{:S(2)}) collective-permute-start(bf16[256,1024]{1,0:T(8,128)(2,1)S(1)} %collective-permute-done.9.refs_3_.refs_5_), channel_id=1, source_target_pairs={{0,2},{1,3},{2,0},{3,1},{4,6},{5,7},{6,4},{7,5},{8,10},{9,11},{10,... | collective-permute-start | bytes 1572872 | tf_op jit(solution)/shard_map/ppermute | solution.py:328
  52.2 13.5 %collective-permute-start.14 = (bf16[256,1024]{1,0:T(8,128)(2,1)S(1)}, bf16[256,1024]{1,0:T(8,128)(2,1)S(1)}, u32[]{:S(2)}, u32[]{:S(2)}) collective-permute-start(bf16[256,1024]{1,0:T(8,128)(2,1)S(1)} %get-tuple-element.108.refs_4_.refs_7_), channel_id=1, source_target_pairs={{0,4},{1,5},{2,6},{3,7},{4,0},{5,1},{6,2},{7,3},{8,12},{9,13},{10,... | collective-permute-start | bytes 1572872 | tf_op jit(solution)/shard_map/ppermute | solution.py:331
  53.5 12.9 %collective-permute-start.10 = (bf16[256,1024]{1,0:T(8,128)(2,1)S(1)}, bf16[256,1024]{1,0:T(8,128)(2,1)S(1)}, u32[]{:S(2)}, u32[]{:S(2)}) collective-permute-start(bf16[256,1024]{1,0:T(8,128)(2,1)S(1)} %get-tuple-element.108.refs_4_.refs_7_), channel_id=1, source_target_pairs={{0,2},{1,3},{2,0},{3,1},{4,6},{5,7},{6,4},{7,5},{8,10},{9,11},{10,... | collective-permute-start | bytes 1572872 | tf_op jit(solution)/shard_map/ppermute | solution.py:328
  65.8 9.8 %collective-permute-start.15 = (bf16[128,1024]{1,0:T(8,128)(2,1)S(1)}, bf16[128,1024]{1,0:T(8,128)(2,1)S(1)}, u32[]{:S(2)}, u32[]{:S(2)}) collective-permute-start(bf16[128,1024]{1,0:T(8,128)(2,1)S(1)} %slice.24), channel_id=1, source_target_pairs={{0,2},{1,3},{2,0},{3,1},{4,6},{5,7},{6,4},{7,5},{8,10},{9,11},{10,... | collective-permute-start | bytes 786440 | tf_op jit(solution)/shard_map/ppermute | solution.py:328
  66.4 9.1 %collective-permute-start.13 = (bf16[128,1024]{1,0:T(8,128)(2,1)S(1)}, bf16[128,1024]{1,0:T(8,128)(2,1)S(1)}, u32[]{:S(2)}, u32[]{:S(2)}) collective-permute-start(bf16[128,1024]{1,0:T(8,128)(2,1)S(1)} %slice.22), channel_id=1, source_target_pairs={{0,4},{1,5},{2,6},{3,7},{4,0},{5,1},{6,2},{7,3},{8,12},{9,13},{10,... | collective-permute-start | bytes 786440 | tf_op jit(solution)/shard_map/ppermute | solution.py:331
  81.6 2.7 %collective-permute-start.16 = (bf16[128,4096]{1,0:T(8,128)(2,1)S(1)}, bf16[128,4096]{1,0:T(8,128)(2,1)S(1)}, u32[]{:S(2)}, u32[]{:S(2)}) collective-permute-start(bf16[128,4096]{1,0:T(8,128)(2,1)S(1)} %get-tuple-element.122), channel_id=1, source_target_pairs={{0,1},{1,0},{2,3},{3,2},{4,5},{5,4},{6,7},{7,6},{8,9},{9,8},{10,11... | collective-permute-start | bytes 3145736 | tf_op jit(solution)/shard_map/ppermute | solution.py:325

commit v14 on v13

--- a/solution.py
+++ b/solution.py
@@ -19,7 +19,7 @@
 KEY_CHUNK = 256
 
 
-def attend_kernel(ny, rows, arrays, groups, first, last, *refs):
+def attend_kernel(ny, rows, arrays, groups, sides, first, last, *refs):
     refs = list(refs)
     take = lambda count: [refs.pop(0) for _ in range(count)]
     exp_ref, off_ref = take(2)
@@ -30,7 +30,7 @@
     if not first:
         take(3)
     if last:
-        outs = take(2)
+        outs = take(len(sides))
     else:
         take(1)[0][...] = jnp.zeros((8, HD), jnp.float32)
     held, qs = take(2)
@@ -61,7 +61,7 @@
         values = jnp.concatenate(cut(value_refs), axis=0)
         values = jnp.concatenate([values, jnp.ones_like(values)], axis=1)
         size = min(ROW_BLOCK, stacked)
-        todo = [(s, slice(base, base + size)) for s in range(2) for base in range(0, stacked, size)]
+        todo = [(s, slice(base, base + size)) for s in sides for base in range(0, stacked, size)]
 
         chunks = [slice(c, min(c + KEY_CHUNK, width)) for c in range(0, width, KEY_CHUNK)]
         biases = {}
@@ -143,11 +143,11 @@
             pl.when(jnp.logical_not(full) & some)(functools.partial(step, members, limits, True, False))
 
     if last:
-        for s in range(2):
+        for out_ref, s in zip(outs, sides):
             for g in range(GW):
                 here = slice(g * rows, (g + 1) * rows)
                 done = held[head, s, here, :HD] / held[head, s, here, HD : 2 * HD]
-                outs[s][:, g * HD : (g + 1) * HD] = done.astype(jnp.bfloat16)
+                out_ref[:, g * HD : (g + 1) * HD] = done.astype(jnp.bfloat16)
 
 
 WHOLE = pl.BlockSpec(memory_space=pltpu.VMEM)
@@ -267,7 +267,7 @@
     )(mine, got)
 
 
-def attend(ny, rows, tables, arrays, groups, queries, state, last):
+def attend(ny, rows, tables, arrays, groups, queries, state, last, sides=(0, 1)):
     stacked = GW * rows
     first = state is None
     smem = pl.BlockSpec(memory_space=pltpu.SMEM)
@@ -285,8 +285,8 @@
             specs.append(pl.BlockSpec((array.shape[0], HD), functools.partial(lambda s, h: (0, s + h), shift)))
     aliases = {}
     if last:
-        out_shape = [jax.ShapeDtypeStruct((rows, HALF_KV * GW * HD), jnp.bfloat16)] * 2
-        out_specs = [row_spec, row_spec]
+        out_shape = [jax.ShapeDtypeStruct((rows, HALF_KV * GW * HD), jnp.bfloat16)] * len(sides)
+        out_specs = [row_spec] * len(sides)
     else:
         out_shape = [jax.ShapeDtypeStruct((8, HD), jnp.float32)]
         out_specs = [pl.BlockSpec((8, HD), lambda h: (0, 0))]
@@ -297,9 +297,9 @@
     out_shape.append(pltpu.VMEM((HALF_KV, 2, stacked, 3 * HD), jnp.float32))
     out_shape.append(pltpu.VMEM((HALF_KV, 2, stacked, HD), jnp.bfloat16))
     out_specs += [WHOLE, WHOLE]
-    scores = HALF_KV * 2 * stacked * rows * sum(len(members) for members in groups)
+    scores = HALF_KV * len(sides) * stacked * rows * sum(len(members) for members in groups)
     out = pl.pallas_call(
-        functools.partial(attend_kernel, ny, rows, len(arrays), groups, first, last),
+        functools.partial(attend_kernel, ny, rows, len(arrays), groups, sides, first, last),
         grid=(HALF_KV,),
         in_specs=specs,
         out_specs=out_specs,
@@ -308,7 +308,7 @@
         compiler_params=pltpu.CompilerParams(vmem_limit_bytes=24 * 2**20),
         cost_estimate=pl.CostEstimate(flops=8 * scores * HD, bytes_accessed=4 * 2**20, transcendentals=scores),
     )(*operands)
-    return out[:2] if last else list(out)
+    return list(out)
 
 
 def on_device(queries, seg_keys, seg_values, root_keys, root_values, expansion, root_offsets):
@@ -411,8 +411,10 @@
     groups = [members(0, "kin") + members(1, "kin")] + [members(step, "kin") for step in steps if step > 1]
     state = run([kin_x, *kin_y], tuple(groups), None, state, False)
     groups = [members(i, "kin", flips=(0,)) + members(len(tops) + i, "kin", flips=(1,)) for i in range(len(tops))]
-    out_mine, out_other = run([*tops, *lows], tuple(groups), None, state, True)
-    return assemble(out_mine, to_core(out_other))
+    out_other, *kept = run([*tops, *lows], tuple(groups), None, state, True, (1,))
+    out_got = to_core(out_other)
+    out_mine, *_ = run([*tops, *lows], tuple(groups), None, [state[0], *kept], True, (0,))
+    return assemble(out_mine, out_got)
 
 
 def solution(mesh):

time: 86.1 us -> 85.2 us (0.990)
  waiting for transfers between devices: 10.6 us -> 7.71 us
  Pallas kernels: 46.4 us -> 48.3 us
    ppermute x3, waiting for transfers between devices: 2.65 us -> 0.01 us  [to_core(): lax.ppermute(array, 'ctx', [(index(x, y, k), index(x, y, k + 1)) for x, y...]
    pallas_call x6 -> x7, Pallas kernels: 40.7 us -> 42.6 us  [attend(): pl.pallas_call(functools.partial(attend_kernel, ny, rows, len(arrays), gr...]
  transfers between devices with their start and end apart: 17 -> 17, of which waited for: 4 -> 3; matrix products, arithmetic and copies ran while one was open for 0% -> 0% of each run, Pallas kernels for 44% -> 49%
where the time goes in v14:
time: 85.2 us; the launch traced here: 84.9 us
  Pallas kernels  48.3 us (57%)
  starting transfers between devices  28.3 us (33%)
  waiting for transfers between devices  7.71 us (9%)
    pallas_call x7, Pallas kernels, attend(): pl.pallas_call(functools.partial(attend_kernel, ny, rows, len(arrays), gr...  42.6 us
    ppermute x5, starting transfers between devices, to_y(): lax.ppermute(array, 'ctx', [(index(x, y, k), index(x, y + step, k)) for x...  9.27 us
    ppermute x5, starting transfers between devices, to_x(): lax.ppermute(array, 'ctx', [(index(x, y, k), index(x + 1, y, k)) for x, y...  6.44 us
    ppermute x2, starting transfers between devices, on_device(): ahead.append(lax.ppermute(own, 'leaf', pairs))  5.82 us
    ppermute x1, starting transfers between devices, on_device(): before = lax.ppermute(sent_up, 'leaf', ((0, 1), (1, 2)))  4.56 us
    ppermute x1, waiting for transfers between devices, on_device(): ahead += [before, lax.ppermute(relay, 'leaf', [(1, 0)])]  3.38 us
    ppermute x5, waiting for transfers between devices, to_y(): lax.ppermute(array, 'ctx', [(index(x, y, k), index(x, y + step, k)) for x...  3.37 us
    pallas_call x2, Pallas kernels, pack(): pl.pallas_call(kernel, in_specs=[anywhere] * len(arrays), out_specs=[anyw...  2.9 us
  transfers between devices with their start and end apart: 17, of which 3 were waited for; matrix products, arithmetic and copies ran while one was open for 0% of the time, Pallas kernels for 49%

profile of v14, /device:TPU:0, one launch (start us, length us, event | category | flops | bytes accessed | tf_op | source)
XLA Modules:
  0.0 84.9 jit_solution(4419517869249366312)
XLA Ops:
  0.0 1.3 %shard_map.73 = (bf16[256,1024]{1,0:T(8,128)(2,1)S(1)}, bf16[256,1024]{1,0:T(8,128)(2,1)S(1)}) custom-call(bf16[128,1024]{1,0:T(8,128)(2,1)} %refs_0_.8, bf16[128,1024]{1,0:T(8,128)(2,1)} %refs_1_.8, bf16[128,1024]{1,0:T(8,128)(2,1)} %refs_2_.1, bf16[128,1024]{1,0:T(8,128)(2,1)} %refs_3_.1), custom_call_target="tpu_custom_call" | custom-call | tf_op jit(solution)/shard_map/pallas_call | solution.py:236
  1.4 0.5 collective-permute-start
  1.9 1.6 %shard_map.74 = (bf16[128,4096]{1,0:T(8,128)(2,1)S(1)}, bf16[128,4096]{1,0:T(8,128)(2,1)S(1)}) custom-call(bf16[128,8192]{1,0:T(8,128)(2,1)} %refs_0_.9), custom_call_target="tpu_custom_call" | custom-call | tf_op jit(solution)/shard_map/pallas_call | solution.py:236
  3.5 0.3 collective-permute-start.1
  3.9 2.8 %collective-permute-start.5 = (bf16[256,1024]{1,0:T(8,128)(2,1)S(1)}, bf16[256,1024]{1,0:T(8,128)(2,1)S(1)}, u32[]{:S(2)}, u32[]{:S(2)}) collective-permute-start(bf16[256,1024]{1,0:T(8,128)(2,1)S(1)} %pad_maximum_fusion.refs_4_.refs_6_.refs_0_), channel_id=1, source_target_pairs={{0,4},{1,5},{2,6},{3,7},{4,0},{5,1},{6,2},{7,3},{8,12},{9,13},{10,... | collective-permute-start | bytes 1572872 | tf_op jit(solution)/shard_map/ppermute | solution.py:331
  6.7 1.5 %collective-permute-start.4 = (bf16[256,1024]{1,0:T(8,128)(2,1)S(1)}, bf16[256,1024]{1,0:T(8,128)(2,1)S(1)}, u32[]{:S(2)}, u32[]{:S(2)}) collective-permute-start(bf16[256,1024]{1,0:T(8,128)(2,1)S(1)} %pad_maximum_fusion.refs_4_.refs_6_.refs_0_), channel_id=1, source_target_pairs={{0,2},{1,3},{2,0},{3,1},{4,6},{5,7},{6,4},{7,5},{8,10},{9,11},{10,... | collective-permute-start | bytes 1572872 | tf_op jit(solution)/shard_map/ppermute | solution.py:328
  8.3 4.5 %collective-permute-start.3 = (bf16[256,1024]{1,0:T(8,128)(2,1)S(1)}, bf16[256,1024]{1,0:T(8,128)(2,1)S(1)}, u32[]{:S(2)}, u32[]{:S(2)}) collective-permute-start(bf16[256,1024]{1,0:T(8,128)(2,1)S(1)} %pad_maximum_fusion.refs_4_.refs_6_.refs_0_), channel_id=1, source_target_pairs={{0,16},{24,8},{1,17},{25,9},{2,18},{26,10},{3,19},{27,11},{4,20},{... | collective-permute-start | bytes 1572872 | tf_op jit(solution)/shard_map/ppermute | solution.py:360
  12.8 1.3 %collective-permute-start.2 = (bf16[256,1024]{1,0:T(8,128)(2,1)S(1)}, bf16[256,1024]{1,0:T(8,128)(2,1)S(1)}, u32[]{:S(2)}, u32[]{:S(2)}) collective-permute-start(bf16[256,1024]{1,0:T(8,128)(2,1)S(1)} %pad_maximum_fusion.refs_4_.refs_6_.refs_0_), channel_id=1, source_target_pairs={{8,0},{16,8},{24,16},{9,1},{17,9},{25,17},{10,2},{18,10},{26,18},{... | collective-permute-start | bytes 1572872 | tf_op jit(solution)/shard_map/ppermute | solution.py:360
  14.1 7.3 %shard_map.75 = (f32[8,128]{1,0:T(8,128)S(1)}, f32[4,2,1024,384]{3,2,1,0:T(8,128)S(1)}, bf16[4,2,1024,128]{3,2,1,0:T(8,128)(2,1)S(1)}) custom-call(s32[2,4]{1,0:T(2,128)S(1)} %copy-done, s32[4]{0:T(128)S(1)} %copy-done.1, bf16[128,4096]{1,0:T(8,128)(2,1)S(1)} %get-tuple-element.74.refs_2_, bf16[128,4096]{1,0:T(8,128)(2,1)S(1)} %collective-permute-done.1.refs_3_, ...), custom_call_target="tpu_custom_call" | custom-call | flops 4294967296 | bytes 4194304 | tf_op jit(solution)/shard_map/pallas_call | solution.py:301
  21.5 0.7 collective-permute-start.9
  22.2 1.5 %collective-permute-start.8 = (bf16[256,1024]{1,0:T(8,128)(2,1)S(1)}, bf16[256,1024]{1,0:T(8,128)(2,1)S(1)}, u32[]{:S(2)}, u32[]{:S(2)}) collective-permute-start(bf16[256,1024]{1,0:T(8,128)(2,1)S(1)} %pad_maximum_fusion.1.refs_5_.refs_7_), channel_id=1, source_target_pairs={{0,2},{1,3},{2,0},{3,1},{4,6},{5,7},{6,4},{7,5},{8,10},{9,11},{10,... | collective-permute-start | bytes 1572872 | tf_op jit(solution)/shard_map/ppermute | solution.py:328
  23.7 4.6 %collective-permute-start.6 = (bf16[256,1024]{1,0:T(8,128)(2,1)S(1)}, bf16[256,1024]{1,0:T(8,128)(2,1)S(1)}, u32[]{:S(2)}, u32[]{:S(2)}) collective-permute-start(bf16[256,1024]{1,0:T(8,128)(2,1)S(1)} %pad_maximum_fusion.refs_4_.refs_6_.refs_0_), channel_id=1, source_target_pairs={{0,8},{8,16},{1,9},{9,17},{2,10},{10,18},{3,11},{11,19},{4,12},{12... | collective-permute-start | bytes 1572872 | tf_op jit(solution)/shard_map/ppermute | solution.py:367
  28.3 1.2 %shard_map.76 = (f32[8,128]{1,0:T(8,128)S(1)}, f32[4,2,1024,384]{3,2,1,0:T(8,128)S(1)}, bf16[4,2,1024,128]{3,2,1,0:T(8,128)(2,1)S(1)}) custom-call(s32[2,4]{1,0:T(2,128)S(1)} %copy-done, s32[4]{0:T(128)S(1)} %copy-done.1, bf16[256,1024]{1,0:T(8,128)(2,1)S(1)} %collective-permute-done.4.refs_2_.refs_4_, ...), custom_call_target="tpu_custom_call", output_to_operand_aliasing={{1}: (7, {}), {2}: (8, {})} | custom-call | flops 4294967296 | bytes 4194304 | tf_op jit(solution)/shard_map/pallas_call | solution.py:301
  29.5 0.6 shard_map.77
  30.1 1.3 %collective-permute-start.7 = (bf16[256,1024]{1,0:T(8,128)(2,1)S(1)}, bf16[256,1024]{1,0:T(8,128)(2,1)S(1)}, u32[]{:S(2)}, u32[]{:S(2)}) collective-permute-start(bf16[256,1024]{1,0:T(8,128)(2,1)S(1)} %get-tuple-element.91), channel_id=1, source_target_pairs={{8,0},{9,1},{10,2},{11,3},{12,4},{13,5},{14,6},{15,7}} | collective-permute-start | bytes 1572872 | tf_op jit(solution)/shard_map/ppermute | solution.py:383
  31.4 3.4 %collective-permute-done.9.refs_3_.refs_5_ = bf16[256,1024]{1,0:T(8,128)(2,1)S(1)} collective-permute-done((bf16[256,1024]{1,0:T(8,128)(2,1)S(1)}, bf16[256,1024]{1,0:T(8,128)(2,1)S(1)}, u32[]{:S(2)}, u32[]{:S(2)}) %collective-permute-start.9) | collective-permute-done | bytes 524320 | tf_op jit(solution)/shard_map/ppermute | solution.py:331
  34.8 0.9 %collective-permute-done.8.refs_2_.refs_4_ = bf16[256,1024]{1,0:T(8,128)(2,1)S(1)} collective-permute-done((bf16[256,1024]{1,0:T(8,128)(2,1)S(1)}, bf16[256,1024]{1,0:T(8,128)(2,1)S(1)}, u32[]{:S(2)}, u32[]{:S(2)}) %collective-permute-start.8) | collective-permute-done | bytes 524320 | tf_op jit(solution)/shard_map/ppermute | solution.py:328
  35.7 3.0 %collective-permute-start.11 = (bf16[256,1024]{1,0:T(8,128)(2,1)S(1)}, bf16[256,1024]{1,0:T(8,128)(2,1)S(1)}, u32[]{:S(2)}, u32[]{:S(2)}) collective-permute-start(bf16[256,1024]{1,0:T(8,128)(2,1)S(1)} %collective-permute-done.4.refs_2_.refs_4_), channel_id=1, source_target_pairs={{0,4},{1,5},{2,6},{3,7},{4,0},{5,1},{6,2},{7,3},{8,12},{9,13},{10,... | collective-permute-start | bytes 1572872 | tf_op jit(solution)/shard_map/ppermute | solution.py:331
  38.8 1.4 %collective-permute-start.12 = (bf16[256,1024]{1,0:T(8,128)(2,1)S(1)}, bf16[256,1024]{1,0:T(8,128)(2,1)S(1)}, u32[]{:S(2)}, u32[]{:S(2)}) collective-permute-start(bf16[256,1024]{1,0:T(8,128)(2,1)S(1)} %collective-permute-done.9.refs_3_.refs_5_), channel_id=1, source_target_pairs={{0,2},{1,3},{2,0},{3,1},{4,6},{5,7},{6,4},{7,5},{8,10},{9,11},{10,... | collective-permute-start | bytes 1572872 | tf_op jit(solution)/shard_map/ppermute | solution.py:328
  40.1 7.9 %shard_map.78 = (f32[8,128]{1,0:T(8,128)S(1)}, f32[4,2,1024,384]{3,2,1,0:T(8,128)S(1)}, bf16[4,2,1024,128]{3,2,1,0:T(8,128)(2,1)S(1)}) custom-call(s32[2,4]{1,0:T(2,128)S(1)} %copy-done, s32[4]{0:T(128)S(1)} %copy-done.1, bf16[256,1024]{1,0:T(8,128)(2,1)S(1)} %collective-permute-done.8.refs_2_.refs_4_, ...), custom_call_target="tpu_custom_call", output_to_operand_aliasing={{1}: (7, {}), {2}: (8, {})} | custom-call | flops 4294967296 | bytes 4194304 | tf_op jit(solution)/shard_map/pallas_call | solution.py:301
  48.0 3.4 %collective-permute-done.7.refs_4_ = bf16[256,1024]{1,0:T(8,128)(2,1)S(1)} collective-permute-done((bf16[256,1024]{1,0:T(8,128)(2,1)S(1)}, bf16[256,1024]{1,0:T(8,128)(2,1)S(1)}, u32[]{:S(2)}, u32[]{:S(2)}) %collective-permute-start.7) | collective-permute-done | bytes 524320 | tf_op jit(solution)/shard_map/ppermute | solution.py:383
  51.4 0.8 shard_map.79
  52.2 1.3 %collective-permute-start.14 = (bf16[256,1024]{1,0:T(8,128)(2,1)S(1)}, bf16[256,1024]{1,0:T(8,128)(2,1)S(1)}, u32[]{:S(2)}, u32[]{:S(2)}) collective-permute-start(bf16[256,1024]{1,0:T(8,128)(2,1)S(1)} %get-tuple-element.110.refs_4_.refs_7_), channel_id=1, source_target_pairs={{0,4},{1,5},{2,6},{3,7},{4,0},{5,1},{6,2},{7,3},{8,12},{9,13},{10,... | collective-permute-start | bytes 1572872 | tf_op jit(solution)/shard_map/ppermute | solution.py:331
  53.5 1.5 %collective-permute-start.10 = (bf16[256,1024]{1,0:T(8,128)(2,1)S(1)}, bf16[256,1024]{1,0:T(8,128)(2,1)S(1)}, u32[]{:S(2)}, u32[]{:S(2)}) collective-permute-start(bf16[256,1024]{1,0:T(8,128)(2,1)S(1)} %get-tuple-element.110.refs_4_.refs_7_), channel_id=1, source_target_pairs={{0,2},{1,3},{2,0},{3,1},{4,6},{5,7},{6,4},{7,5},{8,10},{9,11},{10,... | collective-permute-start | bytes 1572872 | tf_op jit(solution)/shard_map/ppermute | solution.py:328
  55.0 10.7 %shard_map.80 = (f32[8,128]{1,0:T(8,128)S(1)}, f32[4,2,1024,384]{3,2,1,0:T(8,128)S(1)}, bf16[4,2,1024,128]{3,2,1,0:T(8,128)(2,1)S(1)}) custom-call(s32[2,4]{1,0:T(2,128)S(1)} %copy-done, s32[4]{0:T(128)S(1)} %copy-done.1, bf16[256,1024]{1,0:T(8,128)(2,1)S(1)} %collective-permute-done.11.refs_2_.refs_5_, ...), custom_call_target="tpu_custom_call", output_to_operand_aliasing={{1}: (9, {}), {2}: (10, {})} | custom-call | flops 6442450944 | bytes 4194304 | tf_op jit(solution)/shard_map/pallas_call | solution.py:301
  65.8 0.6 collective-permute-start.15
  66.4 1.4 %collective-permute-start.13 = (bf16[128,1024]{1,0:T(8,128)(2,1)S(1)}, bf16[128,1024]{1,0:T(8,128)(2,1)S(1)}, u32[]{:S(2)}, u32[]{:S(2)}) collective-permute-start(bf16[128,1024]{1,0:T(8,128)(2,1)S(1)} %slice.22), channel_id=1, source_target_pairs={{0,4},{1,5},{2,6},{3,7},{4,0},{5,1},{6,2},{7,3},{8,12},{9,13},{10,... | collective-permute-start | bytes 786440 | tf_op jit(solution)/shard_map/ppermute | solution.py:331
  67.8 7.8 %shard_map.81 = (f32[8,128]{1,0:T(8,128)S(1)}, f32[4,2,1024,384]{3,2,1,0:T(8,128)S(1)}, bf16[4,2,1024,128]{3,2,1,0:T(8,128)(2,1)S(1)}) custom-call(s32[2,4]{1,0:T(2,128)S(1)} %copy-done, s32[4]{0:T(128)S(1)} %copy-done.1, bf16[256,1024]{1,0:T(8,128)(2,1)S(1)} %collective-permute-done.10.refs_2_.refs_4_, ...), custom_call_target="tpu_custom_call", output_to_operand_aliasing={{1}: (7, {}), {2}: (8, {})} | custom-call | flops 4294967296 | bytes 4194304 | tf_op jit(solution)/shard_map/pallas_call | solution.py:301
  75.6 3.9 %shard_map.82 = (bf16[128,4096]{1,0:T(8,128)(2,1)S(1)}, f32[4,2,1024,384]{3,2,1,0:T(8,128)S(1)}, bf16[4,2,1024,128]{3,2,1,0:T(8,128)(2,1)S(1)}) custom-call(s32[2,4]{1,0:T(2,128)S(1)} %copy-done, s32[4]{0:T(128)S(1)} %copy-done.1, bf16[128,1024]{1,0:T(8,128)(2,1)S(1)} %collective-permute-done.13.refs_2_.refs_4_, ...), custom_call_target="tpu_custom_call", output_to_operand_aliasing={{1}: (7, {}), {2}: (8, {})} | custom-call | flops 1073741824 | bytes 4194304 | tf_op jit(solution)/shard_map/pallas_call | solution.py:301
  79.4 0.1 collective-permute-start.16
  79.5 3.9 %shard_map.83 = (bf16[128,4096]{1,0:T(8,128)(2,1)S(1)}, f32[4,2,1024,384]{3,2,1,0:T(8,128)S(1)}, bf16[4,2,1024,128]{3,2,1,0:T(8,128)(2,1)S(1)}) custom-call(s32[2,4]{1,0:T(2,128)S(1)} %copy-done, s32[4]{0:T(128)S(1)} %copy-done.1, bf16[128,1024]{1,0:T(8,128)(2,1)S(1)} %collective-permute-done.13.refs_2_.refs_4_, ...), custom_call_target="tpu_custom_call", output_to_operand_aliasing={{1}: (7, {}), {2}: (8, {})} | custom-call | flops 1073741824 | bytes 4194304 | tf_op jit(solution)/shard_map/pallas_call | solution.py:301
  83.4 1.3 %shard_map.84 = bf16[128,8192]{1,0:T(8,128)(2,1)} custom-call(bf16[128,4096]{1,0:T(8,128)(2,1)S(1)} %get-tuple-element.125.mine_ref, bf16[128,4096]{1,0:T(8,128)(2,1)S(1)} %collective-permute-done.16.got_ref), custom_call_target="tpu_custom_call" | custom-call | tf_op jit(solution)/shard_map/pallas_call | solution.py:260
  (24 shorter events, 0.2 us)
Async XLA Ops:
  1.4 2.1 %collective-permute-start = (bf16[256,1024]{1,0:T(8,128)(2,1)S(1)}, bf16[256,1024]{1,0:T(8,128)(2,1)S(1)}, u32[]{:S(2)}, u32[]{:S(2)}) collective-permute-start(bf16[256,1024]{1,0:T(8,128)(2,1)S(1)} %get-tuple-element.70), channel_id=1, source_target_pairs={{0,1},{1,0},{2,3},{3,2},{4,5},{5,4},{6,7},{7,6},{8,9},{9,8},{10,11... | collective-permute-start | bytes 1572872 | tf_op jit(solution)/shard_map/ppermute | solution.py:325
  3.5 4.8 %collective-permute-start.1 = (bf16[128,4096]{1,0:T(8,128)(2,1)S(1)}, bf16[128,4096]{1,0:T(8,128)(2,1)S(1)}, u32[]{:S(2)}, u32[]{:S(2)}) collective-permute-start(bf16[128,4096]{1,0:T(8,128)(2,1)S(1)} %get-tuple-element.72), channel_id=1, source_target_pairs={{0,1},{1,0},{2,3},{3,2},{4,5},{5,4},{6,7},{7,6},{8,9},{9,8},{10,11... | collective-permute-start | bytes 3145736 | tf_op jit(solution)/shard_map/ppermute | solution.py:325
  3.8 10.3 %copy-start = (s32[2,4]{1,0:T(2,128)S(1)}, s32[2,4]{1,0:T(2,128)}, u32[]{:S(2)}) copy-start(s32[2,4]{1,0:T(2,128)} %refs_0_.16) | copy-start | bytes 100
  3.8 10.3 %copy-start.1 = (s32[4]{0:T(128)S(1)}, s32[4]{0:T(128)}, u32[]{:S(2)}) copy-start(s32[4]{0:T(128)} %refs_1_.15) | copy-start | bytes 52
  3.9 18.3 %collective-permute-start.5 = (bf16[256,1024]{1,0:T(8,128)(2,1)S(1)}, bf16[256,1024]{1,0:T(8,128)(2,1)S(1)}, u32[]{:S(2)}, u32[]{:S(2)}) collective-permute-start(bf16[256,1024]{1,0:T(8,128)(2,1)S(1)} %pad_maximum_fusion.refs_4_.refs_6_.refs_0_), channel_id=1, source_target_pairs={{0,4},{1,5},{2,6},{3,7},{4,0},{5,1},{6,2},{7,3},{8,12},{9,13},{10,... | collective-permute-start | bytes 1572872 | tf_op jit(solution)/shard_map/ppermute | solution.py:331
  6.7 17.0 %collective-permute-start.4 = (bf16[256,1024]{1,0:T(8,128)(2,1)S(1)}, bf16[256,1024]{1,0:T(8,128)(2,1)S(1)}, u32[]{:S(2)}, u32[]{:S(2)}) collective-permute-start(bf16[256,1024]{1,0:T(8,128)(2,1)S(1)} %pad_maximum_fusion.refs_4_.refs_6_.refs_0_), channel_id=1, source_target_pairs={{0,2},{1,3},{2,0},{3,1},{4,6},{5,7},{6,4},{7,5},{8,10},{9,11},{10,... | collective-permute-start | bytes 1572872 | tf_op jit(solution)/shard_map/ppermute | solution.py:328
  8.3 21.2 %collective-permute-start.3 = (bf16[256,1024]{1,0:T(8,128)(2,1)S(1)}, bf16[256,1024]{1,0:T(8,128)(2,1)S(1)}, u32[]{:S(2)}, u32[]{:S(2)}) collective-permute-start(bf16[256,1024]{1,0:T(8,128)(2,1)S(1)} %pad_maximum_fusion.refs_4_.refs_6_.refs_0_), channel_id=1, source_target_pairs={{0,16},{24,8},{1,17},{25,9},{2,18},{26,10},{3,19},{27,11},{4,20},{... | collective-permute-start | bytes 1572872 | tf_op jit(solution)/shard_map/ppermute | solution.py:360
  12.8 16.7 %collective-permute-start.2 = (bf16[256,1024]{1,0:T(8,128)(2,1)S(1)}, bf16[256,1024]{1,0:T(8,128)(2,1)S(1)}, u32[]{:S(2)}, u32[]{:S(2)}) collective-permute-start(bf16[256,1024]{1,0:T(8,128)(2,1)S(1)} %pad_maximum_fusion.refs_4_.refs_6_.refs_0_), channel_id=1, source_target_pairs={{8,0},{16,8},{24,16},{9,1},{17,9},{25,17},{10,2},{18,10},{26,18},{... | collective-permute-start | bytes 1572872 | tf_op jit(solution)/shard_map/ppermute | solution.py:360
  21.5 13.3 %collective-permute-start.9 = (bf16[256,1024]{1,0:T(8,128)(2,1)S(1)}, bf16[256,1024]{1,0:T(8,128)(2,1)S(1)}, u32[]{:S(2)}, u32[]{:S(2)}) collective-permute-start(bf16[256,1024]{1,0:T(8,128)(2,1)S(1)} %pad_maximum_fusion.1.refs_5_.refs_7_), channel_id=1, source_target_pairs={{0,4},{1,5},{2,6},{3,7},{4,0},{5,1},{6,2},{7,3},{8,12},{9,13},{10,... | collective-permute-start | bytes 1572872 | tf_op jit(solution)/shard_map/ppermute | solution.py:331
  22.2 13.5 %collective-permute-start.8 = (bf16[256,1024]{1,0:T(8,128)(2,1)S(1)}, bf16[256,1024]{1,0:T(8,128)(2,1)S(1)}, u32[]{:S(2)}, u32[]{:S(2)}) collective-permute-start(bf16[256,1024]{1,0:T(8,128)(2,1)S(1)} %pad_maximum_fusion.1.refs_5_.refs_7_), channel_id=1, source_target_pairs={{0,2},{1,3},{2,0},{3,1},{4,6},{5,7},{6,4},{7,5},{8,10},{9,11},{10,... | collective-permute-start | bytes 1572872 | tf_op jit(solution)/shard_map/ppermute | solution.py:328
  23.7 24.3 %collective-permute-start.6 = (bf16[256,1024]{1,0:T(8,128)(2,1)S(1)}, bf16[256,1024]{1,0:T(8,128)(2,1)S(1)}, u32[]{:S(2)}, u32[]{:S(2)}) collective-permute-start(bf16[256,1024]{1,0:T(8,128)(2,1)S(1)} %pad_maximum_fusion.refs_4_.refs_6_.refs_0_), channel_id=1, source_target_pairs={{0,8},{8,16},{1,9},{9,17},{2,10},{10,18},{3,11},{11,19},{4,12},{12... | collective-permute-start | bytes 1572872 | tf_op jit(solution)/shard_map/ppermute | solution.py:367
  30.1 21.3 %collective-permute-start.7 = (bf16[256,1024]{1,0:T(8,128)(2,1)S(1)}, bf16[256,1024]{1,0:T(8,128)(2,1)S(1)}, u32[]{:S(2)}, u32[]{:S(2)}) collective-permute-start(bf16[256,1024]{1,0:T(8,128)(2,1)S(1)} %get-tuple-element.91), channel_id=1, source_target_pairs={{8,0},{9,1},{10,2},{11,3},{12,4},{13,5},{14,6},{15,7}} | collective-permute-start | bytes 1572872 | tf_op jit(solution)/shard_map/ppermute | solution.py:383
  35.7 19.3 %collective-permute-start.11 = (bf16[256,1024]{1,0:T(8,128)(2,1)S(1)}, bf16[256,1024]{1,0:T(8,128)(2,1)S(1)}, u32[]{:S(2)}, u32[]{:S(2)}) collective-permute-start(bf16[256,1024]{1,0:T(8,128)(2,1)S(1)} %collective-permute-done.4.refs_2_.refs_4_), channel_id=1, source_target_pairs={{0,4},{1,5},{2,6},{3,7},{4,0},{5,1},{6,2},{7,3},{8,12},{9,13},{10,... | collective-permute-start | bytes 1572872 | tf_op jit(solution)/shard_map/ppermute | solution.py:331
  38.8 16.3 %collective-permute-start.12 = (bf16[256,1024]{1,0:T(8,128)(2,1)S(1)}, bf16[256,1024]{1,0:T(8,128)(2,1)S(1)}, u32[]{:S(2)}, u32[]{:S(2)}) collective-permute-start(bf16[256,1024]{1,0:T(8,128)(2,1)S(1)} %collective-permute-done.9.refs_3_.refs_5_), channel_id=1, source_target_pairs={{0,2},{1,3},{2,0},{3,1},{4,6},{5,7},{6,4},{7,5},{8,10},{9,11},{10,... | collective-permute-start | bytes 1572872 | tf_op jit(solution)/shard_map/ppermute | solution.py:328
  52.2 13.5 %collective-permute-start.14 = (bf16[256,1024]{1,0:T(8,128)(2,1)S(1)}, bf16[256,1024]{1,0:T(8,128)(2,1)S(1)}, u32[]{:S(2)}, u32[]{:S(2)}) collective-permute-start(bf16[256,1024]{1,0:T(8,128)(2,1)S(1)} %get-tuple-element.110.refs_4_.refs_7_), channel_id=1, source_target_pairs={{0,4},{1,5},{2,6},{3,7},{4,0},{5,1},{6,2},{7,3},{8,12},{9,13},{10,... | collective-permute-start | bytes 1572872 | tf_op jit(solution)/shard_map/ppermute | solution.py:331
  53.5 12.9 %collective-permute-start.10 = (bf16[256,1024]{1,0:T(8,128)(2,1)S(1)}, bf16[256,1024]{1,0:T(8,128)(2,1)S(1)}, u32[]{:S(2)}, u32[]{:S(2)}) collective-permute-start(bf16[256,1024]{1,0:T(8,128)(2,1)S(1)} %get-tuple-element.110.refs_4_.refs_7_), channel_id=1, source_target_pairs={{0,2},{1,3},{2,0},{3,1},{4,6},{5,7},{6,4},{7,5},{8,10},{9,11},{10,... | collective-permute-start | bytes 1572872 | tf_op jit(solution)/shard_map/ppermute | solution.py:328
  65.8 9.8 %collective-permute-start.15 = (bf16[128,1024]{1,0:T(8,128)(2,1)S(1)}, bf16[128,1024]{1,0:T(8,128)(2,1)S(1)}, u32[]{:S(2)}, u32[]{:S(2)}) collective-permute-start(bf16[128,1024]{1,0:T(8,128)(2,1)S(1)} %slice.24), channel_id=1, source_target_pairs={{0,2},{1,3},{2,0},{3,1},{4,6},{5,7},{6,4},{7,5},{8,10},{9,11},{10,... | collective-permute-start | bytes 786440 | tf_op jit(solution)/shard_map/ppermute | solution.py:328
  66.4 9.1 %collective-permute-start.13 = (bf16[128,1024]{1,0:T(8,128)(2,1)S(1)}, bf16[128,1024]{1,0:T(8,128)(2,1)S(1)}, u32[]{:S(2)}, u32[]{:S(2)}) collective-permute-start(bf16[128,1024]{1,0:T(8,128)(2,1)S(1)} %slice.22), channel_id=1, source_target_pairs={{0,4},{1,5},{2,6},{3,7},{4,0},{5,1},{6,2},{7,3},{8,12},{9,13},{10,... | collective-permute-start | bytes 786440 | tf_op jit(solution)/shard_map/ppermute | solution.py:331
  79.4 4.0 %collective-permute-start.16 = (bf16[128,4096]{1,0:T(8,128)(2,1)S(1)}, bf16[128,4096]{1,0:T(8,128)(2,1)S(1)}, u32[]{:S(2)}, u32[]{:S(2)}) collective-permute-start(bf16[128,4096]{1,0:T(8,128)(2,1)S(1)} %get-tuple-element.126), channel_id=1, source_target_pairs={{0,1},{1,0},{2,3},{3,2},{4,5},{5,4},{6,7},{7,6},{8,9},{9,8},{10,11... | collective-permute-start | bytes 3145736 | tf_op jit(solution)/shard_map/ppermute | solution.py:325

commit v15 on v14

--- a/solution.py
+++ b/solution.py
@@ -362,9 +362,7 @@
         ahead.append(hop(1, own))
     state = run([own, root], (members(0, "own") + members(1, "root"),), q_pair, None, False)
 
-    root, sent_up = after(state, root, own)
-    if direct:
-        before = lax.ppermute(sent_up, "leaf", ((0, 1), (1, 2)))
+    (root,) = after(state, root)
     root_x, root_y = to_x(root), [to_y(root, step) for step in steps]
 
     def near(kind):
@@ -378,6 +376,8 @@
     own_x, *own_y = after(state, own_x, *own_y)
     state = run([own_x, *own_y], tuple(near("own")), None, state, False)
     if direct:
+        (sent_up,) = after(state, own)
+        before = lax.ppermute(sent_up, "leaf", ((0, 1), (1, 2)))
         ahead = after(state, *ahead)
         relay = pick(state, expansion, lambda table, g: jnp.where(table[0, 0] == 3, 1, 0), ahead[1:])
         ahead += [before, lax.ppermute(relay, "leaf", [(1, 0)])]

time: 85.2 us -> 85.2 us (level)
  no operation moved by 1% of the time
where the time goes in v15:
time: 85.2 us; the launch traced here: 84.9 us
  Pallas kernels  48 us (56%)
  starting transfers between devices  28.3 us (33%)
  waiting for transfers between devices  7.96 us (9%)
    pallas_call x7, Pallas kernels, attend(): pl.pallas_call(functools.partial(attend_kernel, ny, rows, len(arrays), gr...  42.4 us
    ppermute x5, starting transfers between devices, to_y(): lax.ppermute(array, 'ctx', [(index(x, y, k), index(x, y + step, k)) for x...  9.29 us
    ppermute x5, starting transfers between devices, to_x(): lax.ppermute(array, 'ctx', [(index(x, y, k), index(x + 1, y, k)) for x, y...  6.43 us
    ppermute x2, starting transfers between devices, on_device(): ahead.append(lax.ppermute(own, 'leaf', pairs))  5.82 us
    ppermute x1, starting transfers between devices, on_device(): before = lax.ppermute(sent_up, 'leaf', ((0, 1), (1, 2)))  4.58 us
    ppermute x1, waiting for transfers between devices, on_device(): ahead += [before, lax.ppermute(relay, 'leaf', [(1, 0)])]  3.61 us
    ppermute x5, waiting for transfers between devices, to_y(): lax.ppermute(array, 'ctx', [(index(x, y, k), index(x, y + step, k)) for x...  3.39 us
    pallas_call x2, Pallas kernels, pack(): pl.pallas_call(kernel, in_specs=[anywhere] * len(arrays), out_specs=[anyw...  2.9 us
  transfers between devices with their start and end apart: 17, of which 3 were waited for; matrix products, arithmetic and copies ran while one was open for 0% of the time, Pallas kernels for 49%

profile of v15, /device:TPU:0, one launch (start us, length us, event | category | flops | bytes accessed | tf_op | source)
XLA Modules:
  0.0 84.9 jit_solution(2282566699796382106)
XLA Ops:
  0.0 1.3 %shard_map.73 = (bf16[256,1024]{1,0:T(8,128)(2,1)S(1)}, bf16[256,1024]{1,0:T(8,128)(2,1)S(1)}) custom-call(bf16[128,1024]{1,0:T(8,128)(2,1)} %refs_0_.8, bf16[128,1024]{1,0:T(8,128)(2,1)} %refs_1_.8, bf16[128,1024]{1,0:T(8,128)(2,1)} %refs_2_.1, bf16[128,1024]{1,0:T(8,128)(2,1)} %refs_3_.1), custom_call_target="tpu_custom_call" | custom-call | tf_op jit(solution)/shard_map/pallas_call | solution.py:236
  1.4 0.5 collective-permute-start
  1.9 1.6 %shard_map.74 = (bf16[128,4096]{1,0:T(8,128)(2,1)S(1)}, bf16[128,4096]{1,0:T(8,128)(2,1)S(1)}) custom-call(bf16[128,8192]{1,0:T(8,128)(2,1)} %refs_0_.9), custom_call_target="tpu_custom_call" | custom-call | tf_op jit(solution)/shard_map/pallas_call | solution.py:236
  3.5 0.3 collective-permute-start.1
  3.9 2.8 %collective-permute-start.5 = (bf16[256,1024]{1,0:T(8,128)(2,1)S(1)}, bf16[256,1024]{1,0:T(8,128)(2,1)S(1)}, u32[]{:S(2)}, u32[]{:S(2)}) collective-permute-start(bf16[256,1024]{1,0:T(8,128)(2,1)S(1)} %pad_maximum_fusion.refs_4_.refs_6_.refs_0_), channel_id=1, source_target_pairs={{0,4},{1,5},{2,6},{3,7},{4,0},{5,1},{6,2},{7,3},{8,12},{9,13},{10,... | collective-permute-start | bytes 1572872 | tf_op jit(solution)/shard_map/ppermute | solution.py:331
  6.7 1.5 %collective-permute-start.4 = (bf16[256,1024]{1,0:T(8,128)(2,1)S(1)}, bf16[256,1024]{1,0:T(8,128)(2,1)S(1)}, u32[]{:S(2)}, u32[]{:S(2)}) collective-permute-start(bf16[256,1024]{1,0:T(8,128)(2,1)S(1)} %pad_maximum_fusion.refs_4_.refs_6_.refs_0_), channel_id=1, source_target_pairs={{0,2},{1,3},{2,0},{3,1},{4,6},{5,7},{6,4},{7,5},{8,10},{9,11},{10,... | collective-permute-start | bytes 1572872 | tf_op jit(solution)/shard_map/ppermute | solution.py:328
  8.3 4.5 %collective-permute-start.3 = (bf16[256,1024]{1,0:T(8,128)(2,1)S(1)}, bf16[256,1024]{1,0:T(8,128)(2,1)S(1)}, u32[]{:S(2)}, u32[]{:S(2)}) collective-permute-start(bf16[256,1024]{1,0:T(8,128)(2,1)S(1)} %pad_maximum_fusion.refs_4_.refs_6_.refs_0_), channel_id=1, source_target_pairs={{0,16},{24,8},{1,17},{25,9},{2,18},{26,10},{3,19},{27,11},{4,20},{... | collective-permute-start | bytes 1572872 | tf_op jit(solution)/shard_map/ppermute | solution.py:360
  12.8 1.3 %collective-permute-start.2 = (bf16[256,1024]{1,0:T(8,128)(2,1)S(1)}, bf16[256,1024]{1,0:T(8,128)(2,1)S(1)}, u32[]{:S(2)}, u32[]{:S(2)}) collective-permute-start(bf16[256,1024]{1,0:T(8,128)(2,1)S(1)} %pad_maximum_fusion.refs_4_.refs_6_.refs_0_), channel_id=1, source_target_pairs={{8,0},{16,8},{24,16},{9,1},{17,9},{25,17},{10,2},{18,10},{26,18},{... | collective-permute-start | bytes 1572872 | tf_op jit(solution)/shard_map/ppermute | solution.py:360
  14.1 7.3 %shard_map.75 = (f32[8,128]{1,0:T(8,128)S(1)}, f32[4,2,1024,384]{3,2,1,0:T(8,128)S(1)}, bf16[4,2,1024,128]{3,2,1,0:T(8,128)(2,1)S(1)}) custom-call(s32[2,4]{1,0:T(2,128)S(1)} %copy-done, s32[4]{0:T(128)S(1)} %copy-done.1, bf16[128,4096]{1,0:T(8,128)(2,1)S(1)} %get-tuple-element.75.refs_2_, bf16[128,4096]{1,0:T(8,128)(2,1)S(1)} %collective-permute-done.1.refs_3_, ...), custom_call_target="tpu_custom_call" | custom-call | flops 4294967296 | bytes 4194304 | tf_op jit(solution)/shard_map/pallas_call | solution.py:301
  21.5 0.7 collective-permute-start.9
  22.2 1.5 %collective-permute-start.8 = (bf16[256,1024]{1,0:T(8,128)(2,1)S(1)}, bf16[256,1024]{1,0:T(8,128)(2,1)S(1)}, u32[]{:S(2)}, u32[]{:S(2)}) collective-permute-start(bf16[256,1024]{1,0:T(8,128)(2,1)S(1)} %pad_maximum_fusion.1.refs_5_.refs_7_), channel_id=1, source_target_pairs={{0,2},{1,3},{2,0},{3,1},{4,6},{5,7},{6,4},{7,5},{8,10},{9,11},{10,... | collective-permute-start | bytes 1572872 | tf_op jit(solution)/shard_map/ppermute | solution.py:328
  23.7 1.2 %shard_map.76 = (f32[8,128]{1,0:T(8,128)S(1)}, f32[4,2,1024,384]{3,2,1,0:T(8,128)S(1)}, bf16[4,2,1024,128]{3,2,1,0:T(8,128)(2,1)S(1)}) custom-call(s32[2,4]{1,0:T(2,128)S(1)} %copy-done, s32[4]{0:T(128)S(1)} %copy-done.1, bf16[256,1024]{1,0:T(8,128)(2,1)S(1)} %collective-permute-done.4.refs_2_.refs_4_, ...), custom_call_target="tpu_custom_call", output_to_operand_aliasing={{1}: (7, {}), {2}: (8, {})} | custom-call | flops 4294967296 | bytes 4194304 | tf_op jit(solution)/shard_map/pallas_call | solution.py:301
  24.9 4.6 %collective-permute-start.6 = (bf16[256,1024]{1,0:T(8,128)(2,1)S(1)}, bf16[256,1024]{1,0:T(8,128)(2,1)S(1)}, u32[]{:S(2)}, u32[]{:S(2)}) collective-permute-start(bf16[256,1024]{1,0:T(8,128)(2,1)S(1)} %pad_maximum_fusion.refs_4_.refs_6_.refs_0_), channel_id=1, source_target_pairs={{0,8},{8,16},{1,9},{9,17},{2,10},{10,18},{3,11},{11,19},{4,12},{12... | collective-permute-start | bytes 1572872 | tf_op jit(solution)/shard_map/ppermute | solution.py:380
  29.5 0.6 shard_map.77
  30.1 1.3 %collective-permute-start.7 = (bf16[256,1024]{1,0:T(8,128)(2,1)S(1)}, bf16[256,1024]{1,0:T(8,128)(2,1)S(1)}, u32[]{:S(2)}, u32[]{:S(2)}) collective-permute-start(bf16[256,1024]{1,0:T(8,128)(2,1)S(1)} %get-tuple-element.93), channel_id=1, source_target_pairs={{8,0},{9,1},{10,2},{11,3},{12,4},{13,5},{14,6},{15,7}} | collective-permute-start | bytes 1572872 | tf_op jit(solution)/shard_map/ppermute | solution.py:383
  31.4 3.4 %collective-permute-done.9.refs_3_.refs_5_ = bf16[256,1024]{1,0:T(8,128)(2,1)S(1)} collective-permute-done((bf16[256,1024]{1,0:T(8,128)(2,1)S(1)}, bf16[256,1024]{1,0:T(8,128)(2,1)S(1)}, u32[]{:S(2)}, u32[]{:S(2)}) %collective-permute-start.9) | collective-permute-done | bytes 524320 | tf_op jit(solution)/shard_map/ppermute | solution.py:331
  34.8 0.9 %collective-permute-done.8.refs_2_.refs_4_ = bf16[256,1024]{1,0:T(8,128)(2,1)S(1)} collective-permute-done((bf16[256,1024]{1,0:T(8,128)(2,1)S(1)}, bf16[256,1024]{1,0:T(8,128)(2,1)S(1)}, u32[]{:S(2)}, u32[]{:S(2)}) %collective-permute-start.8) | collective-permute-done | bytes 524320 | tf_op jit(solution)/shard_map/ppermute | solution.py:328
  35.7 3.0 %collective-permute-start.11 = (bf16[256,1024]{1,0:T(8,128)(2,1)S(1)}, bf16[256,1024]{1,0:T(8,128)(2,1)S(1)}, u32[]{:S(2)}, u32[]{:S(2)}) collective-permute-start(bf16[256,1024]{1,0:T(8,128)(2,1)S(1)} %collective-permute-done.4.refs_2_.refs_4_), channel_id=1, source_target_pairs={{0,4},{1,5},{2,6},{3,7},{4,0},{5,1},{6,2},{7,3},{8,12},{9,13},{10,... | collective-permute-start | bytes 1572872 | tf_op jit(solution)/shard_map/ppermute | solution.py:331
  38.7 1.4 %collective-permute-start.12 = (bf16[256,1024]{1,0:T(8,128)(2,1)S(1)}, bf16[256,1024]{1,0:T(8,128)(2,1)S(1)}, u32[]{:S(2)}, u32[]{:S(2)}) collective-permute-start(bf16[256,1024]{1,0:T(8,128)(2,1)S(1)} %collective-permute-done.9.refs_3_.refs_5_), channel_id=1, source_target_pairs={{0,2},{1,3},{2,0},{3,1},{4,6},{5,7},{6,4},{7,5},{8,10},{9,11},{10,... | collective-permute-start | bytes 1572872 | tf_op jit(solution)/shard_map/ppermute | solution.py:328
  40.1 7.7 %shard_map.78 = (f32[8,128]{1,0:T(8,128)S(1)}, f32[4,2,1024,384]{3,2,1,0:T(8,128)S(1)}, bf16[4,2,1024,128]{3,2,1,0:T(8,128)(2,1)S(1)}) custom-call(s32[2,4]{1,0:T(2,128)S(1)} %copy-done, s32[4]{0:T(128)S(1)} %copy-done.1, bf16[256,1024]{1,0:T(8,128)(2,1)S(1)} %collective-permute-done.8.refs_2_.refs_4_, ...), custom_call_target="tpu_custom_call", output_to_operand_aliasing={{1}: (7, {}), {2}: (8, {})} | custom-call | flops 4294967296 | bytes 4194304 | tf_op jit(solution)/shard_map/pallas_call | solution.py:301
  47.8 3.6 %collective-permute-done.7.refs_4_ = bf16[256,1024]{1,0:T(8,128)(2,1)S(1)} collective-permute-done((bf16[256,1024]{1,0:T(8,128)(2,1)S(1)}, bf16[256,1024]{1,0:T(8,128)(2,1)S(1)}, u32[]{:S(2)}, u32[]{:S(2)}) %collective-permute-start.7) | collective-permute-done | bytes 524320 | tf_op jit(solution)/shard_map/ppermute | solution.py:383
  51.4 0.8 shard_map.79
  52.2 1.3 %collective-permute-start.14 = (bf16[256,1024]{1,0:T(8,128)(2,1)S(1)}, bf16[256,1024]{1,0:T(8,128)(2,1)S(1)}, u32[]{:S(2)}, u32[]{:S(2)}) collective-permute-start(bf16[256,1024]{1,0:T(8,128)(2,1)S(1)} %get-tuple-element.112.refs_4_.refs_7_), channel_id=1, source_target_pairs={{0,4},{1,5},{2,6},{3,7},{4,0},{5,1},{6,2},{7,3},{8,12},{9,13},{10,... | collective-permute-start | bytes 1572872 | tf_op jit(solution)/shard_map/ppermute | solution.py:331
  53.5 1.5 %collective-permute-start.10 = (bf16[256,1024]{1,0:T(8,128)(2,1)S(1)}, bf16[256,1024]{1,0:T(8,128)(2,1)S(1)}, u32[]{:S(2)}, u32[]{:S(2)}) collective-permute-start(bf16[256,1024]{1,0:T(8,128)(2,1)S(1)} %get-tuple-element.112.refs_4_.refs_7_), channel_id=1, source_target_pairs={{0,2},{1,3},{2,0},{3,1},{4,6},{5,7},{6,4},{7,5},{8,10},{9,11},{10,... | collective-permute-start | bytes 1572872 | tf_op jit(solution)/shard_map/ppermute | solution.py:328
  55.0 10.7 %shard_map.80 = (f32[8,128]{1,0:T(8,128)S(1)}, f32[4,2,1024,384]{3,2,1,0:T(8,128)S(1)}, bf16[4,2,1024,128]{3,2,1,0:T(8,128)(2,1)S(1)}) custom-call(s32[2,4]{1,0:T(2,128)S(1)} %copy-done, s32[4]{0:T(128)S(1)} %copy-done.1, bf16[256,1024]{1,0:T(8,128)(2,1)S(1)} %collective-permute-done.11.refs_2_.refs_5_, ...), custom_call_target="tpu_custom_call", output_to_operand_aliasing={{1}: (9, {}), {2}: (10, {})} | custom-call | flops 6442450944 | bytes 4194304 | tf_op jit(solution)/shard_map/pallas_call | solution.py:301
  65.8 0.6 collective-permute-start.15
  66.4 1.4 %collective-permute-start.13 = (bf16[128,1024]{1,0:T(8,128)(2,1)S(1)}, bf16[128,1024]{1,0:T(8,128)(2,1)S(1)}, u32[]{:S(2)}, u32[]{:S(2)}) collective-permute-start(bf16[128,1024]{1,0:T(8,128)(2,1)S(1)} %slice.22), channel_id=1, source_target_pairs={{0,4},{1,5},{2,6},{3,7},{4,0},{5,1},{6,2},{7,3},{8,12},{9,13},{10,... | collective-permute-start | bytes 786440 | tf_op jit(solution)/shard_map/ppermute | solution.py:331
  67.8 7.7 %shard_map.81 = (f32[8,128]{1,0:T(8,128)S(1)}, f32[4,2,1024,384]{3,2,1,0:T(8,128)S(1)}, bf16[4,2,1024,128]{3,2,1,0:T(8,128)(2,1)S(1)}) custom-call(s32[2,4]{1,0:T(2,128)S(1)} %copy-done, s32[4]{0:T(128)S(1)} %copy-done.1, bf16[256,1024]{1,0:T(8,128)(2,1)S(1)} %collective-permute-done.10.refs_2_.refs_4_, ...), custom_call_target="tpu_custom_call", output_to_operand_aliasing={{1}: (7, {}), {2}: (8, {})} | custom-call | flops 4294967296 | bytes 4194304 | tf_op jit(solution)/shard_map/pallas_call | solution.py:301
  75.6 3.9 %shard_map.82 = (bf16[128,4096]{1,0:T(8,128)(2,1)S(1)}, f32[4,2,1024,384]{3,2,1,0:T(8,128)S(1)}, bf16[4,2,1024,128]{3,2,1,0:T(8,128)(2,1)S(1)}) custom-call(s32[2,4]{1,0:T(2,128)S(1)} %copy-done, s32[4]{0:T(128)S(1)} %copy-done.1, bf16[128,1024]{1,0:T(8,128)(2,1)S(1)} %collective-permute-done.13.refs_2_.refs_4_, ...), custom_call_target="tpu_custom_call", output_to_operand_aliasing={{1}: (7, {}), {2}: (8, {})} | custom-call | flops 1073741824 | bytes 4194304 | tf_op jit(solution)/shard_map/pallas_call | solution.py:301
  79.5 0.1 collective-permute-start.16
  79.6 3.9 %shard_map.83 = (bf16[128,4096]{1,0:T(8,128)(2,1)S(1)}, f32[4,2,1024,384]{3,2,1,0:T(8,128)S(1)}, bf16[4,2,1024,128]{3,2,1,0:T(8,128)(2,1)S(1)}) custom-call(s32[2,4]{1,0:T(2,128)S(1)} %copy-done, s32[4]{0:T(128)S(1)} %copy-done.1, bf16[128,1024]{1,0:T(8,128)(2,1)S(1)} %collective-permute-done.13.refs_2_.refs_4_, ...), custom_call_target="tpu_custom_call", output_to_operand_aliasing={{1}: (7, {}), {2}: (8, {})} | custom-call | flops 1073741824 | bytes 4194304 | tf_op jit(solution)/shard_map/pallas_call | solution.py:301
  83.4 1.3 %shard_map.84 = bf16[128,8192]{1,0:T(8,128)(2,1)} custom-call(bf16[128,4096]{1,0:T(8,128)(2,1)S(1)} %get-tuple-element.127.mine_ref, bf16[128,4096]{1,0:T(8,128)(2,1)S(1)} %collective-permute-done.16.got_ref), custom_call_target="tpu_custom_call" | custom-call | tf_op jit(solution)/shard_map/pallas_call | solution.py:260
  (24 shorter events, 0.2 us)
Async XLA Ops:
  1.4 2.1 %collective-permute-start = (bf16[256,1024]{1,0:T(8,128)(2,1)S(1)}, bf16[256,1024]{1,0:T(8,128)(2,1)S(1)}, u32[]{:S(2)}, u32[]{:S(2)}) collective-permute-start(bf16[256,1024]{1,0:T(8,128)(2,1)S(1)} %get-tuple-element.71), channel_id=1, source_target_pairs={{0,1},{1,0},{2,3},{3,2},{4,5},{5,4},{6,7},{7,6},{8,9},{9,8},{10,11... | collective-permute-start | bytes 1572872 | tf_op jit(solution)/shard_map/ppermute | solution.py:325
  3.5 4.8 %collective-permute-start.1 = (bf16[128,4096]{1,0:T(8,128)(2,1)S(1)}, bf16[128,4096]{1,0:T(8,128)(2,1)S(1)}, u32[]{:S(2)}, u32[]{:S(2)}) collective-permute-start(bf16[128,4096]{1,0:T(8,128)(2,1)S(1)} %get-tuple-element.73), channel_id=1, source_target_pairs={{0,1},{1,0},{2,3},{3,2},{4,5},{5,4},{6,7},{7,6},{8,9},{9,8},{10,11... | collective-permute-start | bytes 3145736 | tf_op jit(solution)/shard_map/ppermute | solution.py:325
  3.8 10.3 %copy-start = (s32[2,4]{1,0:T(2,128)S(1)}, s32[2,4]{1,0:T(2,128)}, u32[]{:S(2)}) copy-start(s32[2,4]{1,0:T(2,128)} %refs_0_.16) | copy-start | bytes 100
  3.8 10.3 %copy-start.1 = (s32[4]{0:T(128)S(1)}, s32[4]{0:T(128)}, u32[]{:S(2)}) copy-start(s32[4]{0:T(128)} %refs_1_.15) | copy-start | bytes 52
  3.9 18.3 %collective-permute-start.5 = (bf16[256,1024]{1,0:T(8,128)(2,1)S(1)}, bf16[256,1024]{1,0:T(8,128)(2,1)S(1)}, u32[]{:S(2)}, u32[]{:S(2)}) collective-permute-start(bf16[256,1024]{1,0:T(8,128)(2,1)S(1)} %pad_maximum_fusion.refs_4_.refs_6_.refs_0_), channel_id=1, source_target_pairs={{0,4},{1,5},{2,6},{3,7},{4,0},{5,1},{6,2},{7,3},{8,12},{9,13},{10,... | collective-permute-start | bytes 1572872 | tf_op jit(solution)/shard_map/ppermute | solution.py:331
  6.7 17.0 %collective-permute-start.4 = (bf16[256,1024]{1,0:T(8,128)(2,1)S(1)}, bf16[256,1024]{1,0:T(8,128)(2,1)S(1)}, u32[]{:S(2)}, u32[]{:S(2)}) collective-permute-start(bf16[256,1024]{1,0:T(8,128)(2,1)S(1)} %pad_maximum_fusion.refs_4_.refs_6_.refs_0_), channel_id=1, source_target_pairs={{0,2},{1,3},{2,0},{3,1},{4,6},{5,7},{6,4},{7,5},{8,10},{9,11},{10,... | collective-permute-start | bytes 1572872 | tf_op jit(solution)/shard_map/ppermute | solution.py:328
  8.3 21.2 %collective-permute-start.3 = (bf16[256,1024]{1,0:T(8,128)(2,1)S(1)}, bf16[256,1024]{1,0:T(8,128)(2,1)S(1)}, u32[]{:S(2)}, u32[]{:S(2)}) collective-permute-start(bf16[256,1024]{1,0:T(8,128)(2,1)S(1)} %pad_maximum_fusion.refs_4_.refs_6_.refs_0_), channel_id=1, source_target_pairs={{0,16},{24,8},{1,17},{25,9},{2,18},{26,10},{3,19},{27,11},{4,20},{... | collective-permute-start | bytes 1572872 | tf_op jit(solution)/shard_map/ppermute | solution.py:360
  12.8 16.7 %collective-permute-start.2 = (bf16[256,1024]{1,0:T(8,128)(2,1)S(1)}, bf16[256,1024]{1,0:T(8,128)(2,1)S(1)}, u32[]{:S(2)}, u32[]{:S(2)}) collective-permute-start(bf16[256,1024]{1,0:T(8,128)(2,1)S(1)} %pad_maximum_fusion.refs_4_.refs_6_.refs_0_), channel_id=1, source_target_pairs={{8,0},{16,8},{24,16},{9,1},{17,9},{25,17},{10,2},{18,10},{26,18},{... | collective-permute-start | bytes 1572872 | tf_op jit(solution)/shard_map/ppermute | solution.py:360
  21.5 13.3 %collective-permute-start.9 = (bf16[256,1024]{1,0:T(8,128)(2,1)S(1)}, bf16[256,1024]{1,0:T(8,128)(2,1)S(1)}, u32[]{:S(2)}, u32[]{:S(2)}) collective-permute-start(bf16[256,1024]{1,0:T(8,128)(2,1)S(1)} %pad_maximum_fusion.1.refs_5_.refs_7_), channel_id=1, source_target_pairs={{0,4},{1,5},{2,6},{3,7},{4,0},{5,1},{6,2},{7,3},{8,12},{9,13},{10,... | collective-permute-start | bytes 1572872 | tf_op jit(solution)/shard_map/ppermute | solution.py:331
  22.2 13.5 %collective-permute-start.8 = (bf16[256,1024]{1,0:T(8,128)(2,1)S(1)}, bf16[256,1024]{1,0:T(8,128)(2,1)S(1)}, u32[]{:S(2)}, u32[]{:S(2)}) collective-permute-start(bf16[256,1024]{1,0:T(8,128)(2,1)S(1)} %pad_maximum_fusion.1.refs_5_.refs_7_), channel_id=1, source_target_pairs={{0,2},{1,3},{2,0},{3,1},{4,6},{5,7},{6,4},{7,5},{8,10},{9,11},{10,... | collective-permute-start | bytes 1572872 | tf_op jit(solution)/shard_map/ppermute | solution.py:328
  24.9 22.9 %collective-permute-start.6 = (bf16[256,1024]{1,0:T(8,128)(2,1)S(1)}, bf16[256,1024]{1,0:T(8,128)(2,1)S(1)}, u32[]{:S(2)}, u32[]{:S(2)}) collective-permute-start(bf16[256,1024]{1,0:T(8,128)(2,1)S(1)} %pad_maximum_fusion.refs_4_.refs_6_.refs_0_), channel_id=1, source_target_pairs={{0,8},{8,16},{1,9},{9,17},{2,10},{10,18},{3,11},{11,19},{4,12},{12... | collective-permute-start | bytes 1572872 | tf_op jit(solution)/shard_map/ppermute | solution.py:380
  30.1 21.3 %collective-permute-start.7 = (bf16[256,1024]{1,0:T(8,128)(2,1)S(1)}, bf16[256,1024]{1,0:T(8,128)(2,1)S(1)}, u32[]{:S(2)}, u32[]{:S(2)}) collective-permute-start(bf16[256,1024]{1,0:T(8,128)(2,1)S(1)} %get-tuple-element.93), channel_id=1, source_target_pairs={{8,0},{9,1},{10,2},{11,3},{12,4},{13,5},{14,6},{15,7}} | collective-permute-start | bytes 1572872 | tf_op jit(solution)/shard_map/ppermute | solution.py:383
  35.7 19.3 %collective-permute-start.11 = (bf16[256,1024]{1,0:T(8,128)(2,1)S(1)}, bf16[256,1024]{1,0:T(8,128)(2,1)S(1)}, u32[]{:S(2)}, u32[]{:S(2)}) collective-permute-start(bf16[256,1024]{1,0:T(8,128)(2,1)S(1)} %collective-permute-done.4.refs_2_.refs_4_), channel_id=1, source_target_pairs={{0,4},{1,5},{2,6},{3,7},{4,0},{5,1},{6,2},{7,3},{8,12},{9,13},{10,... | collective-permute-start | bytes 1572872 | tf_op jit(solution)/shard_map/ppermute | solution.py:331
  38.7 16.3 %collective-permute-start.12 = (bf16[256,1024]{1,0:T(8,128)(2,1)S(1)}, bf16[256,1024]{1,0:T(8,128)(2,1)S(1)}, u32[]{:S(2)}, u32[]{:S(2)}) collective-permute-start(bf16[256,1024]{1,0:T(8,128)(2,1)S(1)} %collective-permute-done.9.refs_3_.refs_5_), channel_id=1, source_target_pairs={{0,2},{1,3},{2,0},{3,1},{4,6},{5,7},{6,4},{7,5},{8,10},{9,11},{10,... | collective-permute-start | bytes 1572872 | tf_op jit(solution)/shard_map/ppermute | solution.py:328
  52.2 13.5 %collective-permute-start.14 = (bf16[256,1024]{1,0:T(8,128)(2,1)S(1)}, bf16[256,1024]{1,0:T(8,128)(2,1)S(1)}, u32[]{:S(2)}, u32[]{:S(2)}) collective-permute-start(bf16[256,1024]{1,0:T(8,128)(2,1)S(1)} %get-tuple-element.112.refs_4_.refs_7_), channel_id=1, source_target_pairs={{0,4},{1,5},{2,6},{3,7},{4,0},{5,1},{6,2},{7,3},{8,12},{9,13},{10,... | collective-permute-start | bytes 1572872 | tf_op jit(solution)/shard_map/ppermute | solution.py:331
  53.5 12.9 %collective-permute-start.10 = (bf16[256,1024]{1,0:T(8,128)(2,1)S(1)}, bf16[256,1024]{1,0:T(8,128)(2,1)S(1)}, u32[]{:S(2)}, u32[]{:S(2)}) collective-permute-start(bf16[256,1024]{1,0:T(8,128)(2,1)S(1)} %get-tuple-element.112.refs_4_.refs_7_), channel_id=1, source_target_pairs={{0,2},{1,3},{2,0},{3,1},{4,6},{5,7},{6,4},{7,5},{8,10},{9,11},{10,... | collective-permute-start | bytes 1572872 | tf_op jit(solution)/shard_map/ppermute | solution.py:328
  65.8 9.8 %collective-permute-start.15 = (bf16[128,1024]{1,0:T(8,128)(2,1)S(1)}, bf16[128,1024]{1,0:T(8,128)(2,1)S(1)}, u32[]{:S(2)}, u32[]{:S(2)}) collective-permute-start(bf16[128,1024]{1,0:T(8,128)(2,1)S(1)} %slice.24), channel_id=1, source_target_pairs={{0,2},{1,3},{2,0},{3,1},{4,6},{5,7},{6,4},{7,5},{8,10},{9,11},{10,... | collective-permute-start | bytes 786440 | tf_op jit(solution)/shard_map/ppermute | solution.py:328
  66.4 9.2 %collective-permute-start.13 = (bf16[128,1024]{1,0:T(8,128)(2,1)S(1)}, bf16[128,1024]{1,0:T(8,128)(2,1)S(1)}, u32[]{:S(2)}, u32[]{:S(2)}) collective-permute-start(bf16[128,1024]{1,0:T(8,128)(2,1)S(1)} %slice.22), channel_id=1, source_target_pairs={{0,4},{1,5},{2,6},{3,7},{4,0},{5,1},{6,2},{7,3},{8,12},{9,13},{10,... | collective-permute-start | bytes 786440 | tf_op jit(solution)/shard_map/ppermute | solution.py:331
  79.5 4.0 %collective-permute-start.16 = (bf16[128,4096]{1,0:T(8,128)(2,1)S(1)}, bf16[128,4096]{1,0:T(8,128)(2,1)S(1)}, u32[]{:S(2)}, u32[]{:S(2)}) collective-permute-start(bf16[128,4096]{1,0:T(8,128)(2,1)S(1)} %get-tuple-element.128), channel_id=1, source_target_pairs={{0,1},{1,0},{2,3},{3,2},{4,5},{5,4},{6,7},{7,6},{8,9},{9,8},{10,11... | collective-permute-start | bytes 3145736 | tf_op jit(solution)/shard_map/ppermute | solution.py:325
